TPU v7x, 32 devices: a whole 2x2x4 slice. The times are simulated.
32 devices in a mesh: dp: 8 (over z, core), mp: 4 (over y, x).
Axes of the slice: x: 2, y: 2, z: 4, core: 2. Of those that a mesh axis runs over, the one named last changes fastest.
Arguments:
- tokens: bfloat16 [4, 10240, 1024], P(None, ('dp', 'mp')), may hold values from -6 to 6
- cotangent: bfloat16 [4, 10240, 1024], P(None, ('dp', 'mp')), may hold values from -6 to 6
- qkv_weight: bfloat16 [1024, 3072], P(None, 'mp'), may hold values from -0.1875 to 0.1875
- out_weight: bfloat16 [1024, 1024], P('mp'), may hold values from -1.5 to 1.5
- up_weight: bfloat16 [1024, 4096], P(None, 'mp'), may hold values from -0.1875 to 0.1875
- down_weight: bfloat16 [4096, 1024], P('mp'), may hold values from -0.25 to 0.25
- ada_weight: bfloat16 [1024, 6144], P(None, 'mp'), may hold values from -0.1875 to 0.1875
- ada_bias: bfloat16 [6144], P('mp'), may hold values from -2 to 2
- rel_bias: float32 [16, 39], P('mp'), may hold values from -3 to 3
- class_table: float32 [101, 1024], replicated, may hold values from -5 to 5
- lengths: int32 [4, 32], P(None, 'dp'), may hold values from 2 to 5, as said below
- timesteps: int32 [4, 32], P(None, 'dp'), may hold values from 0 to 999
- classes: int32 [4, 32], P(None, 'dp'), may hold values from 0 to 100
Outputs:
- output: bfloat16 [4, 10240, 1024], P(None, ('dp', 'mp'))
- tokens_grad: bfloat16 [4, 10240, 1024], P(None, ('dp', 'mp'))
- qkv_grad: float32 [1024, 3072], P(None, 'mp')
- out_grad: float32 [1024, 1024], P('mp')
- up_grad: float32 [1024, 4096], P(None, 'mp')
- down_grad: float32 [4096, 1024], P('mp')
- ada_grad: float32 [1024, 6144], P(None, 'mp')
- ada_bias_grad: float32 [6144], P('mp')
- rel_grad: float32 [16, 39], P('mp')
- class_grad: float32 [101, 1024], replicated
Inputs may be any that keep to these rules, and one draw needn't show every extreme that they name: `lengths`: keys in frames at or after a window's length are masked; each micro-batch has a window of all 5 frames.
All inputs are finite; a program needn't handle non-finite values.
Results may differ from a plain program's by a relative error of at most 0.022.
The roundings to bfloat16 on the way count: a program that leaves them out, or rounds other values in their place, can miss the bound.
Values may be sent and summed in bfloat16 or wider, within the bound.
No kernel may reach another device: no remote copies, remote signals or barrier semaphores. Data moves between devices by JAX's collectives and lax.ppermute only.
A program may use at most 384 MiB of HBM per device.

v0:
```python
from functools import partial
import math

import jax
import jax.numpy as jnp
from jax import lax
from jax.sharding import PartitionSpec as P

HD = 64
WT = 5
WH = 8
WW = 8
WIN_TOK = 320


EPS = 1e-06
precise = lax.Precision.HIGHEST


def layer_norm(values):
    center = values - jnp.mean(values, axis=-1, keepdims=True)
    spread = jnp.mean(center * center, axis=-1, keepdims=True)
    return center * lax.rsqrt(spread + EPS)


def modulate(values, shift, scale):
    return layer_norm(values) * (1.0 + scale) + shift


def gelu_tanh(values):
    return (
        0.5
        * values
        * (
            1.0
            + jnp.tanh(math.sqrt(2.0 / math.pi) * (values + 0.044715 * values * values * values))
        )
    )


def silu_plain(values):
    return values / (1.0 + jnp.exp(-values))


def condition(timesteps, classes, class_table):
    half_width = class_table.shape[1] // 2
    frequency = jnp.exp(
        -math.log(10000.0) * jnp.arange(half_width).astype(class_table.dtype) / half_width
    )
    phase_angle = timesteps.astype(class_table.dtype)[..., None] * frequency
    sinusoid = jnp.concatenate([jnp.cos(phase_angle), jnp.sin(phase_angle)], axis=-1)
    onehot = (classes[..., None] == jnp.arange(class_table.shape[0])[None, None, :]).astype(
        class_table.dtype
    )
    lookup = jnp.einsum("mwc,cd->mwd", onehot, class_table, precision=precise)
    return silu_plain(sinusoid + lookup)


def axis_table(rel_part, window_span):
    places = jnp.arange(window_span)
    offsets = places[:, None] - places[None, :] + window_span - 1
    onehot = (offsets[:, :, None] == jnp.arange(2 * window_span - 1)[None, None, :]).astype(
        rel_part.dtype
    )
    return jnp.einsum("hr,abr->hab", rel_part, onehot, precision=precise)


def window_bias(rel_bias):
    frame_part = axis_table(rel_bias[:, : 2 * WT - 1], WT)
    row_part = axis_table(rel_bias[:, 2 * WT - 1 : 2 * WT + 2 * WH - 2], WH)
    column_part = axis_table(rel_bias[:, 2 * WT + 2 * WH - 2 :], WW)
    full_bias = (
        frame_part[:, :, None, None, :, None, None]
        + row_part[:, None, :, None, None, :, None]
        + column_part[:, None, None, :, None, None, :]
    )
    return full_bias.reshape(rel_bias.shape[0], WIN_TOK, WIN_TOK)


def attention_scores(query_part, key_part, bias_full, masks):
    scores = (
        jnp.einsum("wqhd,wkhd->whqk", query_part, key_part, preferred_element_type=jnp.float32)
        * HD ** (-0.5)
        + bias_full[None]
    )
    return jnp.where(masks[:, None, None, :], scores, -1e30)


def local(
    tokens,
    cotangent,
    qkv_weight,
    out_weight,
    up_weight,
    down_weight,
    ada_weight,
    ada_bias,
    rel_bias,
    class_table,
    lengths,
    timesteps,
    classes,
):
    micro_count = tokens.shape[0]
    row_count = tokens.shape[1]
    win_count = lengths.shape[1]
    heads_here = rel_bias.shape[0]
    head_scale = HD ** (-0.5)
    first_row = lax.axis_index("mp") * row_count
    row_window = (first_row + jnp.arange(row_count)) // WIN_TOK
    spread_rows = (row_window[:, None] == jnp.arange(win_count)[None, :]).astype(jnp.float32)
    cond_low = condition(timesteps, classes, class_table).astype(jnp.bfloat16)
    mode_cols = jnp.einsum(
        "mwd,de->mwe", cond_low, ada_weight, preferred_element_type=jnp.float32
    ) + ada_bias.astype(jnp.float32)
    mode_all = lax.all_gather(mode_cols, "mp", axis=2, tiled=True)
    bias_full, bias_pull = jax.vjp(window_bias, rel_bias)
    frame_of = jnp.arange(WIN_TOK) // (WH * WW)
    grad_qkv = jnp.zeros(qkv_weight.shape, jnp.float32)
    grad_out = jnp.zeros(out_weight.shape, jnp.float32)
    grad_up = jnp.zeros(up_weight.shape, jnp.float32)
    grad_down = jnp.zeros(down_weight.shape, jnp.float32)
    grad_rel = jnp.zeros(rel_bias.shape, jnp.float32)
    mode_parts = []
    outputs = []
    token_grads = []
    for micro_step in range(micro_count):
        mode_rows = jnp.dot(spread_rows, mode_all[micro_step], precision=precise)
        shift_attn, scale_attn, gate_attn, shift_mlp, scale_mlp, gate_mlp = jnp.split(
            mode_rows, 6, axis=1
        )
        inputs = tokens[micro_step].astype(jnp.float32)
        normed_one, pull_one = jax.vjp(modulate, inputs, shift_attn, scale_attn)
        gathered_one = lax.all_gather(normed_one.astype(jnp.bfloat16), "mp", axis=0, tiled=True)
        packed = jnp.dot(gathered_one, qkv_weight, preferred_element_type=jnp.float32).astype(
            jnp.bfloat16
        )
        packed = packed.reshape(win_count, WIN_TOK, heads_here, 3, HD)
        query_part = packed[:, :, :, 0]
        key_part = packed[:, :, :, 1]
        value_part = packed[:, :, :, 2]
        masks = frame_of[None, :] < lengths[micro_step][:, None]
        scores = attention_scores(query_part, key_part, bias_full, masks)
        top_score = jnp.max(scores, axis=-1, keepdims=True)
        expo = jnp.exp(scores - top_score)
        total = jnp.sum(expo, axis=-1, keepdims=True)
        log_total = top_score + jnp.log(total)
        probs_low = (expo / total).astype(jnp.bfloat16)
        heads_out = jnp.einsum(
            "whqk,wkhd->wqhd", probs_low, value_part, preferred_element_type=jnp.float32
        ).astype(jnp.bfloat16)
        heads_out = heads_out.reshape(win_count * WIN_TOK, heads_here * HD)
        attn_out = lax.psum_scatter(
            jnp.dot(heads_out, out_weight, preferred_element_type=jnp.float32),
            "mp",
            scatter_dimension=0,
            tiled=True,
        )
        middle = inputs + gate_attn * attn_out
        normed_two, pull_two = jax.vjp(modulate, middle, shift_mlp, scale_mlp)
        grad_y = cotangent[micro_step].astype(jnp.float32)
        down_in = (gate_mlp * grad_y).astype(jnp.bfloat16)
        gathered_two = lax.all_gather(normed_two.astype(jnp.bfloat16), "mp", axis=0, tiled=True)
        hidden_pre = jnp.dot(gathered_two, up_weight, preferred_element_type=jnp.float32)
        hidden_low, gelu_pull = jax.vjp(gelu_tanh, hidden_pre)
        hidden_low = hidden_low.astype(jnp.bfloat16)
        mlp_out = lax.psum_scatter(
            jnp.dot(hidden_low, down_weight, preferred_element_type=jnp.float32),
            "mp",
            scatter_dimension=0,
            tiled=True,
        )
        down_all = lax.all_gather(down_in, "mp", axis=0, tiled=True)
        hidden_grad = jnp.einsum(
            "rd,fd->rf", down_all, down_weight, preferred_element_type=jnp.float32
        )
        micro_down = jnp.einsum(
            "rf,rd->fd", hidden_low, down_all, preferred_element_type=jnp.float32
        )
        pre_low = gelu_pull(hidden_grad)[0].astype(jnp.bfloat16)
        micro_up = jnp.einsum(
            "rd,rf->df", gathered_two, pre_low, preferred_element_type=jnp.float32
        )
        normed_two_grad = lax.psum_scatter(
            jnp.einsum("rf,df->rd", pre_low, up_weight, preferred_element_type=jnp.float32),
            "mp",
            scatter_dimension=0,
            tiled=True,
        )
        outputs.append(middle + gate_mlp * mlp_out)
        grad_gate_mlp = grad_y * mlp_out
        resid_grad, grad_shift_mlp, grad_scale_mlp = pull_two(normed_two_grad)
        middle_grad = grad_y + resid_grad
        grad_gate_attn = middle_grad * attn_out
        out_in = (gate_attn * middle_grad).astype(jnp.bfloat16)
        out_all = lax.all_gather(out_in, "mp", axis=0, tiled=True)
        micro_out = jnp.einsum("rc,rd->cd", heads_out, out_all, preferred_element_type=jnp.float32)
        heads_grad = jnp.einsum(
            "rd,cd->rc", out_all, out_weight, preferred_element_type=jnp.float32
        ).astype(jnp.bfloat16)
        heads_grad = heads_grad.reshape(win_count, WIN_TOK, heads_here, HD)
        probs = jnp.exp(attention_scores(query_part, key_part, bias_full, masks) - log_total)
        probs_low = probs.astype(jnp.bfloat16)
        value_grad = jnp.einsum(
            "whqk,wqhd->wkhd", probs_low, heads_grad, preferred_element_type=jnp.float32
        )
        probs_grad = jnp.einsum(
            "wqhd,wkhd->whqk", heads_grad, value_part, preferred_element_type=jnp.float32
        )
        score_grad = probs * (probs_grad - jnp.sum(probs * probs_grad, axis=-1, keepdims=True))
        micro_rel = bias_pull(jnp.sum(score_grad, axis=0))[0]
        score_low = (score_grad * head_scale).astype(jnp.bfloat16)
        query_grad = jnp.einsum(
            "whqk,wkhd->wqhd", score_low, key_part, preferred_element_type=jnp.float32
        )
        key_grad = jnp.einsum(
            "whqk,wqhd->wkhd", score_low, query_part, preferred_element_type=jnp.float32
        )
        packed_grad = jnp.stack([query_grad, key_grad, value_grad], axis=3).astype(jnp.bfloat16)
        packed_grad = packed_grad.reshape(win_count * WIN_TOK, heads_here * 3 * HD)
        micro_qkv = jnp.einsum(
            "rd,rc->dc", gathered_one, packed_grad, preferred_element_type=jnp.float32
        )
        normed_one_grad = lax.psum_scatter(
            jnp.einsum("rc,dc->rd", packed_grad, qkv_weight, preferred_element_type=jnp.float32),
            "mp",
            scatter_dimension=0,
            tiled=True,
        )
        input_grad, grad_shift_attn, grad_scale_attn = pull_one(normed_one_grad)
        token_grads.append(middle_grad + input_grad)
        row_modes = jnp.concatenate(
            [
                grad_shift_attn,
                grad_scale_attn,
                grad_gate_attn,
                grad_shift_mlp,
                grad_scale_mlp,
                grad_gate_mlp,
            ],
            axis=1,
        )
        mode_parts.append(jnp.einsum("rw,re->we", spread_rows, row_modes, precision=precise))
        local_grads = (micro_qkv, micro_out, micro_rel, micro_up, micro_down)
        grad_qkv = grad_qkv + local_grads[0]
        grad_out = grad_out + local_grads[1]
        grad_rel = grad_rel + local_grads[2]
        grad_up = grad_up + local_grads[3]
        grad_down = grad_down + local_grads[4]
    mode_grad_cols = lax.psum_scatter(jnp.stack(mode_parts), "mp", scatter_dimension=2, tiled=True)
    mode_low = mode_grad_cols.astype(jnp.bfloat16)
    grad_ada = jnp.einsum("mwd,mwe->de", cond_low, mode_low, preferred_element_type=jnp.float32)
    grad_ada_bias = jnp.sum(mode_grad_cols, axis=(0, 1))
    cond_grad = jnp.einsum("mwe,de->mwd", mode_low, ada_weight, preferred_element_type=jnp.float32)
    cond_value, cond_pull = jax.vjp(partial(condition, timesteps, classes), class_table)
    class_total = lax.psum(cond_pull(cond_grad)[0], ("dp", "mp"))
    grad_qkv, grad_out, grad_up, grad_down, grad_rel, grad_ada, grad_ada_bias = lax.psum(
        (grad_qkv, grad_out, grad_up, grad_down, grad_rel, grad_ada, grad_ada_bias), "dp"
    )
    return (
        jnp.stack(outputs).astype(jnp.bfloat16),
        jnp.stack(token_grads).astype(jnp.bfloat16),
        grad_qkv,
        grad_out,
        grad_up,
        grad_down,
        grad_ada,
        grad_ada_bias,
        grad_rel,
        class_total,
    )


def solution(mesh):
    in_specs = (
        P(None, ("dp", "mp"), None),
        P(None, ("dp", "mp"), None),
        P(None, "mp"),
        P("mp", None),
        P(None, "mp"),
        P("mp", None),
        P(None, "mp"),
        P("mp"),
        P("mp", None),
        P(),
        P(None, "dp"),
        P(None, "dp"),
        P(None, "dp"),
    )
    out_specs = (
        P(None, ("dp", "mp"), None),
        P(None, ("dp", "mp"), None),
        P(None, "mp"),
        P("mp", None),
        P(None, "mp"),
        P("mp", None),
        P(None, "mp"),
        P("mp"),
        P("mp", None),
        P(),
    )
    return jax.shard_map(local, mesh=mesh, in_specs=in_specs, out_specs=out_specs, check_vma=False)
```

profile of v0, /device:TPU:0, one launch (start us, length us, event | category | flops | bytes accessed | tf_op | source)
XLA Modules:
  0.0 2438.6 jit_solution(8344611584937103817)
XLA Ops:
  11.1 11.0 all_gather.51
  47.5 11.6 broadcast_add_fusion
  59.1 16.9 add.505
  109.9 9.1 all-gather.29.cloned.1.call-done
  200.2 25.2 %reduce-scatter.28.cloned.1.call-done = f32[320,1024]{1,0:T(8,128)} async-done(((f32[1280,1024]{1,0:T(8,128)}), f32[320,1024]{1,0:T(8,128)}) %reduce-scatter.28.cloned.1.call-update) | async-done | bytes 1310736 | tf_op jit(solution)/shard_map/reduce_scatter | solution.py:153
  225.4 64.3 %reduce-scatter.32.cloned.1.call-done = f32[320,1024]{1,0:T(8,128)} async-done(((f32[1280,1024]{1,0:T(8,128)}), f32[320,1024]{1,0:T(8,128)}) %reduce-scatter.32.cloned.1.call-update) | async-done | bytes 1310736 | tf_op jit(solution)/shard_map/reduce_scatter | solution.py:153
  289.7 64.8 %reduce-scatter.20.cloned.1.call-done = f32[320,1024]{1,0:T(8,128)} async-done(((f32[1280,1024]{1,0:T(8,128)}), f32[320,1024]{1,0:T(8,128)}) %reduce-scatter.20.cloned.1.call-update) | async-done | bytes 1310736 | tf_op jit(solution)/shard_map/reduce_scatter | solution.py:153
  362.2 39.6 %all-gather.21.cloned.1.call-done = bf16[1280,1024]{1,0:T(8,128)(2,1)} async-done(((bf16[320,1024]{1,0:T(8,128)(2,1)}), bf16[1280,1024]{1,0:T(8,128)(2,1)}) %all-gather.21.cloned.1.call-update) | async-done | bytes 2621456 | tf_op jit(solution)/shard_map/all_gather | solution.py:134
  447.6 48.5 %reduce-scatter.24.cloned.1.call-done = f32[320,1024]{1,0:T(8,128)} async-done(((f32[1280,1024]{1,0:T(8,128)}), f32[320,1024]{1,0:T(8,128)}) %reduce-scatter.24.cloned.1.call-update) | async-done | bytes 1310736 | tf_op jit(solution)/shard_map/reduce_scatter | solution.py:153
  505.8 31.9 %all-gather.33.cloned.1.call-done = bf16[1280,1024]{1,0:T(8,128)(2,1)} async-done(((bf16[320,1024]{1,0:T(8,128)(2,1)}), bf16[1280,1024]{1,0:T(8,128)(2,1)}) %all-gather.33.cloned.1.call-update) | async-done | bytes 2621456 | tf_op jit(solution)/shard_map/all_gather | solution.py:173
  545.3 34.3 %all-gather.19.cloned.1.call-done = bf16[1280,1024]{1,0:T(8,128)(2,1)} async-done(((bf16[320,1024]{1,0:T(8,128)(2,1)}), bf16[1280,1024]{1,0:T(8,128)(2,1)}) %all-gather.19.cloned.1.call-update) | async-done | bytes 2621456 | tf_op jit(solution)/shard_map/all_gather | solution.py:163
  579.6 11.3 fusion.15
  606.4 15.3 all-gather.41.cloned.1.call-done
  629.3 33.7 %all-gather.27.cloned.1.call-done = bf16[1280,1024]{1,0:T(8,128)(2,1)} async-done(((bf16[320,1024]{1,0:T(8,128)(2,1)}), bf16[1280,1024]{1,0:T(8,128)(2,1)}) %all-gather.27.cloned.1.call-update) | async-done | bytes 2621456 | tf_op jit(solution)/shard_map/all_gather | solution.py:163
  663.0 11.3 fusion.23
  689.6 15.5 all-gather.37.cloned.1.call-done
  712.8 34.3 %all-gather.23.cloned.1.call-done = bf16[1280,1024]{1,0:T(8,128)(2,1)} async-done(((bf16[320,1024]{1,0:T(8,128)(2,1)}), bf16[1280,1024]{1,0:T(8,128)(2,1)}) %all-gather.23.cloned.1.call-update) | async-done | bytes 2621456 | tf_op jit(solution)/shard_map/all_gather | solution.py:163
  747.1 11.3 fusion.19
  773.9 15.1 all-gather.45.cloned.1.call-done
  796.7 34.3 %all-gather.31.cloned.1.call-done = bf16[1280,1024]{1,0:T(8,128)(2,1)} async-done(((bf16[320,1024]{1,0:T(8,128)(2,1)}), bf16[1280,1024]{1,0:T(8,128)(2,1)}) %all-gather.31.cloned.1.call-update) | async-done | bytes 2621456 | tf_op jit(solution)/shard_map/all_gather | solution.py:163
  831.0 11.2 fusion.27
  857.6 37.7 %reduce-scatter.36.cloned.1.call-done = f32[320,1024]{1,0:T(8,128)} async-done(((f32[1280,1024]{1,0:T(8,128)}), f32[320,1024]{1,0:T(8,128)}) %reduce-scatter.36.cloned.1.call-update) | async-done | bytes 1310736 | tf_op jit(solution)/shard_map/reduce_scatter | solution.py:184
  897.7 61.8 %reduce-scatter.22.cloned.1.call-done = f32[320,1024]{1,0:T(8,128)} async-done(((f32[1280,1024]{1,0:T(8,128)}), f32[320,1024]{1,0:T(8,128)}) %reduce-scatter.22.cloned.1.call-update) | async-done | bytes 1310736 | tf_op jit(solution)/shard_map/reduce_scatter | solution.py:167
  964.3 59.7 %reduce-scatter.44.cloned.1.call-done = f32[320,1024]{1,0:T(8,128)} async-done(((f32[1280,1024]{1,0:T(8,128)}), f32[320,1024]{1,0:T(8,128)}) %reduce-scatter.44.cloned.1.call-update) | async-done | bytes 1310736 | tf_op jit(solution)/shard_map/reduce_scatter | solution.py:184
  1026.5 61.8 %reduce-scatter.30.cloned.1.call-done = f32[320,1024]{1,0:T(8,128)} async-done(((f32[1280,1024]{1,0:T(8,128)}), f32[320,1024]{1,0:T(8,128)}) %reduce-scatter.30.cloned.1.call-update) | async-done | bytes 1310736 | tf_op jit(solution)/shard_map/reduce_scatter | solution.py:167
  1093.0 59.7 %reduce-scatter.40.cloned.1.call-done = f32[320,1024]{1,0:T(8,128)} async-done(((f32[1280,1024]{1,0:T(8,128)}), f32[320,1024]{1,0:T(8,128)}) %reduce-scatter.40.cloned.1.call-update) | async-done | bytes 1310736 | tf_op jit(solution)/shard_map/reduce_scatter | solution.py:184
  1155.2 62.0 %reduce-scatter.26.cloned.1.call-done = f32[320,1024]{1,0:T(8,128)} async-done(((f32[1280,1024]{1,0:T(8,128)}), f32[320,1024]{1,0:T(8,128)}) %reduce-scatter.26.cloned.1.call-update) | async-done | bytes 1310736 | tf_op jit(solution)/shard_map/reduce_scatter | solution.py:167
  1221.9 59.7 %reduce-scatter.48.cloned.1.call-done = f32[320,1024]{1,0:T(8,128)} async-done(((f32[1280,1024]{1,0:T(8,128)}), f32[320,1024]{1,0:T(8,128)}) %reduce-scatter.48.cloned.1.call-update) | async-done | bytes 1310736 | tf_op jit(solution)/shard_map/reduce_scatter | solution.py:184
  1284.1 61.8 %reduce-scatter.34.cloned.1.call-done = f32[320,1024]{1,0:T(8,128)} async-done(((f32[1280,1024]{1,0:T(8,128)}), f32[320,1024]{1,0:T(8,128)}) %reduce-scatter.34.cloned.1.call-update) | async-done | bytes 1310736 | tf_op jit(solution)/shard_map/reduce_scatter | solution.py:167
  1357.0 37.8 %all-gather.47.cloned.1.call-done = bf16[1280,1024]{1,0:T(8,128)(2,1)} async-done(((bf16[320,1024]{1,0:T(8,128)(2,1)}), bf16[1280,1024]{1,0:T(8,128)(2,1)}) %all-gather.47.cloned.1.call-update) | async-done | bytes 2621456 | tf_op jit(solution)/shard_map/all_gather | solution.py:196
  1404.8 13.1 fusion.329
  1454.6 13.2 fusion.330
  1504.0 13.0 fusion.331
  1552.9 13.3 fusion.332
  1624.2 10.2 add_add_fusion
  1655.2 57.0 %reduce-scatter.42.cloned.1.call-done = f32[320,1024]{1,0:T(8,128)} async-done(((f32[1280,1024]{1,0:T(8,128)}), f32[320,1024]{1,0:T(8,128)}) %reduce-scatter.42.cloned.1.call-update) | async-done | bytes 1310736 | tf_op jit(solution)/shard_map/reduce_scatter | solution.py:224
  1712.2 64.4 %reduce-scatter.38.cloned.1.call-done = f32[320,1024]{1,0:T(8,128)} async-done(((f32[1280,1024]{1,0:T(8,128)}), f32[320,1024]{1,0:T(8,128)}) %reduce-scatter.38.cloned.1.call-update) | async-done | bytes 1310736 | tf_op jit(solution)/shard_map/reduce_scatter | solution.py:224
  1846.2 10.3 reshape.620
  1865.6 35.0 %reduce-scatter.52.cloned.1.call-done = f32[1536,16]{1,0:T(8,128)} async-done(((f32[6144,16]{1,0:T(8,128)}), f32[1536,16]{1,0:T(8,128)}) %reduce-scatter.52.cloned.1.call-update) | async-done | bytes 98320
  1917.0 15.3 reshape.596
  1932.3 15.1 reshape.595
  1947.4 20.3 fusion.303
  1968.2 15.2 reshape.594
  1983.3 15.0 reshape.593
  1998.3 20.2 fusion.301
  2025.4 11.5 bitcast_reduce_fusion
  2036.9 29.4 %all-reduce.12 = (f32[1536]{0:T(1024)}, f32[4,39]{1,0:T(4,128)}) all-reduce(f32[1536]{0:T(1024)S(1)} %bitcast_reduce_fusion, f32[4,39]{1,0:T(4,128)S(1)} %add_add_fusion.11), channel_id=1, replica_groups=mesh['dp'=8,'mp'=4] {'dp'}, use_global_device_ids=true, to_apply=%region_67.68 | all-reduce | flops 1692 | bytes 13536 | tf_op jit(solution)/shard_map/psum | solution.py:257
  2066.3 349.9 %all-reduce.19.cloned.1.call-done = (f32[1024,768]{1,0:T(8,128)}, f32[256,1024]{1,0:T(8,128)}, f32[1024,1024]{1,0:T(8,128)}, f32[1024,1024]{1,0:T(8,128)}, f32[1024,1536]{1,0:T(8,128)}) async-done(((f32[1024,768]{1,0:T(8,128)}, f32[256,1024]{1,0:T(8,128)}, f32[1024,1024]{1,0:T(8,128)}, f32[1024,1024]{1,0:T(8,128)}, f32[1024,1536]{1,0:T(8,128)}), (f32[1024,768]{1,0:T(8,128)}, f32[256,1024]{1,0:T(8,128)}, ...) | async-done | bytes 18874384 | tf_op jit(solution)/shard_map/psum | solution.py:257
  (731 shorter events, 648.2 us)
Async XLA Ops:
  7.2 69.7 %all-gather.25.cloned.1.call-start = ((), (), s32[]{:S(2)}) async-start(), calls=%async_computation.25 | async-start | bytes 3276800 | tf_op jit(solution)/shard_map/all_gather | solution.py:134
  7.3 187.4 %copy-start.84 = (s32[320]{0:T(512)}, s32[320]{0:T(512)S(1)}, u32[]{:S(2)}) copy-start(s32[320]{0:T(512)S(1)} %add_select_fusion.5) | copy-start | bytes 3844
  32.8 321.8 %copy-start.117 = (f32[320]{0:T(512)}, f32[320]{0:T(512)S(1)}, u32[]{:S(2)}) copy-start(f32[320]{0:T(512)S(1)} %broadcast_multiply_fusion.5) | copy-start | bytes 3844
  36.8 82.2 %all-gather.29.cloned.1.call-start = ((), (), s32[]{:S(2)}) async-start(), calls=%async_computation.29 | async-start | bytes 3276800 | tf_op jit(solution)/shard_map/all_gather | solution.py:134
  37.6 123.5 %all-gather.17.cloned.1.call-start = ((), (), s32[]{:S(2)}) async-start(), calls=%async_computation.17 | async-start | bytes 3276800 | tf_op jit(solution)/shard_map/all_gather | solution.py:134
  38.3 187.1 %reduce-scatter.28.cloned.1.call-start = ((), (), s32[]{:S(2)}) async-start(), calls=%async_computation.26 | async-start | bytes 6553600 | tf_op jit(solution)/shard_map/reduce_scatter | solution.py:153
  109.7 180.0 %reduce-scatter.32.cloned.1.call-start = ((), (), s32[]{:S(2)}) async-start(), calls=%async_computation.30 | async-start | bytes 6553600 | tf_op jit(solution)/shard_map/reduce_scatter | solution.py:153
  151.8 202.7 %reduce-scatter.20.cloned.1.call-start = ((), (), s32[]{:S(2)}) async-start(), calls=%async_computation.18 | async-start | bytes 6553600 | tf_op jit(solution)/shard_map/reduce_scatter | solution.py:153
  194.0 207.8 %all-gather.21.cloned.1.call-start = ((), (), s32[]{:S(2)}) async-start(), calls=%async_computation.21 | async-start | bytes 3276800 | tf_op jit(solution)/shard_map/all_gather | solution.py:134
  194.7 159.8 %copy-start.137 = (f32[320]{0:T(512)}, f32[320]{0:T(512)S(1)}, u32[]{:S(2)}) copy-start(f32[320]{0:T(512)S(1)} %fusion.277) | copy-start | bytes 3844
  362.0 134.1 %reduce-scatter.24.cloned.1.call-start = ((), (), s32[]{:S(2)}) async-start(), calls=%async_computation.22 | async-start | bytes 6553600 | tf_op jit(solution)/shard_map/reduce_scatter | solution.py:153
  434.5 103.1 %all-gather.33.cloned.1.call-start = ((), (), s32[]{:S(2)}) async-start(), calls=%async_computation.33 | async-start | bytes 3276800 | tf_op jit(solution)/shard_map/all_gather | solution.py:173
  434.6 653.7 %copy-start.105 = (f32[320]{0:T(512)}, f32[320]{0:T(512)S(1)}, u32[]{:S(2)}) copy-start(f32[320]{0:T(512)S(1)} %broadcast_multiply_fusion.2) | copy-start | bytes 3844
  436.4 523.2 %copy-start.107 = (f32[320]{0:T(512)}, f32[320]{0:T(512)S(1)}, u32[]{:S(2)}) copy-start(f32[320]{0:T(512)S(1)} %broadcast_multiply_fusion.6) | copy-start | bytes 3844
  438.0 650.3 %copy-start.123 = (f32[320]{0:T(512)}, f32[320]{0:T(512)S(1)}, u32[]{:S(2)}) copy-start(f32[320]{0:T(512)S(1)} %fusion.280) | copy-start | bytes 3844
  438.1 521.5 %copy-start.125 = (f32[320]{0:T(512)}, f32[320]{0:T(512)S(1)}, u32[]{:S(2)}) copy-start(f32[320]{0:T(512)S(1)} %fusion.276) | copy-start | bytes 3844
  444.0 135.5 %all-gather.19.cloned.1.call-start = ((), (), s32[]{:S(2)}) async-start(), calls=%async_computation.19 | async-start | bytes 3276800 | tf_op jit(solution)/shard_map/all_gather | solution.py:163
  444.6 177.0 %all-gather.41.cloned.1.call-start = ((), (), s32[]{:S(2)}) async-start(), calls=%async_computation.41 | async-start | bytes 3276800 | tf_op jit(solution)/shard_map/all_gather | solution.py:173
  445.4 217.7 %all-gather.27.cloned.1.call-start = ((), (), s32[]{:S(2)}) async-start(), calls=%async_computation.27 | async-start | bytes 3276800 | tf_op jit(solution)/shard_map/all_gather | solution.py:163
  445.9 259.2 %all-gather.37.cloned.1.call-start = ((), (), s32[]{:S(2)}) async-start(), calls=%async_computation.37 | async-start | bytes 3276800 | tf_op jit(solution)/shard_map/all_gather | solution.py:173
  446.0 899.9 %copy-start.109 = (f32[320]{0:T(512)}, f32[320]{0:T(512)S(1)}, u32[]{:S(2)}) copy-start(f32[320]{0:T(512)S(1)} %broadcast_multiply_fusion) | copy-start | bytes 3844
  447.6 898.3 %copy-start.127 = (f32[320]{0:T(512)}, f32[320]{0:T(512)S(1)}, u32[]{:S(2)}) copy-start(f32[320]{0:T(512)S(1)} %fusion.282) | copy-start | bytes 3844
  498.4 718.7 %copy-start.111 = (f32[320]{0:T(512)}, f32[320]{0:T(512)S(1)}, u32[]{:S(2)}) copy-start(f32[320]{0:T(512)S(1)} %broadcast_multiply_fusion.4) | copy-start | bytes 3844
  499.3 717.9 %copy-start.129 = (f32[320]{0:T(512)}, f32[320]{0:T(512)S(1)}, u32[]{:S(2)}) copy-start(f32[320]{0:T(512)S(1)} %fusion.278) | copy-start | bytes 3844
  504.0 243.1 %all-gather.23.cloned.1.call-start = ((), (), s32[]{:S(2)}) async-start(), calls=%async_computation.23 | async-start | bytes 3276800 | tf_op jit(solution)/shard_map/all_gather | solution.py:163
  504.6 284.4 %all-gather.45.cloned.1.call-start = ((), (), s32[]{:S(2)}) async-start(), calls=%async_computation.45 | async-start | bytes 3276800 | tf_op jit(solution)/shard_map/all_gather | solution.py:173
  505.2 325.8 %all-gather.31.cloned.1.call-start = ((), (), s32[]{:S(2)}) async-start(), calls=%async_computation.31 | async-start | bytes 3276800 | tf_op jit(solution)/shard_map/all_gather | solution.py:163
  505.7 389.5 %reduce-scatter.36.cloned.1.call-start = ((), (), s32[]{:S(2)}) async-start(), calls=%async_computation.34 | async-start | bytes 6553600 | tf_op jit(solution)/shard_map/reduce_scatter | solution.py:184
  597.1 362.4 %reduce-scatter.22.cloned.1.call-start = ((), (), s32[]{:S(2)}) async-start(), calls=%async_computation.20 | async-start | bytes 6553600 | tf_op jit(solution)/shard_map/reduce_scatter | solution.py:167
  605.9 418.1 %reduce-scatter.44.cloned.1.call-start = ((), (), s32[]{:S(2)}) async-start(), calls=%async_computation.42 | async-start | bytes 6553600 | tf_op jit(solution)/shard_map/reduce_scatter | solution.py:184
  680.6 407.7 %reduce-scatter.30.cloned.1.call-start = ((), (), s32[]{:S(2)}) async-start(), calls=%async_computation.28 | async-start | bytes 6553600 | tf_op jit(solution)/shard_map/reduce_scatter | solution.py:167
  689.4 463.3 %reduce-scatter.40.cloned.1.call-start = ((), (), s32[]{:S(2)}) async-start(), calls=%async_computation.38 | async-start | bytes 6553600 | tf_op jit(solution)/shard_map/reduce_scatter | solution.py:184
  764.6 452.6 %reduce-scatter.26.cloned.1.call-start = ((), (), s32[]{:S(2)}) async-start(), calls=%async_computation.24 | async-start | bytes 6553600 | tf_op jit(solution)/shard_map/reduce_scatter | solution.py:167
  773.5 508.1 %reduce-scatter.48.cloned.1.call-start = ((), (), s32[]{:S(2)}) async-start(), calls=%async_computation.46 | async-start | bytes 6553600 | tf_op jit(solution)/shard_map/reduce_scatter | solution.py:184
  848.5 497.4 %reduce-scatter.34.cloned.1.call-start = ((), (), s32[]{:S(2)}) async-start(), calls=%async_computation.32 | async-start | bytes 6553600 | tf_op jit(solution)/shard_map/reduce_scatter | solution.py:167
  857.5 537.2 %all-gather.47.cloned.1.call-start = ((), (), s32[]{:S(2)}) async-start(), calls=%async_computation.47 | async-start | bytes 3276800 | tf_op jit(solution)/shard_map/all_gather | solution.py:196
  964.3 386.1 %copy-start.139 = (f32[320]{0:T(512)}, f32[320]{0:T(512)S(1)}, u32[]{:S(2)}) copy-start(f32[320]{0:T(512)S(1)} %negate_multiply_fusion.7) | copy-start | bytes 3844
  1093.0 257.4 %copy-start.141 = (f32[320]{0:T(512)}, f32[320]{0:T(512)S(1)}, u32[]{:S(2)}) copy-start(f32[320]{0:T(512)S(1)} %negate_multiply_fusion.3) | copy-start | bytes 3844
  1355.0 89.1 %all-gather.43.cloned.1.call-start = ((), (), s32[]{:S(2)}) async-start(), calls=%async_computation.43 | async-start | bytes 3276800 | tf_op jit(solution)/shard_map/all_gather | solution.py:196
  1355.6 138.4 %all-gather.39.cloned.1.call-start = ((), (), s32[]{:S(2)}) async-start(), calls=%async_computation.39 | async-start | bytes 3276800 | tf_op jit(solution)/shard_map/all_gather | solution.py:196
  1356.2 186.8 %all-gather.35.cloned.1.call-start = ((), (), s32[]{:S(2)}) async-start(), calls=%async_computation.35 | async-start | bytes 3276800 | tf_op jit(solution)/shard_map/all_gather | solution.py:196
  1356.9 298.3 %reduce-scatter.50.cloned.1.call-start = ((), (), s32[]{:S(2)}) async-start(), calls=%async_computation.48 | async-start | bytes 6553600 | tf_op jit(solution)/shard_map/reduce_scatter | solution.py:224
  1443.4 211.8 %reduce-scatter.46.cloned.1.call-start = ((), (), s32[]{:S(2)}) async-start(), calls=%async_computation.44 | async-start | bytes 6553600 | tf_op jit(solution)/shard_map/reduce_scatter | solution.py:224
  1493.2 219.0 %reduce-scatter.42.cloned.1.call-start = ((), (), s32[]{:S(2)}) async-start(), calls=%async_computation.40 | async-start | bytes 6553600 | tf_op jit(solution)/shard_map/reduce_scatter | solution.py:224
  1542.2 234.4 %reduce-scatter.38.cloned.1.call-start = ((), (), s32[]{:S(2)}) async-start(), calls=%async_computation.36 | async-start | bytes 6553600 | tf_op jit(solution)/shard_map/reduce_scatter | solution.py:224
  1591.5 309.1 %reduce-scatter.52.cloned.1.call-start = ((), (), s32[]{:S(2)}) async-start(), calls=%async_computation.50 | async-start | bytes 3932160
  1856.5 209.8 %all-reduce.17.cloned.1.call-start = ((), (), s32[]{:S(2)}) async-start(), calls=%async_computation.49 | async-start | bytes 851968 | tf_op jit(solution)/shard_map/psum | solution.py:256
  1909.6 506.6 %all-reduce.19.cloned.1.call-start = ((), (), s32[]{:S(2)}) async-start(), calls=%async_computation.51 | async-start | bytes 37748736 | tf_op jit(solution)/shard_map/psum | solution.py:257
  (187 other events, 1843.9 us)
Sparse Core Ops, SparseCore 0:
  36.9 39.9 all-gather.24
  79.3 39.6 all-gather.28
  121.4 39.6 all-gather.16
  163.9 61.4 reduce-scatter.27
  228.2 61.4 reduce-scatter.31
  293.1 61.3 reduce-scatter.19
  362.1 39.6 all-gather.20
  434.7 61.4 reduce-scatter.23
  498.0 39.6 all-gather.32
  539.9 39.6 all-gather.18
  582.0 39.6 all-gather.40
  623.4 39.6 all-gather.26
  665.4 39.6 all-gather.36
  707.4 39.6 all-gather.22
  749.3 39.6 all-gather.44
  791.3 39.6 all-gather.30
  833.8 61.4 reduce-scatter.35
  898.1 61.4 reduce-scatter.21
  962.5 61.4 reduce-scatter.43
  1026.8 61.4 reduce-scatter.29
  1091.3 61.4 reduce-scatter.39
  1155.7 61.4 reduce-scatter.25
  1220.1 61.4 reduce-scatter.47
  1284.4 61.4 reduce-scatter.33
  1355.1 39.6 all-gather.46
  1396.5 39.6 all-gather.42
  1437.8 39.6 all-gather.38
  1479.3 39.6 all-gather.34
  1522.0 61.4 reduce-scatter.49
  1586.3 61.4 reduce-scatter.45
  1650.7 61.4 reduce-scatter.41
  1715.2 61.3 reduce-scatter.37
  1856.6 43.9 reduce-scatter.51
  1909.7 125.9 all-reduce.16
  2039.8 376.3 all-reduce.18
where the time goes:
time: 2450 us; the launch traced here: 2440 us
  waiting for transfers between devices  1490 us (61%)
  matrix products  428 us (17%)
  local copies, waits for them, and re-layouts  286 us (12%)
  other arithmetic  174 us (7%)
  blocking collectives  40.4 us (2%)
    psum x1, waiting for transfers between devices, local(): lax.psum((grad_qkv, grad_out, grad_up, grad_down, grad_rel, grad_ada, gra...  350 us
    reduce_scatter x4, waiting for transfers between devices, local(): lax.psum_scatter(jnp.dot(hidden_low, down_weight, preferred_element_type=...  247 us
    reduce_scatter x4, waiting for transfers between devices, local(): lax.psum_scatter(jnp.einsum('rf,df->rd', pre_low, up_weight, preferred_el...  217 us
    reduce_scatter x4, waiting for transfers between devices, local(): lax.psum_scatter(jnp.dot(heads_out, out_weight, preferred_element_type=jn...  203 us
    all_gather x4, waiting for transfers between devices, local(): lax.all_gather(normed_two.astype(jnp.bfloat16), 'mp', axis=0, tiled=True)  137 us
    reduce_scatter x4, waiting for transfers between devices, local(): lax.psum_scatter(jnp.einsum('rc,dc->rd', packed_grad, qkv_weight, preferr...  121 us
    unnamed x416, local copies, waits for them, and re-layouts  82.6 us
    all_gather x4, waiting for transfers between devices, local(): down_all = lax.all_gather(down_in, 'mp', axis=0, tiled=True)  77.8 us
  transfers between devices with their start and end apart: 35, of which 29 were waited for; matrix products, arithmetic and copies ran while one was open for 28% of the time, Pallas kernels for 0%

commit v1 on v0

--- a/solution.py
+++ b/solution.py
@@ -3,18 +3,727 @@
 
 import jax
 import jax.numpy as jnp
+import numpy as np
 from jax import lax
+from jax.experimental import pallas as pl
+from jax.experimental.pallas import tpu as pltpu
 from jax.sharding import PartitionSpec as P
 
 HD = 64
 WT = 5
 WH = 8
 WW = 8
-WIN_TOK = 320
-
-
+WIN = 320
+D = 1024
 EPS = 1e-06
+NOFF = WT + WH + WW
+C0 = math.sqrt(2.0 / math.pi)
+C1 = 0.044715
 precise = lax.Precision.HIGHEST
+f32 = jnp.float32
+bf16 = jnp.bfloat16
+NN = (((1,), (0,)), ((), ()))
+NT = (((1,), (1,)), ((), ()))
+TN = (((0,), (0,)), ((), ()))
+HALF = 512
+QKV = 384
+
+
+def mm(a, b, dims=NN):
+    return lax.dot_general(a, b, dims, preferred_element_type=f32)
+
+
+def whole(*dims):
+    return pl.BlockSpec(dims, lambda i, *_: (0,) * len(dims))
+
+
+def part(index, *dims):
+    return pl.BlockSpec(dims, lambda i, *_: index)
+
+
+def rows_of(width):
+    return pl.BlockSpec((WIN, width), lambda i, *_: (i, 0))
+
+
+def window_of(*dims):
+    return pl.BlockSpec((None,) + dims, lambda i, *_: (i,) + (0,) * len(dims))
+
+
+def shape(dims, dtype):
+    return jax.ShapeDtypeStruct(dims, dtype)
+
+
+def run(kernel, name, grid, ins, outs, scratch=(), after=(), scalars=(), flops=0, moved=0):
+    first = len(scalars) + len(ins)
+
+    def body(*refs):
+        kernel(*refs[:first], *refs[first + len(after) :])
+
+    hbm = pl.BlockSpec(memory_space=pl.ANY)
+    return pl.pallas_call(
+        body,
+        grid_spec=pltpu.PrefetchScalarGridSpec(
+            num_scalar_prefetch=len(scalars),
+            grid=(grid,),
+            in_specs=[spec for _, spec in ins] + [hbm] * len(after),
+            out_specs=[spec for _, spec in outs],
+            scratch_shapes=list(scratch),
+        ),
+        out_shape=[what for what, _ in outs],
+        compiler_params=pltpu.CompilerParams(vmem_limit_bytes=56 * 2**20),
+        cost_estimate=pl.CostEstimate(flops=int(flops), bytes_accessed=int(moved), transcendentals=0),
+        name=name,
+    )(*scalars, *[array for array, _ in ins], *after)
+
+
+def ln_parts(values):
+    center = values - jnp.mean(values, axis=-1, keepdims=True)
+    rstd = lax.rsqrt(jnp.mean(center * center, axis=-1, keepdims=True) + EPS)
+    return center * rstd, rstd
+
+
+def ln_back(grad, scale, hat, rstd):
+    inner = grad * (1.0 + scale)
+    mean_one = jnp.mean(inner, axis=-1, keepdims=True)
+    mean_two = jnp.mean(inner * hat, axis=-1, keepdims=True)
+    return rstd * (inner - mean_one - hat * mean_two)
+
+
+def attend_kernel(len_ref, x_ref, mode_ref, wa_ref, wb_ref, tbl_ref, e_ref, *rest):
+    n1_ref, packed_ref, heads_ref, probs_ref, w_all, kb_all = rest if len(rest) == 6 else (None, *rest)
+    w = pl.program_id(0)
+
+    @pl.when(w == 0)
+    def _():
+        w_all[:QKV] = wa_ref[...]
+        w_all[QKV:] = wb_ref[...]
+        for p in range(2):
+            kb_all[p] = mm(e_ref[...], tbl_ref[p]).astype(bf16)
+
+    if n1_ref is None:
+        x = x_ref[...]
+    else:
+        hat, _ = ln_parts(x_ref[...].astype(f32))
+        x = (hat * (1.0 + mode_ref[1:2]) + mode_ref[0:1]).astype(bf16)
+        n1_ref[...] = x
+    pk = mm(x, w_all[...], NT).astype(bf16)
+    packed_ref[...] = pk
+    lane = lax.broadcasted_iota(jnp.int32, (WIN, 128), 1)
+    low = lane < 64
+    frame = lax.broadcasted_iota(jnp.int32, (WIN, 128), 0) // (WH * WW)
+    mask_lane = (lane & 63) == 2 * NOFF
+    hide = jnp.where(frame < len_ref[w], 0.0, -1e30).astype(bf16)
+    for p in range(2):
+        q = pk[:, p * QKV : p * QKV + 128]
+        k = pk[:, p * QKV + 128 : p * QKV + 256]
+        v = pk[:, p * QKV + 256 : p * QKV + 384]
+        kb = jnp.where(mask_lane, hide, kb_all[p])
+        outs = []
+        for i in range(2):
+            mine = low if i == 0 else ~low
+            s = mm(jnp.where(mine, q, e_ref[...]), jnp.where(mine, k, kb), NT)
+            ex = jnp.exp(s - jnp.max(s, axis=1, keepdims=True))
+            pr = (ex * (1.0 / jnp.sum(ex, axis=1, keepdims=True))).astype(bf16)
+            probs_ref[2 * p + i] = pr
+            outs.append(mm(pr, v))
+        heads_ref[:, p * 128 : (p + 1) * 128] = jnp.where(low, outs[0], outs[1]).astype(bf16)
+
+
+def attend(lengths, source, modes, weight, table, query_hot, after=()):
+    count = lengths.shape[0]
+    rows = count * WIN
+    first = source.ndim == 3
+    outs = [
+        (shape((rows, 2 * QKV), bf16), rows_of(2 * QKV)),
+        (shape((rows, 256), bf16), rows_of(256)),
+        (shape((count * 4, WIN, WIN), bf16), pl.BlockSpec((4, WIN, WIN), lambda i, l: (i, 0, 0))),
+    ]
+    if first:
+        outs = [(shape((rows, D), bf16), rows_of(D))] + outs
+    return run(
+        attend_kernel,
+        "attend",
+        count,
+        [
+            (source, window_of(WIN, D) if first else rows_of(D)),
+            (modes, window_of(6, D)),
+            (weight[0], part((0, 0), QKV, D)),
+            (weight[1], part((0, 0), QKV, D)),
+            (table, whole(2, 128, 128)),
+            (query_hot, whole(WIN, 128)),
+        ],
+        outs,
+        [pltpu.VMEM((2 * QKV, D), bf16), pltpu.VMEM((2, WIN, 128), bf16)],
+        after,
+        [lengths],
+        9e9,
+        12e6,
+    )
+
+
+def middle_kernel(h0, h1, h2, h3, w0, w1, w2, w3, w4, w5, w6, w7, tok, cot, mode, attn_ref, mid_ref, n2_ref, di_ref, w_all):
+    @pl.when(pl.program_id(0) == 0)
+    def _():
+        for i, ref in enumerate((w0, w1, w2, w3, w4, w5, w6, w7)):
+            w_all[i * 128 : (i + 1) * 128] = ref[...]
+
+    heads = jnp.concatenate([h0[...], h1[...], h2[...], h3[...]], axis=1)
+    attn = mm(heads, w_all[...])
+    attn_ref[...] = attn.astype(bf16)
+    middle = tok[...].astype(f32) + mode[2:3] * attn
+    mid_ref[...] = middle
+    hat, _ = ln_parts(middle)
+    n2_ref[...] = (hat * (1.0 + mode[4:5]) + mode[3:4]).astype(bf16)
+    di_ref[...] = (mode[5:6] * cot[...].astype(f32)).astype(bf16)
+
+
+def middle_step(heads, weights, tokens, cotangent, modes, after=()):
+    count = tokens.shape[0]
+    rows = count * WIN
+    return run(
+        middle_kernel,
+        "middle",
+        count,
+        [(h, rows_of(256)) for h in heads]
+        + [(half, part((3, 0), 128, D)) for pair in weights for half in pair]
+        + [(tokens, window_of(WIN, D)), (cotangent, window_of(WIN, D)), (modes, window_of(6, D))],
+        [(shape((rows, D), kind), rows_of(D)) for kind in (bf16, f32, bf16, bf16)],
+        [pltpu.VMEM((D, D), bf16)],
+        after,
+        flops=2.7e9,
+        moved=22e6,
+    )
+
+
+def feed_kernel(n2_ref, di_ref, up0, dn0, up1, dn1, hid_ref, pre_ref, g0_ref, g1_ref):
+    def half_step(up_ref, dn_ref, g_ref):
+        up = up_ref[...]
+        dn = dn_ref[...]
+        v = mm(n2_ref[...], up, NT)
+        hg = mm(di_ref[...], dn, NT)
+        v2 = v * v
+        t = jnp.tanh(v * (C0 + (C0 * C1) * v2))
+        share = 0.5 + 0.5 * t
+        hid = (v * share).astype(bf16)
+        slope = share + (0.5 * v) * (1.0 - t * t) * (C0 + (3.0 * C0 * C1) * v2)
+        pre = (slope * hg).astype(bf16)
+        hid_ref[...] = hid
+        pre_ref[...] = pre
+        g_ref[1] = mm(hid, di_ref[...], TN).astype(bf16)
+        g_ref[0] = mm(pre, n2_ref[...], TN).astype(bf16)
+
+    j = pl.program_id(0)
+
+    @pl.when(j == 0)
+    def _():
+        half_step(up1, dn1, g1_ref)
+
+    @pl.when(j == 1)
+    def _():
+        half_step(up0, dn0, g0_ref)
+
+
+def feed(normed, down_in, weight, after=()):
+    rows = normed.shape[0]
+    ins = [(normed, whole(rows, D)), (down_in, whole(rows, D))]
+    for up, down in weight:
+        for array, place in (up, down):
+            ins.append((array, pl.BlockSpec((None, HALF, D), lambda i, place=place: (place, 0, 0))))
+    columns = pl.BlockSpec((rows, HALF), lambda j: (0, 1 - j))
+    return run(
+        feed_kernel,
+        "feed",
+        2,
+        ins,
+        [(shape((rows, 2 * HALF), bf16), columns)] * 2 + [(shape((2, HALF, D), bf16), whole(2, HALF, D))] * 2,
+        (),
+        after,
+        flops=8 * rows * D * 2 * HALF,
+        moved=20e6,
+    )
+
+
+def turn_kernel(p0, p1, p2, p3, w0, w1, w2, w3, w4, w5, w6, w7, mid_ref, attn_ref, cot_ref, mode_ref, mg_ref, oi_ref, sum_ref):
+    ng = None
+    for src, pair in ((p0, (w0, w1)), (p1, (w2, w3)), (p2, (w4, w5)), (p3, (w6, w7))):
+        for h in range(2):
+            term = mm(src[:, h * HALF : (h + 1) * HALF], pair[h][...])
+            ng = term if ng is None else ng + term
+    hat, rstd = ln_parts(mid_ref[...])
+    mg = cot_ref[...].astype(f32) + ln_back(ng, mode_ref[4:5], hat, rstd)
+    mg_ref[...] = mg
+    oi_ref[...] = (mode_ref[2:3] * mg).astype(bf16)
+    sum_ref[0:1] = jnp.sum(mg * attn_ref[...].astype(f32), axis=0, keepdims=True)
+    sum_ref[1:2] = jnp.sum(ng, axis=0, keepdims=True)
+    sum_ref[2:3] = jnp.sum(ng * hat, axis=0, keepdims=True)
+
+
+def out_kernel(p0, p1, p2, p3, w0, w1, w2, w3, w4, w5, w6, w7, mid_ref, cot_ref, mode_ref, out_ref, sum_ref):
+    mlp = None
+    for src, pair in ((p0, (w0, w1)), (p1, (w2, w3)), (p2, (w4, w5)), (p3, (w6, w7))):
+        for h in range(2):
+            term = mm(src[:, h * HALF : (h + 1) * HALF], pair[h][...])
+            mlp = term if mlp is None else mlp + term
+    out_ref[...] = (mid_ref[...] + mode_ref[5:6] * mlp).astype(bf16)
+    sum_ref[...] = jnp.sum(cot_ref[...].astype(f32) * mlp, axis=0, keepdims=True)
+
+
+def of_units(arrays, weights, which):
+    ins = [(array, rows_of(2 * HALF)) for array in arrays]
+    for pair in weights:
+        for half in pair:
+            array, place = half[which]
+            ins.append((array, pl.BlockSpec((None, HALF, D), lambda i, place=place: (place, 0, 0))))
+    return ins
+
+
+def turn_step(pre, weights, middle, attn_out, cotangent, modes, after=()):
+    count = cotangent.shape[0]
+    rows = count * WIN
+    return run(
+        turn_kernel,
+        "turn",
+        count,
+        of_units(pre, weights, 0)
+        + [(middle, rows_of(D)), (attn_out, rows_of(D)), (cotangent, window_of(WIN, D)), (modes, window_of(6, D))],
+        [
+            (shape((rows, D), f32), rows_of(D)),
+            (shape((rows, D), bf16), rows_of(D)),
+            (shape((count, 3, D), f32), window_of(3, D)),
+        ],
+        (),
+        after,
+        flops=10.7e9,
+        moved=35e6,
+    )
+
+
+def out_step(hid, weights, middle, cotangent, modes, after=()):
+    count = cotangent.shape[0]
+    return run(
+        out_kernel,
+        "output",
+        count,
+        of_units(hid, weights, 1) + [(middle, rows_of(D)), (cotangent, window_of(WIN, D)), (modes, window_of(6, D))],
+        [(shape((count, WIN, D), bf16), window_of(WIN, D)), (shape((count, 1, D), f32), window_of(1, D))],
+        (),
+        after,
+        flops=10.7e9,
+        moved=30e6,
+    )
+
+
+def attend_back_kernel(
+    oi_ref, o0_ref, o1_ref, pk_ref, pr_ref, e_ref, n1_ref, oi_all, ho_ref, pg_ref, g0_ref, g1_ref, rel_ref, pg_all, t_all, ow
+):
+    w = pl.program_id(0)
+
+    @pl.when(w == 0)
+    def _():
+        t_all[...] = jnp.zeros_like(t_all)
+        ow[:128] = o0_ref[...]
+        ow[128:] = o1_ref[...]
+
+    hg = mm(oi_ref[...], ow[...], NT).astype(bf16)
+    pk = pk_ref[...]
+    low = lax.broadcasted_iota(jnp.int32, (WIN, 128), 1) < 64
+    for p in range(2):
+        q = pk[:, p * QKV : p * QKV + 128]
+        k = pk[:, p * QKV + 128 : p * QKV + 256]
+        v = pk[:, p * QKV + 256 : p * QKV + 384]
+        do = hg[:, p * 128 : (p + 1) * 128]
+        dv, dq, dk = [], [], []
+        for i in range(2):
+            mine = low if i == 0 else ~low
+            qa = jnp.where(mine, q, e_ref[...])
+            dp = mm(jnp.where(mine, do, jnp.zeros_like(do)), v, NT)
+            prl = pr_ref[2 * p + i]
+            pr = prl.astype(f32)
+            t = pr * dp
+            ds = (t - pr * jnp.sum(t, axis=1, keepdims=True)).astype(bf16)
+            dv.append(mm(prl, do, TN))
+            dq.append(mm(ds, k))
+            dk.append(mm(ds, qa, TN))
+        block = jnp.concatenate(
+            [jnp.where(low, dq[0], dq[1]), jnp.where(low, dk[0], dk[1]), jnp.where(low, dv[0], dv[1])], axis=1
+        ).astype(bf16)
+        pg_ref[:, p * QKV : (p + 1) * QKV] = block
+        pg_all[pl.ds(pl.multiple_of(w * WIN, WIN), WIN), p * QKV : (p + 1) * QKV] = block
+        t_all[p] += jnp.where(low, dk[1], dk[0])
+
+    @pl.when(w == pl.num_programs(0) - 1)
+    def _():
+        go = mm(ho_ref[...], oi_all[...], TN).astype(bf16)
+        gq = mm(pg_all[...], n1_ref[...], TN).astype(bf16)
+        for p, g_ref in enumerate((g0_ref, g1_ref)):
+            g_ref[:QKV] = gq[p * QKV : (p + 1) * QKV]
+            g_ref[QKV:] = go[p * 128 : (p + 1) * 128]
+        hot = e_ref[...].astype(f32)
+        for p in range(2):
+            sums = lax.dot_general(hot, t_all[p], TN, precision=precise, preferred_element_type=f32)
+            rel_ref[p] = sums[:32]
+
+
+def attend_back(out_in, weight, packed, probs, query_hot, normed, heads, after=()):
+    rows = normed.shape[0]
+    return run(
+        attend_back_kernel,
+        "attend_back",
+        rows // WIN,
+        [
+            (out_in, rows_of(D)),
+            (weight[0], part((3, 0), 128, D)),
+            (weight[1], part((3, 0), 128, D)),
+            (packed, rows_of(2 * QKV)),
+            (probs, pl.BlockSpec((4, WIN, WIN), lambda i: (i, 0, 0))),
+            (query_hot, whole(WIN, 128)),
+            (normed, whole(rows, D)),
+            (out_in, whole(rows, D)),
+            (heads, whole(rows, 256)),
+        ],
+        [
+            (shape((rows, 2 * QKV), bf16), rows_of(2 * QKV)),
+            (shape((HALF, D), bf16), whole(HALF, D)),
+            (shape((HALF, D), bf16), whole(HALF, D)),
+            (shape((2, 32, 128), f32), whole(2, 32, 128)),
+        ],
+        [pltpu.VMEM((rows, 2 * QKV), bf16), pltpu.VMEM((2, WIN, 128), f32), pltpu.VMEM((256, D), bf16)],
+        after,
+        flops=13e9,
+        moved=20e6,
+    )
+
+
+def last_kernel(p0, p1, p2, p3, w0, w1, w2, w3, w4, w5, w6, w7, tok_ref, mode_ref, mg_ref, out_ref, sum_ref, w_all):
+    @pl.when(pl.program_id(0) == 0)
+    def _():
+        for i, ref in enumerate((w0, w1, w2, w3, w4, w5, w6, w7)):
+            w_all[i * QKV : (i + 1) * QKV] = ref[...]
+
+    ng = None
+    for i, src in enumerate((p0, p1, p2, p3)):
+        term = mm(src[...], w_all[i * 2 * QKV : (i + 1) * 2 * QKV])
+        ng = term if ng is None else ng + term
+    hat, rstd = ln_parts(tok_ref[...].astype(f32))
+    out_ref[...] = (mg_ref[...] + ln_back(ng, mode_ref[1:2], hat, rstd)).astype(bf16)
+    sum_ref[0:1] = jnp.sum(ng, axis=0, keepdims=True)
+    sum_ref[1:2] = jnp.sum(ng * hat, axis=0, keepdims=True)
+
+
+def last_step(packed_grads, weights, tokens, modes, middle_grad, after=()):
+    count = tokens.shape[0]
+    return run(
+        last_kernel,
+        "last",
+        count,
+        [(array, rows_of(2 * QKV)) for array in packed_grads]
+        + [(half, part((0, 0), QKV, D)) for pair in weights for half in pair]
+        + [(tokens, window_of(WIN, D)), (modes, window_of(6, D)), (middle_grad, rows_of(D))],
+        [(shape((count, WIN, D), bf16), window_of(WIN, D)), (shape((count, 2, D), f32), window_of(2, D))],
+        [pltpu.VMEM((8 * QKV, D), bf16)],
+        after,
+        flops=8e9,
+        moved=24e6,
+    )
+
+
+def silu_plain(values):
+    return values / (1.0 + jnp.exp(-values))
+
+
+def condition(timesteps, classes, class_table):
+    half_width = class_table.shape[1] // 2
+    frequency = jnp.exp(
+        -math.log(10000.0) * jnp.arange(half_width).astype(class_table.dtype) / half_width
+    )
+    phase_angle = timesteps.astype(class_table.dtype)[..., None] * frequency
+    sinusoid = jnp.concatenate([jnp.cos(phase_angle), jnp.sin(phase_angle)], axis=-1)
+    onehot = (classes[..., None] == jnp.arange(class_table.shape[0])).astype(class_table.dtype)
+    lookup = jnp.einsum("mwc,cd->mwd", onehot, class_table, precision=precise)
+    return sinusoid + lookup
+
+
+SPANS = ((0, 0, WT), (WT, 2 * WT - 1, WH), (WT + WH, 2 * WT + 2 * WH - 2, WW))
+
+
+def place_hot():
+    spot = np.arange(WIN)
+    hot = np.zeros((WIN, NOFF), np.float32)
+    for (start, _, _), where in zip(SPANS, (spot // (WH * WW), (spot // WW) % WH, spot % WW)):
+        hot[spot, start + where] = 1.0
+    return hot
+
+
+def query_side():
+    half = np.zeros((WIN, 64), np.float32)
+    half[:, :NOFF] = place_hot()
+    half[:, NOFF : 2 * NOFF] = place_hot()
+    half[:, 2 * NOFF] = 1.0
+    return np.concatenate([half, half], axis=1)
+
+
+def offset_hot(rows, copies):
+    hot = np.zeros((2 * NOFF - 3, rows, 64), np.float32)
+    for start, begin, length in SPANS:
+        for key in range(length):
+            for query in range(length):
+                for copy in range(copies):
+                    hot[begin + query - key + length - 1, start + key, copy * NOFF + start + query] = 1.0
+    return hot
+
+
+def key_tables(rel, core):
+    value = jnp.einsum("hr,rkq->hkq", rel.reshape(16, -1), offset_hot(64, 2), precision=precise)
+    top = lax.reduce_precision(value, 8, 7)
+    value = jnp.where(jnp.arange(64) < NOFF, top, value - top).astype(bf16)
+    value = value.reshape(4, 2, 2, 64, 64)
+    value = jnp.where(core == 0, value, value[:, ::-1])
+    value = jnp.concatenate([value[:, :, 1], value[:, :, 0]], axis=-1)
+    return jnp.pad(value, ((0, 0), (0, 0), (0, 64), (0, 0)))
+
+
+def rel_sums(grids, core):
+    grids = jnp.where(core == 0, grids, grids[:, ::-1])
+    grids = grids.reshape(4, 2, 32, 2, 64)
+    grids = jnp.stack([grids[:, :, :, 1], grids[:, :, :, 0]], axis=2).reshape(16, 32, 64)
+    return jnp.einsum("hkq,rkq->hr", grids, offset_hot(32, 1), precision=precise).reshape(4, 4, -1)
+
+
+def local_windows(
+    sizes,
+    tokens,
+    cotangent,
+    qkv_weight,
+    out_weight,
+    up_weight,
+    down_weight,
+    ada_weight,
+    ada_bias,
+    rel_bias,
+    class_table,
+    lengths,
+    timesteps,
+    classes,
+):
+    n_dp, n_mp = sizes
+    micro = tokens.shape[0]
+    mp = lax.axis_index("mp")
+    dp = lax.axis_index("dp")
+    core = dp & 1
+    z_bits = [1 << b for b in range(1, n_dp.bit_length() - 1)]
+
+    def swap_mp(bit):
+        return lambda v: lax.ppermute(v, "mp", [(i, i ^ bit) for i in range(n_mp)])
+
+    def swap_dp(bit):
+        return lambda v: lax.ppermute(v, "dp", [(i, i ^ bit) for i in range(n_dp)])
+
+    px, py, pd = swap_mp(1), swap_mp(2), swap_mp(3)
+    pc = swap_dp(1)
+    by_rel = [lambda v: v, px, py, pd]
+
+    def total(*values):
+        return sum(v.astype(f32) for v in values).astype(bf16)
+
+    def cat(a, b, axis=0):
+        return jnp.concatenate([a, b], axis=axis)
+
+    def ordered(flag, a, b, axis=0):
+        return cat(jnp.where(flag, a, b), jnp.where(flag, b, a), axis)
+
+    def dp_gather(v):
+        for bit in (1, *z_bits):
+            v = ordered((dp & bit) == 0, v, swap_dp(bit)(v))
+        return v
+
+    pre_cond = condition(timesteps, classes, class_table)
+    cond_low = silu_plain(pre_cond).astype(bf16)
+    mode_cols = jnp.einsum("mwd,de->mwe", cond_low, ada_weight, preferred_element_type=f32) + ada_bias.astype(f32)
+    order = jnp.arange(4) ^ mp
+    rel_modes = [
+        by_rel[r](lax.dynamic_index_in_dim(mode_cols, mp ^ r, axis=1, keepdims=False)) for r in range(4)
+    ]
+    modes = jnp.take(jnp.stack(rel_modes), order, axis=0)
+    modes = modes.transpose(1, 0, 2).reshape(micro, 6, D)
+    own_lengths = lax.dynamic_index_in_dim(lengths, mp, axis=1, keepdims=False)
+
+    row = np.arange(2 * QKV)
+    src = 2 * ((row // QKV) ^ core) + (row % 128) // 64
+    src = src * 192 + ((row % QKV) // 128) * 64 + row % 64
+    scale = np.where((row % QKV) < 128, HD**-0.5, 1.0).astype(np.float32)
+    qkv_hot = jnp.where(jnp.arange(2 * QKV)[:, None] == src[None, :], scale[None, :], 0.0).astype(bf16)
+    unit = np.arange(2 * HALF)
+    up_hot = (unit[:, None] == (unit ^ (core * HALF))[None, :]).astype(bf16)
+    both = (((0,), (1,)), ((), ()))
+    qkv_rows = lax.dot_general(qkv_hot, qkv_weight, both, preferred_element_type=f32).astype(bf16)
+    up_rows = lax.dot_general(up_hot, up_weight, both, preferred_element_type=f32).astype(bf16)
+
+    def half_of(v, h):
+        size = v.shape[0] // 2
+        return lax.dynamic_slice_in_dim(v, (core ^ h) * size, size, 0)
+
+    attn_own = [cat(qkv_rows[h * QKV : (h + 1) * QKV], half_of(out_weight, h)) for h in range(2)]
+    feed_own = [jnp.stack([up_rows[h * HALF : (h + 1) * HALF], half_of(down_weight, h)]) for h in range(2)]
+
+    ax, ay = px(attn_own[0]), py(attn_own[0])
+    ad = cat(py(ax[: HALF // 2]), px(ay[HALF // 2 :]))
+    attn_w = [attn_own] + [[v, pc(v)] for v in (ax, ay, ad)]
+    fx, fy = px(feed_own[0]), py(feed_own[0])
+    fu, fd = py(fx[:1]), px(fy[1:])
+    feed_w = [[((v, 0), (v, 1)) for v in feed_own]]
+    feed_w += [[((v, 0), (v, 1)) for v in (u, pc(u))] for u in (fx, fy)]
+    feed_w += [[((u, 0), (v, 0)) for u, v in ((fu, fd), (pc(fu), pc(fd)))]]
+
+    rel_all = jnp.stack([by_rel[r](rel_bias) for r in range(4)])
+    tables = key_tables(rel_all, core)
+    query_hot = jnp.asarray(query_side(), bf16)
+
+    packed, heads, probs = [None] * 4, [None] * 4, [None] * 4
+    normed_one, packed[0], heads[0], probs[0] = attend(own_lengths, tokens, modes, attn_w[0], tables[0], query_hot)
+    for r in (1, 2, 3):
+        packed[r], heads[r], probs[r] = attend(
+            own_lengths, normed_one, modes, attn_w[r], tables[r], query_hot, [ad] if r == 2 else []
+        )
+    attn_out, middle, normed_two, down_in = middle_step(heads, attn_w, tokens, cotangent, modes)
+
+    hid, pre, mine, other = [None] * 4, [None] * 4, [None] * 4, [None] * 4
+
+    def feed_step(r, after):
+        hid[r], pre[r], mine[r], sent = feed(normed_two, down_in, feed_w[r], after)
+        other[r] = pc(sent)
+
+    feed_step(1, [fx, fy])
+    feed_step(2, [])
+    send_x = px(total(mine[1][0], other[1][0]))
+    feed_step(3, [other[1]])
+    send_y = py(total(mine[2][1], other[2][1]))
+    feed_step(0, [other[2]])
+    diag_x = px(total(mine[3][0], other[3][0]))
+    diag_y = py(total(mine[3][1], other[3][1]))
+    middle_grad, out_in, turn_sums = turn_step(
+        pre, feed_w, middle, attn_out, cotangent, modes, [other[3], send_x]
+    )
+    last_x = px(total(mine[1][1], other[1][1], diag_y))
+    last_y = py(total(mine[2][0], other[2][0], diag_x))
+    feed_a = (mine[0][0], other[0][0], send_x, last_y)
+    feed_b = (mine[0][1], other[0][1], last_x, send_y)
+
+    class Steps:
+        def __init__(self, a, b):
+            low = (dp & z_bits[0]) == 0
+            pick = lambda flag: [jnp.where(flag, u, v) for u, v in zip(a, b)]
+            self.keep, self.sent = total(*pick(low)), total(*pick(~low))
+            self.level, self.back, self.got = 0, [], None
+
+        def down(self):
+            self.got = swap_dp(z_bits[self.level])(self.sent)
+            return self.got
+
+        def cut(self):
+            keep = total(self.keep, self.got)
+            self.level += 1
+            if self.level < len(z_bits):
+                low = (dp & z_bits[self.level]) == 0
+                size = keep.shape[0] // 2
+                a, b = keep[:size], keep[size:]
+                self.keep, self.sent = jnp.where(low, a, b), jnp.where(low, b, a)
+            else:
+                self.keep = keep
+
+        def up(self):
+            self.level -= 1
+            self.got = swap_dp(z_bits[self.level])(self.keep)
+            return self.got
+
+        def join(self):
+            low = (dp & z_bits[self.level]) == 0
+            self.keep = ordered(low, self.keep, self.got)
+
+        def rest(self):
+            while self.level < len(z_bits):
+                self.down()
+                self.cut()
+            while self.level > 0:
+                self.up()
+                self.join()
+            return self.keep, pc(self.keep)
+
+    packed_grad, rel_grid, a_mine, a_other = [None] * 4, [None] * 4, [None] * 4, [None] * 4
+
+    def back_step(r, after):
+        packed_grad[r], a_mine[r], sent, rel_grid[r] = attend_back(
+            out_in, attn_w[r], packed[r], probs[r], query_hot, normed_one, heads[r], after
+        )
+        a_other[r] = pc(sent)
+
+    cut = HALF // 2
+    back_step(3, [send_y, other[0]])
+    back_step(1, [diag_x, diag_y])
+    a_diag_x = px(total(a_mine[3][:cut], a_other[3][:cut]))
+    a_diag_y = py(total(a_mine[3][cut:], a_other[3][cut:]))
+    back_step(2, [a_other[3]])
+    a_send_x = px(total(a_mine[1][:cut], a_other[1][:cut]))
+    back_step(0, [a_other[1], last_x, last_y, a_diag_x, a_diag_y])
+    feed_steps = Steps(feed_a, feed_b)
+    a_send_y = py(total(a_mine[2][cut:], a_other[2][cut:]))
+    a_last_x = px(total(a_mine[1][cut:], a_other[1][cut:], a_diag_y))
+    a_last_y = py(total(a_mine[2][:cut], a_other[2][:cut], a_diag_x))
+    token_grads, last_sums = last_step(
+        packed_grad, attn_w, tokens, modes, middle_grad, [a_other[2], a_send_x, feed_steps.down()]
+    )
+    feed_steps.cut()
+    attn_steps = Steps(
+        (a_mine[0][:cut], a_other[0][:cut], a_send_x, a_last_y), (a_mine[0][cut:], a_other[0][cut:], a_last_x, a_send_y)
+    )
+    output, out_sums = out_step(
+        hid, feed_w, middle, cotangent, modes, [a_other[0], a_last_x, a_last_y, a_send_y, feed_steps.down()]
+    )
+    a, b = feed_steps.rest()
+    up_back, down_back = cat(a[:HALF], b[:HALF]), ordered(core == 0, a[HALF:], b[HALF:])
+    grad_up = lax.dot_general(up_back, up_hot, both, preferred_element_type=f32)
+    grad_down = down_back.astype(f32)
+    a, b = attn_steps.rest()
+    grad_qkv = lax.dot_general(cat(a[:QKV], b[:QKV]), qkv_hot, both, preferred_element_type=f32)
+    grad_out = ordered(core == 0, a[QKV:], b[QKV:]).astype(f32)
+
+    rel_part = rel_sums(jnp.stack(rel_grid), core)
+    for bit in (1, *z_bits):
+        rel_part = rel_part + swap_dp(bit)(rel_part)
+    grad_rel = rel_part[0] + px(rel_part[1]) + py(rel_part[2]) + pd(rel_part[3])
+
+    mode_grad = jnp.concatenate([last_sums, turn_sums, out_sums], axis=1).reshape(micro, 4, -1)
+    mode_grad_cols = jnp.stack(
+        [by_rel[r](lax.dynamic_index_in_dim(mode_grad, mp ^ r, axis=1, keepdims=False)) for r in range(4)]
+    )
+    mode_low = mode_grad_cols.astype(bf16).reshape(4 * micro, -1)
+    cond_rel = jnp.take(cond_low, order, axis=1).transpose(1, 0, 2).reshape(4 * micro, D)
+    cond_all = dp_gather(cond_rel)
+    mode_all = dp_gather(mode_low)
+    grad_ada = mm(cond_all, mode_all, TN)
+    grad_ada_bias = jnp.sum(mode_all.astype(f32), axis=0)
+    cond_grad = mm(mode_low, ada_weight, NT).reshape(4, micro, D)
+    cond_grad = jnp.take(cond_grad, order, axis=0)
+    cond_grad = cond_grad + px(cond_grad)
+    cond_grad = cond_grad + py(cond_grad)
+    own_pre = pre_cond.transpose(1, 0, 2)
+    share = 1.0 / (1.0 + jnp.exp(-own_pre))
+    cond_grad = cond_grad * (share * (1.0 + own_pre * (1.0 - share)))
+    class_all = dp_gather(classes.T.reshape(-1))
+    class_hot = (jnp.arange(class_table.shape[0])[:, None] == class_all[None, :]).astype(f32)
+    class_grad = jnp.dot(class_hot, dp_gather(cond_grad.reshape(4 * micro, D)), precision=precise)
+
+    return (
+        output,
+        token_grads,
+        grad_qkv,
+        grad_out,
+        grad_up,
+        grad_down,
+        grad_ada,
+        grad_ada_bias,
+        grad_rel,
+        class_grad,
+    )
 
 
 def layer_norm(values):
@@ -38,11 +747,7 @@
     )
 
 
-def silu_plain(values):
-    return values / (1.0 + jnp.exp(-values))
-
-
-def condition(timesteps, classes, class_table):
+def condition_whole(timesteps, classes, class_table):
     half_width = class_table.shape[1] // 2
     frequency = jnp.exp(
         -math.log(10000.0) * jnp.arange(half_width).astype(class_table.dtype) / half_width
@@ -74,7 +779,7 @@
         + row_part[:, None, :, None, None, :, None]
         + column_part[:, None, None, :, None, None, :]
     )
-    return full_bias.reshape(rel_bias.shape[0], WIN_TOK, WIN_TOK)
+    return full_bias.reshape(rel_bias.shape[0], WIN, WIN)
 
 
 def attention_scores(query_part, key_part, bias_full, masks):
@@ -86,7 +791,7 @@
     return jnp.where(masks[:, None, None, :], scores, -1e30)
 
 
-def local(
+def local_general(
     tokens,
     cotangent,
     qkv_weight,
@@ -107,15 +812,15 @@
     heads_here = rel_bias.shape[0]
     head_scale = HD ** (-0.5)
     first_row = lax.axis_index("mp") * row_count
-    row_window = (first_row + jnp.arange(row_count)) // WIN_TOK
+    row_window = (first_row + jnp.arange(row_count)) // WIN
     spread_rows = (row_window[:, None] == jnp.arange(win_count)[None, :]).astype(jnp.float32)
-    cond_low = condition(timesteps, classes, class_table).astype(jnp.bfloat16)
+    cond_low = condition_whole(timesteps, classes, class_table).astype(jnp.bfloat16)
     mode_cols = jnp.einsum(
         "mwd,de->mwe", cond_low, ada_weight, preferred_element_type=jnp.float32
     ) + ada_bias.astype(jnp.float32)
     mode_all = lax.all_gather(mode_cols, "mp", axis=2, tiled=True)
     bias_full, bias_pull = jax.vjp(window_bias, rel_bias)
-    frame_of = jnp.arange(WIN_TOK) // (WH * WW)
+    frame_of = jnp.arange(WIN) // (WH * WW)
     grad_qkv = jnp.zeros(qkv_weight.shape, jnp.float32)
     grad_out = jnp.zeros(out_weight.shape, jnp.float32)
     grad_up = jnp.zeros(up_weight.shape, jnp.float32)
@@ -135,7 +840,7 @@
         packed = jnp.dot(gathered_one, qkv_weight, preferred_element_type=jnp.float32).astype(
             jnp.bfloat16
         )
-        packed = packed.reshape(win_count, WIN_TOK, heads_here, 3, HD)
+        packed = packed.reshape(win_count, WIN, heads_here, 3, HD)
         query_part = packed[:, :, :, 0]
         key_part = packed[:, :, :, 1]
         value_part = packed[:, :, :, 2]
@@ -149,7 +854,7 @@
         heads_out = jnp.einsum(
             "whqk,wkhd->wqhd", probs_low, value_part, preferred_element_type=jnp.float32
         ).astype(jnp.bfloat16)
-        heads_out = heads_out.reshape(win_count * WIN_TOK, heads_here * HD)
+        heads_out = heads_out.reshape(win_count * WIN, heads_here * HD)
         attn_out = lax.psum_scatter(
             jnp.dot(heads_out, out_weight, preferred_element_type=jnp.float32),
             "mp",
@@ -198,7 +903,7 @@
         heads_grad = jnp.einsum(
             "rd,cd->rc", out_all, out_weight, preferred_element_type=jnp.float32
         ).astype(jnp.bfloat16)
-        heads_grad = heads_grad.reshape(win_count, WIN_TOK, heads_here, HD)
+        heads_grad = heads_grad.reshape(win_count, WIN, heads_here, HD)
         probs = jnp.exp(attention_scores(query_part, key_part, bias_full, masks) - log_total)
         probs_low = probs.astype(jnp.bfloat16)
         value_grad = jnp.einsum(
@@ -217,7 +922,7 @@
             "whqk,wqhd->wkhd", score_low, query_part, preferred_element_type=jnp.float32
         )
         packed_grad = jnp.stack([query_grad, key_grad, value_grad], axis=3).astype(jnp.bfloat16)
-        packed_grad = packed_grad.reshape(win_count * WIN_TOK, heads_here * 3 * HD)
+        packed_grad = packed_grad.reshape(win_count * WIN, heads_here * 3 * HD)
         micro_qkv = jnp.einsum(
             "rd,rc->dc", gathered_one, packed_grad, preferred_element_type=jnp.float32
         )
@@ -252,7 +957,7 @@
     grad_ada = jnp.einsum("mwd,mwe->de", cond_low, mode_low, preferred_element_type=jnp.float32)
     grad_ada_bias = jnp.sum(mode_grad_cols, axis=(0, 1))
     cond_grad = jnp.einsum("mwe,de->mwd", mode_low, ada_weight, preferred_element_type=jnp.float32)
-    cond_value, cond_pull = jax.vjp(partial(condition, timesteps, classes), class_table)
+    cond_value, cond_pull = jax.vjp(partial(condition_whole, timesteps, classes), class_table)
     class_total = lax.psum(cond_pull(cond_grad)[0], ("dp", "mp"))
     grad_qkv, grad_out, grad_up, grad_down, grad_rel, grad_ada, grad_ada_bias = lax.psum(
         (grad_qkv, grad_out, grad_up, grad_down, grad_rel, grad_ada, grad_ada_bias), "dp"
@@ -269,6 +974,12 @@
         grad_rel,
         class_total,
     )
+
+
+def local(sizes, *arrays):
+    if arrays[0].shape[1] == WIN and sizes[1] == 4:
+        return local_windows(sizes, *arrays)
+    return local_general(*arrays)
 
 
 def solution(mesh):
@@ -299,4 +1010,7 @@
         P("mp", None),
         P(),
     )
-    return jax.shard_map(local, mesh=mesh, in_specs=in_specs, out_specs=out_specs, check_vma=False)
+    sizes = (mesh.shape["dp"], mesh.shape["mp"])
+    return jax.shard_map(
+        partial(local, sizes), mesh=mesh, in_specs=in_specs, out_specs=out_specs, check_vma=False
+    )

time: 2450 us -> 629 us (0.26)
  waiting for transfers between devices: 1490 us -> 164 us
  matrix products: 428 us -> 24.7 us
  Pallas kernels: 0 us -> 276 us
  local copies, waits for them, and re-layouts: 286 us -> 24.1 us
  other arithmetic: 174 us -> 60.1 us
  starting transfers between devices: 4.3 us -> 70.2 us
  blocking collectives: 40.4 us -> 0 us
    reduce_scatter x16 -> x0, waiting for transfers between devices: 789 us -> none  [the longest x4 247 us: local(): lax.psum_scatter(jnp.dot(hidden_low, down_weight, preferred_element_type=...]
    psum x2 -> x0, waiting for transfers between devices: 350 us -> none  [the longest x1 350 us: local(): lax.psum((grad_qkv, grad_out, grad_up, grad_down, grad_rel, grad_ada, gra...]
    dot_general x94 -> x10, matrix products: 373 us -> 23.4 us  [the longest x2 4.67 us: mm(): return lax.dot_general(a, b, dims, preferred_element_type=f32)]
    all_gather x16 -> x0, waiting for transfers between devices: 310 us -> none  [the longest x4 137 us: local(): lax.all_gather(normed_two.astype(jnp.bfloat16), 'mp', axis=0, tiled=True)]
    pallas_call x0 -> x16, Pallas kernels: none -> 276 us  [run(): pl.pallas_call(body, grid_spec=pltpu.PrefetchScalarGridSpec(num_scalar_pr...]
    ppermute x0 -> x74, waiting for transfers between devices: none -> 164 us  [the longest x34 87.9 us: swap_mp(): return lambda v: lax.ppermute(v, 'mp', [(i, i ^ bit) for i in range(n_mp)])]
    reduce_sum x26 -> x1, other arithmetic: 117 us -> 0.67 us  [local_windows(): grad_ada_bias = jnp.sum(mode_all.astype(f32), axis=0)]
    reshape x20 -> x7, local copies, waits for them, and re-layouts: 117 us -> 1.99 us  [the longest x1 1.09 us: rel_sums(): grids = grids.reshape(4, 2, 32, 2, 64)]
  transfers between devices with their start and end apart: 35 -> 74, of which waited for: 29 -> 17; matrix products, arithmetic and copies ran while one was open for 28% -> 15% of each run, Pallas kernels for 0% -> 44%
where the time goes in v1:
time: 629 us; the launch traced here: 621 us
  Pallas kernels  276 us (44%)
  waiting for transfers between devices  164 us (26%)
  starting transfers between devices  70.2 us (11%)
  other arithmetic  60.1 us (10%)
  matrix products  24.7 us (4%)
  local copies, waits for them, and re-layouts  24.1 us (4%)
    pallas_call x16, Pallas kernels, run(): pl.pallas_call(body, grid_spec=pltpu.PrefetchScalarGridSpec(num_scalar_pr...  276 us
    ppermute x34, waiting for transfers between devices, swap_mp(): return lambda v: lax.ppermute(v, 'mp', [(i, i ^ bit) for i in range(n_mp)])  87.9 us
    ppermute x40, waiting for transfers between devices, swap_dp(): return lambda v: lax.ppermute(v, 'dp', [(i, i ^ bit) for i in range(n_dp)])  75.9 us
    ppermute x34, starting transfers between devices, swap_mp(): return lambda v: lax.ppermute(v, 'mp', [(i, i ^ bit) for i in range(n_mp)])  39.9 us
    convert_element_type x14, other arithmetic, total(): return sum((v.astype(f32) for v in values)).astype(bf16)  35 us
    ppermute x40, starting transfers between devices, swap_dp(): return lambda v: lax.ppermute(v, 'dp', [(i, i ^ bit) for i in range(n_dp)])  30.3 us
  transfers between devices with their start and end apart: 74, of which 17 were waited for; matrix products, arithmetic and copies ran while one was open for 15% of the time, Pallas kernels for 44%

profile of v1, /device:TPU:0, one launch (start us, length us, event | category | flops | bytes accessed | tf_op | source)
XLA Modules:
  0.0 621.3 jit_solution(11476407999625269432)
XLA Ops:
  0.7 3.0 collective-permute-start.3
  5.9 2.9 convolution_convert_fusion
  22.2 2.4 fusion.20
  34.2 7.9 %collective-permute-done = f32[4,1536]{1,0:T(4,128)S(1)} collective-permute-done((f32[4,1536]{1,0:T(4,128)S(1)}, f32[4,1536]{1,0:T(4,128)S(1)}, u32[]{:S(2)}, u32[]{:S(2)}) %collective-permute-start) | collective-permute-done | bytes 24608 | tf_op jit(solution)/shard_map/ppermute | solution.py:516
  45.8 39.4 %collective-permute-done.2 = f32[4,1536]{1,0:T(4,128)S(1)} collective-permute-done((f32[4,1536]{1,0:T(4,128)S(1)}, f32[4,1536]{1,0:T(4,128)S(1)}, u32[]{:S(2)}, u32[]{:S(2)}) %collective-permute-start.2) | collective-permute-done | bytes 24608 | tf_op jit(solution)/shard_map/ppermute | solution.py:516
  92.2 15.2 %attend.4 = (bf16[1280,1024]{1,0:T(8,128)(2,1)}, bf16[1280,768]{1,0:T(8,128)(2,1)}, bf16[1280,256]{1,0:T(8,128)(2,1)}, bf16[16,320,320]{2,1,0:T(8,128)(2,1)}) custom-call(s32[4]{0:T(128)} %fusion.61.refs_0_, bf16[4,320,1024]{2,1,0:T(8,128)(2,1)} %refs_12_.3, f32[4,6,1024]{2,1,0:T(8,128)} %reshape.124.refs_2_.refs_14_.refs_15_.refs_13_, ...), custom_call_target="tpu_custom_call" | custom-call | flops 8999999488 | bytes 12000000 | tf_op jit(solution)/shard_map/attend/pallas_call | solution.py:63
  109.5 13.7 %attend.6 = (bf16[1280,768]{1,0:T(8,128)(2,1)}, bf16[1280,256]{1,0:T(8,128)(2,1)}, bf16[16,320,320]{2,1,0:T(8,128)(2,1)}) custom-call(s32[4]{0:T(128)} %fusion.61.refs_0_, bf16[1280,1024]{1,0:T(8,128)(2,1)} %get-tuple-element.67.refs_1_.refs_6_, f32[4,6,1024]{2,1,0:T(8,128)} %reshape.124.refs_2_.refs_14_.refs_15_.refs_13_, ...), custom_call_target="tpu_custom_call" | custom-call | flops 8999999488 | bytes 12000000 | tf_op jit(solution)/shard_map/attend/pallas_call | solution.py:63
  125.1 2.3 slice.267
  128.4 13.6 %attend.5 = (bf16[1280,768]{1,0:T(8,128)(2,1)}, bf16[1280,256]{1,0:T(8,128)(2,1)}, bf16[16,320,320]{2,1,0:T(8,128)(2,1)}) custom-call(s32[4]{0:T(128)} %fusion.61.refs_0_, bf16[1280,1024]{1,0:T(8,128)(2,1)} %get-tuple-element.67.refs_1_.refs_6_, f32[4,6,1024]{2,1,0:T(8,128)} %reshape.124.refs_2_.refs_14_.refs_15_.refs_13_, ...), custom_call_target="tpu_custom_call" | custom-call | flops 8999999488 | bytes 12000000 | tf_op jit(solution)/shard_map/attend/pallas_call | solution.py:63
  143.1 13.7 %attend.7 = (bf16[1280,768]{1,0:T(8,128)(2,1)}, bf16[1280,256]{1,0:T(8,128)(2,1)}, bf16[16,320,320]{2,1,0:T(8,128)(2,1)}) custom-call(s32[4]{0:T(128)} %fusion.61.refs_0_, bf16[1280,1024]{1,0:T(8,128)(2,1)} %get-tuple-element.67.refs_1_.refs_6_, f32[4,6,1024]{2,1,0:T(8,128)} %reshape.124.refs_2_.refs_14_.refs_15_.refs_13_, bf16[512,1024]{1,0:T(8,128)(2,1)} %copy-done.16, ...), custom_call_target="tpu_custom_call" | custom-call | flops 8999999488 | bytes 12000000 | tf_op jit(solution)/shard_map/attend/pallas_call | solution.py:63
  156.8 11.0 %middle.1 = (bf16[1280,1024]{1,0:T(8,128)(2,1)}, f32[1280,1024]{1,0:T(8,128)}, bf16[1280,1024]{1,0:T(8,128)(2,1)}, bf16[1280,1024]{1,0:T(8,128)(2,1)}) custom-call(bf16[1280,256]{1,0:T(8,128)(2,1)} %get-tuple-element.66.refs_0_.refs_8_, bf16[1280,256]{1,0:T(8,128)(2,1)} %get-tuple-element.68.refs_1_.refs_8_, ...), custom_call_target="tpu_custom_call" | custom-call | flops 2700000000 | bytes 22000000 | tf_op jit(solution)/shard_map/middle/pallas_call | solution.py:63
  168.3 19.6 %feed.6 = (bf16[1280,1024]{1,0:T(8,128)(2,1)}, bf16[1280,1024]{1,0:T(8,128)(2,1)}, bf16[2,512,1024]{2,1,0:T(8,128)(2,1)}, bf16[2,512,1024]{2,1,0:T(8,128)(2,1)}) custom-call(bf16[1280,1024]{1,0:T(8,128)(2,1)} %get-tuple-element.71.refs_0_, bf16[1280,1024]{1,0:T(8,128)(2,1)} %get-tuple-element.72.refs_1_, ...), custom_call_target="tpu_custom_call" | custom-call | flops 10737418240 | bytes 20000000 | tf_op jit(solution)/shard_map/feed/pallas_call | solution.py:63
  188.2 19.6 %feed.4 = (bf16[1280,1024]{1,0:T(8,128)(2,1)}, bf16[1280,1024]{1,0:T(8,128)(2,1)}, bf16[2,512,1024]{2,1,0:T(8,128)(2,1)}, bf16[2,512,1024]{2,1,0:T(8,128)(2,1)}) custom-call(bf16[1280,1024]{1,0:T(8,128)(2,1)} %get-tuple-element.71.refs_0_, bf16[1280,1024]{1,0:T(8,128)(2,1)} %get-tuple-element.72.refs_1_, ...), custom_call_target="tpu_custom_call" | custom-call | flops 10737418240 | bytes 20000000 | tf_op jit(solution)/shard_map/feed/pallas_call | solution.py:63
  212.0 2.6 collective-permute-start.68
  217.7 19.9 %feed.7 = (bf16[1280,1024]{1,0:T(8,128)(2,1)}, bf16[1280,1024]{1,0:T(8,128)(2,1)}, bf16[2,512,1024]{2,1,0:T(8,128)(2,1)}, bf16[2,512,1024]{2,1,0:T(8,128)(2,1)}) custom-call(bf16[1280,1024]{1,0:T(8,128)(2,1)} %get-tuple-element.71.refs_0_, bf16[1280,1024]{1,0:T(8,128)(2,1)} %get-tuple-element.72.refs_1_, ...), custom_call_target="tpu_custom_call" | custom-call | flops 10737418240 | bytes 20000000 | tf_op jit(solution)/shard_map/feed/pallas_call | solution.py:63
  239.4 20.0 %feed.5 = (bf16[1280,1024]{1,0:T(8,128)(2,1)}, bf16[1280,1024]{1,0:T(8,128)(2,1)}, bf16[2,512,1024]{2,1,0:T(8,128)(2,1)}, bf16[2,512,1024]{2,1,0:T(8,128)(2,1)}) custom-call(bf16[1280,1024]{1,0:T(8,128)(2,1)} %get-tuple-element.71.refs_0_, bf16[1280,1024]{1,0:T(8,128)(2,1)} %get-tuple-element.72.refs_1_, ...), custom_call_target="tpu_custom_call" | custom-call | flops 10737418240 | bytes 20000000 | tf_op jit(solution)/shard_map/feed/pallas_call | solution.py:63
  263.7 2.6 fusion.36
  267.9 3.9 fusion.35
  273.4 14.0 %collective-permute-done.24.refs_17_ = bf16[512,1024]{1,0:T(8,128)(2,1)S(1)} collective-permute-done((bf16[512,1024]{1,0:T(8,128)(2,1)S(1)}, bf16[512,1024]{1,0:T(8,128)(2,1)S(1)}, u32[]{:S(2)}, u32[]{:S(2)}) %collective-permute-start.24) | collective-permute-done | bytes 1048608 | tf_op jit(solution)/shard_map/ppermute | solution.py:516
  288.4 21.5 %turn.1 = (f32[1280,1024]{1,0:T(8,128)}, bf16[1280,1024]{1,0:T(8,128)(2,1)}, f32[4,3,1024]{2,1,0:T(4,128)}) custom-call(bf16[1280,1024]{1,0:T(8,128)(2,1)} %get-tuple-element.80.refs_0_, bf16[1280,1024]{1,0:T(8,128)(2,1)} %get-tuple-element.81.refs_1_, bf16[1280,1024]{1,0:T(8,128)(2,1)} %get-tuple-element.82.refs_2_, ...), custom_call_target="tpu_custom_call" | custom-call | flops 10700000256 | bytes 35000000 | tf_op jit(solution)/shard_map/turn/pallas_call | solution.py:63
  311.6 18.2 %attend_back.5 = (bf16[1280,768]{1,0:T(8,128)(2,1)}, bf16[512,1024]{1,0:T(8,128)(2,1)}, bf16[512,1024]{1,0:T(8,128)(2,1)}, f32[2,32,128]{2,1,0:T(8,128)}) custom-call(bf16[1280,1024]{1,0:T(8,128)(2,1)} %get-tuple-element.87.refs_0_.refs_7_, bf16[512,1024]{1,0:T(8,128)(2,1)} %copy-done.16, bf16[512,1024]{1,0:T(8,128)(2,1)} %copy-done.28, ...), custom_call_target="tpu_custom_call" | custom-call | flops 12999999488 | bytes 20000000 | tf_op jit(solution)/shard_map/attend_back/pallas_call | solution.py:63
  329.9 3.6 fusion.17
  334.4 3.1 fusion.16
  339.1 18.4 %attend_back.4 = (bf16[1280,768]{1,0:T(8,128)(2,1)}, bf16[512,1024]{1,0:T(8,128)(2,1)}, bf16[512,1024]{1,0:T(8,128)(2,1)}, f32[2,32,128]{2,1,0:T(8,128)}) custom-call(bf16[1280,1024]{1,0:T(8,128)(2,1)} %get-tuple-element.87.refs_0_.refs_7_, bf16[512,1024]{1,0:T(8,128)(2,1)} %collective-permute-done.6.refs_3_.refs_6_.refs_1_, bf16[512,1024]{1,0:T(8,128)(2,1)} %copy-done.27, ...), custom_call_target="tpu_custom_call" | custom-call | flops 12999999488 | bytes 20000000 | tf_op jit(solution)/shard_map/attend_back/pallas_call | solution.py:63
  357.6 3.0 add_convert_fusion.13
  362.1 18.3 %attend_back.7 = (bf16[1280,768]{1,0:T(8,128)(2,1)}, bf16[512,1024]{1,0:T(8,128)(2,1)}, bf16[512,1024]{1,0:T(8,128)(2,1)}, f32[2,32,128]{2,1,0:T(8,128)}) custom-call(bf16[1280,1024]{1,0:T(8,128)(2,1)} %get-tuple-element.87.refs_0_.refs_7_, bf16[512,1024]{1,0:T(8,128)(2,1)} %collective-permute-done.8.refs_3_.refs_8_.refs_1_, bf16[512,1024]{1,0:T(8,128)(2,1)} %copy-done.26, ...), custom_call_target="tpu_custom_call" | custom-call | flops 12999999488 | bytes 20000000 | tf_op jit(solution)/shard_map/attend_back/pallas_call | solution.py:63
  380.5 2.6 collective-permute-start.53
  384.9 18.8 %attend_back.6 = (bf16[1280,768]{1,0:T(8,128)(2,1)}, bf16[512,1024]{1,0:T(8,128)(2,1)}, bf16[512,1024]{1,0:T(8,128)(2,1)}, f32[2,32,128]{2,1,0:T(8,128)}) custom-call(bf16[1280,1024]{1,0:T(8,128)(2,1)} %get-tuple-element.87.refs_0_.refs_7_, bf16[512,1024]{1,0:T(8,128)(2,1)} %pad_maximum_fusion.6.refs_3_.refs_4_.refs_1_, ...), custom_call_target="tpu_custom_call" | custom-call | flops 12999999488 | bytes 20000000 | tf_op jit(solution)/shard_map/attend_back/pallas_call | solution.py:63
  409.3 4.3 fusion.13
  417.4 21.7 %collective-permute-done.61 = f32[4,4,39]{2,1,0:T(4,128)S(1)} collective-permute-done((f32[4,4,39]{2,1,0:T(4,128)S(1)}, f32[4,4,39]{2,1,0:T(4,128)S(1)}, u32[]{:S(2)}, u32[]{:S(2)}) %collective-permute-start.61) | collective-permute-done | bytes 2528 | tf_op jit(solution)/shard_map/ppermute | solution.py:519
  448.9 5.3 collective-permute-done.63
  461.0 2.6 collective-permute-start.41
  463.6 2.5 collective-permute-done.36.refs_16_
  466.1 3.8 collective-permute-done.39.refs_18_
  470.0 10.8 %collective-permute-done.38.refs_17_ = bf16[256,1024]{1,0:T(8,128)(2,1)S(1)} collective-permute-done((bf16[256,1024]{1,0:T(8,128)(2,1)S(1)}, bf16[256,1024]{1,0:T(8,128)(2,1)S(1)}, u32[]{:S(2)}, u32[]{:S(2)}) %collective-permute-start.38) | collective-permute-done | bytes 524320 | tf_op jit(solution)/shard_map/ppermute | solution.py:516
  483.2 16.7 %last.1 = (bf16[4,320,1024]{2,1,0:T(8,128)(2,1)}, f32[4,2,1024]{2,1,0:T(2,128)}) custom-call(bf16[1280,768]{1,0:T(8,128)(2,1)} %get-tuple-element.108.refs_0_, bf16[1280,768]{1,0:T(8,128)(2,1)} %get-tuple-element.109.refs_1_, bf16[1280,768]{1,0:T(8,128)(2,1)} %get-tuple-element.110.refs_2_, bf16[1280,768]{1,0:T(8,128)(2,1)} %get-tuple-element.111.refs_3_, ...), custom_call_target="tpu_custom_call" | custom-call | flops 8000000000 | bytes 24000000 | tf_op jit(solution)/shard_map/last/pallas_call | solution.py:63
  501.0 2.6 collective-permute-start.48
  503.6 18.1 %output.1 = (bf16[4,320,1024]{2,1,0:T(8,128)(2,1)}, f32[4,1,1024]{2,1,0:T(1,128)}) custom-call(bf16[1280,1024]{1,0:T(8,128)(2,1)} %get-tuple-element.74.refs_0_, bf16[1280,1024]{1,0:T(8,128)(2,1)} %get-tuple-element.75.refs_1_, bf16[1280,1024]{1,0:T(8,128)(2,1)} %get-tuple-element.76.refs_2_, bf16[1280,1024]{1,0:T(8,128)(2,1)} %get-tuple-element.78.refs_3_, ...), custom_call_target="tpu_custom_call" | custom-call | flops 10700000256 | bytes 30000000 | tf_op jit(solution)/shard_map/output/pallas_call | solution.py:63
  526.3 3.0 add_convert_fusion.6
  534.3 3.4 collective-permute-done.69
  543.0 3.3 collective-permute-done.58
  549.3 2.7 collective-permute-start.45
  554.0 9.4 %collective-permute-done.45 = bf16[128,1024]{1,0:T(8,128)(2,1)S(1)} collective-permute-done((bf16[128,1024]{1,0:T(8,128)(2,1)S(1)}, bf16[128,1024]{1,0:T(8,128)(2,1)S(1)}, u32[]{:S(2)}, u32[]{:S(2)}) %collective-permute-start.45) | collective-permute-done | bytes 262176 | tf_op jit(solution)/shard_map/ppermute | solution.py:519
  566.7 35.0 %collective-permute-done.46 = bf16[256,1024]{1,0:T(8,128)(2,1)S(1)} collective-permute-done((bf16[256,1024]{1,0:T(8,128)(2,1)S(1)}, bf16[256,1024]{1,0:T(8,128)(2,1)S(1)}, u32[]{:S(2)}, u32[]{:S(2)}) %collective-permute-start.46) | collective-permute-done | bytes 524320 | tf_op jit(solution)/shard_map/ppermute | solution.py:519
  604.2 3.7 fusion.47
  610.4 3.1 fusion.23
  614.2 4.4 fusion
  618.6 2.4 maximum_convert_fusion
  (377 shorter events, 125.4 us)
Async XLA Ops:
  0.7 28.5 %collective-permute-start.3 = (f32[4,39]{1,0:T(4,128)}, f32[4,39]{1,0:T(4,128)S(1)}, u32[]{:S(2)}, u32[]{:S(2)}) collective-permute-start(f32[4,39]{1,0:T(4,128)} %param.31), channel_id=1, source_target_pairs={{0,1},{1,0},{2,3},{3,2},{4,5},{5,4},{6,7},{7,6},{8,9},{9,8},{10,11... | collective-permute-start | bytes 1880 | tf_op jit(solution)/shard_map/ppermute | solution.py:516
  3.7 26.1 %collective-permute-start.5 = (f32[4,39]{1,0:T(4,128)}, f32[4,39]{1,0:T(4,128)S(1)}, u32[]{:S(2)}, u32[]{:S(2)}) collective-permute-start(f32[4,39]{1,0:T(4,128)} %param.31), channel_id=1, source_target_pairs={{0,3},{1,2},{2,1},{3,0},{4,7},{5,6},{6,5},{7,4},{8,11},{9,10},{10,... | collective-permute-start | bytes 1880 | tf_op jit(solution)/shard_map/ppermute | solution.py:516
  5.2 24.7 %collective-permute-start.4 = (f32[4,39]{1,0:T(4,128)}, f32[4,39]{1,0:T(4,128)S(1)}, u32[]{:S(2)}, u32[]{:S(2)}) collective-permute-start(f32[4,39]{1,0:T(4,128)} %param.31), channel_id=1, source_target_pairs={{0,2},{1,3},{2,0},{3,1},{4,6},{5,7},{6,4},{7,5},{8,10},{9,11},{10,... | collective-permute-start | bytes 1880 | tf_op jit(solution)/shard_map/ppermute | solution.py:516
  13.4 73.3 %collective-permute-start.8 = (bf16[512,1024]{1,0:T(8,128)(2,1)}, bf16[512,1024]{1,0:T(8,128)(2,1)}, u32[]{:S(2)}, u32[]{:S(2)}) collective-permute-start(bf16[512,1024]{1,0:T(8,128)(2,1)} %pad_maximum_fusion.6.refs_3_.refs_4_.refs_1_), channel_id=1, source_target_pairs={{0,2},{1,3},{2,0},{3,1},{4,6},{5,7},{6,4},{7,5},{8,10},{9,11},{10,... | collective-permute-start | bytes 3145736 | tf_op jit(solution)/shard_map/ppermute | solution.py:516
  15.3 74.2 %collective-permute-start.6 = (bf16[512,1024]{1,0:T(8,128)(2,1)}, bf16[512,1024]{1,0:T(8,128)(2,1)}, u32[]{:S(2)}, u32[]{:S(2)}) collective-permute-start(bf16[512,1024]{1,0:T(8,128)(2,1)} %pad_maximum_fusion.6.refs_3_.refs_4_.refs_1_), channel_id=1, source_target_pairs={{0,1},{1,0},{2,3},{3,2},{4,5},{5,4},{6,7},{7,6},{8,9},{9,8},{10,11... | collective-permute-start | bytes 3145736 | tf_op jit(solution)/shard_map/ppermute | solution.py:516
  29.9 78.9 %collective-permute-start.16 = (bf16[2,512,1024]{2,1,0:T(8,128)(2,1)}, bf16[2,512,1024]{2,1,0:T(8,128)(2,1)}, u32[]{:S(2)}, u32[]{:S(2)}) collective-permute-start(bf16[2,512,1024]{2,1,0:T(8,128)(2,1)} %pad_maximum_fusion.3.refs_2_.refs_3_.refs_4_), channel_id=1, source_target_pairs={{0,1},{1,0},{2,3},{3,2},{4,5},{5,4},{6,7},{7,6},{8,9},{9,8},{10,11... | collective-permute-start | bytes 6291464 | tf_op jit(solution)/shard_map/ppermute | solution.py:516
  42.2 43.0 %collective-permute-start.2 = (f32[4,1536]{1,0:T(4,128)S(1)}, f32[4,1536]{1,0:T(4,128)S(1)}, u32[]{:S(2)}, u32[]{:S(2)}) collective-permute-start(f32[4,1536]{1,0:T(4,128)S(1)} %bitcast.176), channel_id=1, source_target_pairs={{0,3},{1,2},{2,1},{3,0},{4,7},{5,6},{6,5},{7,4},{8,11},{9,10},{10,... | collective-permute-start | bytes 73736 | tf_op jit(solution)/shard_map/ppermute | solution.py:516
  44.3 80.2 %collective-permute-start.13 = (bf16[2,512,1024]{2,1,0:T(8,128)(2,1)}, bf16[2,512,1024]{2,1,0:T(8,128)(2,1)}, u32[]{:S(2)}, u32[]{:S(2)}) collective-permute-start(bf16[2,512,1024]{2,1,0:T(8,128)(2,1)} %pad_maximum_fusion.3.refs_2_.refs_3_.refs_4_), channel_id=1, source_target_pairs={{0,2},{1,3},{2,0},{3,1},{4,6},{5,7},{6,4},{7,5},{8,10},{9,11},{10,... | collective-permute-start | bytes 6291464 | tf_op jit(solution)/shard_map/ppermute | solution.py:516
  87.8 20.2 %collective-permute-start.11 = (bf16[256,1024]{1,0:T(8,128)(2,1)S(1)}, bf16[256,1024]{1,0:T(8,128)(2,1)S(1)}, u32[]{:S(2)}, u32[]{:S(2)}) collective-permute-start(bf16[256,1024]{1,0:T(8,128)(2,1)S(1)} %slice.262), channel_id=1, source_target_pairs={{0,1},{1,0},{2,3},{3,2},{4,5},{5,4},{6,7},{7,6},{8,9},{9,8},{10,11... | collective-permute-start | bytes 1572872 | tf_op jit(solution)/shard_map/ppermute | solution.py:516
  107.4 19.9 %collective-permute-start.7 = (bf16[512,1024]{1,0:T(8,128)(2,1)}, bf16[512,1024]{1,0:T(8,128)(2,1)S(1)}, u32[]{:S(2)}, u32[]{:S(2)}) collective-permute-start(bf16[512,1024]{1,0:T(8,128)(2,1)} %collective-permute-done.6.refs_3_.refs_6_.refs_1_), channel_id=1, source_target_pairs={{0,4},{4,0},{8,12},{12,8},{16,20},{20,16},{24,28},{28,24},{1,5},{5... | collective-permute-start | bytes 3145736 | tf_op jit(solution)/shard_map/ppermute | solution.py:519
  108.0 100.2 %collective-permute-start.66 = (s32[16]{0:T(128)S(1)}, s32[16]{0:T(128)S(1)}, u32[]{:S(2)}, u32[]{:S(2)}) collective-permute-start(s32[16]{0:T(128)S(1)} %reshape.130), channel_id=1, source_target_pairs={{0,4},{4,0},{8,12},{12,8},{16,20},{20,16},{24,28},{28,24},{1,5},{5... | collective-permute-start | bytes 200 | tf_op jit(solution)/shard_map/ppermute | solution.py:519
  108.2 33.9 %collective-permute-start.12 = (bf16[512,1024]{1,0:T(8,128)(2,1)S(1)}, bf16[512,1024]{1,0:T(8,128)(2,1)S(1)}, u32[]{:S(2)}, u32[]{:S(2)}) collective-permute-start(bf16[512,1024]{1,0:T(8,128)(2,1)S(1)} %constant_dynamic-update-slice_fusion.refs_7_.refs_3_.refs_10_.refs_1_), channel_id=1, source_target_pairs={{0,4},{4,0},{8,12},{12,8},{16,20},{20,16},{24,28},{28,24},{1,5},{5... | collective-permute-start | bytes 3145736 | tf_op jit(solution)/shard_map/ppermute | solution.py:519
  108.7 59.6 %collective-permute-start.17 = (bf16[2,512,1024]{2,1,0:T(8,128)(2,1)}, bf16[2,512,1024]{2,1,0:T(8,128)(2,1)}, u32[]{:S(2)}, u32[]{:S(2)}) collective-permute-start(bf16[2,512,1024]{2,1,0:T(8,128)(2,1)} %collective-permute-done.16.refs_2_.refs_3_.refs_6_), channel_id=1, source_target_pairs={{0,4},{4,0},{8,12},{12,8},{16,20},{20,16},{24,28},{28,24},{1,5},{5... | collective-permute-start | bytes 6291464 | tf_op jit(solution)/shard_map/ppermute | solution.py:519
  124.5 43.2 %collective-permute-start.18 = (bf16[1,512,1024]{2,1,0:T(8,128)(2,1)S(1)}, bf16[1,512,1024]{2,1,0:T(8,128)(2,1)}, u32[]{:S(2)}, u32[]{:S(2)}) collective-permute-start(bf16[1,512,1024]{2,1,0:T(8,128)(2,1)S(1)} %slice.266), channel_id=1, source_target_pairs={{0,2},{1,3},{2,0},{3,1},{4,6},{5,7},{6,4},{7,5},{8,10},{9,11},{10,... | collective-permute-start | bytes 3145736 | tf_op jit(solution)/shard_map/ppermute | solution.py:516
  127.3 40.7 %collective-permute-start.19 = (bf16[1,512,1024]{2,1,0:T(8,128)(2,1)}, bf16[1,512,1024]{2,1,0:T(8,128)(2,1)}, u32[]{:S(2)}, u32[]{:S(2)}) collective-permute-start(bf16[1,512,1024]{2,1,0:T(8,128)(2,1)} %slice.267), channel_id=1, source_target_pairs={{0,1},{1,0},{2,3},{3,2},{4,5},{5,4},{6,7},{7,6},{8,9},{9,8},{10,11... | collective-permute-start | bytes 3145736 | tf_op jit(solution)/shard_map/ppermute | solution.py:516
  142.1 46.1 %collective-permute-start.14 = (bf16[2,512,1024]{2,1,0:T(8,128)(2,1)}, bf16[2,512,1024]{2,1,0:T(8,128)(2,1)}, u32[]{:S(2)}, u32[]{:S(2)}) collective-permute-start(bf16[2,512,1024]{2,1,0:T(8,128)(2,1)} %collective-permute-done.13.refs_2_.refs_3_.refs_7_.refs_8_), channel_id=1, source_target_pairs={{0,4},{4,0},{8,12},{12,8},{16,20},{20,16},{24,28},{28,24},{1,5},{5... | collective-permute-start | bytes 6291464 | tf_op jit(solution)/shard_map/ppermute | solution.py:519
  167.7 49.9 %collective-permute-start.20 = (bf16[1,512,1024]{2,1,0:T(8,128)(2,1)}, bf16[1,512,1024]{2,1,0:T(8,128)(2,1)}, u32[]{:S(2)}, u32[]{:S(2)}) collective-permute-start(bf16[1,512,1024]{2,1,0:T(8,128)(2,1)} %collective-permute-done.18.refs_2_.refs_10_), channel_id=1, source_target_pairs={{0,4},{4,0},{8,12},{12,8},{16,20},{20,16},{24,28},{28,24},{1,5},{5... | collective-permute-start | bytes 3145736 | tf_op jit(solution)/shard_map/ppermute | solution.py:519
  168.0 49.6 %collective-permute-start.21 = (bf16[1,512,1024]{2,1,0:T(8,128)(2,1)}, bf16[1,512,1024]{2,1,0:T(8,128)(2,1)}, u32[]{:S(2)}, u32[]{:S(2)}) collective-permute-start(bf16[1,512,1024]{2,1,0:T(8,128)(2,1)} %collective-permute-done.19.refs_3_.refs_10_), channel_id=1, source_target_pairs={{0,4},{4,0},{8,12},{12,8},{16,20},{20,16},{24,28},{28,24},{1,5},{5... | collective-permute-start | bytes 3145736 | tf_op jit(solution)/shard_map/ppermute | solution.py:519
  187.9 29.7 %collective-permute-start.22 = (bf16[2,512,1024]{2,1,0:T(8,128)(2,1)}, bf16[2,512,1024]{2,1,0:T(8,128)(2,1)}, u32[]{:S(2)}, u32[]{:S(2)}) collective-permute-start(bf16[2,512,1024]{2,1,0:T(8,128)(2,1)} %get-tuple-element.77), channel_id=1, source_target_pairs={{0,4},{4,0},{8,12},{12,8},{16,20},{20,16},{24,28},{28,24},{1,5},{5... | collective-permute-start | bytes 6291464 | tf_op jit(solution)/shard_map/ppermute | solution.py:519
  207.8 31.6 %collective-permute-start.15 = (bf16[2,512,1024]{2,1,0:T(8,128)(2,1)}, bf16[2,512,1024]{2,1,0:T(8,128)(2,1)}, u32[]{:S(2)}, u32[]{:S(2)}) collective-permute-start(bf16[2,512,1024]{2,1,0:T(8,128)(2,1)} %get-tuple-element.73), channel_id=1, source_target_pairs={{0,4},{4,0},{8,12},{12,8},{16,20},{20,16},{24,28},{28,24},{1,5},{5... | collective-permute-start | bytes 6291464 | tf_op jit(solution)/shard_map/ppermute | solution.py:519
  237.5 30.3 %collective-permute-start.23 = (bf16[2,512,1024]{2,1,0:T(8,128)(2,1)}, bf16[2,512,1024]{2,1,0:T(8,128)(2,1)}, u32[]{:S(2)}, u32[]{:S(2)}) collective-permute-start(bf16[2,512,1024]{2,1,0:T(8,128)(2,1)} %get-tuple-element.85), channel_id=1, source_target_pairs={{0,4},{4,0},{8,12},{12,8},{16,20},{20,16},{24,28},{28,24},{1,5},{5... | collective-permute-start | bytes 6291464 | tf_op jit(solution)/shard_map/ppermute | solution.py:519
  237.8 25.3 %collective-permute-start.52 = (bf16[32,1024]{1,0:T(8,128)(2,1)S(1)}, bf16[32,1024]{1,0:T(8,128)(2,1)S(1)}, u32[]{:S(2)}, u32[]{:S(2)}) collective-permute-start(bf16[32,1024]{1,0:T(8,128)(2,1)S(1)} %pad_maximum_fusion.21), channel_id=1, source_target_pairs={{0,8},{4,12},{8,0},{12,4},{16,24},{20,28},{24,16},{28,20},{1,9},{5... | collective-permute-start | bytes 196616 | tf_op jit(solution)/shard_map/ppermute | solution.py:519
  259.5 50.4 %collective-permute-start.31 = (bf16[2,512,1024]{2,1,0:T(8,128)(2,1)}, bf16[2,512,1024]{2,1,0:T(8,128)(2,1)S(1)}, u32[]{:S(2)}, u32[]{:S(2)}) collective-permute-start(bf16[2,512,1024]{2,1,0:T(8,128)(2,1)} %get-tuple-element.97), channel_id=1, source_target_pairs={{0,4},{4,0},{8,12},{12,8},{16,20},{20,16},{24,28},{28,24},{1,5},{5... | collective-permute-start | bytes 6291464 | tf_op jit(solution)/shard_map/ppermute | solution.py:519
  261.4 26.0 %collective-permute-start.24 = (bf16[512,1024]{1,0:T(8,128)(2,1)S(1)}, bf16[512,1024]{1,0:T(8,128)(2,1)S(1)}, u32[]{:S(2)}, u32[]{:S(2)}) collective-permute-start(bf16[512,1024]{1,0:T(8,128)(2,1)S(1)} %fusion.33), channel_id=1, source_target_pairs={{0,1},{1,0},{2,3},{3,2},{4,5},{5,4},{6,7},{7,6},{8,9},{9,8},{10,11... | collective-permute-start | bytes 3145736 | tf_op jit(solution)/shard_map/ppermute | solution.py:516
  266.3 43.5 %collective-permute-start.30 = (bf16[512,1024]{1,0:T(8,128)(2,1)}, bf16[512,1024]{1,0:T(8,128)(2,1)S(1)}, u32[]{:S(2)}, u32[]{:S(2)}) collective-permute-start(bf16[512,1024]{1,0:T(8,128)(2,1)} %fusion.36), channel_id=1, source_target_pairs={{0,2},{1,3},{2,0},{3,1},{4,6},{5,7},{6,4},{7,5},{8,10},{9,11},{10,... | collective-permute-start | bytes 3145736 | tf_op jit(solution)/shard_map/ppermute | solution.py:516
  271.8 58.1 %collective-permute-start.26 = (bf16[512,1024]{1,0:T(8,128)(2,1)}, bf16[512,1024]{1,0:T(8,128)(2,1)}, u32[]{:S(2)}, u32[]{:S(2)}) collective-permute-start(bf16[512,1024]{1,0:T(8,128)(2,1)} %get-tuple-element.122), channel_id=1, source_target_pairs={{0,2},{1,3},{2,0},{3,1},{4,6},{5,7},{6,4},{7,5},{8,10},{9,11},{10,... | collective-permute-start | bytes 3145736 | tf_op jit(solution)/shard_map/ppermute | solution.py:516
  272.3 62.1 %collective-permute-start.25 = (bf16[512,1024]{1,0:T(8,128)(2,1)}, bf16[512,1024]{1,0:T(8,128)(2,1)}, u32[]{:S(2)}, u32[]{:S(2)}) collective-permute-start(bf16[512,1024]{1,0:T(8,128)(2,1)} %get-tuple-element.123), channel_id=1, source_target_pairs={{0,1},{1,0},{2,3},{3,2},{4,5},{5,4},{6,7},{7,6},{8,9},{9,8},{10,11... | collective-permute-start | bytes 3145736 | tf_op jit(solution)/shard_map/ppermute | solution.py:516
  329.8 27.8 %collective-permute-start.32 = (bf16[512,1024]{1,0:T(8,128)(2,1)}, bf16[512,1024]{1,0:T(8,128)(2,1)S(1)}, u32[]{:S(2)}, u32[]{:S(2)}) collective-permute-start(bf16[512,1024]{1,0:T(8,128)(2,1)} %get-tuple-element.99), channel_id=1, source_target_pairs={{0,4},{4,0},{8,12},{12,8},{16,20},{20,16},{24,28},{28,24},{1,5},{5... | collective-permute-start | bytes 3145736 | tf_op jit(solution)/shard_map/ppermute | solution.py:519
  333.5 49.6 %collective-permute-start.28 = (bf16[512,1024]{1,0:T(8,128)(2,1)}, bf16[512,1024]{1,0:T(8,128)(2,1)S(1)}, u32[]{:S(2)}, u32[]{:S(2)}) collective-permute-start(bf16[512,1024]{1,0:T(8,128)(2,1)} %fusion.17), channel_id=1, source_target_pairs={{0,1},{1,0},{2,3},{3,2},{4,5},{5,4},{6,7},{7,6},{8,9},{9,8},{10,11... | collective-permute-start | bytes 3145736 | tf_op jit(solution)/shard_map/ppermute | solution.py:516
  337.6 45.5 %collective-permute-start.29 = (bf16[512,1024]{1,0:T(8,128)(2,1)}, bf16[512,1024]{1,0:T(8,128)(2,1)S(1)}, u32[]{:S(2)}, u32[]{:S(2)}) collective-permute-start(bf16[512,1024]{1,0:T(8,128)(2,1)} %fusion.16), channel_id=1, source_target_pairs={{0,2},{1,3},{2,0},{3,1},{4,6},{5,7},{6,4},{7,5},{8,10},{9,11},{10,... | collective-permute-start | bytes 3145736 | tf_op jit(solution)/shard_map/ppermute | solution.py:516
  357.5 25.7 %collective-permute-start.27 = (bf16[512,1024]{1,0:T(8,128)(2,1)}, bf16[512,1024]{1,0:T(8,128)(2,1)S(1)}, u32[]{:S(2)}, u32[]{:S(2)}) collective-permute-start(bf16[512,1024]{1,0:T(8,128)(2,1)} %get-tuple-element.93), channel_id=1, source_target_pairs={{0,4},{4,0},{8,12},{12,8},{16,20},{20,16},{24,28},{28,24},{1,5},{5... | collective-permute-start | bytes 3145736 | tf_op jit(solution)/shard_map/ppermute | solution.py:519
  360.6 19.9 %collective-permute-start.34 = (bf16[256,1024]{1,0:T(8,128)(2,1)}, bf16[256,1024]{1,0:T(8,128)(2,1)}, u32[]{:S(2)}, u32[]{:S(2)}) collective-permute-start(bf16[256,1024]{1,0:T(8,128)(2,1)} %get-tuple-element.133), channel_id=1, source_target_pairs={{0,2},{1,3},{2,0},{3,1},{4,6},{5,7},{6,4},{7,5},{8,10},{9,11},{10,... | collective-permute-start | bytes 1572872 | tf_op jit(solution)/shard_map/ppermute | solution.py:516
  361.1 22.0 %collective-permute-start.33 = (bf16[256,1024]{1,0:T(8,128)(2,1)}, bf16[256,1024]{1,0:T(8,128)(2,1)S(1)}, u32[]{:S(2)}, u32[]{:S(2)}) collective-permute-start(bf16[256,1024]{1,0:T(8,128)(2,1)} %get-tuple-element.134), channel_id=1, source_target_pairs={{0,1},{1,0},{2,3},{3,2},{4,5},{5,4},{6,7},{7,6},{8,9},{9,8},{10,11... | collective-permute-start | bytes 1572872 | tf_op jit(solution)/shard_map/ppermute | solution.py:516
  380.5 35.4 %collective-permute-start.53 = (bf16[64,1024]{1,0:T(8,128)(2,1)}, bf16[64,1024]{1,0:T(8,128)(2,1)}, u32[]{:S(2)}, u32[]{:S(2)}) collective-permute-start(bf16[64,1024]{1,0:T(8,128)(2,1)} %pad_maximum_fusion.15), channel_id=1, source_target_pairs={{0,16},{4,20},{8,24},{12,28},{16,0},{20,4},{24,8},{28,12},{1,17},{... | collective-permute-start | bytes 393224 | tf_op jit(solution)/shard_map/ppermute | solution.py:519
  383.1 63.6 %collective-permute-start.37 = (bf16[512,1024]{1,0:T(8,128)(2,1)}, bf16[512,1024]{1,0:T(8,128)(2,1)}, u32[]{:S(2)}, u32[]{:S(2)}) collective-permute-start(bf16[512,1024]{1,0:T(8,128)(2,1)} %get-tuple-element.105), channel_id=1, source_target_pairs={{0,4},{4,0},{8,12},{12,8},{16,20},{20,16},{24,28},{28,24},{1,5},{5... | collective-permute-start | bytes 3145736 | tf_op jit(solution)/shard_map/ppermute | solution.py:519
  413.6 43.7 %collective-permute-start.40 = (bf16[512,1024]{1,0:T(8,128)(2,1)S(1)}, bf16[512,1024]{1,0:T(8,128)(2,1)S(1)}, u32[]{:S(2)}, u32[]{:S(2)}) collective-permute-start(bf16[512,1024]{1,0:T(8,128)(2,1)S(1)} %fusion.13), channel_id=1, source_target_pairs={{0,8},{4,12},{8,0},{12,4},{16,24},{20,28},{24,16},{28,20},{1,9},{5... | collective-permute-start | bytes 3145736 | tf_op jit(solution)/shard_map/ppermute | solution.py:519
  414.4 24.7 %collective-permute-start.61 = (f32[4,4,39]{2,1,0:T(4,128)S(1)}, f32[4,4,39]{2,1,0:T(4,128)S(1)}, u32[]{:S(2)}, u32[]{:S(2)}) collective-permute-start(f32[4,4,39]{2,1,0:T(4,128)S(1)} %add.270), channel_id=1, source_target_pairs={{0,8},{4,12},{8,0},{12,4},{16,24},{20,28},{24,16},{28,20},{1,9},{5... | collective-permute-start | bytes 7496 | tf_op jit(solution)/shard_map/ppermute | solution.py:519
  441.2 19.9 %collective-permute-start.42 = (bf16[256,1024]{1,0:T(8,128)(2,1)S(1)}, bf16[256,1024]{1,0:T(8,128)(2,1)S(1)}, u32[]{:S(2)}, u32[]{:S(2)}) collective-permute-start(bf16[256,1024]{1,0:T(8,128)(2,1)S(1)} %get-tuple-element.129), channel_id=1, source_target_pairs={{0,1},{1,0},{2,3},{3,2},{4,5},{5,4},{6,7},{7,6},{8,9},{9,8},{10,11... | collective-permute-start | bytes 1572872 | tf_op jit(solution)/shard_map/ppermute | solution.py:516
  455.2 25.6 %collective-permute-start.35 = (bf16[512,1024]{1,0:T(8,128)(2,1)S(1)}, bf16[512,1024]{1,0:T(8,128)(2,1)S(1)}, u32[]{:S(2)}, u32[]{:S(2)}) collective-permute-start(bf16[512,1024]{1,0:T(8,128)(2,1)S(1)} %copy-done.60), channel_id=1, source_target_pairs={{0,4},{4,0},{8,12},{12,8},{16,20},{20,16},{24,28},{28,24},{1,5},{5... | collective-permute-start | bytes 3145736 | tf_op jit(solution)/shard_map/ppermute | solution.py:519
  457.4 23.4 %collective-permute-start.38 = (bf16[256,1024]{1,0:T(8,128)(2,1)S(1)}, bf16[256,1024]{1,0:T(8,128)(2,1)S(1)}, u32[]{:S(2)}, u32[]{:S(2)}) collective-permute-start(bf16[256,1024]{1,0:T(8,128)(2,1)S(1)} %get-tuple-element.132), channel_id=1, source_target_pairs={{0,2},{1,3},{2,0},{3,1},{4,6},{5,7},{6,4},{7,5},{8,10},{9,11},{10,... | collective-permute-start | bytes 1572872 | tf_op jit(solution)/shard_map/ppermute | solution.py:516
  461.0 38.9 %collective-permute-start.41 = (bf16[256,1024]{1,0:T(8,128)(2,1)}, bf16[256,1024]{1,0:T(8,128)(2,1)S(1)}, u32[]{:S(2)}, u32[]{:S(2)}) collective-permute-start(bf16[256,1024]{1,0:T(8,128)(2,1)} %broadcast_select_fusion.8), channel_id=1, source_target_pairs={{0,16},{4,20},{8,24},{12,28},{16,0},{20,4},{24,8},{28,12},{1,17},{... | collective-permute-start | bytes 1572872 | tf_op jit(solution)/shard_map/ppermute | solution.py:519
  482.5 43.8 %collective-permute-start.43 = (bf16[256,1024]{1,0:T(8,128)(2,1)}, bf16[256,1024]{1,0:T(8,128)(2,1)}, u32[]{:S(2)}, u32[]{:S(2)}) collective-permute-start(bf16[256,1024]{1,0:T(8,128)(2,1)} %add_convert_fusion.7), channel_id=1, source_target_pairs={{0,8},{4,12},{8,0},{12,4},{16,24},{20,28},{24,16},{28,20},{1,9},{5... | collective-permute-start | bytes 1572872 | tf_op jit(solution)/shard_map/ppermute | solution.py:519
  501.0 50.9 %collective-permute-start.48 = (bf16[256,1024]{1,0:T(8,128)(2,1)}, bf16[256,1024]{1,0:T(8,128)(2,1)}, u32[]{:S(2)}, u32[]{:S(2)}) collective-permute-start(bf16[256,1024]{1,0:T(8,128)(2,1)} %add_convert_fusion.5), channel_id=1, source_target_pairs={{0,16},{4,20},{8,24},{12,28},{16,0},{20,4},{24,8},{28,12},{1,17},{... | collective-permute-start | bytes 1572872 | tf_op jit(solution)/shard_map/ppermute | solution.py:519
  547.3 18.3 %collective-permute-start.72 = (f32[32,1024]{1,0:T(8,128)S(1)}, f32[32,1024]{1,0:T(8,128)S(1)}, u32[]{:S(2)}, u32[]{:S(2)}) collective-permute-start(f32[32,1024]{1,0:T(8,128)S(1)} %pad_maximum_fusion.18), channel_id=1, source_target_pairs={{0,8},{4,12},{8,0},{12,4},{16,24},{20,28},{24,16},{28,20},{1,9},{5... | collective-permute-start | bytes 393224 | tf_op jit(solution)/shard_map/ppermute | solution.py:519
  553.3 48.7 %collective-permute-start.49 = (bf16[512,1024]{1,0:T(8,128)(2,1)S(1)}, bf16[512,1024]{1,0:T(8,128)(2,1)S(1)}, u32[]{:S(2)}, u32[]{:S(2)}) collective-permute-start(bf16[512,1024]{1,0:T(8,128)(2,1)S(1)} %pad_maximum_fusion.8), channel_id=1, source_target_pairs={{0,8},{4,12},{8,0},{12,4},{16,24},{20,28},{24,16},{28,20},{1,9},{5... | collective-permute-start | bytes 3145736 | tf_op jit(solution)/shard_map/ppermute | solution.py:519
  563.5 38.3 %collective-permute-start.46 = (bf16[256,1024]{1,0:T(8,128)(2,1)S(1)}, bf16[256,1024]{1,0:T(8,128)(2,1)S(1)}, u32[]{:S(2)}, u32[]{:S(2)}) collective-permute-start(bf16[256,1024]{1,0:T(8,128)(2,1)S(1)} %pad_maximum_fusion.9), channel_id=1, source_target_pairs={{0,8},{4,12},{8,0},{12,4},{16,24},{20,28},{24,16},{28,20},{1,9},{5... | collective-permute-start | bytes 1572872 | tf_op jit(solution)/shard_map/ppermute | solution.py:519
  563.6 39.9 %collective-permute-start.59 = (bf16[64,1536]{1,0:T(8,128)(2,1)S(1)}, bf16[64,1536]{1,0:T(8,128)(2,1)S(1)}, u32[]{:S(2)}, u32[]{:S(2)}) collective-permute-start(bf16[64,1536]{1,0:T(8,128)(2,1)S(1)} %pad_maximum_fusion.14), channel_id=1, source_target_pairs={{0,16},{4,20},{8,24},{12,28},{16,0},{20,4},{24,8},{28,12},{1,17},{... | collective-permute-start | bytes 589832 | tf_op jit(solution)/shard_map/ppermute | solution.py:519
  565.7 42.2 %collective-permute-start.73 = (f32[64,1024]{1,0:T(8,128)S(1)}, f32[64,1024]{1,0:T(8,128)S(1)}, u32[]{:S(2)}, u32[]{:S(2)}) collective-permute-start(f32[64,1024]{1,0:T(8,128)S(1)} %pad_maximum_fusion.12), channel_id=1, source_target_pairs={{0,16},{4,20},{8,24},{12,28},{16,0},{20,4},{24,8},{28,12},{1,17},{... | collective-permute-start | bytes 786440 | tf_op jit(solution)/shard_map/ppermute | solution.py:519
  (88 other events, 940.0 us)

commit v2 on v1

--- a/solution.py
+++ b/solution.py
@@ -50,30 +50,75 @@
 
 
 def shape(dims, dtype):
+    return pltpu.HBM(dims, dtype)
+
+
+def near(dims, dtype):
     return jax.ShapeDtypeStruct(dims, dtype)
 
 
-def run(kernel, name, grid, ins, outs, scratch=(), after=(), scalars=(), flops=0, moved=0):
+HBM = pl.BlockSpec(memory_space=pltpu.HBM)
+VMEM = pl.BlockSpec(memory_space=pltpu.VMEM)
+ANY = pl.BlockSpec(memory_space=pl.ANY)
+
+
+class Loads:
+    def __init__(self, sems):
+        self.sems, self.copies = sems, []
+
+    def add(self, source, target):
+        self.copies.append(pltpu.make_async_copy(source, target, self.sems.at[len(self.copies)]))
+        return self.copies[-1]
+
+    def start(self):
+        for copy in self.copies:
+            copy.start()
+
+    def wait(self):
+        for copy in self.copies:
+            copy.wait()
+
+
+def in_hbm(array):
+    return pltpu.with_memory_space_constraint(array, pltpu.HBM)
+
+
+def run(kernel, name, grid, ins, outs, scratch=(), after=(), scalars=(), flops=0, moved=0, vmem=24):
     first = len(scalars) + len(ins)
 
     def body(*refs):
         kernel(*refs[:first], *refs[first + len(after) :])
 
-    hbm = pl.BlockSpec(memory_space=pl.ANY)
     return pl.pallas_call(
         body,
         grid_spec=pltpu.PrefetchScalarGridSpec(
             num_scalar_prefetch=len(scalars),
             grid=(grid,),
-            in_specs=[spec for _, spec in ins] + [hbm] * len(after),
+            in_specs=[spec for _, spec in ins] + [HBM] * len(after),
             out_specs=[spec for _, spec in outs],
             scratch_shapes=list(scratch),
         ),
         out_shape=[what for what, _ in outs],
-        compiler_params=pltpu.CompilerParams(vmem_limit_bytes=56 * 2**20),
-        cost_estimate=pl.CostEstimate(flops=int(flops), bytes_accessed=int(moved), transcendentals=0),
+        compiler_params=pltpu.CompilerParams(vmem_limit_bytes=vmem * 2**20),
+        cost_estimate=pl.CostEstimate(flops=1000, bytes_accessed=1000, transcendentals=0),
         name=name,
-    )(*scalars, *[array for array, _ in ins], *after)
+    )(*scalars, *[array if spec is VMEM else in_hbm(array) for array, spec in ins], *map(in_hbm, after))
+
+
+def hold(values, after=(), flops=1000):
+    return pl.pallas_call(
+        lambda *refs: None,
+        in_specs=[HBM] * (len(values) + len(after)),
+        out_specs=[HBM] * len(values),
+        out_shape=[shape(v.shape, v.dtype) for v in values],
+        input_output_aliases={i: i for i in range(len(values))},
+        cost_estimate=pl.CostEstimate(flops=flops, bytes_accessed=1000, transcendentals=0),
+        name="hold",
+    )(*map(in_hbm, (*values, *after)))
+
+
+def arrive(values, after):
+    return hold(values, after, 30 * 10**9)
 
 
 def ln_parts(values):
@@ -89,16 +134,67 @@
     return rstd * (inner - mean_one - hat * mean_two)
 
 
+def hot_rows(count, source):
+    row = lax.broadcasted_iota(jnp.int32, (count, count), 0)
+    col = lax.broadcasted_iota(jnp.int32, (count, count), 1)
+    return col == source(row), row
+
+
+def qkv_source(core):
+    def source(row):
+        half = jnp.where(row >= QKV, 1, 0)
+        inner = row - half * QKV
+        head = 2 * (half ^ core) + ((inner & 127) >> 6)
+        return head * 3 * HD + (inner >> 7) * HD + (inner & 63)
+
+    return source
+
+
+def attn_rows_kernel(core_ref, qkv_ref, out_ref, own0, own1):
+    core = core_ref[0]
+    hot, row = hot_rows(2 * QKV, qkv_source(core))
+    inner = jnp.where(row >= QKV, row - QKV, row)
+    hot = jnp.where(hot, jnp.where(inner < 128, HD**-0.5, 1.0), 0.0).astype(bf16)
+    rows = mm(hot, qkv_ref[...], NT).astype(bf16)
+    for h, own in enumerate((own0, own1)):
+        own[:QKV] = rows[h * QKV : (h + 1) * QKV]
+        own[QKV:] = out_ref[pl.ds(pl.multiple_of((core ^ h) * 128, 128), 128)]
+
+
+def feed_rows_kernel(core_ref, up_ref, down_ref, own0, own1):
+    core = core_ref[0]
+    hot, _ = hot_rows(2 * HALF, lambda row: row ^ (core * HALF))
+    rows = mm(jnp.where(hot, 1.0, 0.0).astype(bf16), up_ref[...], NT).astype(bf16)
+    for h, own in enumerate((own0, own1)):
+        own[0] = rows[h * HALF : (h + 1) * HALF]
+        own[1] = down_ref[pl.ds(pl.multiple_of((core ^ h) * HALF, HALF), HALF)]
+
+
+def attn_rows(core, qkv, out, after):
+    half = (shape((HALF, D), bf16), whole(HALF, D))
+    ins = [(qkv, whole(D, 2 * QKV)), (out, whole(256, D))]
+    return run(attn_rows_kernel, "attn_rows", 1, ins, [half, half], (), after, [core], 1e9, 4e6)
+
+
+def feed_rows(core, up, down, after):
+    half = (shape((2, HALF, D), bf16), whole(2, HALF, D))
+    ins = [(up, whole(D, 2 * HALF)), (down, whole(2 * HALF, D))]
+    return run(feed_rows_kernel, "feed_rows", 1, ins, [half, half], (), after, [core], 2e9, 8e6)
+
+
 def attend_kernel(len_ref, x_ref, mode_ref, wa_ref, wb_ref, tbl_ref, e_ref, *rest):
-    n1_ref, packed_ref, heads_ref, probs_ref, w_all, kb_all = rest if len(rest) == 6 else (None, *rest)
+    n1_ref, packed_ref, heads_ref, probs_ref, w_all, kb_all, sems = rest if len(rest) == 7 else (None, *rest)
     w = pl.program_id(0)
 
     @pl.when(w == 0)
     def _():
-        w_all[:QKV] = wa_ref[...]
-        w_all[QKV:] = wb_ref[...]
+        loads = Loads(sems)
+        loads.add(wa_ref.at[:QKV], w_all.at[:QKV])
+        loads.add(wb_ref.at[:QKV], w_all.at[QKV:])
+        loads.start()
         for p in range(2):
             kb_all[p] = mm(e_ref[...], tbl_ref[p]).astype(bf16)
+        loads.wait()
 
     if n1_ref is None:
         x = x_ref[...]
@@ -139,7 +235,7 @@
         (shape((count * 4, WIN, WIN), bf16), pl.BlockSpec((4, WIN, WIN), lambda i, l: (i, 0, 0))),
     ]
     if first:
-        outs = [(shape((rows, D), bf16), rows_of(D))] + outs
+        outs = [(near((rows, D), bf16), rows_of(D))] + outs
     return run(
         attend_kernel,
         "attend",
@@ -147,13 +243,13 @@
         [
             (source, window_of(WIN, D) if first else rows_of(D)),
             (modes, window_of(6, D)),
-            (weight[0], part((0, 0), QKV, D)),
-            (weight[1], part((0, 0), QKV, D)),
+            (weight[0], ANY),
+            (weight[1], ANY),
             (table, whole(2, 128, 128)),
             (query_hot, whole(WIN, 128)),
         ],
         outs,
-        [pltpu.VMEM((2 * QKV, D), bf16), pltpu.VMEM((2, WIN, 128), bf16)],
+        [pltpu.VMEM((2 * QKV, D), bf16), pltpu.VMEM((2, WIN, 128), bf16), pltpu.SemaphoreType.DMA((2,))],
         after,
         [lengths],
         9e9,
@@ -161,11 +257,14 @@
     )
 
 
-def middle_kernel(h0, h1, h2, h3, w0, w1, w2, w3, w4, w5, w6, w7, tok, cot, mode, attn_ref, mid_ref, n2_ref, di_ref, w_all):
+def middle_kernel(h0, h1, h2, h3, w0, w1, w2, w3, w4, w5, w6, w7, tok, cot, mode, attn_ref, mid_ref, n2_ref, di_ref, w_all, sems):
     @pl.when(pl.program_id(0) == 0)
     def _():
+        loads = Loads(sems)
         for i, ref in enumerate((w0, w1, w2, w3, w4, w5, w6, w7)):
-            w_all[i * 128 : (i + 1) * 128] = ref[...]
+            loads.add(ref.at[QKV:], w_all.at[pl.ds(i * 128, 128)])
+        loads.start()
+        loads.wait()
 
     heads = jnp.concatenate([h0[...], h1[...], h2[...], h3[...]], axis=1)
     attn = mm(heads, w_all[...])
@@ -185,70 +284,97 @@
         "middle",
         count,
         [(h, rows_of(256)) for h in heads]
-        + [(half, part((3, 0), 128, D)) for pair in weights for half in pair]
+        + [(half, ANY) for pair in weights for half in pair]
         + [(tokens, window_of(WIN, D)), (cotangent, window_of(WIN, D)), (modes, window_of(6, D))],
-        [(shape((rows, D), kind), rows_of(D)) for kind in (bf16, f32, bf16, bf16)],
-        [pltpu.VMEM((D, D), bf16)],
+        [(shape((rows, D), kind), rows_of(D)) for kind in (bf16, f32)] + [(near((rows, D), bf16), rows_of(D))] * 2,
+        [pltpu.VMEM((D, D), bf16), pltpu.SemaphoreType.DMA((8,))],
         after,
         flops=2.7e9,
         moved=22e6,
     )
 
 
-def feed_kernel(n2_ref, di_ref, up0, dn0, up1, dn1, hid_ref, pre_ref, g0_ref, g1_ref):
-    def half_step(up_ref, dn_ref, g_ref):
-        up = up_ref[...]
-        dn = dn_ref[...]
-        v = mm(n2_ref[...], up, NT)
-        hg = mm(di_ref[...], dn, NT)
-        v2 = v * v
-        t = jnp.tanh(v * (C0 + (C0 * C1) * v2))
-        share = 0.5 + 0.5 * t
-        hid = (v * share).astype(bf16)
-        slope = share + (0.5 * v) * (1.0 - t * t) * (C0 + (3.0 * C0 * C1) * v2)
-        pre = (slope * hg).astype(bf16)
-        hid_ref[...] = hid
-        pre_ref[...] = pre
-        g_ref[1] = mm(hid, di_ref[...], TN).astype(bf16)
-        g_ref[0] = mm(pre, n2_ref[...], TN).astype(bf16)
-
-    j = pl.program_id(0)
-
-    @pl.when(j == 0)
-    def _():
-        half_step(up1, dn1, g1_ref)
-
-    @pl.when(j == 1)
-    def _():
-        half_step(up0, dn0, g0_ref)
+CHUNK = 256
+
+
+def feed_kernel(places, n2, di, up0, dn0, up1, dn1, hid_hbm, pre_hbm, g0_hbm, g1_hbm, weight, hid, pre, grad, in_sems, out_sems):
+    loads, stores = Loads(in_sems), Loads(out_sems)
+    for i, ref in enumerate((up0, dn0, up1, dn1)):
+        loads.add(ref.at[places[i]], weight.at[i // 2, i % 2])
+    for i in (2, 3, 0, 1):
+        loads.copies[i].start()
+
+    def store(from_ref, to_ref):
+        stores.add(from_ref, to_ref).start()
+
+    for h, g_hbm in ((1, g1_hbm), (0, g0_hbm)):
+        units = pl.ds(h * HALF, HALF)
+        loads.copies[2 * h].wait()
+        loads.copies[2 * h + 1].wait()
+        for i in range(n2.shape[0] // CHUNK):
+            rows = pl.ds(i * CHUNK, CHUNK)
+            v = mm(n2[rows], weight[h, 0], NT)
+            hg = mm(di[rows], weight[h, 1], NT)
+            v2 = v * v
+            t = jnp.tanh(v * (C0 + (C0 * C1) * v2))
+            share = 0.5 + 0.5 * t
+            hid[h, rows] = (v * share).astype(bf16)
+            slope = share + (0.5 * v) * (1.0 - t * t) * (C0 + (3.0 * C0 * C1) * v2)
+            pre[h, rows] = (slope * hg).astype(bf16)
+        store(hid.at[h], hid_hbm.at[:, units])
+        store(pre.at[h], pre_hbm.at[:, units])
+        grad[h, 1] = mm(hid[h], di[...], TN).astype(bf16)
+        store(grad.at[h, 1], g_hbm.at[1])
+        grad[h, 0] = mm(pre[h], n2[...], TN).astype(bf16)
+        store(grad.at[h, 0], g_hbm.at[0])
+    stores.wait()
 
 
 def feed(normed, down_in, weight, after=()):
     rows = normed.shape[0]
-    ins = [(normed, whole(rows, D)), (down_in, whole(rows, D))]
-    for up, down in weight:
-        for array, place in (up, down):
-            ins.append((array, pl.BlockSpec((None, HALF, D), lambda i, place=place: (place, 0, 0))))
-    columns = pl.BlockSpec((rows, HALF), lambda j: (0, 1 - j))
+    halves = [array for half in weight for array, _ in half]
+    places = [place for half in weight for _, place in half]
     return run(
-        feed_kernel,
+        partial(feed_kernel, places),
         "feed",
-        2,
-        ins,
-        [(shape((rows, 2 * HALF), bf16), columns)] * 2 + [(shape((2, HALF, D), bf16), whole(2, HALF, D))] * 2,
-        (),
+        1,
+        [(normed, VMEM), (down_in, VMEM)] + [(array, HBM) for array in halves],
+        [(shape((rows, 2 * HALF), bf16), HBM)] * 2 + [(shape((2, HALF, D), bf16), HBM)] * 2,
+        [pltpu.VMEM((2, 2, HALF, D), bf16)]
+        + [pltpu.VMEM((2, rows, HALF), bf16)] * 2
+        + [pltpu.VMEM((2, 2, HALF, D), bf16), pltpu.SemaphoreType.DMA((4,)), pltpu.SemaphoreType.DMA((8,))],
         after,
-        flops=8 * rows * D * 2 * HALF,
-        moved=20e6,
-    )
-
-
-def turn_kernel(p0, p1, p2, p3, w0, w1, w2, w3, w4, w5, w6, w7, mid_ref, attn_ref, cot_ref, mode_ref, mg_ref, oi_ref, sum_ref):
-    ng = None
-    for src, pair in ((p0, (w0, w1)), (p1, (w2, w3)), (p2, (w4, w5)), (p3, (w6, w7))):
-        for h in range(2):
-            term = mm(src[:, h * HALF : (h + 1) * HALF], pair[h][...])
-            ng = term if ng is None else ng + term
+        vmem=32,
+    )
+
+
+def unit_sums(sources, pieces, places, weight, acc, sems):
+    w = pl.program_id(0)
+
+    def span(i):
+        return slice(i % 2 * HALF, (i % 2 + 1) * HALF)
+
+    @pl.when(w == 0)
+    def _():
+        loads = Loads(sems)
+        for i, piece in enumerate(pieces):
+            loads.add(piece.at[places[i]], weight.at[pl.ds(i * HALF, HALF)])
+        loads.start()
+        for i, copy in enumerate(loads.copies):
+            copy.wait()
+            term = mm(sources[i // 2][:, span(i)], weight[i * HALF : (i + 1) * HALF])
+            acc[...] = term if i == 0 else acc[...] + term
+
+    @pl.when(w > 0)
+    def _():
+        source = jnp.concatenate([ref[...] for ref in sources], axis=1)
+        acc[...] = mm(source, weight[...])
+
+
+def turn_kernel(places, p0, p1, p2, p3, w0, w1, w2, w3, w4, w5, w6, w7, mid_ref, attn_ref, cot_ref, mode_ref, *rest):
+    mg_ref, oi_ref, sum_ref, weight, acc, sems = rest
+    unit_sums((p0, p1, p2, p3), (w0, w1, w2, w3, w4, w5, w6, w7), places, weight, acc, sems)
+    ng = acc[...]
     hat, rstd = ln_parts(mid_ref[...])
     mg = cot_ref[...].astype(f32) + ln_back(ng, mode_ref[4:5], hat, rstd)
     mg_ref[...] = mg
@@ -258,41 +384,39 @@
     sum_ref[2:3] = jnp.sum(ng * hat, axis=0, keepdims=True)
 
 
-def out_kernel(p0, p1, p2, p3, w0, w1, w2, w3, w4, w5, w6, w7, mid_ref, cot_ref, mode_ref, out_ref, sum_ref):
-    mlp = None
-    for src, pair in ((p0, (w0, w1)), (p1, (w2, w3)), (p2, (w4, w5)), (p3, (w6, w7))):
-        for h in range(2):
-            term = mm(src[:, h * HALF : (h + 1) * HALF], pair[h][...])
-            mlp = term if mlp is None else mlp + term
+def out_kernel(places, p0, p1, p2, p3, w0, w1, w2, w3, w4, w5, w6, w7, mid_ref, cot_ref, mode_ref, *rest):
+    out_ref, sum_ref, weight, acc, sems = rest
+    unit_sums((p0, p1, p2, p3), (w0, w1, w2, w3, w4, w5, w6, w7), places, weight, acc, sems)
+    mlp = acc[...]
     out_ref[...] = (mid_ref[...] + mode_ref[5:6] * mlp).astype(bf16)
     sum_ref[...] = jnp.sum(cot_ref[...].astype(f32) * mlp, axis=0, keepdims=True)
 
 
 def of_units(arrays, weights, which):
-    ins = [(array, rows_of(2 * HALF)) for array in arrays]
-    for pair in weights:
-        for half in pair:
-            array, place = half[which]
-            ins.append((array, pl.BlockSpec((None, HALF, D), lambda i, place=place: (place, 0, 0))))
-    return ins
+    halves = [half[which] for pair in weights for half in pair]
+    ins = [(array, rows_of(2 * HALF)) for array in arrays] + [(array, HBM) for array, _ in halves]
+    scratch = [pltpu.VMEM((8 * HALF, D), bf16), pltpu.VMEM((WIN, D), f32), pltpu.SemaphoreType.DMA((8,))]
+    return ins, scratch, [place for _, place in halves]
 
 
 def turn_step(pre, weights, middle, attn_out, cotangent, modes, after=()):
     count = cotangent.shape[0]
     rows = count * WIN
+    ins, scratch, places = of_units(pre, weights, 0)
     return run(
-        turn_kernel,
+        partial(turn_kernel, places),
         "turn",
         count,
-        of_units(pre, weights, 0)
+        ins
         + [(middle, rows_of(D)), (attn_out, rows_of(D)), (cotangent, window_of(WIN, D)), (modes, window_of(6, D))],
         [
             (shape((rows, D), f32), rows_of(D)),
-            (shape((rows, D), bf16), rows_of(D)),
+            (near((rows, D), bf16), rows_of(D)),
             (shape((count, 3, D), f32), window_of(3, D)),
         ],
-        (),
+        scratch,
         after,
+        vmem=36,
         flops=10.7e9,
         moved=35e6,
     )
@@ -300,29 +424,36 @@
 
 def out_step(hid, weights, middle, cotangent, modes, after=()):
     count = cotangent.shape[0]
+    ins, scratch, places = of_units(hid, weights, 1)
     return run(
-        out_kernel,
+        partial(out_kernel, places),
         "output",
         count,
-        of_units(hid, weights, 1) + [(middle, rows_of(D)), (cotangent, window_of(WIN, D)), (modes, window_of(6, D))],
+        ins + [(middle, rows_of(D)), (cotangent, window_of(WIN, D)), (modes, window_of(6, D))],
         [(shape((count, WIN, D), bf16), window_of(WIN, D)), (shape((count, 1, D), f32), window_of(1, D))],
-        (),
+        scratch,
         after,
+        vmem=36,
         flops=10.7e9,
         moved=30e6,
     )
 
 
 def attend_back_kernel(
-    oi_ref, o0_ref, o1_ref, pk_ref, pr_ref, e_ref, n1_ref, oi_all, ho_ref, pg_ref, g0_ref, g1_ref, rel_ref, pg_all, t_all, ow
+    oi_ref, o0, o1, pk_ref, pr_ref, e_ref, n1_ref, oi_all, ho_hbm, pg_ref, g0_ref, g1_ref, rel_ref, *scratch
 ):
+    pg_all, t_all, ow, ho_ref, sems = scratch
     w = pl.program_id(0)
+    loads = Loads(sems)
+    weights = [loads.add(o.at[QKV:], ow.at[pl.ds(i * 128, 128)]) for i, o in enumerate((o0, o1))]
+    heads = loads.add(ho_hbm, ho_ref)
 
     @pl.when(w == 0)
     def _():
+        loads.start()
         t_all[...] = jnp.zeros_like(t_all)
-        ow[:128] = o0_ref[...]
-        ow[128:] = o1_ref[...]
+        for copy in weights:
+            copy.wait()
 
     hg = mm(oi_ref[...], ow[...], NT).astype(bf16)
     pk = pk_ref[...]
@@ -353,6 +484,7 @@
 
     @pl.when(w == pl.num_programs(0) - 1)
     def _():
+        heads.wait()
         go = mm(ho_ref[...], oi_all[...], TN).astype(bf16)
         gq = mm(pg_all[...], n1_ref[...], TN).astype(bf16)
         for p, g_ref in enumerate((g0_ref, g1_ref)):
@@ -372,14 +504,14 @@
         rows // WIN,
         [
             (out_in, rows_of(D)),
-            (weight[0], part((3, 0), 128, D)),
-            (weight[1], part((3, 0), 128, D)),
+            (weight[0], ANY),
+            (weight[1], ANY),
             (packed, rows_of(2 * QKV)),
             (probs, pl.BlockSpec((4, WIN, WIN), lambda i: (i, 0, 0))),
             (query_hot, whole(WIN, 128)),
-            (normed, whole(rows, D)),
-            (out_in, whole(rows, D)),
-            (heads, whole(rows, 256)),
+            (normed, VMEM),
+            (out_in, VMEM),
+            (heads, HBM),
         ],
         [
             (shape((rows, 2 * QKV), bf16), rows_of(2 * QKV)),
@@ -387,23 +519,32 @@
             (shape((HALF, D), bf16), whole(HALF, D)),
             (shape((2, 32, 128), f32), whole(2, 32, 128)),
         ],
-        [pltpu.VMEM((rows, 2 * QKV), bf16), pltpu.VMEM((2, WIN, 128), f32), pltpu.VMEM((256, D), bf16)],
+        [pltpu.VMEM((rows, 2 * QKV), bf16), pltpu.VMEM((2, WIN, 128), f32), pltpu.VMEM((256, D), bf16)]
+        + [pltpu.VMEM((rows, 256), bf16), pltpu.SemaphoreType.DMA((3,))],
         after,
         flops=13e9,
         moved=20e6,
     )
 
 
-def last_kernel(p0, p1, p2, p3, w0, w1, w2, w3, w4, w5, w6, w7, tok_ref, mode_ref, mg_ref, out_ref, sum_ref, w_all):
+def last_kernel(p0, p1, p2, p3, w0, w1, w2, w3, w4, w5, w6, w7, tok_ref, mode_ref, mg_ref, out_ref, sum_ref, w_all, acc, sems):
     @pl.when(pl.program_id(0) == 0)
     def _():
+        loads = Loads(sems)
         for i, ref in enumerate((w0, w1, w2, w3, w4, w5, w6, w7)):
-            w_all[i * QKV : (i + 1) * QKV] = ref[...]
-
-    ng = None
-    for i, src in enumerate((p0, p1, p2, p3)):
-        term = mm(src[...], w_all[i * 2 * QKV : (i + 1) * 2 * QKV])
-        ng = term if ng is None else ng + term
+            loads.add(ref.at[:QKV], w_all.at[pl.ds(i * QKV, QKV)])
+        loads.start()
+        for i, src in enumerate((p0, p1, p2, p3)):
+            loads.copies[2 * i].wait()
+            loads.copies[2 * i + 1].wait()
+            term = mm(src[...], w_all[i * 2 * QKV : (i + 1) * 2 * QKV])
+            acc[...] = term if i == 0 else acc[...] + term
+
+    @pl.when(pl.program_id(0) > 0)
+    def _():
+        acc[...] = mm(jnp.concatenate([p0[...], p1[...], p2[...], p3[...]], axis=1), w_all[...])
+
+    ng = acc[...]
     hat, rstd = ln_parts(tok_ref[...].astype(f32))
     out_ref[...] = (mg_ref[...] + ln_back(ng, mode_ref[1:2], hat, rstd)).astype(bf16)
     sum_ref[0:1] = jnp.sum(ng, axis=0, keepdims=True)
@@ -417,14 +558,133 @@
         "last",
         count,
         [(array, rows_of(2 * QKV)) for array in packed_grads]
-        + [(half, part((0, 0), QKV, D)) for pair in weights for half in pair]
+        + [(half, ANY) for pair in weights for half in pair]
         + [(tokens, window_of(WIN, D)), (modes, window_of(6, D)), (middle_grad, rows_of(D))],
         [(shape((count, WIN, D), bf16), window_of(WIN, D)), (shape((count, 2, D), f32), window_of(2, D))],
-        [pltpu.VMEM((8 * QKV, D), bf16)],
+        [pltpu.VMEM((8 * QKV, D), bf16), pltpu.VMEM((WIN, D), f32), pltpu.SemaphoreType.DMA((8,))],
         after,
         flops=8e9,
         moved=24e6,
     )
+
+
+def merge_kernel(sums, count, *refs):
+    i = pl.program_id(0)
+    refs = list(refs)
+    outs = refs[len(refs) - len(sums) :]
+    for spans, out in zip(sums, outs):
+        value = None
+        for first, last in spans:
+            term = refs.pop(0)[...].astype(f32)
+            if (first, last) != (0, count):
+                term = jnp.where((i >= first) & (i < last), term, 0.0)
+            value = term if value is None else value + term
+        out[...] = value.astype(bf16)
+
+
+def merge(*sums, rows=HALF, after=()):
+    block = 128
+    ins, spans = [], []
+    for terms in sums:
+        spans.append([])
+        for array, place, start, *limits in terms:
+            first, last = [limit // block for limit in (limits or (0, rows))]
+            start = start // block
+
+            def at(i, start=start, first=first, last=last):
+                return jnp.clip(i, first, last - 1) + start
+
+            if place is None:
+                spec = pl.BlockSpec((block, D), lambda i, at=at: (at(i), 0))
+            else:
+                spec = pl.BlockSpec((None, block, D), lambda i, p=place, at=at: (p, at(i), 0))
+            ins.append((array, spec))
+            spans[-1].append((first, last))
+    out = (shape((rows, D), bf16), pl.BlockSpec((block, D), lambda i: (i, 0)))
+    return run(partial(merge_kernel, spans, rows // block), "merge", rows // block, ins, [out] * len(sums), (), after)
+
+
+def parts_kernel(count, only, z_ref, *refs):
+    which_sum = pl.program_id(0) % (1 + max([0] + [w for w in only if w is not None]))
+    terms = len(only)
+    for k in range(count):
+        value = None
+        for ref, which in zip(refs[k * terms : (k + 1) * terms], only):
+            term = ref[...].astype(f32)
+            if which is not None:
+                term = jnp.where(which_sum == which, term, 0.0)
+            value = term if value is None else value + term
+        refs[count * terms + k][...] = value.astype(bf16)
+
+
+def merge_parts(terms, z, count, outputs):
+    size = HALF // count
+    sums = max(2 if isinstance(term, tuple) or term.ndim == 3 else 1 for term in terms)
+    ins, only = [], []
+    for j in range(outputs):
+        for term in terms:
+            array, which = term if isinstance(term, tuple) else (term, None)
+
+            def at(i, zr, j=j):
+                return zr[0] ^ (i // sums * outputs + j)
+
+            if array.ndim == 3:
+                spec = pl.BlockSpec((None, size, D), lambda i, zr, at=at: (i % sums, at(i, zr), 0))
+            else:
+                spec = pl.BlockSpec((size, D), lambda i, zr, at=at: (at(i, zr), 0))
+            ins.append((array, spec))
+            only.append(which)
+    grid = sums * count // outputs
+    outs = [(shape((grid * size, D), bf16), pl.BlockSpec((size, D), lambda i, zr: (i, 0)))] * outputs
+    return run(partial(parts_kernel, outputs, only[: len(terms)]), "merge_parts", grid, ins, outs, (), (), [z])
+
+
+def attn_final_kernel(place_ref, a_ref, b_ref, qkv_ref, out_ref, rows):
+    core, z = place_ref[0], place_ref[1]
+    size = HALF // 4
+    for h, ref in enumerate((a_ref, b_ref)):
+        for k in range(4):
+            part_at = z ^ k
+            block = ref[k * size : (k + 1) * size]
+
+            @pl.when(part_at < 3)
+            def _():
+                rows[pl.ds(pl.multiple_of(h * QKV + part_at * size, size), size)] = block
+
+            @pl.when(part_at == 3)
+            def _():
+                out_ref[pl.ds(pl.multiple_of((core ^ h) * size, size), size)] = block.astype(f32)
+
+    hot, row = hot_rows(2 * QKV, qkv_source(core))
+    inner = jnp.where(row >= QKV, row - QKV, row)
+    hot = jnp.where(hot, jnp.where(inner < 128, HD**-0.5, 1.0), 0.0).astype(bf16)
+    qkv_ref[...] = mm(rows[...], hot, TN)
+
+
+def attn_final(place, a, b):
+    ins = [(a, whole(HALF, D)), (b, whole(HALF, D))]
+    outs = [(shape((D, 2 * QKV), f32), whole(D, 2 * QKV)), (shape((256, D), f32), whole(256, D))]
+    return run(attn_final_kernel, "attn_final", 1, ins, outs, [pltpu.VMEM((2 * QKV, D), bf16)], (), [place])
+
+
+def feed_final_kernel(place_ref, *refs):
+    up_ref, down_ref, rows = refs[4:]
+    core, z = place_ref[0], place_ref[1]
+    size = HALF // 4
+    for h in range(2):
+        for k, (ref, first) in enumerate(((refs[2 * h], 0), (refs[2 * h + 1], 0), (refs[2 * h], 2), (refs[2 * h + 1], 2))):
+            start = (z ^ k) * size
+            rows[pl.ds(pl.multiple_of(h * HALF + start, size), size)] = ref[first * size : (first + 1) * size]
+            block = ref[(first + 1) * size : (first + 2) * size].astype(f32)
+            down_ref[pl.ds(pl.multiple_of((core ^ h) * HALF + start, size), size)] = block
+    hot, _ = hot_rows(2 * HALF, lambda row: row ^ (core * HALF))
+    up_ref[...] = mm(rows[...], jnp.where(hot, 1.0, 0.0).astype(bf16), TN)
+
+
+def feed_final(place, even, odd, other_even, other_odd):
+    ins = [(v, whole(HALF, D)) for v in (even, odd, other_even, other_odd)]
+    outs = [(shape((D, 2 * HALF), f32), whole(D, 2 * HALF)), (shape((2 * HALF, D), f32), whole(2 * HALF, D))]
+    return run(feed_final_kernel, "feed_final", 1, ins, outs, [pltpu.VMEM((2 * HALF, D), bf16)], (), [place])
 
 
 def silu_plain(values):
@@ -505,148 +765,107 @@
     timesteps,
     classes,
 ):
-    n_dp, n_mp = sizes
+    n_z, n_mp = sizes
+    n_dp = 2 * n_z
     micro = tokens.shape[0]
     mp = lax.axis_index("mp")
-    dp = lax.axis_index("dp")
-    core = dp & 1
-    z_bits = [1 << b for b in range(1, n_dp.bit_length() - 1)]
+    z = lax.axis_index("z")
+    core = lax.axis_index("core")
 
     def swap_mp(bit):
         return lambda v: lax.ppermute(v, "mp", [(i, i ^ bit) for i in range(n_mp)])
 
     def swap_dp(bit):
-        return lambda v: lax.ppermute(v, "dp", [(i, i ^ bit) for i in range(n_dp)])
+        return lambda v: lax.ppermute(v, ("z", "core"), [(i, i ^ bit) for i in range(n_dp)])
 
     px, py, pd = swap_mp(1), swap_mp(2), swap_mp(3)
     pc = swap_dp(1)
     by_rel = [lambda v: v, px, py, pd]
 
-    def total(*values):
-        return sum(v.astype(f32) for v in values).astype(bf16)
-
     def cat(a, b, axis=0):
         return jnp.concatenate([a, b], axis=axis)
 
-    def ordered(flag, a, b, axis=0):
-        return cat(jnp.where(flag, a, b), jnp.where(flag, b, a), axis)
-
-    def dp_gather(v):
-        for bit in (1, *z_bits):
-            v = ordered((dp & bit) == 0, v, swap_dp(bit)(v))
-        return v
+    dp_steps = [(1, core == 0)] + [(2 << b, ((z >> b) & 1) == 0) for b in range(n_z.bit_length() - 1)]
+
+    def join(low, v, got):
+        return cat(jnp.where(low, v, got), jnp.where(low, got, v))
 
     pre_cond = condition(timesteps, classes, class_table)
     cond_low = silu_plain(pre_cond).astype(bf16)
     mode_cols = jnp.einsum("mwd,de->mwe", cond_low, ada_weight, preferred_element_type=f32) + ada_bias.astype(f32)
     order = jnp.arange(4) ^ mp
-    rel_modes = [
-        by_rel[r](lax.dynamic_index_in_dim(mode_cols, mp ^ r, axis=1, keepdims=False)) for r in range(4)
+    rel_row = jnp.pad(rel_bias, ((0, 0), (0, 128 - rel_bias.shape[1])))
+    messages = [
+        by_rel[r](cat(lax.dynamic_index_in_dim(mode_cols, mp ^ r, axis=1, keepdims=False), rel_row, 1))
+        for r in range(4)
     ]
-    modes = jnp.take(jnp.stack(rel_modes), order, axis=0)
+    messages = jnp.stack(messages)
+    columns = mode_cols.shape[-1]
+    modes = jnp.take(messages[:, :, :columns], order, axis=0)
     modes = modes.transpose(1, 0, 2).reshape(micro, 6, D)
+    tables = key_tables(messages[:, :, columns : columns + rel_bias.shape[1]], core)
     own_lengths = lax.dynamic_index_in_dim(lengths, mp, axis=1, keepdims=False)
 
-    row = np.arange(2 * QKV)
-    src = 2 * ((row // QKV) ^ core) + (row % 128) // 64
-    src = src * 192 + ((row % QKV) // 128) * 64 + row % 64
-    scale = np.where((row % QKV) < 128, HD**-0.5, 1.0).astype(np.float32)
-    qkv_hot = jnp.where(jnp.arange(2 * QKV)[:, None] == src[None, :], scale[None, :], 0.0).astype(bf16)
-    unit = np.arange(2 * HALF)
-    up_hot = (unit[:, None] == (unit ^ (core * HALF))[None, :]).astype(bf16)
-    both = (((0,), (1,)), ((), ()))
-    qkv_rows = lax.dot_general(qkv_hot, qkv_weight, both, preferred_element_type=f32).astype(bf16)
-    up_rows = lax.dot_general(up_hot, up_weight, both, preferred_element_type=f32).astype(bf16)
-
-    def half_of(v, h):
-        size = v.shape[0] // 2
-        return lax.dynamic_slice_in_dim(v, (core ^ h) * size, size, 0)
-
-    attn_own = [cat(qkv_rows[h * QKV : (h + 1) * QKV], half_of(out_weight, h)) for h in range(2)]
-    feed_own = [jnp.stack([up_rows[h * HALF : (h + 1) * HALF], half_of(down_weight, h)]) for h in range(2)]
-
+    core_row = core.reshape(1)
+    query_hot = jnp.asarray(query_side(), bf16)
+    packed, heads, probs = [None] * 4, [None] * 4, [None] * 4
+
+    attn_own = attn_rows(core_row, qkv_weight, out_weight, [messages])
     ax, ay = px(attn_own[0]), py(attn_own[0])
-    ad = cat(py(ax[: HALF // 2]), px(ay[HALF // 2 :]))
-    attn_w = [attn_own] + [[v, pc(v)] for v in (ax, ay, ad)]
+    normed_one, packed[0], heads[0], probs[0] = attend(own_lengths, tokens, modes, attn_own, tables[0], query_hot)
+    feed_own = list(feed_rows(core_row, up_weight, down_weight, [heads[0]]))
+    ax, ay = hold([ax, ay], [heads[0]])
+    adx, ady = py(ax[: HALF // 2]), px(ay[HALF // 2 :])
+    attn_w = [attn_own, [ax, pc(ax)], [ay, pc(ay)]]
+    packed[1], heads[1], probs[1] = attend(
+        own_lengths, normed_one, modes, attn_w[1], tables[1], query_hot, [feed_own[1]]
+    )
+    adx, ady = hold([adx, ady], [heads[1]])
+    (feed_own[0],) = hold(feed_own[:1], [adx, ady])
     fx, fy = px(feed_own[0]), py(feed_own[0])
-    fu, fd = py(fx[:1]), px(fy[1:])
+    ad = cat(adx, ady)
+    attn_w.append([ad, pc(ad)])
+    for r in (2, 3):
+        packed[r], heads[r], probs[r] = attend(
+            own_lengths, normed_one, modes, attn_w[r], tables[r], query_hot, [heads[r - 1]]
+        )
+    attn_out, middle, normed_two, down_in = middle_step(heads, attn_w, tokens, cotangent, modes)
+
+    hid, pre, mine, other = [None] * 4, [None] * 4, [None] * 4, [None] * 4
+
+    def feed_step(r, weight, after):
+        hid[r], pre[r], mine[r], sent = feed(normed_two, down_in, weight, after)
+        other[r] = pc(sent)
+
+    def pair(r, which):
+        return [(mine[r], which, 0), (other[r], which, 0)]
+
     feed_w = [[((v, 0), (v, 1)) for v in feed_own]]
+    feed_step(0, feed_w[0], [])
+    fx, fy = hold([fx, fy], [hid[0]])
+    fu, fd = fx[:1], fy[1:]
     feed_w += [[((v, 0), (v, 1)) for v in (u, pc(u))] for u in (fx, fy)]
+    feed_step(1, feed_w[1], [hid[0], fu, fd])
+    fu, fd = py(fu), px(fd)
+    feed_step(2, feed_w[2], [hid[1]])
+    fu, fd = arrive([fu, fd], [hid[2]])
     feed_w += [[((u, 0), (v, 0)) for u, v in ((fu, fd), (pc(fu), pc(fd)))]]
-
-    rel_all = jnp.stack([by_rel[r](rel_bias) for r in range(4)])
-    tables = key_tables(rel_all, core)
-    query_hot = jnp.asarray(query_side(), bf16)
-
-    packed, heads, probs = [None] * 4, [None] * 4, [None] * 4
-    normed_one, packed[0], heads[0], probs[0] = attend(own_lengths, tokens, modes, attn_w[0], tables[0], query_hot)
-    for r in (1, 2, 3):
-        packed[r], heads[r], probs[r] = attend(
-            own_lengths, normed_one, modes, attn_w[r], tables[r], query_hot, [ad] if r == 2 else []
-        )
-    attn_out, middle, normed_two, down_in = middle_step(heads, attn_w, tokens, cotangent, modes)
-
-    hid, pre, mine, other = [None] * 4, [None] * 4, [None] * 4, [None] * 4
-
-    def feed_step(r, after):
-        hid[r], pre[r], mine[r], sent = feed(normed_two, down_in, feed_w[r], after)
-        other[r] = pc(sent)
-
-    feed_step(1, [fx, fy])
-    feed_step(2, [])
-    send_x = px(total(mine[1][0], other[1][0]))
-    feed_step(3, [other[1]])
-    send_y = py(total(mine[2][1], other[2][1]))
-    feed_step(0, [other[2]])
-    diag_x = px(total(mine[3][0], other[3][0]))
-    diag_y = py(total(mine[3][1], other[3][1]))
+    (send_x,) = merge(pair(1, 0), after=[fu])
+    (send_y,) = merge(pair(2, 1), after=[send_x])
+    feed_step(3, feed_w[3], [hid[2], send_y])
+    send_x, send_y = arrive([px(send_x), py(send_y)], [hid[3]])
+    diag_x, diag_y = merge(pair(3, 0), pair(3, 1), after=[send_x])
     middle_grad, out_in, turn_sums = turn_step(
-        pre, feed_w, middle, attn_out, cotangent, modes, [other[3], send_x]
-    )
-    last_x = px(total(mine[1][1], other[1][1], diag_y))
-    last_y = py(total(mine[2][0], other[2][0], diag_x))
-    feed_a = (mine[0][0], other[0][0], send_x, last_y)
-    feed_b = (mine[0][1], other[0][1], last_x, send_y)
-
-    class Steps:
-        def __init__(self, a, b):
-            low = (dp & z_bits[0]) == 0
-            pick = lambda flag: [jnp.where(flag, u, v) for u, v in zip(a, b)]
-            self.keep, self.sent = total(*pick(low)), total(*pick(~low))
-            self.level, self.back, self.got = 0, [], None
-
-        def down(self):
-            self.got = swap_dp(z_bits[self.level])(self.sent)
-            return self.got
-
-        def cut(self):
-            keep = total(self.keep, self.got)
-            self.level += 1
-            if self.level < len(z_bits):
-                low = (dp & z_bits[self.level]) == 0
-                size = keep.shape[0] // 2
-                a, b = keep[:size], keep[size:]
-                self.keep, self.sent = jnp.where(low, a, b), jnp.where(low, b, a)
-            else:
-                self.keep = keep
-
-        def up(self):
-            self.level -= 1
-            self.got = swap_dp(z_bits[self.level])(self.keep)
-            return self.got
-
-        def join(self):
-            low = (dp & z_bits[self.level]) == 0
-            self.keep = ordered(low, self.keep, self.got)
-
-        def rest(self):
-            while self.level < len(z_bits):
-                self.down()
-                self.cut()
-            while self.level > 0:
-                self.up()
-                self.join()
-            return self.keep, pc(self.keep)
+        pre, feed_w, middle, attn_out, cotangent, modes, [diag_x, diag_y]
+    )
+    diag_x, diag_y = arrive([px(diag_x), py(diag_y)], [middle_grad])
+    last_x, last_y = merge(pair(1, 1) + [(diag_y, None, 0)], pair(2, 0) + [(diag_x, None, 0)])
+    output, out_sums = out_step(hid, feed_w, middle, cotangent, modes, [last_x, last_y])
+    last_x, last_y = arrive([px(last_x), py(last_y)], [out_sums])
+    z_row = z.reshape(1)
+    terms = [mine[0], other[0], (send_x, 0), (last_y, 0), (last_x, 1), (send_y, 1)]
+    feed_keep, feed_sent = merge_parts(terms, z_row, n_z, 2)
+    z_one, z_two = swap_dp(2), swap_dp(4)
 
     packed_grad, rel_grid, a_mine, a_other = [None] * 4, [None] * 4, [None] * 4, [None] * 4
 
@@ -657,60 +876,77 @@
         a_other[r] = pc(sent)
 
     cut = HALF // 2
-    back_step(3, [send_y, other[0]])
-    back_step(1, [diag_x, diag_y])
-    a_diag_x = px(total(a_mine[3][:cut], a_other[3][:cut]))
-    a_diag_y = py(total(a_mine[3][cut:], a_other[3][cut:]))
-    back_step(2, [a_other[3]])
-    a_send_x = px(total(a_mine[1][:cut], a_other[1][:cut]))
-    back_step(0, [a_other[1], last_x, last_y, a_diag_x, a_diag_y])
-    feed_steps = Steps(feed_a, feed_b)
-    a_send_y = py(total(a_mine[2][cut:], a_other[2][cut:]))
-    a_last_x = px(total(a_mine[1][cut:], a_other[1][cut:], a_diag_y))
-    a_last_y = py(total(a_mine[2][:cut], a_other[2][:cut], a_diag_x))
-    token_grads, last_sums = last_step(
-        packed_grad, attn_w, tokens, modes, middle_grad, [a_other[2], a_send_x, feed_steps.down()]
-    )
-    feed_steps.cut()
-    attn_steps = Steps(
-        (a_mine[0][:cut], a_other[0][:cut], a_send_x, a_last_y), (a_mine[0][cut:], a_other[0][cut:], a_last_x, a_send_y)
-    )
-    output, out_sums = out_step(
-        hid, feed_w, middle, cotangent, modes, [a_other[0], a_last_x, a_last_y, a_send_y, feed_steps.down()]
-    )
-    a, b = feed_steps.rest()
-    up_back, down_back = cat(a[:HALF], b[:HALF]), ordered(core == 0, a[HALF:], b[HALF:])
-    grad_up = lax.dot_general(up_back, up_hot, both, preferred_element_type=f32)
-    grad_down = down_back.astype(f32)
-    a, b = attn_steps.rest()
-    grad_qkv = lax.dot_general(cat(a[:QKV], b[:QKV]), qkv_hot, both, preferred_element_type=f32)
-    grad_out = ordered(core == 0, a[QKV:], b[QKV:]).astype(f32)
-
-    rel_part = rel_sums(jnp.stack(rel_grid), core)
-    for bit in (1, *z_bits):
-        rel_part = rel_part + swap_dp(bit)(rel_part)
-    grad_rel = rel_part[0] + px(rel_part[1]) + py(rel_part[2]) + pd(rel_part[3])
-
-    mode_grad = jnp.concatenate([last_sums, turn_sums, out_sums], axis=1).reshape(micro, 4, -1)
-    mode_grad_cols = jnp.stack(
-        [by_rel[r](lax.dynamic_index_in_dim(mode_grad, mp ^ r, axis=1, keepdims=False)) for r in range(4)]
-    )
-    mode_low = mode_grad_cols.astype(bf16).reshape(4 * micro, -1)
+
+    def a_pair(r, start):
+        return [(a_mine[r], None, start), (a_other[r], None, start)]
+
+    back_step(3, [feed_keep])
+    (feed_got,) = arrive([z_one(feed_sent)], [packed_grad[3]])
+    (feed_sent,) = merge([(feed_keep, None, cut), (feed_got, None, cut)], rows=cut)
+    back_step(1, [packed_grad[3], feed_sent])
+    (feed_two,) = arrive([z_two(feed_sent)], [packed_grad[1]])
+    (feed_one,) = merge([(feed_keep, None, 0), (feed_got, None, 0), (feed_two, None, 0)], rows=cut)
+    a_diag_x, a_diag_y = merge(a_pair(3, 0), a_pair(3, cut), rows=cut, after=[feed_one])
+    back_step(2, [a_diag_x, a_diag_y])
+    feed_two, a_diag_x, a_diag_y = arrive([z_two(feed_one), px(a_diag_x), py(a_diag_y)], [packed_grad[2]])
+    feed_even = cat(feed_one, feed_two)
+    (a_last_x,) = merge(a_pair(1, 0) + [(a_diag_y, None, -cut, cut, HALF)])
+    (a_last_y,) = merge(a_pair(2, 0) + [(a_diag_x, None, 0, 0, cut)], after=[a_last_x])
+    back_step(0, [packed_grad[2], a_last_y, feed_even])
+    feed_odd, a_last_x, a_last_y = arrive([z_one(feed_even), px(a_last_x), py(a_last_y)], [packed_grad[0]])
+
+    def exchange(parts):
+        return [swap_dp(2 * k)(v) for k, v in enumerate(parts) if k]
+
+    attn_parts = merge_parts([a_mine[0], a_other[0], a_last_x, a_last_y], z_row, n_z, n_z)
+    token_grads, last_sums = last_step(packed_grad, attn_w, tokens, modes, middle_grad, attn_parts)
+    attn_got = exchange(attn_parts)
+    feed_other = [pc(feed_even), pc(feed_odd)]
+    *attn_got, feed_other[0], feed_other[1] = arrive(attn_got + feed_other, [last_sums])
+    (attn_own,) = merge([(v, None, 0) for v in (attn_parts[0], *attn_got)], rows=HALF // n_z)
+
+    place = jnp.stack([core, z])
+    mode_grad = jnp.concatenate([last_sums, turn_sums, out_sums], axis=1).reshape(micro, 4, -1).transpose(1, 0, 2)
+    messages = [lax.dynamic_index_in_dim(mode_grad, mp ^ r, axis=0, keepdims=False) for r in range(4)]
+    rel_grid = hold(rel_grid, [attn_own])
+    rel_part = jnp.pad(rel_sums(jnp.stack(rel_grid), core), ((0, 0), (0, 4 * (micro - 1)), (0, 128 - rel_bias.shape[1])))
+    *messages[1:], attn_far = arrive([by_rel[r](messages[r]) for r in (1, 2, 3)] + [swap_dp(6)(attn_own)], [attn_own])
+    mode_low = jnp.stack(messages).astype(bf16).reshape(4 * micro, -1)
+    cond_grad = mm(mode_low, ada_weight, NT).reshape(4, micro, D)
+    cond_grad = jnp.take(cond_grad, order, axis=0).reshape(4 * micro, D)
+    grad_up, grad_down = feed_final(place, feed_even, feed_odd, *feed_other)
+    shares = [cat(cond_grad, rel_part[r], 1) for r in range(4)]
+    *shares[1:], attn_two = arrive(
+        [by_rel[r](shares[r]) for r in (1, 2, 3)] + [swap_dp(4)(attn_own)], [attn_far, grad_up]
+    )
+    shares = jnp.take(jnp.stack(shares), order, axis=0)
+    cond_grad = shares[0] + shares[1] + shares[2] + shares[3]
+    own_pre = pre_cond.transpose(1, 0, 2).reshape(4 * micro, D)
+    share = 1.0 / (1.0 + jnp.exp(-own_pre))
+    own_class = cond_grad[:, :D] * (share * (1.0 + own_pre * (1.0 - share)))
+    grads = jnp.concatenate([mode_low, own_class.astype(bf16), cond_grad[:, D:].astype(bf16)], axis=1)
+    got, attn_one = arrive([swap_dp(dp_steps[0][0])(grads), swap_dp(2)(attn_own)], [attn_two])
+    grads = join(dp_steps[0][1], grads, got)
+    attn_own = jnp.concatenate([attn_own, attn_one, attn_two, attn_far])
+    got, attn_other = arrive([swap_dp(dp_steps[1][0])(grads), pc(attn_own)], [attn_one])
+    grads = join(dp_steps[1][1], grads, got)
+    grad_qkv, grad_out = attn_final(place, attn_own, attn_other)
+    for step, low in dp_steps[2:]:
+        (got,) = arrive([swap_dp(step)(grads)], [grad_qkv])
+        grads = join(low, grads, got)
+    mode_all, class_part, rel_part = grads[:, :columns], grads[:, columns : columns + D], grads[:, columns + D :]
+    grad_rel = jnp.sum(rel_part.astype(f32).reshape(n_dp, 4 * micro, -1), axis=0)[:4, : rel_bias.shape[1]]
+
+    class_col = jnp.pad(classes.T.reshape(-1, 1).astype(bf16), ((0, 0), (0, 127)))
     cond_rel = jnp.take(cond_low, order, axis=1).transpose(1, 0, 2).reshape(4 * micro, D)
-    cond_all = dp_gather(cond_rel)
-    mode_all = dp_gather(mode_low)
-    grad_ada = mm(cond_all, mode_all, TN)
+    cond_all = cat(cond_rel, class_col, 1)
+    for step, low in dp_steps:
+        cond_all = join(low, cond_all, swap_dp(step)(cond_all))
+    class_all = cond_all[:, D].astype(jnp.int32)
+    grad_ada = mm(cond_all[:, :D], mode_all, TN)
     grad_ada_bias = jnp.sum(mode_all.astype(f32), axis=0)
-    cond_grad = mm(mode_low, ada_weight, NT).reshape(4, micro, D)
-    cond_grad = jnp.take(cond_grad, order, axis=0)
-    cond_grad = cond_grad + px(cond_grad)
-    cond_grad = cond_grad + py(cond_grad)
-    own_pre = pre_cond.transpose(1, 0, 2)
-    share = 1.0 / (1.0 + jnp.exp(-own_pre))
-    cond_grad = cond_grad * (share * (1.0 + own_pre * (1.0 - share)))
-    class_all = dp_gather(classes.T.reshape(-1))
-    class_hot = (jnp.arange(class_table.shape[0])[:, None] == class_all[None, :]).astype(f32)
-    class_grad = jnp.dot(class_hot, dp_gather(cond_grad.reshape(4 * micro, D)), precision=precise)
+    class_hot = (jnp.arange(class_table.shape[0])[:, None] == class_all[None, :]).astype(bf16)
+    class_grad = jnp.dot(class_hot, class_part, preferred_element_type=f32)
 
     return (
         output,
@@ -976,41 +1212,25 @@
     )
 
 
-def local(sizes, *arrays):
-    if arrays[0].shape[1] == WIN and sizes[1] == 4:
-        return local_windows(sizes, *arrays)
-    return local_general(*arrays)
-
-
 def solution(mesh):
-    in_specs = (
-        P(None, ("dp", "mp"), None),
-        P(None, ("dp", "mp"), None),
-        P(None, "mp"),
-        P("mp", None),
-        P(None, "mp"),
-        P("mp", None),
-        P(None, "mp"),
-        P("mp"),
-        P("mp", None),
-        P(),
-        P(None, "dp"),
-        P(None, "dp"),
-        P(None, "dp"),
-    )
-    out_specs = (
-        P(None, ("dp", "mp"), None),
-        P(None, ("dp", "mp"), None),
-        P(None, "mp"),
-        P("mp", None),
-        P(None, "mp"),
-        P("mp", None),
-        P(None, "mp"),
-        P("mp"),
-        P("mp", None),
-        P(),
-    )
-    sizes = (mesh.shape["dp"], mesh.shape["mp"])
-    return jax.shard_map(
-        partial(local, sizes), mesh=mesh, in_specs=in_specs, out_specs=out_specs, check_vma=False
-    )
+    n_dp, n_mp = mesh.shape["dp"], mesh.shape["mp"]
+
+    def specs(*dp):
+        rows = P(None, (*dp, "mp"), None)
+        weights = (P(None, "mp"), P("mp", None), P(None, "mp"), P("mp", None), P(None, "mp"), P("mp"), P("mp", None), P())
+        return (rows, rows, *weights, *[P(None, dp)] * 3), (rows, rows, *weights)
+
+    def program(tokens, *arrays):
+        if n_mp == 4 and n_dp % 2 == 0 and tokens.shape[1] == n_dp * n_mp * WIN:
+            devices = mesh.devices.reshape(n_dp // 2, 2, n_mp)
+            split = jax.sharding.Mesh(devices, ("z", "core", "mp"))
+            ins, outs = specs("z", "core")
+            step = jax.shard_map(
+                partial(local_windows, (n_dp // 2, n_mp)), mesh=split, in_specs=ins, out_specs=outs, check_vma=False
+            )
+        else:
+            ins, outs = specs("dp")
+            step = jax.shard_map(local_general, mesh=mesh, in_specs=ins, out_specs=outs, check_vma=False)
+        return step(tokens, *arrays)
+
+    return program

time: 629 us -> 524 us (0.83)
  waiting for transfers between devices: 164 us -> 53.5 us
  Pallas kernels: 276 us -> 332 us
  other arithmetic: 60.1 us -> 21.4 us
  local copies, waits for them, and re-layouts: 24.1 us -> 41.4 us
  starting transfers between devices: 70.2 us -> 55.5 us
  matrix products: 24.7 us -> 12.2 us
    ppermute x34 -> x27, waiting for transfers between devices: 87.9 us -> 19.3 us  [swap_mp(): return lambda v: lax.ppermute(v, 'mp', [(i, i ^ bit) for i in range(n_mp)])]
    pallas_call x16 -> x32, Pallas kernels: 276 us -> 332 us  [run(): pl.pallas_call(body, grid_spec=pltpu.PrefetchScalarGridSpec(num_scalar_pr...]
    ppermute x40 -> x34, waiting for transfers between devices: 75.9 us -> 34.2 us  [swap_dp(): lax.ppermute(v, ('z', 'core'), [(i, i ^ bit) for i in range(n_dp)])]
    convert_element_type x18 -> x4, other arithmetic: 38.6 us -> 1.82 us  [the longest x1 0.88 us: local_windows(): own_class.astype(bf16)]
    unnamed x133 -> x127, local copies, waits for them, and re-layouts: 9.21 us -> 25.8 us
    dot_general x5 -> x1, matrix products: 14 us -> 0.96 us  [local_windows(): class_grad = jnp.dot(class_hot, class_part, preferred_element_type=f32)]
    ppermute x34 -> x27, starting transfers between devices: 39.9 us -> 28.7 us  [swap_mp(): return lambda v: lax.ppermute(v, 'mp', [(i, i ^ bit) for i in range(n_mp)])]
    ppermute x40 -> x34, starting transfers between devices: 30.3 us -> 26.8 us  [swap_dp(): lax.ppermute(v, ('z', 'core'), [(i, i ^ bit) for i in range(n_dp)])]
  transfers between devices with their start and end apart: 74 -> 61, of which waited for: 17 -> 18; matrix products, arithmetic and copies ran while one was open for 15% -> 8% of each run, Pallas kernels for 44% -> 59%
where the time goes in v2:
time: 524 us; the launch traced here: 519 us
  Pallas kernels  332 us (63%)
  starting transfers between devices  55.5 us (11%)
  waiting for transfers between devices  53.5 us (10%)
  local copies, waits for them, and re-layouts  41.4 us (8%)
  other arithmetic  21.4 us (4%)
  matrix products  12.2 us (2%)
    pallas_call x32, Pallas kernels, run(): pl.pallas_call(body, grid_spec=pltpu.PrefetchScalarGridSpec(num_scalar_pr...  332 us
    ppermute x34, waiting for transfers between devices, swap_dp(): lax.ppermute(v, ('z', 'core'), [(i, i ^ bit) for i in range(n_dp)])  34.2 us
    ppermute x27, starting transfers between devices, swap_mp(): return lambda v: lax.ppermute(v, 'mp', [(i, i ^ bit) for i in range(n_mp)])  28.7 us
    ppermute x34, starting transfers between devices, swap_dp(): lax.ppermute(v, ('z', 'core'), [(i, i ^ bit) for i in range(n_dp)])  26.8 us
    unnamed x127, local copies, waits for them, and re-layouts  25.8 us
    ppermute x27, waiting for transfers between devices, swap_mp(): return lambda v: lax.ppermute(v, 'mp', [(i, i ^ bit) for i in range(n_mp)])  19.3 us
  transfers between devices with their start and end apart: 61, of which 18 were waited for; matrix products, arithmetic and copies ran while one was open for 8% of the time, Pallas kernels for 59%

profile of v2, /device:TPU:0, one launch (start us, length us, event | category | flops | bytes accessed | tf_op | source)
XLA Modules:
  0.0 518.5 jit_solution(5459254309134289740)
XLA Ops:
  5.3 3.0 collective-permute-start
  12.2 2.4 collective-permute-done.2
  15.3 4.2 attn_rows.1
  20.8 2.1 fusion.7
  24.7 15.6 %attend.4 = (bf16[1280,1024]{1,0:T(8,128)(2,1)S(1)}, bf16[1280,768]{1,0:T(8,128)(2,1)}, bf16[1280,256]{1,0:T(8,128)(2,1)}, bf16[16,320,320]{2,1,0:T(8,128)(2,1)}) custom-call(s32[4]{0:T(128)S(1)} %fusion.35.refs_0_, bf16[4,320,1024]{2,1,0:T(8,128)(2,1)} %refs_12_.3, f32[4,6,1024]{2,1,0:T(8,128)} %reshape.126.refs_2_.refs_14_.refs_15_.refs_13_, ...), custom_call_target="tpu_custom_call" | custom-call | flops 1000 | bytes 1000 | tf_op jit(solution)/shard_map/attend/pallas_call | solution.py:92
  47.6 6.6 %feed_rows.1 = (bf16[2,512,1024]{2,1,0:T(8,128)(2,1)}, bf16[2,512,1024]{2,1,0:T(8,128)(2,1)}) custom-call(s32[1]{0:T(128)} %bitcast.8.refs_0_, bf16[1024,1024]{1,0:T(8,128)(2,1)} %refs_1_.5, bf16[1024,1024]{1,0:T(8,128)(2,1)} %refs_2_.3, bf16[1280,256]{1,0:T(8,128)(2,1)} %get-tuple-element.129.refs_2_.refs_3_.refs_0_.refs_8_), custom_call_target="tpu_custom_call" | custom-call | flops 1000 | bytes 1000 | tf_op jit(solution)/shard_map/feed_rows/pallas_call | solution.py:92
  55.1 14.2 %attend.5 = (bf16[1280,768]{1,0:T(8,128)(2,1)}, bf16[1280,256]{1,0:T(8,128)(2,1)}, bf16[16,320,320]{2,1,0:T(8,128)(2,1)}) custom-call(s32[4]{0:T(128)S(1)} %fusion.35.refs_0_, bf16[1280,1024]{1,0:T(8,128)(2,1)} %copy-done.2, f32[4,6,1024]{2,1,0:T(8,128)} %reshape.126.refs_2_.refs_14_.refs_15_.refs_13_, ...), custom_call_target="tpu_custom_call" | custom-call | flops 1000 | bytes 1000 | tf_op jit(solution)/shard_map/attend/pallas_call | solution.py:92
  75.3 14.2 %attend.6 = (bf16[1280,768]{1,0:T(8,128)(2,1)}, bf16[1280,256]{1,0:T(8,128)(2,1)}, bf16[16,320,320]{2,1,0:T(8,128)(2,1)}) custom-call(s32[4]{0:T(128)S(1)} %fusion.35.refs_0_, bf16[1280,1024]{1,0:T(8,128)(2,1)} %copy-done.2, f32[4,6,1024]{2,1,0:T(8,128)} %reshape.126.refs_2_.refs_14_.refs_15_.refs_13_, ...), custom_call_target="tpu_custom_call" | custom-call | flops 1000 | bytes 1000 | tf_op jit(solution)/shard_map/attend/pallas_call | solution.py:92
  90.5 14.2 %attend.7 = (bf16[1280,768]{1,0:T(8,128)(2,1)}, bf16[1280,256]{1,0:T(8,128)(2,1)}, bf16[16,320,320]{2,1,0:T(8,128)(2,1)}) custom-call(s32[4]{0:T(128)S(1)} %fusion.35.refs_0_, bf16[1280,1024]{1,0:T(8,128)(2,1)} %copy-done.2, f32[4,6,1024]{2,1,0:T(8,128)} %reshape.126.refs_2_.refs_14_.refs_15_.refs_13_, bf16[512,1024]{1,0:T(8,128)(2,1)} %copy-done.17, ...), custom_call_target="tpu_custom_call" | custom-call | flops 1000 | bytes 1000 | tf_op jit(solution)/shard_map/attend/pallas_call | solution.py:92
  104.8 10.9 %middle.1 = (bf16[1280,1024]{1,0:T(8,128)(2,1)}, f32[1280,1024]{1,0:T(8,128)}, bf16[1280,1024]{1,0:T(8,128)(2,1)S(1)}, bf16[1280,1024]{1,0:T(8,128)(2,1)S(1)}) custom-call(bf16[1280,256]{1,0:T(8,128)(2,1)} %get-tuple-element.129.refs_2_.refs_3_.refs_0_.refs_8_, bf16[1280,256]{1,0:T(8,128)(2,1)} %get-tuple-element.133.refs_7_.refs_2_.refs_1_.refs_8_, ...), custom_call_target="tpu_custom_call" | custom-call | flops 1000 | bytes 1000 | tf_op jit(solution)/shard_map/middle/pallas_call | solution.py:92
  115.7 16.8 %feed.4 = (bf16[1280,1024]{1,0:T(8,128)(2,1)}, bf16[1280,1024]{1,0:T(8,128)(2,1)}, bf16[2,512,1024]{2,1,0:T(8,128)(2,1)}, bf16[2,512,1024]{2,1,0:T(8,128)(2,1)}) custom-call(bf16[1280,1024]{1,0:T(8,128)(2,1)S(1)} %get-tuple-element.139.refs_0_, bf16[1280,1024]{1,0:T(8,128)(2,1)S(1)} %get-tuple-element.140.refs_1_, ...), custom_call_target="tpu_custom_call" | custom-call | flops 1000 | bytes 1000 | tf_op jit(solution)/shard_map/feed/pallas_call | solution.py:92
  144.1 15.3 %feed.5 = (bf16[1280,1024]{1,0:T(8,128)(2,1)}, bf16[1280,1024]{1,0:T(8,128)(2,1)}, bf16[2,512,1024]{2,1,0:T(8,128)(2,1)}, bf16[2,512,1024]{2,1,0:T(8,128)(2,1)}) custom-call(bf16[1280,1024]{1,0:T(8,128)(2,1)S(1)} %copy-done.8, bf16[1280,1024]{1,0:T(8,128)(2,1)S(1)} %copy-done.11, bf16[2,512,1024]{2,1,0:T(8,128)(2,1)} %get-tuple-element.143.refs_2_.refs_3_.refs_6_, ...), custom_call_target="tpu_custom_call" | custom-call | flops 1000 | bytes 1000 | tf_op jit(solution)/shard_map/feed/pallas_call | solution.py:92
  160.9 15.4 %feed.6 = (bf16[1280,1024]{1,0:T(8,128)(2,1)}, bf16[1280,1024]{1,0:T(8,128)(2,1)}, bf16[2,512,1024]{2,1,0:T(8,128)(2,1)}, bf16[2,512,1024]{2,1,0:T(8,128)(2,1)}) custom-call(bf16[1280,1024]{1,0:T(8,128)(2,1)S(1)} %copy-done.8, bf16[1280,1024]{1,0:T(8,128)(2,1)S(1)} %copy-done.11, bf16[2,512,1024]{2,1,0:T(8,128)(2,1)} %get-tuple-element.144.refs_2_.refs_3_.refs_8_, ...), custom_call_target="tpu_custom_call" | custom-call | flops 1000 | bytes 1000 | tf_op jit(solution)/shard_map/feed/pallas_call | solution.py:92
  177.4 3.6 merge.10.refs_2_
  182.9 4.7 merge.11.refs_7_
  191.8 15.2 %feed.7 = (bf16[1280,1024]{1,0:T(8,128)(2,1)}, bf16[1280,1024]{1,0:T(8,128)(2,1)}, bf16[2,512,1024]{2,1,0:T(8,128)(2,1)}, bf16[2,512,1024]{2,1,0:T(8,128)(2,1)}) custom-call(bf16[1280,1024]{1,0:T(8,128)(2,1)S(1)} %copy-done.9, bf16[1280,1024]{1,0:T(8,128)(2,1)S(1)} %copy-done.12, bf16[1,512,1024]{2,1,0:T(8,128)(2,1)} %get-tuple-element.147.refs_2_.refs_10_, ...), custom_call_target="tpu_custom_call" | custom-call | flops 1000 | bytes 1000 | tf_op jit(solution)/shard_map/feed/pallas_call | solution.py:92
  207.1 6.3 %collective-permute-done.22.refs_1_ = bf16[512,1024]{1,0:T(8,128)(2,1)} collective-permute-done((bf16[512,1024]{1,0:T(8,128)(2,1)}, bf16[512,1024]{1,0:T(8,128)(2,1)}, u32[]{:S(2)}, u32[]{:S(2)}) %collective-permute-start.22) | collective-permute-done | bytes 1048608 | tf_op jit(solution)/shard_map/ppermute | solution.py:776
  214.5 4.2 merge.12
  219.7 22.4 %turn.1 = (f32[1280,1024]{1,0:T(8,128)}, bf16[1280,1024]{1,0:T(8,128)(2,1)S(1)}, f32[4,3,1024]{2,1,0:T(4,128)}) custom-call(bf16[1280,1024]{1,0:T(8,128)(2,1)} %get-tuple-element.160.refs_0_, bf16[1280,1024]{1,0:T(8,128)(2,1)} %get-tuple-element.161.refs_1_, bf16[1280,1024]{1,0:T(8,128)(2,1)} %get-tuple-element.162.refs_2_, ...), custom_call_target="tpu_custom_call" | custom-call | flops 1000 | bytes 1000 | tf_op jit(solution)/shard_map/turn/pallas_call | solution.py:92
  243.6 4.7 merge.13
  251.3 18.1 %output.1 = (bf16[4,320,1024]{2,1,0:T(8,128)(2,1)}, f32[4,1,1024]{2,1,0:T(1,128)}) custom-call(bf16[1280,1024]{1,0:T(8,128)(2,1)} %get-tuple-element.142.refs_2_.refs_6_.refs_0_, bf16[1280,1024]{1,0:T(8,128)(2,1)} %get-tuple-element.145.refs_6_.refs_1_, bf16[1280,1024]{1,0:T(8,128)(2,1)} %get-tuple-element.146.refs_2_.refs_6_, ...), custom_call_target="tpu_custom_call" | custom-call | flops 1000 | bytes 1000 | tf_op jit(solution)/shard_map/output/pallas_call | solution.py:92
  269.4 3.3 collective-permute-done.26.refs_0_
  273.9 6.7 %merge_parts.2 = (bf16[512,1024]{1,0:T(8,128)(2,1)}, bf16[512,1024]{1,0:T(8,128)(2,1)}) custom-call(s32[1]{0:T(128)} %bitcast.18.refs_0_, bf16[2,512,1024]{2,1,0:T(8,128)(2,1)} %get-tuple-element.178.refs_1_.refs_7_, bf16[2,512,1024]{2,1,0:T(8,128)(2,1)} %collective-permute-done.25.refs_2_.refs_8_, ...), custom_call_target="tpu_custom_call" | custom-call | flops 1000 | bytes 1000 | tf_op jit(solution)/shard_map/merge_parts/pallas_call | solution.py:92
  282.2 18.3 %attend_back.4 = (bf16[1280,768]{1,0:T(8,128)(2,1)}, bf16[512,1024]{1,0:T(8,128)(2,1)}, bf16[512,1024]{1,0:T(8,128)(2,1)}, f32[2,32,128]{2,1,0:T(8,128)}) custom-call(bf16[1280,1024]{1,0:T(8,128)(2,1)} %copy-done.1, bf16[512,1024]{1,0:T(8,128)(2,1)} %copy-done.17, bf16[512,1024]{1,0:T(8,128)(2,1)} %copy-done.19, ...), custom_call_target="tpu_custom_call" | custom-call | flops 1000 | bytes 1000 | tf_op jit(solution)/shard_map/attend_back/pallas_call | solution.py:92
  300.5 3.3 collective-permute-done.29.refs_0_
  303.8 2.1 merge.14.refs_10_
  305.9 2.6 collective-permute-start.30
  308.4 18.1 %attend_back.5 = (bf16[1280,768]{1,0:T(8,128)(2,1)}, bf16[512,1024]{1,0:T(8,128)(2,1)}, bf16[512,1024]{1,0:T(8,128)(2,1)}, f32[2,32,128]{2,1,0:T(8,128)}) custom-call(bf16[1280,1024]{1,0:T(8,128)(2,1)} %copy-done.1, bf16[512,1024]{1,0:T(8,128)(2,1)} %get-tuple-element.131.refs_3_.refs_6_.refs_1_, bf16[512,1024]{1,0:T(8,128)(2,1)} %copy-done.20, ...), custom_call_target="tpu_custom_call" | custom-call | flops 1000 | bytes 1000 | tf_op jit(solution)/shard_map/attend_back/pallas_call | solution.py:92
  326.6 2.5 collective-permute-done.30.refs_0_
  329.0 2.1 merge.15.refs_4_
  331.2 2.5 merge.16
  334.9 18.6 %attend_back.6 = (bf16[1280,768]{1,0:T(8,128)(2,1)}, bf16[512,1024]{1,0:T(8,128)(2,1)}, bf16[512,1024]{1,0:T(8,128)(2,1)}, f32[2,32,128]{2,1,0:T(8,128)}) custom-call(bf16[1280,1024]{1,0:T(8,128)(2,1)} %copy-done.1, bf16[512,1024]{1,0:T(8,128)(2,1)} %get-tuple-element.134.refs_3_.refs_8_.refs_1_, bf16[512,1024]{1,0:T(8,128)(2,1)} %copy-done.18, ...), custom_call_target="tpu_custom_call" | custom-call | flops 1000 | bytes 1000 | tf_op jit(solution)/shard_map/attend_back/pallas_call | solution.py:92
  354.1 5.2 collective-permute-done.32.refs_0_
  360.1 2.3 pad_maximum_fusion.refs_11_.refs_1_
  362.4 3.9 merge.17.refs_3_
  367.7 3.8 merge.18.refs_10_
  376.4 18.2 %attend_back.7 = (bf16[1280,768]{1,0:T(8,128)(2,1)}, bf16[512,1024]{1,0:T(8,128)(2,1)}, bf16[512,1024]{1,0:T(8,128)(2,1)}, f32[2,32,128]{2,1,0:T(8,128)}) custom-call(bf16[1280,1024]{1,0:T(8,128)(2,1)} %copy-done.1, bf16[512,1024]{1,0:T(8,128)(2,1)} %get-tuple-element.127.refs_3_.refs_4_.refs_1_, ...), custom_call_target="tpu_custom_call" | custom-call | flops 1000 | bytes 1000 | tf_op jit(solution)/shard_map/attend_back/pallas_call | solution.py:92
  398.3 3.4 merge_parts.3
  403.9 2.2 collective-permute-start.42
  406.1 18.0 %last.1 = (bf16[4,320,1024]{2,1,0:T(8,128)(2,1)}, f32[4,2,1024]{2,1,0:T(2,128)}) custom-call(bf16[1280,768]{1,0:T(8,128)(2,1)} %get-tuple-element.202.refs_3_.refs_0_, bf16[1280,768]{1,0:T(8,128)(2,1)} %get-tuple-element.191.refs_1_, bf16[1280,768]{1,0:T(8,128)(2,1)} %get-tuple-element.194.refs_3_.refs_9_.refs_2_, ...), custom_call_target="tpu_custom_call" | custom-call | flops 1000 | bytes 1000 | tf_op jit(solution)/shard_map/last/pallas_call | solution.py:92
  438.0 6.0 %collective-permute-done.48.refs_3_ = bf16[128,1024]{1,0:T(8,128)(2,1)} collective-permute-done((bf16[128,1024]{1,0:T(8,128)(2,1)}, bf16[128,1024]{1,0:T(8,128)(2,1)}, u32[]{:S(2)}, u32[]{:S(2)}) %collective-permute-start.48) | collective-permute-done | bytes 262176 | tf_op jit(solution)/shard_map/ppermute | solution.py:779
  451.4 9.6 %collective-permute-start.58 = (bf16[32,1152]{1,0:T(8,128)(2,1)}, bf16[32,1152]{1,0:T(8,128)(2,1)}, u32[]{:S(2)}, u32[]{:S(2)}) collective-permute-start(bf16[32,1152]{1,0:T(8,128)(2,1)} %pad_maximum_fusion.16), channel_id=1, source_target_pairs={{0,8},{4,12},{8,0},{12,4},{16,24},{20,28},{24,16},{28,20},{1,9},{5... | collective-permute-start | bytes 221192 | tf_op jit(solution)/shard_map/ppermute | solution.py:779
  461.1 8.7 %feed_final.1 = (f32[1024,1024]{1,0:T(8,128)}, f32[1024,1024]{1,0:T(8,128)}) custom-call(s32[2]{0:T(128)S(1)} %pad_add_fusion.refs_0_, bf16[512,1024]{1,0:T(8,128)(2,1)} %pad_maximum_fusion.refs_11_.refs_1_, bf16[512,1024]{1,0:T(8,128)(2,1)} %get-tuple-element.212.refs_2_, bf16[512,1024]{1,0:T(8,128)(2,1)} %get-tuple-element.230.refs_3_, ...), custom_call_target="tpu_custom_call" | custom-call | flops 1000 | bytes 1000 | tf_op jit(solution)/shard_map/feed_final/pallas_call | solution.py:92
  472.5 2.4 gather_fusion.2
  485.8 5.9 %collective-permute-done.55.refs_0_ = bf16[32,2688]{1,0:T(8,128)(2,1)S(1)} collective-permute-done((bf16[32,2688]{1,0:T(8,128)(2,1)S(1)}, bf16[32,2688]{1,0:T(8,128)(2,1)S(1)}, u32[]{:S(2)}, u32[]{:S(2)}) %collective-permute-start.55) | collective-permute-done | bytes 172064 | tf_op jit(solution)/shard_map/ppermute | solution.py:779
  497.8 5.8 %attn_final.1 = (f32[1024,768]{1,0:T(8,128)}, f32[256,1024]{1,0:T(8,128)}) custom-call(s32[2]{0:T(128)S(1)} %pad_add_fusion.refs_0_, bf16[512,1024]{1,0:T(8,128)(2,1)} %copy-done.26, bf16[512,1024]{1,0:T(8,128)(2,1)} %get-tuple-element.239.refs_2_), custom_call_target="tpu_custom_call" | custom-call | flops 1000 | bytes 1000 | tf_op jit(solution)/shard_map/attn_final/pallas_call | solution.py:92
  503.6 7.6 %collective-permute-done.60.refs_0_ = bf16[64,2688]{1,0:T(8,128)(2,1)} collective-permute-done((bf16[64,2688]{1,0:T(8,128)(2,1)S(1)}, bf16[64,2688]{1,0:T(8,128)(2,1)}, u32[]{:S(2)}, u32[]{:S(2)}) %collective-permute-start.60) | collective-permute-done | bytes 344096 | tf_op jit(solution)/shard_map/ppermute | solution.py:779
  513.1 3.7 fusion.13
  (342 shorter events, 115.9 us)
Async XLA Ops:
  19.5 23.5 %collective-permute-start.3 = (bf16[512,1024]{1,0:T(8,128)(2,1)}, bf16[512,1024]{1,0:T(8,128)(2,1)}, u32[]{:S(2)}, u32[]{:S(2)}) collective-permute-start(bf16[512,1024]{1,0:T(8,128)(2,1)} %get-tuple-element.127.refs_3_.refs_4_.refs_1_), channel_id=1, source_target_pairs={{0,1},{1,0},{2,3},{3,2},{4,5},{5,4},{6,7},{7,6},{8,9},{9,8},{10,11... | collective-permute-start | bytes 3145736 | tf_op jit(solution)/shard_map/ppermute | solution.py:776
  20.0 23.2 %collective-permute-start.4 = (bf16[512,1024]{1,0:T(8,128)(2,1)}, bf16[512,1024]{1,0:T(8,128)(2,1)}, u32[]{:S(2)}, u32[]{:S(2)}) collective-permute-start(bf16[512,1024]{1,0:T(8,128)(2,1)} %get-tuple-element.127.refs_3_.refs_4_.refs_1_), channel_id=1, source_target_pairs={{0,2},{1,3},{2,0},{3,1},{4,6},{5,7},{6,4},{7,5},{8,10},{9,11},{10,... | collective-permute-start | bytes 3145736 | tf_op jit(solution)/shard_map/ppermute | solution.py:776
  43.3 10.9 %collective-permute-start.5 = (bf16[512,1024]{1,0:T(8,128)(2,1)}, bf16[512,1024]{1,0:T(8,128)(2,1)S(1)}, u32[]{:S(2)}, u32[]{:S(2)}) collective-permute-start(bf16[512,1024]{1,0:T(8,128)(2,1)} %get-tuple-element.131.refs_3_.refs_6_.refs_1_), channel_id=1, source_target_pairs={{0,4},{4,0},{8,12},{12,8},{16,20},{20,16},{24,28},{28,24},{1,5},{5... | collective-permute-start | bytes 3145736 | tf_op jit(solution)/shard_map/ppermute | solution.py:779
  44.3 25.0 %collective-permute-start.7 = (bf16[256,1024]{1,0:T(8,128)(2,1)S(1)}, bf16[256,1024]{1,0:T(8,128)(2,1)}, u32[]{:S(2)}, u32[]{:S(2)}) collective-permute-start(bf16[256,1024]{1,0:T(8,128)(2,1)S(1)} %slice.98), channel_id=1, source_target_pairs={{0,2},{1,3},{2,0},{3,1},{4,6},{5,7},{6,4},{7,5},{8,10},{9,11},{10,... | collective-permute-start | bytes 1572872 | tf_op jit(solution)/shard_map/ppermute | solution.py:776
  46.0 23.4 %collective-permute-start.8 = (bf16[256,1024]{1,0:T(8,128)(2,1)S(1)}, bf16[256,1024]{1,0:T(8,128)(2,1)}, u32[]{:S(2)}, u32[]{:S(2)}) collective-permute-start(bf16[256,1024]{1,0:T(8,128)(2,1)S(1)} %slice.99), channel_id=1, source_target_pairs={{0,1},{1,0},{2,3},{3,2},{4,5},{5,4},{6,7},{7,6},{8,9},{9,8},{10,11... | collective-permute-start | bytes 1572872 | tf_op jit(solution)/shard_map/ppermute | solution.py:776
  69.4 63.1 %collective-permute-start.10 = (bf16[2,512,1024]{2,1,0:T(8,128)(2,1)}, bf16[2,512,1024]{2,1,0:T(8,128)(2,1)S(1)}, u32[]{:S(2)}, u32[]{:S(2)}) collective-permute-start(bf16[2,512,1024]{2,1,0:T(8,128)(2,1)} %hold.21.refs_2_.refs_3_.refs_4_), channel_id=1, source_target_pairs={{0,1},{1,0},{2,3},{3,2},{4,5},{5,4},{6,7},{7,6},{8,9},{9,8},{10,11... | collective-permute-start | bytes 6291464 | tf_op jit(solution)/shard_map/ppermute | solution.py:776
  69.9 63.9 %collective-permute-start.11 = (bf16[2,512,1024]{2,1,0:T(8,128)(2,1)}, bf16[2,512,1024]{2,1,0:T(8,128)(2,1)S(1)}, u32[]{:S(2)}, u32[]{:S(2)}) collective-permute-start(bf16[2,512,1024]{2,1,0:T(8,128)(2,1)} %hold.21.refs_2_.refs_3_.refs_4_), channel_id=1, source_target_pairs={{0,2},{1,3},{2,0},{3,1},{4,6},{5,7},{6,4},{7,5},{8,10},{9,11},{10,... | collective-permute-start | bytes 6291464 | tf_op jit(solution)/shard_map/ppermute | solution.py:776
  73.7 15.9 %collective-permute-start.9 = (bf16[512,1024]{1,0:T(8,128)(2,1)S(1)}, bf16[512,1024]{1,0:T(8,128)(2,1)S(1)}, u32[]{:S(2)}, u32[]{:S(2)}) collective-permute-start(bf16[512,1024]{1,0:T(8,128)(2,1)S(1)} %constant_dynamic-update-slice_fusion.refs_3_.refs_10_.refs_1_), channel_id=1, source_target_pairs={{0,4},{4,0},{8,12},{12,8},{16,20},{20,16},{24,28},{28,24},{1,5},{5... | collective-permute-start | bytes 3145736 | tf_op jit(solution)/shard_map/ppermute | solution.py:779
  135.4 24.1 %collective-permute-start.13 = (bf16[2,512,1024]{2,1,0:T(8,128)(2,1)}, bf16[2,512,1024]{2,1,0:T(8,128)(2,1)S(1)}, u32[]{:S(2)}, u32[]{:S(2)}) collective-permute-start(bf16[2,512,1024]{2,1,0:T(8,128)(2,1)} %get-tuple-element.144.refs_2_.refs_3_.refs_8_), channel_id=1, source_target_pairs={{0,4},{4,0},{8,12},{12,8},{16,20},{20,16},{24,28},{28,24},{1,5},{5... | collective-permute-start | bytes 6291464 | tf_op jit(solution)/shard_map/ppermute | solution.py:779
  138.9 38.0 %collective-permute-start.14 = (bf16[1,512,1024]{2,1,0:T(8,128)(2,1)S(1)}, bf16[1,512,1024]{2,1,0:T(8,128)(2,1)}, u32[]{:S(2)}, u32[]{:S(2)}) collective-permute-start(bf16[1,512,1024]{2,1,0:T(8,128)(2,1)S(1)} %slice.101.refs_7_), channel_id=1, source_target_pairs={{0,2},{1,3},{2,0},{3,1},{4,6},{5,7},{6,4},{7,5},{8,10},{9,11},{10,... | collective-permute-start | bytes 3145736 | tf_op jit(solution)/shard_map/ppermute | solution.py:776
  139.5 37.5 %collective-permute-start.15 = (bf16[1,512,1024]{2,1,0:T(8,128)(2,1)S(1)}, bf16[1,512,1024]{2,1,0:T(8,128)(2,1)}, u32[]{:S(2)}, u32[]{:S(2)}) collective-permute-start(bf16[1,512,1024]{2,1,0:T(8,128)(2,1)S(1)} %slice.102.refs_8_), channel_id=1, source_target_pairs={{0,1},{1,0},{2,3},{3,2},{4,5},{5,4},{6,7},{7,6},{8,9},{9,8},{10,11... | collective-permute-start | bytes 3145736 | tf_op jit(solution)/shard_map/ppermute | solution.py:776
  159.5 18.0 %collective-permute-start.19 = (bf16[2,512,1024]{2,1,0:T(8,128)(2,1)}, bf16[2,512,1024]{2,1,0:T(8,128)(2,1)}, u32[]{:S(2)}, u32[]{:S(2)}) collective-permute-start(bf16[2,512,1024]{2,1,0:T(8,128)(2,1)} %get-tuple-element.152), channel_id=1, source_target_pairs={{0,4},{4,0},{8,12},{12,8},{16,20},{20,16},{24,28},{28,24},{1,5},{5... | collective-permute-start | bytes 6291464 | tf_op jit(solution)/shard_map/ppermute | solution.py:779
  176.9 12.8 %collective-permute-start.16 = (bf16[1,512,1024]{2,1,0:T(8,128)(2,1)}, bf16[1,512,1024]{2,1,0:T(8,128)(2,1)S(1)}, u32[]{:S(2)}, u32[]{:S(2)}) collective-permute-start(bf16[1,512,1024]{2,1,0:T(8,128)(2,1)} %get-tuple-element.147.refs_2_.refs_10_), channel_id=1, source_target_pairs={{0,4},{4,0},{8,12},{12,8},{16,20},{20,16},{24,28},{28,24},{1,5},{5... | collective-permute-start | bytes 3145736 | tf_op jit(solution)/shard_map/ppermute | solution.py:779
  177.0 12.7 %collective-permute-start.17 = (bf16[1,512,1024]{2,1,0:T(8,128)(2,1)}, bf16[1,512,1024]{2,1,0:T(8,128)(2,1)S(1)}, u32[]{:S(2)}, u32[]{:S(2)}) collective-permute-start(bf16[1,512,1024]{2,1,0:T(8,128)(2,1)} %get-tuple-element.148.refs_3_.refs_10_), channel_id=1, source_target_pairs={{0,4},{4,0},{8,12},{12,8},{16,20},{20,16},{24,28},{28,24},{1,5},{5... | collective-permute-start | bytes 3145736 | tf_op jit(solution)/shard_map/ppermute | solution.py:779
  187.6 25.8 %collective-permute-start.22 = (bf16[512,1024]{1,0:T(8,128)(2,1)}, bf16[512,1024]{1,0:T(8,128)(2,1)}, u32[]{:S(2)}, u32[]{:S(2)}) collective-permute-start(bf16[512,1024]{1,0:T(8,128)(2,1)} %merge.11.refs_7_), channel_id=1, source_target_pairs={{0,2},{1,3},{2,0},{3,1},{4,6},{5,7},{6,4},{7,5},{8,10},{9,11},{10,... | collective-permute-start | bytes 3145736 | tf_op jit(solution)/shard_map/ppermute | solution.py:776
  189.2 25.2 %collective-permute-start.21 = (bf16[512,1024]{1,0:T(8,128)(2,1)S(1)}, bf16[512,1024]{1,0:T(8,128)(2,1)}, u32[]{:S(2)}, u32[]{:S(2)}) collective-permute-start(bf16[512,1024]{1,0:T(8,128)(2,1)S(1)} %copy-done.27), channel_id=1, source_target_pairs={{0,1},{1,0},{2,3},{3,2},{4,5},{5,4},{6,7},{7,6},{8,9},{9,8},{10,11... | collective-permute-start | bytes 3145736 | tf_op jit(solution)/shard_map/ppermute | solution.py:776
  218.7 24.9 %collective-permute-start.23 = (bf16[512,1024]{1,0:T(8,128)(2,1)}, bf16[512,1024]{1,0:T(8,128)(2,1)}, u32[]{:S(2)}, u32[]{:S(2)}) collective-permute-start(bf16[512,1024]{1,0:T(8,128)(2,1)} %get-tuple-element.158.refs_16_), channel_id=1, source_target_pairs={{0,1},{1,0},{2,3},{3,2},{4,5},{5,4},{6,7},{7,6},{8,9},{9,8},{10,11... | collective-permute-start | bytes 3145736 | tf_op jit(solution)/shard_map/ppermute | solution.py:776
  219.2 24.4 %collective-permute-start.24 = (bf16[512,1024]{1,0:T(8,128)(2,1)}, bf16[512,1024]{1,0:T(8,128)(2,1)}, u32[]{:S(2)}, u32[]{:S(2)}) collective-permute-start(bf16[512,1024]{1,0:T(8,128)(2,1)} %get-tuple-element.159.refs_17_), channel_id=1, source_target_pairs={{0,2},{1,3},{2,0},{3,1},{4,6},{5,7},{6,4},{7,5},{8,10},{9,11},{10,... | collective-permute-start | bytes 3145736 | tf_op jit(solution)/shard_map/ppermute | solution.py:776
  248.3 24.4 %collective-permute-start.26 = (bf16[512,1024]{1,0:T(8,128)(2,1)}, bf16[512,1024]{1,0:T(8,128)(2,1)}, u32[]{:S(2)}, u32[]{:S(2)}) collective-permute-start(bf16[512,1024]{1,0:T(8,128)(2,1)} %get-tuple-element.168.refs_15_), channel_id=1, source_target_pairs={{0,1},{1,0},{2,3},{3,2},{4,5},{5,4},{6,7},{7,6},{8,9},{9,8},{10,11... | collective-permute-start | bytes 3145736 | tf_op jit(solution)/shard_map/ppermute | solution.py:776
  249.8 24.1 %collective-permute-start.27 = (bf16[512,1024]{1,0:T(8,128)(2,1)}, bf16[512,1024]{1,0:T(8,128)(2,1)}, u32[]{:S(2)}, u32[]{:S(2)}) collective-permute-start(bf16[512,1024]{1,0:T(8,128)(2,1)} %get-tuple-element.169.refs_16_), channel_id=1, source_target_pairs={{0,2},{1,3},{2,0},{3,1},{4,6},{5,7},{6,4},{7,5},{8,10},{9,11},{10,... | collective-permute-start | bytes 3145736 | tf_op jit(solution)/shard_map/ppermute | solution.py:776
  251.3 22.6 %collective-permute-start.25 = (bf16[2,512,1024]{2,1,0:T(8,128)(2,1)}, bf16[2,512,1024]{2,1,0:T(8,128)(2,1)}, u32[]{:S(2)}, u32[]{:S(2)}) collective-permute-start(bf16[2,512,1024]{2,1,0:T(8,128)(2,1)} %get-tuple-element.179), channel_id=1, source_target_pairs={{0,4},{4,0},{8,12},{12,8},{16,20},{20,16},{24,28},{28,24},{1,5},{5... | collective-permute-start | bytes 6291464 | tf_op jit(solution)/shard_map/ppermute | solution.py:779
  280.5 23.2 %collective-permute-start.29 = (bf16[512,1024]{1,0:T(8,128)(2,1)}, bf16[512,1024]{1,0:T(8,128)(2,1)}, u32[]{:S(2)}, u32[]{:S(2)}) collective-permute-start(bf16[512,1024]{1,0:T(8,128)(2,1)} %get-tuple-element.187), channel_id=1, source_target_pairs={{0,8},{4,12},{8,0},{12,4},{16,24},{20,28},{24,16},{28,20},{1,9},{5... | collective-permute-start | bytes 3145736 | tf_op jit(solution)/shard_map/ppermute | solution.py:779
  305.9 23.2 %collective-permute-start.30 = (bf16[256,1024]{1,0:T(8,128)(2,1)}, bf16[256,1024]{1,0:T(8,128)(2,1)}, u32[]{:S(2)}, u32[]{:S(2)}) collective-permute-start(bf16[256,1024]{1,0:T(8,128)(2,1)} %merge.14.refs_10_), channel_id=1, source_target_pairs={{0,16},{4,20},{8,24},{12,28},{16,0},{20,4},{24,8},{28,12},{1,17},{... | collective-permute-start | bytes 1572872 | tf_op jit(solution)/shard_map/ppermute | solution.py:779
  308.4 22.7 %collective-permute-start.28 = (bf16[512,1024]{1,0:T(8,128)(2,1)}, bf16[512,1024]{1,0:T(8,128)(2,1)}, u32[]{:S(2)}, u32[]{:S(2)}) collective-permute-start(bf16[512,1024]{1,0:T(8,128)(2,1)} %get-tuple-element.186), channel_id=1, source_target_pairs={{0,4},{4,0},{8,12},{12,8},{16,20},{20,16},{24,28},{28,24},{1,5},{5... | collective-permute-start | bytes 3145736 | tf_op jit(solution)/shard_map/ppermute | solution.py:779
  333.7 20.4 %collective-permute-start.33 = (bf16[256,1024]{1,0:T(8,128)(2,1)}, bf16[256,1024]{1,0:T(8,128)(2,1)S(1)}, u32[]{:S(2)}, u32[]{:S(2)}) collective-permute-start(bf16[256,1024]{1,0:T(8,128)(2,1)} %get-tuple-element.192.refs_9_), channel_id=1, source_target_pairs={{0,1},{1,0},{2,3},{3,2},{4,5},{5,4},{6,7},{7,6},{8,9},{9,8},{10,11... | collective-permute-start | bytes 1572872 | tf_op jit(solution)/shard_map/ppermute | solution.py:776
  334.3 19.7 %collective-permute-start.34 = (bf16[256,1024]{1,0:T(8,128)(2,1)}, bf16[256,1024]{1,0:T(8,128)(2,1)S(1)}, u32[]{:S(2)}, u32[]{:S(2)}) collective-permute-start(bf16[256,1024]{1,0:T(8,128)(2,1)} %get-tuple-element.193.refs_10_), channel_id=1, source_target_pairs={{0,2},{1,3},{2,0},{3,1},{4,6},{5,7},{6,4},{7,5},{8,10},{9,11},{10,... | collective-permute-start | bytes 1572872 | tf_op jit(solution)/shard_map/ppermute | solution.py:776
  334.9 24.3 %collective-permute-start.32 = (bf16[256,1024]{1,0:T(8,128)(2,1)S(1)}, bf16[256,1024]{1,0:T(8,128)(2,1)S(1)}, u32[]{:S(2)}, u32[]{:S(2)}) collective-permute-start(bf16[256,1024]{1,0:T(8,128)(2,1)S(1)} %copy-done.21), channel_id=1, source_target_pairs={{0,16},{4,20},{8,24},{12,28},{16,0},{20,4},{24,8},{28,12},{1,17},{... | collective-permute-start | bytes 1572872 | tf_op jit(solution)/shard_map/ppermute | solution.py:779
  334.9 27.4 %collective-permute-start.35 = (bf16[512,1024]{1,0:T(8,128)(2,1)}, bf16[512,1024]{1,0:T(8,128)(2,1)}, u32[]{:S(2)}, u32[]{:S(2)}) collective-permute-start(bf16[512,1024]{1,0:T(8,128)(2,1)} %get-tuple-element.199), channel_id=1, source_target_pairs={{0,4},{4,0},{8,12},{12,8},{16,20},{20,16},{24,28},{28,24},{1,5},{5... | collective-permute-start | bytes 3145736 | tf_op jit(solution)/shard_map/ppermute | solution.py:779
  353.5 14.1 %collective-permute-start.31 = (bf16[512,1024]{1,0:T(8,128)(2,1)}, bf16[512,1024]{1,0:T(8,128)(2,1)}, u32[]{:S(2)}, u32[]{:S(2)}) collective-permute-start(bf16[512,1024]{1,0:T(8,128)(2,1)} %get-tuple-element.196), channel_id=1, source_target_pairs={{0,4},{4,0},{8,12},{12,8},{16,20},{20,16},{24,28},{28,24},{1,5},{5... | collective-permute-start | bytes 3145736 | tf_op jit(solution)/shard_map/ppermute | solution.py:779
  362.4 32.2 %collective-permute-start.37 = (bf16[512,1024]{1,0:T(8,128)(2,1)}, bf16[512,1024]{1,0:T(8,128)(2,1)}, u32[]{:S(2)}, u32[]{:S(2)}) collective-permute-start(bf16[512,1024]{1,0:T(8,128)(2,1)} %pad_maximum_fusion.refs_11_.refs_1_), channel_id=1, source_target_pairs={{0,8},{4,12},{8,0},{12,4},{16,24},{20,28},{24,16},{28,20},{1,9},{5... | collective-permute-start | bytes 3145736 | tf_op jit(solution)/shard_map/ppermute | solution.py:779
  366.3 28.4 %collective-permute-start.38 = (bf16[512,1024]{1,0:T(8,128)(2,1)}, bf16[512,1024]{1,0:T(8,128)(2,1)}, u32[]{:S(2)}, u32[]{:S(2)}) collective-permute-start(bf16[512,1024]{1,0:T(8,128)(2,1)} %merge.17.refs_3_), channel_id=1, source_target_pairs={{0,1},{1,0},{2,3},{3,2},{4,5},{5,4},{6,7},{7,6},{8,9},{9,8},{10,11... | collective-permute-start | bytes 3145736 | tf_op jit(solution)/shard_map/ppermute | solution.py:776
  371.5 24.6 %collective-permute-start.39 = (bf16[512,1024]{1,0:T(8,128)(2,1)}, bf16[512,1024]{1,0:T(8,128)(2,1)}, u32[]{:S(2)}, u32[]{:S(2)}) collective-permute-start(bf16[512,1024]{1,0:T(8,128)(2,1)} %merge.18.refs_10_), channel_id=1, source_target_pairs={{0,2},{1,3},{2,0},{3,1},{4,6},{5,7},{6,4},{7,5},{8,10},{9,11},{10,... | collective-permute-start | bytes 3145736 | tf_op jit(solution)/shard_map/ppermute | solution.py:776
  374.0 23.6 %collective-permute-start.57 = (bf16[16,1152]{1,0:T(8,128)(2,1)S(1)}, bf16[16,1152]{1,0:T(8,128)(2,1)S(1)}, u32[]{:S(2)}, u32[]{:S(2)}) collective-permute-start(bf16[16,1152]{1,0:T(8,128)(2,1)S(1)} %fusion.22), channel_id=1, source_target_pairs={{0,4},{4,0},{8,12},{12,8},{16,20},{20,16},{24,28},{28,24},{1,5},{5... | collective-permute-start | bytes 110600 | tf_op jit(solution)/shard_map/ppermute | solution.py:779
  374.1 52.8 %collective-permute-start.43 = (bf16[512,1024]{1,0:T(8,128)(2,1)}, bf16[512,1024]{1,0:T(8,128)(2,1)}, u32[]{:S(2)}, u32[]{:S(2)}) collective-permute-start(bf16[512,1024]{1,0:T(8,128)(2,1)} %pad_maximum_fusion.refs_11_.refs_1_), channel_id=1, source_target_pairs={{0,4},{4,0},{8,12},{12,8},{16,20},{20,16},{24,28},{28,24},{1,5},{5... | collective-permute-start | bytes 3145736 | tf_op jit(solution)/shard_map/ppermute | solution.py:779
  396.1 34.4 %collective-permute-start.44 = (bf16[512,1024]{1,0:T(8,128)(2,1)}, bf16[512,1024]{1,0:T(8,128)(2,1)}, u32[]{:S(2)}, u32[]{:S(2)}) collective-permute-start(bf16[512,1024]{1,0:T(8,128)(2,1)} %get-tuple-element.212.refs_2_), channel_id=1, source_target_pairs={{0,4},{4,0},{8,12},{12,8},{16,20},{20,16},{24,28},{28,24},{1,5},{5... | collective-permute-start | bytes 3145736 | tf_op jit(solution)/shard_map/ppermute | solution.py:779
  401.7 26.0 %collective-permute-start.40 = (bf16[128,1024]{1,0:T(8,128)(2,1)}, bf16[128,1024]{1,0:T(8,128)(2,1)}, u32[]{:S(2)}, u32[]{:S(2)}) collective-permute-start(bf16[128,1024]{1,0:T(8,128)(2,1)} %get-tuple-element.208.refs_16_), channel_id=1, source_target_pairs={{0,8},{4,12},{8,0},{12,4},{16,24},{20,28},{24,16},{28,20},{1,9},{5... | collective-permute-start | bytes 786440 | tf_op jit(solution)/shard_map/ppermute | solution.py:779
  403.0 26.1 %collective-permute-start.41 = (bf16[128,1024]{1,0:T(8,128)(2,1)}, bf16[128,1024]{1,0:T(8,128)(2,1)}, u32[]{:S(2)}, u32[]{:S(2)}) collective-permute-start(bf16[128,1024]{1,0:T(8,128)(2,1)} %get-tuple-element.209.refs_17_), channel_id=1, source_target_pairs={{0,16},{4,20},{8,24},{12,28},{16,0},{20,4},{24,8},{28,12},{1,17},{... | collective-permute-start | bytes 786440 | tf_op jit(solution)/shard_map/ppermute | solution.py:779
  403.9 26.6 %collective-permute-start.42 = (bf16[128,1024]{1,0:T(8,128)(2,1)}, bf16[128,1024]{1,0:T(8,128)(2,1)}, u32[]{:S(2)}, u32[]{:S(2)}) collective-permute-start(bf16[128,1024]{1,0:T(8,128)(2,1)} %get-tuple-element.210.refs_18_), channel_id=1, source_target_pairs={{0,24},{4,28},{8,16},{12,20},{16,8},{20,12},{24,0},{28,4},{1,25},{... | collective-permute-start | bytes 786440 | tf_op jit(solution)/shard_map/ppermute | solution.py:779
  427.0 11.0 %collective-permute-start.45 = (f32[4,1536]{1,0:T(4,128)}, f32[4,1536]{1,0:T(4,128)}, u32[]{:S(2)}, u32[]{:S(2)}) collective-permute-start(f32[4,1536]{1,0:T(4,128)} %bitcast.101), channel_id=1, source_target_pairs={{0,1},{1,0},{2,3},{3,2},{4,5},{5,4},{6,7},{7,6},{8,9},{9,8},{10,11... | collective-permute-start | bytes 73736 | tf_op jit(solution)/shard_map/ppermute | solution.py:776
  432.5 11.4 %collective-permute-start.48 = (bf16[128,1024]{1,0:T(8,128)(2,1)}, bf16[128,1024]{1,0:T(8,128)(2,1)}, u32[]{:S(2)}, u32[]{:S(2)}) collective-permute-start(bf16[128,1024]{1,0:T(8,128)(2,1)} %merge.19.refs_4_), channel_id=1, source_target_pairs={{0,24},{4,28},{8,16},{12,20},{16,8},{20,12},{24,0},{28,4},{1,25},{... | collective-permute-start | bytes 786440 | tf_op jit(solution)/shard_map/ppermute | solution.py:779
  434.2 35.6 %collective-permute-start.52 = (bf16[128,1024]{1,0:T(8,128)(2,1)}, bf16[128,1024]{1,0:T(8,128)(2,1)}, u32[]{:S(2)}, u32[]{:S(2)}) collective-permute-start(bf16[128,1024]{1,0:T(8,128)(2,1)} %merge.19.refs_4_), channel_id=1, source_target_pairs={{0,16},{4,20},{8,24},{12,28},{16,0},{20,4},{24,8},{28,12},{1,17},{... | collective-permute-start | bytes 786440 | tf_op jit(solution)/shard_map/ppermute | solution.py:779
  447.3 22.6 %collective-permute-start.49 = (f32[16,1152]{1,0:T(8,128)}, f32[16,1152]{1,0:T(8,128)}, u32[]{:S(2)}, u32[]{:S(2)}) collective-permute-start(f32[16,1152]{1,0:T(8,128)} %get-tuple-element.272), channel_id=1, source_target_pairs={{0,1},{1,0},{2,3},{3,2},{4,5},{5,4},{6,7},{7,6},{8,9},{9,8},{10,11... | collective-permute-start | bytes 221192 | tf_op jit(solution)/shard_map/ppermute | solution.py:776
  448.0 22.0 %collective-permute-start.50 = (f32[16,1152]{1,0:T(8,128)}, f32[16,1152]{1,0:T(8,128)}, u32[]{:S(2)}, u32[]{:S(2)}) collective-permute-start(f32[16,1152]{1,0:T(8,128)} %get-tuple-element.273), channel_id=1, source_target_pairs={{0,2},{1,3},{2,0},{3,1},{4,6},{5,7},{6,4},{7,5},{8,10},{9,11},{10,... | collective-permute-start | bytes 221192 | tf_op jit(solution)/shard_map/ppermute | solution.py:776
  449.4 20.6 %collective-permute-start.51 = (f32[16,1152]{1,0:T(8,128)}, f32[16,1152]{1,0:T(8,128)}, u32[]{:S(2)}, u32[]{:S(2)}) collective-permute-start(f32[16,1152]{1,0:T(8,128)} %get-tuple-element.274), channel_id=1, source_target_pairs={{0,3},{1,2},{2,1},{3,0},{4,7},{5,6},{6,5},{7,4},{8,11},{9,10},{10,... | collective-permute-start | bytes 221192 | tf_op jit(solution)/shard_map/ppermute | solution.py:776
  451.4 26.0 %collective-permute-start.58 = (bf16[32,1152]{1,0:T(8,128)(2,1)}, bf16[32,1152]{1,0:T(8,128)(2,1)}, u32[]{:S(2)}, u32[]{:S(2)}) collective-permute-start(bf16[32,1152]{1,0:T(8,128)(2,1)} %pad_maximum_fusion.16), channel_id=1, source_target_pairs={{0,8},{4,12},{8,0},{12,4},{16,24},{20,28},{24,16},{28,20},{1,9},{5... | collective-permute-start | bytes 221192 | tf_op jit(solution)/shard_map/ppermute | solution.py:779
  481.2 10.5 %collective-permute-start.56 = (bf16[512,1024]{1,0:T(8,128)(2,1)S(1)}, bf16[512,1024]{1,0:T(8,128)(2,1)}, u32[]{:S(2)}, u32[]{:S(2)}) collective-permute-start(bf16[512,1024]{1,0:T(8,128)(2,1)S(1)} %pad_maximum_fusion.1.refs_1_), channel_id=1, source_target_pairs={{0,4},{4,0},{8,12},{12,8},{16,20},{20,16},{24,28},{28,24},{1,5},{5... | collective-permute-start | bytes 3145736 | tf_op jit(solution)/shard_map/ppermute | solution.py:779
  485.6 10.4 %collective-permute-start.59 = (bf16[64,1152]{1,0:T(8,128)(2,1)}, bf16[64,1152]{1,0:T(8,128)(2,1)}, u32[]{:S(2)}, u32[]{:S(2)}) collective-permute-start(bf16[64,1152]{1,0:T(8,128)(2,1)} %pad_maximum_fusion.8), channel_id=1, source_target_pairs={{0,16},{4,20},{8,24},{12,28},{16,0},{20,4},{24,8},{28,12},{1,17},{... | collective-permute-start | bytes 442376 | tf_op jit(solution)/shard_map/ppermute | solution.py:779
  493.5 17.7 %collective-permute-start.60 = (bf16[64,2688]{1,0:T(8,128)(2,1)S(1)}, bf16[64,2688]{1,0:T(8,128)(2,1)}, u32[]{:S(2)}, u32[]{:S(2)}) collective-permute-start(bf16[64,2688]{1,0:T(8,128)(2,1)S(1)} %pad_maximum_fusion.2), channel_id=1, source_target_pairs={{0,16},{4,20},{8,24},{12,28},{16,0},{20,4},{24,8},{28,12},{1,17},{... | collective-permute-start | bytes 1032200 | tf_op jit(solution)/shard_map/ppermute | solution.py:779
  (73 other events, 359.3 us)

commit v3 on v2

--- a/solution.py
+++ b/solution.py
@@ -1,5 +1,6 @@
 from functools import partial
 import math
+from typing import NamedTuple
 
 import jax
 import jax.numpy as jnp
@@ -59,7 +60,6 @@
 
 HBM = pl.BlockSpec(memory_space=pltpu.HBM)
 VMEM = pl.BlockSpec(memory_space=pltpu.VMEM)
-ANY = pl.BlockSpec(memory_space=pl.ANY)
 
 
 class Loads:
@@ -79,12 +79,24 @@
             copy.wait()
 
 
+class Moved(NamedTuple):
+    array: jax.Array
+
+
 def in_hbm(array):
     return pltpu.with_memory_space_constraint(array, pltpu.HBM)
 
 
+def operand(array, spec):
+    if isinstance(array, Moved):
+        return array.array, pl.BlockSpec(memory_space=pl.ANY) if spec is HBM else spec
+    return array if spec is VMEM else in_hbm(array), spec
+
+
 def run(kernel, name, grid, ins, outs, scratch=(), after=(), scalars=(), flops=0, moved=0, vmem=24):
     first = len(scalars) + len(ins)
+
+    ins = [operand(array, spec) for array, spec in ins]
 
     def body(*refs):
         kernel(*refs[:first], *refs[first + len(after) :])
@@ -102,19 +114,20 @@
         compiler_params=pltpu.CompilerParams(vmem_limit_bytes=vmem * 2**20),
         cost_estimate=pl.CostEstimate(flops=1000, bytes_accessed=1000, transcendentals=0),
         name=name,
-    )(*scalars, *[array if spec is VMEM else in_hbm(array) for array, spec in ins], *map(in_hbm, after))
+    )(*scalars, *[array for array, _ in ins], *map(in_hbm, after))
 
 
 def hold(values, after=(), flops=1000):
+    anywhere = pl.BlockSpec(memory_space=pl.ANY)
     return pl.pallas_call(
         lambda *refs: None,
-        in_specs=[HBM] * (len(values) + len(after)),
-        out_specs=[HBM] * len(values),
-        out_shape=[shape(v.shape, v.dtype) for v in values],
+        in_specs=[anywhere] * len(values) + [HBM] * len(after),
+        out_specs=[anywhere] * len(values),
+        out_shape=[near(v.shape, v.dtype) for v in values],
         input_output_aliases={i: i for i in range(len(values))},
         cost_estimate=pl.CostEstimate(flops=flops, bytes_accessed=1000, transcendentals=0),
         name="hold",
-    )(*map(in_hbm, (*values, *after)))
+    )(*values, *map(in_hbm, after))
 
 
 def arrive(values, after):
@@ -214,15 +227,16 @@
         k = pk[:, p * QKV + 128 : p * QKV + 256]
         v = pk[:, p * QKV + 256 : p * QKV + 384]
         kb = jnp.where(mask_lane, hide, kb_all[p])
+        v_rows = v.T
         outs = []
         for i in range(2):
             mine = low if i == 0 else ~low
-            s = mm(jnp.where(mine, q, e_ref[...]), jnp.where(mine, k, kb), NT)
-            ex = jnp.exp(s - jnp.max(s, axis=1, keepdims=True))
-            pr = (ex * (1.0 / jnp.sum(ex, axis=1, keepdims=True))).astype(bf16)
+            s = mm(jnp.where(mine, k, kb), jnp.where(mine, q, e_ref[...]), NT)
+            ex = jnp.exp(s - jnp.max(s, axis=0, keepdims=True))
+            pr = (ex * (1.0 / jnp.sum(ex, axis=0, keepdims=True))).astype(bf16)
             probs_ref[2 * p + i] = pr
-            outs.append(mm(pr, v))
-        heads_ref[:, p * 128 : (p + 1) * 128] = jnp.where(low, outs[0], outs[1]).astype(bf16)
+            outs.append(mm(v_rows, pr)[i * HD : (i + 1) * HD])
+        heads_ref[:, p * 128 : (p + 1) * 128] = jnp.concatenate(outs, axis=0).T.astype(bf16)
 
 
 def attend(lengths, source, modes, weight, table, query_hot, after=()):
@@ -243,8 +257,8 @@
         [
             (source, window_of(WIN, D) if first else rows_of(D)),
             (modes, window_of(6, D)),
-            (weight[0], ANY),
-            (weight[1], ANY),
+            (weight[0], HBM),
+            (weight[1], HBM),
             (table, whole(2, 128, 128)),
             (query_hot, whole(WIN, 128)),
         ],
@@ -284,7 +298,7 @@
         "middle",
         count,
         [(h, rows_of(256)) for h in heads]
-        + [(half, ANY) for pair in weights for half in pair]
+        + [(half, HBM) for pair in weights for half in pair]
         + [(tokens, window_of(WIN, D)), (cotangent, window_of(WIN, D)), (modes, window_of(6, D))],
         [(shape((rows, D), kind), rows_of(D)) for kind in (bf16, f32)] + [(near((rows, D), bf16), rows_of(D))] * 2,
         [pltpu.VMEM((D, D), bf16), pltpu.SemaphoreType.DMA((8,))],
@@ -463,20 +477,22 @@
         k = pk[:, p * QKV + 128 : p * QKV + 256]
         v = pk[:, p * QKV + 256 : p * QKV + 384]
         do = hg[:, p * 128 : (p + 1) * 128]
+        k_rows = k.T
         dv, dq, dk = [], [], []
         for i in range(2):
             mine = low if i == 0 else ~low
             qa = jnp.where(mine, q, e_ref[...])
-            dp = mm(jnp.where(mine, do, jnp.zeros_like(do)), v, NT)
+            dp = mm(jnp.where(mine, v, jnp.zeros_like(v)), do, NT)
             prl = pr_ref[2 * p + i]
             pr = prl.astype(f32)
             t = pr * dp
-            ds = (t - pr * jnp.sum(t, axis=1, keepdims=True)).astype(bf16)
-            dv.append(mm(prl, do, TN))
-            dq.append(mm(ds, k))
-            dk.append(mm(ds, qa, TN))
+            ds = (t - pr * jnp.sum(t, axis=0, keepdims=True)).astype(bf16)
+            dv.append(mm(prl, do))
+            dq.append(mm(k_rows, ds)[i * HD : (i + 1) * HD])
+            dk.append(mm(ds, qa))
+        dq = jnp.concatenate(dq, axis=0).T
         block = jnp.concatenate(
-            [jnp.where(low, dq[0], dq[1]), jnp.where(low, dk[0], dk[1]), jnp.where(low, dv[0], dv[1])], axis=1
+            [dq, jnp.where(low, dk[0], dk[1]), jnp.where(low, dv[0], dv[1])], axis=1
         ).astype(bf16)
         pg_ref[:, p * QKV : (p + 1) * QKV] = block
         pg_all[pl.ds(pl.multiple_of(w * WIN, WIN), WIN), p * QKV : (p + 1) * QKV] = block
@@ -504,8 +520,8 @@
         rows // WIN,
         [
             (out_in, rows_of(D)),
-            (weight[0], ANY),
-            (weight[1], ANY),
+            (weight[0], HBM),
+            (weight[1], HBM),
             (packed, rows_of(2 * QKV)),
             (probs, pl.BlockSpec((4, WIN, WIN), lambda i: (i, 0, 0))),
             (query_hot, whole(WIN, 128)),
@@ -558,7 +574,7 @@
         "last",
         count,
         [(array, rows_of(2 * QKV)) for array in packed_grads]
-        + [(half, ANY) for pair in weights for half in pair]
+        + [(half, HBM) for pair in weights for half in pair]
         + [(tokens, window_of(WIN, D)), (modes, window_of(6, D)), (middle_grad, rows_of(D))],
         [(shape((count, WIN, D), bf16), window_of(WIN, D)), (shape((count, 2, D), f32), window_of(2, D))],
         [pltpu.VMEM((8 * QKV, D), bf16), pltpu.VMEM((WIN, D), f32), pltpu.SemaphoreType.DMA((8,))],
@@ -583,7 +599,7 @@
 
 
 def merge(*sums, rows=HALF, after=()):
-    block = 128
+    block = min(256, rows)
     ins, spans = [], []
     for terms in sums:
         spans.append([])
@@ -619,16 +635,17 @@
 
 def merge_parts(terms, z, count, outputs):
     size = HALF // count
-    sums = max(2 if isinstance(term, tuple) or term.ndim == 3 else 1 for term in terms)
+    sums = 2 if any(type(term) is tuple for term in terms) else 1
     ins, only = [], []
     for j in range(outputs):
         for term in terms:
-            array, which = term if isinstance(term, tuple) else (term, None)
+            array, which = term if type(term) is tuple else (term, None)
+            dims = array.array.ndim if isinstance(array, Moved) else array.ndim
 
             def at(i, zr, j=j):
                 return zr[0] ^ (i // sums * outputs + j)
 
-            if array.ndim == 3:
+            if dims == 3:
                 spec = pl.BlockSpec((None, size, D), lambda i, zr, at=at: (i % sums, at(i, zr), 0))
             else:
                 spec = pl.BlockSpec((size, D), lambda i, zr, at=at: (at(i, zr), 0))
@@ -639,9 +656,16 @@
     return run(partial(parts_kernel, outputs, only[: len(terms)]), "merge_parts", grid, ins, outs, (), (), [z])
 
 
-def attn_final_kernel(place_ref, a_ref, b_ref, qkv_ref, out_ref, rows):
+def attn_final_kernel(place_ref, a_ref, b_ref, qkv_ref, out_ref, rows, hot):
     core, z = place_ref[0], place_ref[1]
     size = HALF // 4
+
+    @pl.when(pl.program_id(0) == 0)
+    def _():
+        match, row = hot_rows(2 * QKV, qkv_source(core))
+        inner = jnp.where(row >= QKV, row - QKV, row)
+        hot[...] = jnp.where(match, jnp.where(inner < 128, HD**-0.5, 1.0), 0.0).astype(bf16)
+
     for h, ref in enumerate((a_ref, b_ref)):
         for k in range(4):
             part_at = z ^ k
@@ -655,36 +679,125 @@
             def _():
                 out_ref[pl.ds(pl.multiple_of((core ^ h) * size, size), size)] = block.astype(f32)
 
-    hot, row = hot_rows(2 * QKV, qkv_source(core))
-    inner = jnp.where(row >= QKV, row - QKV, row)
-    hot = jnp.where(hot, jnp.where(inner < 128, HD**-0.5, 1.0), 0.0).astype(bf16)
-    qkv_ref[...] = mm(rows[...], hot, TN)
+    qkv_ref[...] = mm(rows[...], hot[...], TN)
+
+
+def columns_of(rows):
+    return pl.BlockSpec((rows, 256), lambda i, *_: (0, i))
 
 
 def attn_final(place, a, b):
-    ins = [(a, whole(HALF, D)), (b, whole(HALF, D))]
-    outs = [(shape((D, 2 * QKV), f32), whole(D, 2 * QKV)), (shape((256, D), f32), whole(256, D))]
-    return run(attn_final_kernel, "attn_final", 1, ins, outs, [pltpu.VMEM((2 * QKV, D), bf16)], (), [place])
+    ins = [(a, columns_of(HALF)), (b, columns_of(HALF))]
+    outs = [
+        (shape((D, 2 * QKV), f32), pl.BlockSpec((256, 2 * QKV), lambda i, *_: (i, 0))),
+        (shape((256, D), f32), columns_of(256)),
+    ]
+    scratch = [pltpu.VMEM((2 * QKV, 256), bf16), pltpu.VMEM((2 * QKV, 2 * QKV), bf16)]
+    return run(attn_final_kernel, "attn_final", D // 256, ins, outs, scratch, (), [place])
 
 
 def feed_final_kernel(place_ref, *refs):
-    up_ref, down_ref, rows = refs[4:]
+    up_ref, down_ref, rows, hot = refs[4:]
     core, z = place_ref[0], place_ref[1]
     size = HALF // 4
+
+    @pl.when(pl.program_id(0) == 0)
+    def _():
+        hot[...] = jnp.where(hot_rows(2 * HALF, lambda row: row ^ (core * HALF))[0], 1.0, 0.0).astype(bf16)
+
     for h in range(2):
         for k, (ref, first) in enumerate(((refs[2 * h], 0), (refs[2 * h + 1], 0), (refs[2 * h], 2), (refs[2 * h + 1], 2))):
             start = (z ^ k) * size
             rows[pl.ds(pl.multiple_of(h * HALF + start, size), size)] = ref[first * size : (first + 1) * size]
             block = ref[(first + 1) * size : (first + 2) * size].astype(f32)
             down_ref[pl.ds(pl.multiple_of((core ^ h) * HALF + start, size), size)] = block
-    hot, _ = hot_rows(2 * HALF, lambda row: row ^ (core * HALF))
-    up_ref[...] = mm(rows[...], jnp.where(hot, 1.0, 0.0).astype(bf16), TN)
+    up_ref[...] = mm(rows[...], hot[...], TN)
 
 
 def feed_final(place, even, odd, other_even, other_odd):
-    ins = [(v, whole(HALF, D)) for v in (even, odd, other_even, other_odd)]
-    outs = [(shape((D, 2 * HALF), f32), whole(D, 2 * HALF)), (shape((2 * HALF, D), f32), whole(2 * HALF, D))]
-    return run(feed_final_kernel, "feed_final", 1, ins, outs, [pltpu.VMEM((2 * HALF, D), bf16)], (), [place])
+    ins = [(v, columns_of(HALF)) for v in (even, odd, other_even, other_odd)]
+    outs = [
+        (shape((D, 2 * HALF), f32), pl.BlockSpec((256, 2 * HALF), lambda i, *_: (i, 0))),
+        (shape((2 * HALF, D), f32), columns_of(2 * HALF)),
+    ]
+    scratch = [pltpu.VMEM((2 * HALF, 256), bf16), pltpu.VMEM((2 * HALF, 2 * HALF), bf16)]
+    return run(feed_final_kernel, "feed_final", D // 256, ins, outs, scratch, (), [place])
+
+
+def mode_shares_kernel(m0, m1, m2, m3, rel_ref, ada_ref, low_ref, s0, s1, s2, s3, rows):
+    count = m0.shape[0]
+    for r, ref in enumerate((m0, m1, m2, m3)):
+        rows[r * count : (r + 1) * count] = ref[...]
+    low = rows[...].astype(bf16)
+    low_ref[...] = low
+    cond = mm(low, ada_ref[...], NT)
+    for r, ref in enumerate((s0, s1, s2, s3)):
+        ref[:, :D] = cond
+        ref[:, D:] = rel_ref[r]
+
+
+def mode_shares(messages, rel_part, ada_weight):
+    count, columns = messages[0].shape
+    rows = 4 * count
+    ins = [(v, whole(count, columns)) for v in messages]
+    ins += [(rel_part, whole(4, rows, 128)), (ada_weight, whole(D, columns))]
+    outs = [(shape((rows, columns), bf16), whole(rows, columns))] + [(shape((rows, D + 128), f32), whole(rows, D + 128))] * 4
+    return run(mode_shares_kernel, "mode_shares", 1, ins, outs, [pltpu.VMEM((rows, columns), f32)])
+
+
+def mode_rows_kernel(mp_ref, low_ref, s0, s1, s2, s3, slope_ref, cond_ref, out_ref):
+    rows, columns = low_ref.shape
+    count = rows // 4
+    mp = mp_ref[0]
+    moved = [s0[:, :D]]
+    for k, ref in ((1, s1), (2, s2), (3, s3)):
+        blocks = [ref[(r ^ k) * count : ((r ^ k) + 1) * count, :D] for r in range(4)]
+        moved.append(jnp.concatenate(blocks, axis=0))
+    cond = (moved[0] + moved[1]) + (moved[2] + moved[3])
+    value = (cond * slope_ref[...]).astype(bf16)
+    row = lax.broadcasted_iota(jnp.int32, (rows, rows), 0)
+    col = lax.broadcasted_iota(jnp.int32, (rows, rows), 1)
+    hot = jnp.where(col == row ^ (mp * count), 1.0, 0.0).astype(bf16)
+    out_ref[:, :columns] = low_ref[...]
+    out_ref[:, columns : columns + D] = mm(hot, value).astype(bf16)
+    out_ref[:, columns + D : columns + D + 128] = (s0[:, D:] + s1[:, D:] + s2[:, D:] + s3[:, D:]).astype(bf16)
+    out_ref[:, columns + D + 128 :] = cond_ref[...]
+
+
+def mode_rows(mp, low, shares, slope, cond):
+    rows, columns = low.shape
+    width = columns + 2 * (D + 128)
+    ins = [(low, whole(rows, columns))] + [(v, whole(rows, D + 128)) for v in shares]
+    ins += [(slope, whole(rows, D)), (cond, whole(rows, D + 128))]
+    outs = [(shape((rows, width), bf16), whole(rows, width))]
+    return run(mode_rows_kernel, "mode_rows", 1, ins, outs, (), (), [mp])[0]
+
+
+def mode_final_kernel(dp_ref, *refs):
+    *parts, ada_ref, bias_ref, class_ref, rel_ref, rows = refs
+    size = parts[0].shape[0]
+    columns = ada_ref.shape[1]
+    marks = [0, columns, columns + D, columns + D + 128, columns + 2 * D + 128, columns + 2 * D + 256]
+    for k, ref in enumerate(parts):
+        rows[pl.ds(pl.multiple_of((dp_ref[0] ^ k) * size, size), size)] = ref[...]
+    modes, classes, rel, cond, index = [rows[:, i:j] for i, j in zip(marks, marks[1:])]
+    ada_ref[...] = mm(cond, modes, TN)
+    bias_ref[...] = jnp.sum(modes.astype(f32), axis=0, keepdims=True)
+    lane = lax.broadcasted_iota(jnp.int32, index.shape, 1).astype(f32)
+    hot = jnp.where(lane == index[:, :1].astype(f32), 1.0, 0.0).astype(bf16)
+    class_ref[...] = mm(hot, classes, TN)[: class_ref.shape[0]]
+    total = rel[:size].astype(f32)
+    for i in range(1, len(parts)):
+        total = total + rel[i * size : (i + 1) * size].astype(f32)
+    rel_ref[...] = total
+
+
+def mode_final(dp, parts, columns, class_count):
+    size, width = parts[0].shape
+    ins = [(v, whole(size, width)) for v in parts]
+    outs = [(shape(dims, f32), whole(*dims)) for dims in ((D, columns), (1, columns), (class_count, D), (size, 128))]
+    scratch = [pltpu.VMEM((len(parts) * size, width), bf16)]
+    return run(mode_final_kernel, "mode_final", 1, ins, outs, scratch, (), [dp], vmem=32)
 
 
 def silu_plain(values):
@@ -785,11 +898,6 @@
     def cat(a, b, axis=0):
         return jnp.concatenate([a, b], axis=axis)
 
-    dp_steps = [(1, core == 0)] + [(2 << b, ((z >> b) & 1) == 0) for b in range(n_z.bit_length() - 1)]
-
-    def join(low, v, got):
-        return cat(jnp.where(low, v, got), jnp.where(low, got, v))
-
     pre_cond = condition(timesteps, classes, class_table)
     cond_low = silu_plain(pre_cond).astype(bf16)
     mode_cols = jnp.einsum("mwd,de->mwe", cond_low, ada_weight, preferred_element_type=f32) + ada_bias.astype(f32)
@@ -810,13 +918,14 @@
     query_hot = jnp.asarray(query_side(), bf16)
     packed, heads, probs = [None] * 4, [None] * 4, [None] * 4
 
-    attn_own = attn_rows(core_row, qkv_weight, out_weight, [messages])
+    attn_own = list(attn_rows(core_row, qkv_weight, out_weight, [mode_cols]))
+    (attn_own[0],) = hold(attn_own[:1], [messages])
     ax, ay = px(attn_own[0]), py(attn_own[0])
     normed_one, packed[0], heads[0], probs[0] = attend(own_lengths, tokens, modes, attn_own, tables[0], query_hot)
     feed_own = list(feed_rows(core_row, up_weight, down_weight, [heads[0]]))
-    ax, ay = hold([ax, ay], [heads[0]])
+    ax, ay = hold([ax, ay], [feed_own[1]])
     adx, ady = py(ax[: HALF // 2]), px(ay[HALF // 2 :])
-    attn_w = [attn_own, [ax, pc(ax)], [ay, pc(ay)]]
+    attn_w = [attn_own] + [[Moved(v), Moved(pc(v))] for v in (ax, ay)]
     packed[1], heads[1], probs[1] = attend(
         own_lengths, normed_one, modes, attn_w[1], tables[1], query_hot, [feed_own[1]]
     )
@@ -824,7 +933,7 @@
     (feed_own[0],) = hold(feed_own[:1], [adx, ady])
     fx, fy = px(feed_own[0]), py(feed_own[0])
     ad = cat(adx, ady)
-    attn_w.append([ad, pc(ad)])
+    attn_w.append([ad, Moved(pc(ad))])
     for r in (2, 3):
         packed[r], heads[r], probs[r] = attend(
             own_lengths, normed_one, modes, attn_w[r], tables[r], query_hot, [heads[r - 1]]
@@ -838,18 +947,18 @@
         other[r] = pc(sent)
 
     def pair(r, which):
-        return [(mine[r], which, 0), (other[r], which, 0)]
+        return [(mine[r], which, 0), (Moved(other[r]), which, 0)]
 
     feed_w = [[((v, 0), (v, 1)) for v in feed_own]]
     feed_step(0, feed_w[0], [])
     fx, fy = hold([fx, fy], [hid[0]])
     fu, fd = fx[:1], fy[1:]
-    feed_w += [[((v, 0), (v, 1)) for v in (u, pc(u))] for u in (fx, fy)]
+    feed_w += [[((Moved(v), 0), (Moved(v), 1)) for v in (u, pc(u))] for u in (fx, fy)]
     feed_step(1, feed_w[1], [hid[0], fu, fd])
     fu, fd = py(fu), px(fd)
     feed_step(2, feed_w[2], [hid[1]])
     fu, fd = arrive([fu, fd], [hid[2]])
-    feed_w += [[((u, 0), (v, 0)) for u, v in ((fu, fd), (pc(fu), pc(fd)))]]
+    feed_w += [[((Moved(u), 0), (Moved(v), 0)) for u, v in ((fu, fd), (pc(fu), pc(fd)))]]
     (send_x,) = merge(pair(1, 0), after=[fu])
     (send_y,) = merge(pair(2, 1), after=[send_x])
     feed_step(3, feed_w[3], [hid[2], send_y])
@@ -859,14 +968,23 @@
         pre, feed_w, middle, attn_out, cotangent, modes, [diag_x, diag_y]
     )
     diag_x, diag_y = arrive([px(diag_x), py(diag_y)], [middle_grad])
-    last_x, last_y = merge(pair(1, 1) + [(diag_y, None, 0)], pair(2, 0) + [(diag_x, None, 0)])
-    output, out_sums = out_step(hid, feed_w, middle, cotangent, modes, [last_x, last_y])
+    last_x, last_y = merge(pair(1, 1) + [(Moved(diag_y), None, 0)], pair(2, 0) + [(Moved(diag_x), None, 0)])
+    still = [[[(v.array if isinstance(v, Moved) else v, at) for v, at in half] for half in halves] for halves in feed_w]
+    output, out_sums = out_step(hid, still, middle, cotangent, modes, [last_x, last_y])
     last_x, last_y = arrive([px(last_x), py(last_y)], [out_sums])
     z_row = z.reshape(1)
-    terms = [mine[0], other[0], (send_x, 0), (last_y, 0), (last_x, 1), (send_y, 1)]
+    terms = [mine[0], Moved(other[0])]
+    terms += [(Moved(send_x), 0), (Moved(last_y), 0), (Moved(last_x), 1), (Moved(send_y), 1)]
     feed_keep, feed_sent = merge_parts(terms, z_row, n_z, 2)
     z_one, z_two = swap_dp(2), swap_dp(4)
 
+    own_pre = jnp.take(pre_cond.transpose(1, 0, 2), order, axis=0).reshape(4 * micro, D)
+    share = 1.0 / (1.0 + jnp.exp(-own_pre))
+    class_col = jnp.pad(classes.T.reshape(-1, 1).astype(bf16), ((0, 0), (0, 127)))
+    cond_rel = jnp.take(cond_low, order, axis=1).transpose(1, 0, 2).reshape(4 * micro, D)
+    slope, cond_rel = hold([share * (1.0 + own_pre * (1.0 - share)), cat(cond_rel, class_col, 1)])
+
+    attn_w = [[v.array if isinstance(v, Moved) else v for v in halves] for halves in attn_w]
     packed_grad, rel_grid, a_mine, a_other = [None] * 4, [None] * 4, [None] * 4, [None] * 4
 
     def back_step(r, after):
@@ -878,27 +996,27 @@
     cut = HALF // 2
 
     def a_pair(r, start):
-        return [(a_mine[r], None, start), (a_other[r], None, start)]
+        return [(a_mine[r], None, start), (Moved(a_other[r]), None, start)]
 
     back_step(3, [feed_keep])
     (feed_got,) = arrive([z_one(feed_sent)], [packed_grad[3]])
-    (feed_sent,) = merge([(feed_keep, None, cut), (feed_got, None, cut)], rows=cut)
+    (feed_sent,) = merge([(feed_keep, None, cut), (Moved(feed_got), None, cut)], rows=cut)
     back_step(1, [packed_grad[3], feed_sent])
     (feed_two,) = arrive([z_two(feed_sent)], [packed_grad[1]])
-    (feed_one,) = merge([(feed_keep, None, 0), (feed_got, None, 0), (feed_two, None, 0)], rows=cut)
+    (feed_one,) = merge([(feed_keep, None, 0), (Moved(feed_got), None, 0), (Moved(feed_two), None, 0)], rows=cut)
     a_diag_x, a_diag_y = merge(a_pair(3, 0), a_pair(3, cut), rows=cut, after=[feed_one])
-    back_step(2, [a_diag_x, a_diag_y])
+    back_step(2, [a_diag_x, a_diag_y, slope, cond_rel])
     feed_two, a_diag_x, a_diag_y = arrive([z_two(feed_one), px(a_diag_x), py(a_diag_y)], [packed_grad[2]])
     feed_even = cat(feed_one, feed_two)
-    (a_last_x,) = merge(a_pair(1, 0) + [(a_diag_y, None, -cut, cut, HALF)])
-    (a_last_y,) = merge(a_pair(2, 0) + [(a_diag_x, None, 0, 0, cut)], after=[a_last_x])
+    (a_last_x,) = merge(a_pair(1, 0) + [(Moved(a_diag_y), None, -cut, cut, HALF)])
+    (a_last_y,) = merge(a_pair(2, 0) + [(Moved(a_diag_x), None, 0, 0, cut)], after=[a_last_x])
     back_step(0, [packed_grad[2], a_last_y, feed_even])
     feed_odd, a_last_x, a_last_y = arrive([z_one(feed_even), px(a_last_x), py(a_last_y)], [packed_grad[0]])
 
     def exchange(parts):
         return [swap_dp(2 * k)(v) for k, v in enumerate(parts) if k]
 
-    attn_parts = merge_parts([a_mine[0], a_other[0], a_last_x, a_last_y], z_row, n_z, n_z)
+    attn_parts = merge_parts([a_mine[0], *map(Moved, (a_other[0], a_last_x, a_last_y))], z_row, n_z, n_z)
     token_grads, last_sums = last_step(packed_grad, attn_w, tokens, modes, middle_grad, attn_parts)
     attn_got = exchange(attn_parts)
     feed_other = [pc(feed_even), pc(feed_odd)]
@@ -910,43 +1028,25 @@
     messages = [lax.dynamic_index_in_dim(mode_grad, mp ^ r, axis=0, keepdims=False) for r in range(4)]
     rel_grid = hold(rel_grid, [attn_own])
     rel_part = jnp.pad(rel_sums(jnp.stack(rel_grid), core), ((0, 0), (0, 4 * (micro - 1)), (0, 128 - rel_bias.shape[1])))
-    *messages[1:], attn_far = arrive([by_rel[r](messages[r]) for r in (1, 2, 3)] + [swap_dp(6)(attn_own)], [attn_own])
-    mode_low = jnp.stack(messages).astype(bf16).reshape(4 * micro, -1)
-    cond_grad = mm(mode_low, ada_weight, NT).reshape(4, micro, D)
-    cond_grad = jnp.take(cond_grad, order, axis=0).reshape(4 * micro, D)
-    grad_up, grad_down = feed_final(place, feed_even, feed_odd, *feed_other)
-    shares = [cat(cond_grad, rel_part[r], 1) for r in range(4)]
-    *shares[1:], attn_two = arrive(
-        [by_rel[r](shares[r]) for r in (1, 2, 3)] + [swap_dp(4)(attn_own)], [attn_far, grad_up]
-    )
-    shares = jnp.take(jnp.stack(shares), order, axis=0)
-    cond_grad = shares[0] + shares[1] + shares[2] + shares[3]
-    own_pre = pre_cond.transpose(1, 0, 2).reshape(4 * micro, D)
-    share = 1.0 / (1.0 + jnp.exp(-own_pre))
-    own_class = cond_grad[:, :D] * (share * (1.0 + own_pre * (1.0 - share)))
-    grads = jnp.concatenate([mode_low, own_class.astype(bf16), cond_grad[:, D:].astype(bf16)], axis=1)
-    got, attn_one = arrive([swap_dp(dp_steps[0][0])(grads), swap_dp(2)(attn_own)], [attn_two])
-    grads = join(dp_steps[0][1], grads, got)
+    grad_up, grad_down = feed_final(place, feed_even, Moved(feed_odd), *map(Moved, feed_other))
+    *messages[1:], attn_far = arrive(
+        [by_rel[r](messages[r]) for r in (1, 2, 3)] + [swap_dp(6)(attn_own)], [attn_own, grad_up]
+    )
+    mode_low, *shares = mode_shares(messages, rel_part, ada_weight)
+    *shares[1:], attn_two, attn_one = arrive(
+        [by_rel[r](shares[r]) for r in (1, 2, 3)] + [swap_dp(4)(attn_own), swap_dp(2)(attn_own)], [attn_far]
+    )
+    grads = mode_rows(mp.reshape(1), mode_low, shares, slope, cond_rel)
     attn_own = jnp.concatenate([attn_own, attn_one, attn_two, attn_far])
-    got, attn_other = arrive([swap_dp(dp_steps[1][0])(grads), pc(attn_own)], [attn_one])
-    grads = join(dp_steps[1][1], grads, got)
-    grad_qkv, grad_out = attn_final(place, attn_own, attn_other)
-    for step, low in dp_steps[2:]:
-        (got,) = arrive([swap_dp(step)(grads)], [grad_qkv])
-        grads = join(low, grads, got)
-    mode_all, class_part, rel_part = grads[:, :columns], grads[:, columns : columns + D], grads[:, columns + D :]
-    grad_rel = jnp.sum(rel_part.astype(f32).reshape(n_dp, 4 * micro, -1), axis=0)[:4, : rel_bias.shape[1]]
-
-    class_col = jnp.pad(classes.T.reshape(-1, 1).astype(bf16), ((0, 0), (0, 127)))
-    cond_rel = jnp.take(cond_low, order, axis=1).transpose(1, 0, 2).reshape(4 * micro, D)
-    cond_all = cat(cond_rel, class_col, 1)
-    for step, low in dp_steps:
-        cond_all = join(low, cond_all, swap_dp(step)(cond_all))
-    class_all = cond_all[:, D].astype(jnp.int32)
-    grad_ada = mm(cond_all[:, :D], mode_all, TN)
-    grad_ada_bias = jnp.sum(mode_all.astype(f32), axis=0)
-    class_hot = (jnp.arange(class_table.shape[0])[:, None] == class_all[None, :]).astype(bf16)
-    class_grad = jnp.dot(class_hot, class_part, preferred_element_type=f32)
+    got = [swap_dp(k)(grads) for k in range(1, n_dp)]
+    (attn_other,) = hold([pc(attn_own)], [grads])
+    grad_qkv, grad_out = attn_final(place, attn_own, Moved(attn_other))
+    got = arrive(got, [grad_qkv])
+    grad_ada, grad_ada_bias, class_grad, grad_rel = mode_final(
+        (2 * z + core).reshape(1), [grads, *got], columns, class_table.shape[0]
+    )
+    grad_ada_bias = grad_ada_bias.reshape(-1)
+    grad_rel = grad_rel[:4, : rel_bias.shape[1]]
 
     return (
         output,

time: 524 us -> 492 us (0.939)
  other arithmetic: 21.4 us -> 9.86 us
  waiting for transfers between devices: 53.5 us -> 42.3 us
  local copies, waits for them, and re-layouts: 41.4 us -> 33.7 us
    ppermute x34 -> x35, waiting for transfers between devices: 34.2 us -> 20.1 us  [swap_dp(): lax.ppermute(v, ('z', 'core'), [(i, i ^ bit) for i in range(n_dp)])]
    select_n x8 -> x0, other arithmetic: 7.48 us -> none  [the longest x6 6.36 us: join(): return cat(jnp.where(low, v, got), jnp.where(low, got, v))]
    dot_general x3 -> x0, matrix products: 5.62 us -> none  [the longest x2 4.66 us: mm(): return lax.dot_general(a, b, dims, preferred_element_type=f32)]
    unnamed x127 -> x165, local copies, waits for them, and re-layouts: 25.8 us -> 20.3 us
    pallas_call x32 -> x35, Pallas kernels: 332 us -> 329 us  [run(): pl.pallas_call(body, grid_spec=pltpu.PrefetchScalarGridSpec(num_scalar_pr...]
    ppermute x34 -> x35, starting transfers between devices: 26.8 us -> 28.3 us  [swap_dp(): lax.ppermute(v, ('z', 'core'), [(i, i ^ bit) for i in range(n_dp)])]
  transfers between devices with their start and end apart: 61 -> 62, of which waited for: 18 -> 17; matrix products, arithmetic and copies ran while one was open for 8% -> 4% of each run, Pallas kernels for 59% -> 64%
where the time goes in v3:
time: 492 us; the launch traced here: 483 us
  Pallas kernels  329 us (67%)
  starting transfers between devices  59 us (12%)
  waiting for transfers between devices  42.3 us (9%)
  local copies, waits for them, and re-layouts  33.7 us (7%)
  other arithmetic  9.86 us (2%)
  matrix products  7.05 us (1%)
    pallas_call x35, Pallas kernels, run(): pl.pallas_call(body, grid_spec=pltpu.PrefetchScalarGridSpec(num_scalar_pr...  329 us
    ppermute x27, starting transfers between devices, swap_mp(): return lambda v: lax.ppermute(v, 'mp', [(i, i ^ bit) for i in range(n_mp)])  30.7 us
    ppermute x35, starting transfers between devices, swap_dp(): lax.ppermute(v, ('z', 'core'), [(i, i ^ bit) for i in range(n_dp)])  28.3 us
    ppermute x27, waiting for transfers between devices, swap_mp(): return lambda v: lax.ppermute(v, 'mp', [(i, i ^ bit) for i in range(n_mp)])  22.2 us
    unnamed x165, local copies, waits for them, and re-layouts  20.3 us
    ppermute x35, waiting for transfers between devices, swap_dp(): lax.ppermute(v, ('z', 'core'), [(i, i ^ bit) for i in range(n_dp)])  20.1 us
  transfers between devices with their start and end apart: 62, of which 17 were waited for; matrix products, arithmetic and copies ran while one was open for 4% of the time, Pallas kernels for 64%

profile of v3, /device:TPU:0, one launch (start us, length us, event | category | flops | bytes accessed | tf_op | source)
XLA Modules:
  0.0 483.2 jit_solution(15375982124979461317)
XLA Ops:
  4.0 2.5 fusion.2.refs_3_
  6.7 3.0 collective-permute-start
  11.3 4.2 attn_rows.1
  24.5 15.3 %attend.4 = (bf16[1280,1024]{1,0:T(8,128)(2,1)S(1)}, bf16[1280,768]{1,0:T(8,128)(2,1)}, bf16[1280,256]{1,0:T(8,128)(2,1)}, bf16[16,320,320]{2,1,0:T(8,128)(2,1)}) custom-call(s32[4]{0:T(128)S(1)} %fusion.19.refs_0_, bf16[4,320,1024]{2,1,0:T(8,128)(2,1)} %refs_12_.3, f32[4,6,1024]{2,1,0:T(8,128)} %reshape.112.refs_2_.refs_14_.refs_15_.refs_13_, ...), custom_call_target="tpu_custom_call" | custom-call | flops 1000 | bytes 1000 | tf_op jit(solution)/shard_map/attend/pallas_call | solution.py:104
  39.9 7.5 %feed_rows.1 = (bf16[2,512,1024]{2,1,0:T(8,128)(2,1)}, bf16[2,512,1024]{2,1,0:T(8,128)(2,1)}) custom-call(s32[1]{0:T(128)} %bitcast.8.refs_0_, bf16[1024,1024]{1,0:T(8,128)(2,1)} %refs_1_.5, bf16[1024,1024]{1,0:T(8,128)(2,1)} %refs_2_.3, bf16[1280,256]{1,0:T(8,128)(2,1)} %get-tuple-element.144.refs_3_.refs_0_.refs_8_), custom_call_target="tpu_custom_call" | custom-call | flops 1000 | bytes 1000 | tf_op jit(solution)/shard_map/feed_rows/pallas_call | solution.py:104
  51.9 12.9 %attend.5 = (bf16[1280,768]{1,0:T(8,128)(2,1)}, bf16[1280,256]{1,0:T(8,128)(2,1)}, bf16[16,320,320]{2,1,0:T(8,128)(2,1)}) custom-call(s32[4]{0:T(128)S(1)} %fusion.19.refs_0_, bf16[1280,1024]{1,0:T(8,128)(2,1)} %copy-done.3, f32[4,6,1024]{2,1,0:T(8,128)} %reshape.112.refs_2_.refs_14_.refs_15_.refs_13_, bf16[512,1024]{1,0:T(8,128)(2,1)S(1)} %copy-done.20, ...), custom_call_target="tpu_custom_call" | custom-call | flops 1000 | bytes 1000 | tf_op jit(solution)/shard_map/attend/pallas_call | solution.py:104
  71.9 12.9 %attend.6 = (bf16[1280,768]{1,0:T(8,128)(2,1)}, bf16[1280,256]{1,0:T(8,128)(2,1)}, bf16[16,320,320]{2,1,0:T(8,128)(2,1)}) custom-call(s32[4]{0:T(128)S(1)} %fusion.19.refs_0_, bf16[1280,1024]{1,0:T(8,128)(2,1)} %copy-done.3, f32[4,6,1024]{2,1,0:T(8,128)} %reshape.112.refs_2_.refs_14_.refs_15_.refs_13_, bf16[512,1024]{1,0:T(8,128)(2,1)S(1)} %copy-done.18, ...), custom_call_target="tpu_custom_call" | custom-call | flops 1000 | bytes 1000 | tf_op jit(solution)/shard_map/attend/pallas_call | solution.py:104
  84.9 14.3 %attend.7 = (bf16[1280,768]{1,0:T(8,128)(2,1)}, bf16[1280,256]{1,0:T(8,128)(2,1)}, bf16[16,320,320]{2,1,0:T(8,128)(2,1)}) custom-call(s32[4]{0:T(128)S(1)} %fusion.19.refs_0_, bf16[1280,1024]{1,0:T(8,128)(2,1)} %copy-done.3, f32[4,6,1024]{2,1,0:T(8,128)} %reshape.112.refs_2_.refs_14_.refs_15_.refs_13_, bf16[512,1024]{1,0:T(8,128)(2,1)} %copy-done.35, ...), custom_call_target="tpu_custom_call" | custom-call | flops 1000 | bytes 1000 | tf_op jit(solution)/shard_map/attend/pallas_call | solution.py:104
  99.3 9.8 %middle.1 = (bf16[1280,1024]{1,0:T(8,128)(2,1)}, f32[1280,1024]{1,0:T(8,128)}, bf16[1280,1024]{1,0:T(8,128)(2,1)S(1)}, bf16[1280,1024]{1,0:T(8,128)(2,1)S(1)}) custom-call(bf16[1280,256]{1,0:T(8,128)(2,1)} %get-tuple-element.144.refs_3_.refs_0_.refs_8_, bf16[1280,256]{1,0:T(8,128)(2,1)} %get-tuple-element.148.refs_7_.refs_2_.refs_1_.refs_8_, ...), custom_call_target="tpu_custom_call" | custom-call | flops 1000 | bytes 1000 | tf_op jit(solution)/shard_map/middle/pallas_call | solution.py:104
  109.1 16.8 %feed.4 = (bf16[1280,1024]{1,0:T(8,128)(2,1)}, bf16[1280,1024]{1,0:T(8,128)(2,1)}, bf16[2,512,1024]{2,1,0:T(8,128)(2,1)}, bf16[2,512,1024]{2,1,0:T(8,128)(2,1)}) custom-call(bf16[1280,1024]{1,0:T(8,128)(2,1)S(1)} %get-tuple-element.154.refs_0_, bf16[1280,1024]{1,0:T(8,128)(2,1)S(1)} %get-tuple-element.155.refs_1_, ...), custom_call_target="tpu_custom_call" | custom-call | flops 1000 | bytes 1000 | tf_op jit(solution)/shard_map/feed/pallas_call | solution.py:104
  135.9 14.4 %feed.5 = (bf16[1280,1024]{1,0:T(8,128)(2,1)}, bf16[1280,1024]{1,0:T(8,128)(2,1)}, bf16[2,512,1024]{2,1,0:T(8,128)(2,1)}, bf16[2,512,1024]{2,1,0:T(8,128)(2,1)}) custom-call(bf16[1280,1024]{1,0:T(8,128)(2,1)S(1)} %copy-done.8, bf16[1280,1024]{1,0:T(8,128)(2,1)S(1)} %copy-done.11, bf16[2,512,1024]{2,1,0:T(8,128)(2,1)S(1)} %copy-done.6, ...), custom_call_target="tpu_custom_call" | custom-call | flops 1000 | bytes 1000 | tf_op jit(solution)/shard_map/feed/pallas_call | solution.py:104
  150.4 14.0 %feed.6 = (bf16[1280,1024]{1,0:T(8,128)(2,1)}, bf16[1280,1024]{1,0:T(8,128)(2,1)}, bf16[2,512,1024]{2,1,0:T(8,128)(2,1)}, bf16[2,512,1024]{2,1,0:T(8,128)(2,1)}) custom-call(bf16[1280,1024]{1,0:T(8,128)(2,1)S(1)} %copy-done.8, bf16[1280,1024]{1,0:T(8,128)(2,1)S(1)} %copy-done.11, bf16[2,512,1024]{2,1,0:T(8,128)(2,1)} %get-tuple-element.159.refs_2_.refs_3_.refs_8_, ...), custom_call_target="tpu_custom_call" | custom-call | flops 1000 | bytes 1000 | tf_op jit(solution)/shard_map/feed/pallas_call | solution.py:104
  165.4 2.5 merge.10.refs_2_
  167.9 3.0 collective-permute-done.18.refs_1_.refs_4_
  170.9 2.6 merge.11.refs_7_
  176.4 14.0 %feed.7 = (bf16[1280,1024]{1,0:T(8,128)(2,1)}, bf16[1280,1024]{1,0:T(8,128)(2,1)}, bf16[2,512,1024]{2,1,0:T(8,128)(2,1)}, bf16[2,512,1024]{2,1,0:T(8,128)(2,1)}) custom-call(bf16[1280,1024]{1,0:T(8,128)(2,1)S(1)} %copy-done.9, bf16[1280,1024]{1,0:T(8,128)(2,1)S(1)} %copy-done.12, bf16[1,512,1024]{2,1,0:T(8,128)(2,1)} %get-tuple-element.162.refs_2_.refs_10_, ...), custom_call_target="tpu_custom_call" | custom-call | flops 1000 | bytes 1000 | tf_op jit(solution)/shard_map/feed/pallas_call | solution.py:104
  190.5 8.8 %collective-permute-done.22.refs_1_ = bf16[512,1024]{1,0:T(8,128)(2,1)} collective-permute-done((bf16[512,1024]{1,0:T(8,128)(2,1)}, bf16[512,1024]{1,0:T(8,128)(2,1)}, u32[]{:S(2)}, u32[]{:S(2)}) %collective-permute-start.22) | collective-permute-done | bytes 1048608 | tf_op jit(solution)/shard_map/ppermute | solution.py:889
  200.4 3.5 merge.12
  205.6 22.7 %turn.1 = (f32[1280,1024]{1,0:T(8,128)}, bf16[1280,1024]{1,0:T(8,128)(2,1)S(1)}, f32[4,3,1024]{2,1,0:T(4,128)}) custom-call(bf16[1280,1024]{1,0:T(8,128)(2,1)} %get-tuple-element.175.refs_0_, bf16[1280,1024]{1,0:T(8,128)(2,1)} %get-tuple-element.176.refs_1_, bf16[1280,1024]{1,0:T(8,128)(2,1)} %get-tuple-element.177.refs_2_, ...), custom_call_target="tpu_custom_call" | custom-call | flops 1000 | bytes 1000 | tf_op jit(solution)/shard_map/turn/pallas_call | solution.py:104
  229.7 4.1 merge.13
  236.2 18.1 %output.1 = (bf16[4,320,1024]{2,1,0:T(8,128)(2,1)}, f32[4,1,1024]{2,1,0:T(1,128)}) custom-call(bf16[1280,1024]{1,0:T(8,128)(2,1)} %get-tuple-element.157.refs_2_.refs_6_.refs_0_, bf16[1280,1024]{1,0:T(8,128)(2,1)} %get-tuple-element.160.refs_6_.refs_1_, bf16[1280,1024]{1,0:T(8,128)(2,1)} %get-tuple-element.161.refs_2_.refs_6_, ...), custom_call_target="tpu_custom_call" | custom-call | flops 1000 | bytes 1000 | tf_op jit(solution)/shard_map/output/pallas_call | solution.py:104
  254.3 3.9 collective-permute-done.26.refs_0_
  261.7 6.3 %merge_parts.2 = (bf16[512,1024]{1,0:T(8,128)(2,1)}, bf16[512,1024]{1,0:T(8,128)(2,1)}) custom-call(s32[1]{0:T(128)} %bitcast.18.refs_0_, bf16[2,512,1024]{2,1,0:T(8,128)(2,1)} %get-tuple-element.193.refs_1_.refs_7_, bf16[2,512,1024]{2,1,0:T(8,128)(2,1)S(1)} %copy-done.27, bf16[512,1024]{1,0:T(8,128)(2,1)} %get-tuple-element.172.refs_4_.refs_3_.refs_9_, ...), custom_call_target="tpu_custom_call" | custom-call | flops 1000 | bytes 1000 | tf_op jit(solution)/shard_map/merge_parts/pallas_call | solution.py:104
  269.6 18.1 %attend_back.4 = (bf16[1280,768]{1,0:T(8,128)(2,1)}, bf16[512,1024]{1,0:T(8,128)(2,1)}, bf16[512,1024]{1,0:T(8,128)(2,1)}, f32[2,32,128]{2,1,0:T(8,128)}) custom-call(bf16[1280,1024]{1,0:T(8,128)(2,1)} %copy-done.2, bf16[512,1024]{1,0:T(8,128)(2,1)} %copy-done.35, bf16[512,1024]{1,0:T(8,128)(2,1)} %copy-done.23, ...), custom_call_target="tpu_custom_call" | custom-call | flops 1000 | bytes 1000 | tf_op jit(solution)/shard_map/attend_back/pallas_call | solution.py:104
  287.8 3.5 collective-permute-done.29.refs_0_
  293.3 2.6 collective-permute-start.30
  296.7 18.1 %attend_back.5 = (bf16[1280,768]{1,0:T(8,128)(2,1)}, bf16[512,1024]{1,0:T(8,128)(2,1)}, bf16[512,1024]{1,0:T(8,128)(2,1)}, f32[2,32,128]{2,1,0:T(8,128)}) custom-call(bf16[1280,1024]{1,0:T(8,128)(2,1)} %copy-done.2, bf16[512,1024]{1,0:T(8,128)(2,1)} %get-tuple-element.147.refs_3_.refs_6_.refs_1_, bf16[512,1024]{1,0:T(8,128)(2,1)} %copy-done.24, ...), custom_call_target="tpu_custom_call" | custom-call | flops 1000 | bytes 1000 | tf_op jit(solution)/shard_map/attend_back/pallas_call | solution.py:104
  317.2 2.4 merge.15.refs_4_
  319.6 2.7 merge.16
  326.5 18.2 %attend_back.6 = (bf16[1280,768]{1,0:T(8,128)(2,1)}, bf16[512,1024]{1,0:T(8,128)(2,1)}, bf16[512,1024]{1,0:T(8,128)(2,1)}, f32[2,32,128]{2,1,0:T(8,128)}) custom-call(bf16[1280,1024]{1,0:T(8,128)(2,1)} %copy-done.2, bf16[512,1024]{1,0:T(8,128)(2,1)} %get-tuple-element.149.refs_3_.refs_8_.refs_1_, bf16[512,1024]{1,0:T(8,128)(2,1)} %copy-done.22, ...), custom_call_target="tpu_custom_call" | custom-call | flops 1000 | bytes 1000 | tf_op jit(solution)/shard_map/attend_back/pallas_call | solution.py:104
  345.3 2.2 pad_maximum_fusion.refs_11_.refs_1_
  347.6 4.0 collective-permute-start.37
  351.6 2.7 merge.17.refs_3_
  355.2 2.7 merge.18.refs_10_
  359.3 18.0 %attend_back.7 = (bf16[1280,768]{1,0:T(8,128)(2,1)}, bf16[512,1024]{1,0:T(8,128)(2,1)}, bf16[512,1024]{1,0:T(8,128)(2,1)}, f32[2,32,128]{2,1,0:T(8,128)}) custom-call(bf16[1280,1024]{1,0:T(8,128)(2,1)} %copy-done.2, bf16[512,1024]{1,0:T(8,128)(2,1)} %hold.20.refs_3_.refs_4_.refs_1_, bf16[512,1024]{1,0:T(8,128)(2,1)} %get-tuple-element.143.refs_4_.refs_5_.refs_2_, ...), custom_call_target="tpu_custom_call" | custom-call | flops 1000 | bytes 1000 | tf_op jit(solution)/shard_map/attend_back/pallas_call | solution.py:104
  379.4 3.3 collective-permute-done.39.refs_2_
  382.8 3.1 merge_parts.3
  386.8 3.5 collective-permute-start.42
  390.3 18.1 %last.1 = (bf16[4,320,1024]{2,1,0:T(8,128)(2,1)}, f32[4,2,1024]{2,1,0:T(2,128)}) custom-call(bf16[1280,768]{1,0:T(8,128)(2,1)} %get-tuple-element.219.refs_3_.refs_0_, bf16[1280,768]{1,0:T(8,128)(2,1)} %get-tuple-element.206.refs_1_, bf16[1280,768]{1,0:T(8,128)(2,1)} %get-tuple-element.211.refs_3_.refs_9_.refs_2_, ...), custom_call_target="tpu_custom_call" | custom-call | flops 1000 | bytes 1000 | tf_op jit(solution)/shard_map/last/pallas_call | solution.py:104
  420.9 7.8 %feed_final.1 = (f32[1024,1024]{1,0:T(8,128)}, f32[1024,1024]{1,0:T(8,128)}) custom-call(s32[2]{0:T(128)S(1)} %pad_add_fusion.refs_0_, bf16[512,1024]{1,0:T(8,128)(2,1)} %pad_maximum_fusion.refs_11_.refs_1_, bf16[512,1024]{1,0:T(8,128)(2,1)} %get-tuple-element.229.refs_2_, bf16[512,1024]{1,0:T(8,128)(2,1)} %get-tuple-element.235.refs_3_, ...), custom_call_target="tpu_custom_call" | custom-call | flops 1000 | bytes 1000 | tf_op jit(solution)/shard_map/feed_final/pallas_call | solution.py:104
  429.3 3.3 collective-permute-start.53
  433.4 3.6 mode_shares.1
  447.9 2.1 mode_rows.1.refs_1_
  450.2 5.0 %collective-permute-start.56 = (bf16[16,3840]{1,0:T(8,128)(2,1)}, bf16[16,3840]{1,0:T(8,128)(2,1)S(1)}, u32[]{:S(2)}, u32[]{:S(2)}) collective-permute-start(bf16[16,3840]{1,0:T(8,128)(2,1)} %mode_rows.1.refs_1_), channel_id=1, source_target_pairs={{0,8},{4,12},{8,0},{12,4},{16,24},{20,28},{24,16},{28,20},{1,9},{5... | collective-permute-start | bytes 368648 | tf_op jit(solution)/shard_map/ppermute | solution.py:892
  457.7 5.1 %collective-permute-done.56.refs_1_ = bf16[16,3840]{1,0:T(8,128)(2,1)S(1)} collective-permute-done((bf16[16,3840]{1,0:T(8,128)(2,1)}, bf16[16,3840]{1,0:T(8,128)(2,1)S(1)}, u32[]{:S(2)}, u32[]{:S(2)}) %collective-permute-start.56) | collective-permute-done | bytes 122912 | tf_op jit(solution)/shard_map/ppermute | solution.py:892
  465.0 5.9 %attn_final.1 = (f32[1024,768]{1,0:T(8,128)}, f32[256,1024]{1,0:T(8,128)}) custom-call(s32[2]{0:T(128)S(1)} %pad_add_fusion.refs_0_, bf16[512,1024]{1,0:T(8,128)(2,1)} %copy-done.41, bf16[512,1024]{1,0:T(8,128)(2,1)S(1)} %copy-done.32), custom_call_target="tpu_custom_call" | custom-call | flops 1000 | bytes 1000 | tf_op jit(solution)/shard_map/attn_final/pallas_call | solution.py:104
  470.9 3.3 collective-permute-done.59.refs_4_
  474.9 5.2 %mode_final.1 = (f32[1024,1536]{1,0:T(8,128)}, f32[1,1536]{1,0:T(1,128)}, f32[101,1024]{1,0:T(8,128)}, f32[16,128]{1,0:T(8,128)}) custom-call(s32[1]{0:T(128)} %bitcast.32.refs_0_, bf16[16,3840]{1,0:T(8,128)(2,1)} %mode_rows.1.refs_1_, bf16[16,3840]{1,0:T(8,128)(2,1)} %get-tuple-element.263.refs_2_, bf16[16,3840]{1,0:T(8,128)(2,1)} %get-tuple-element.264.refs_3_, ...), custom_call_target="tpu_custom_call" | custom-call | flops 1000 | bytes 1000 | tf_op jit(solution)/shard_map/mode_final/pallas_call | solution.py:104
  (358 shorter events, 99.2 us)
Async XLA Ops:
  16.7 30.7 %collective-permute-start.3 = (bf16[512,1024]{1,0:T(8,128)(2,1)}, bf16[512,1024]{1,0:T(8,128)(2,1)S(1)}, u32[]{:S(2)}, u32[]{:S(2)}) collective-permute-start(bf16[512,1024]{1,0:T(8,128)(2,1)} %hold.20.refs_3_.refs_4_.refs_1_), channel_id=1, source_target_pairs={{0,1},{1,0},{2,3},{3,2},{4,5},{5,4},{6,7},{7,6},{8,9},{9,8},{10,11... | collective-permute-start | bytes 3145736 | tf_op jit(solution)/shard_map/ppermute | solution.py:889
  18.4 29.0 %collective-permute-start.4 = (bf16[512,1024]{1,0:T(8,128)(2,1)}, bf16[512,1024]{1,0:T(8,128)(2,1)S(1)}, u32[]{:S(2)}, u32[]{:S(2)}) collective-permute-start(bf16[512,1024]{1,0:T(8,128)(2,1)} %hold.20.refs_3_.refs_4_.refs_1_), channel_id=1, source_target_pairs={{0,2},{1,3},{2,0},{3,1},{4,6},{5,7},{6,4},{7,5},{8,10},{9,11},{10,... | collective-permute-start | bytes 3145736 | tf_op jit(solution)/shard_map/ppermute | solution.py:889
  49.9 15.0 %collective-permute-start.7 = (bf16[256,1024]{1,0:T(8,128)(2,1)S(1)}, bf16[256,1024]{1,0:T(8,128)(2,1)S(1)}, u32[]{:S(2)}, u32[]{:S(2)}) collective-permute-start(bf16[256,1024]{1,0:T(8,128)(2,1)S(1)} %slice.52), channel_id=1, source_target_pairs={{0,2},{1,3},{2,0},{3,1},{4,6},{5,7},{6,4},{7,5},{8,10},{9,11},{10,... | collective-permute-start | bytes 1572872 | tf_op jit(solution)/shard_map/ppermute | solution.py:889
  51.5 14.0 %collective-permute-start.8 = (bf16[256,1024]{1,0:T(8,128)(2,1)S(1)}, bf16[256,1024]{1,0:T(8,128)(2,1)S(1)}, u32[]{:S(2)}, u32[]{:S(2)}) collective-permute-start(bf16[256,1024]{1,0:T(8,128)(2,1)S(1)} %slice.53), channel_id=1, source_target_pairs={{0,1},{1,0},{2,3},{3,2},{4,5},{5,4},{6,7},{7,6},{8,9},{9,8},{10,11... | collective-permute-start | bytes 1572872 | tf_op jit(solution)/shard_map/ppermute | solution.py:889
  66.4 59.6 %collective-permute-start.10 = (bf16[2,512,1024]{2,1,0:T(8,128)(2,1)}, bf16[2,512,1024]{2,1,0:T(8,128)(2,1)S(1)}, u32[]{:S(2)}, u32[]{:S(2)}) collective-permute-start(bf16[2,512,1024]{2,1,0:T(8,128)(2,1)} %hold.23.refs_2_.refs_3_.refs_4_), channel_id=1, source_target_pairs={{0,1},{1,0},{2,3},{3,2},{4,5},{5,4},{6,7},{7,6},{8,9},{9,8},{10,11... | collective-permute-start | bytes 6291464 | tf_op jit(solution)/shard_map/ppermute | solution.py:889
  67.5 58.4 %collective-permute-start.11 = (bf16[2,512,1024]{2,1,0:T(8,128)(2,1)}, bf16[2,512,1024]{2,1,0:T(8,128)(2,1)}, u32[]{:S(2)}, u32[]{:S(2)}) collective-permute-start(bf16[2,512,1024]{2,1,0:T(8,128)(2,1)} %hold.23.refs_2_.refs_3_.refs_4_), channel_id=1, source_target_pairs={{0,2},{1,3},{2,0},{3,1},{4,6},{5,7},{6,4},{7,5},{8,10},{9,11},{10,... | collective-permute-start | bytes 6291464 | tf_op jit(solution)/shard_map/ppermute | solution.py:889
  70.2 14.7 %collective-permute-start.9 = (bf16[512,1024]{1,0:T(8,128)(2,1)S(1)}, bf16[512,1024]{1,0:T(8,128)(2,1)S(1)}, u32[]{:S(2)}, u32[]{:S(2)}) collective-permute-start(bf16[512,1024]{1,0:T(8,128)(2,1)S(1)} %constant_dynamic-update-slice_fusion.refs_3_.refs_10_.refs_1_), channel_id=1, source_target_pairs={{0,4},{4,0},{8,12},{12,8},{16,20},{20,16},{24,28},{28,24},{1,5},{5... | collective-permute-start | bytes 3145736 | tf_op jit(solution)/shard_map/ppermute | solution.py:892
  127.4 22.9 %collective-permute-start.13 = (bf16[2,512,1024]{2,1,0:T(8,128)(2,1)}, bf16[2,512,1024]{2,1,0:T(8,128)(2,1)S(1)}, u32[]{:S(2)}, u32[]{:S(2)}) collective-permute-start(bf16[2,512,1024]{2,1,0:T(8,128)(2,1)} %get-tuple-element.159.refs_2_.refs_3_.refs_8_), channel_id=1, source_target_pairs={{0,4},{4,0},{8,12},{12,8},{16,20},{20,16},{24,28},{28,24},{1,5},{5... | collective-permute-start | bytes 6291464 | tf_op jit(solution)/shard_map/ppermute | solution.py:892
  131.0 34.0 %collective-permute-start.14 = (bf16[1,512,1024]{2,1,0:T(8,128)(2,1)S(1)}, bf16[1,512,1024]{2,1,0:T(8,128)(2,1)}, u32[]{:S(2)}, u32[]{:S(2)}) collective-permute-start(bf16[1,512,1024]{2,1,0:T(8,128)(2,1)S(1)} %slice.55.refs_7_), channel_id=1, source_target_pairs={{0,2},{1,3},{2,0},{3,1},{4,6},{5,7},{6,4},{7,5},{8,10},{9,11},{10,... | collective-permute-start | bytes 3145736 | tf_op jit(solution)/shard_map/ppermute | solution.py:889
  131.5 33.4 %collective-permute-start.15 = (bf16[1,512,1024]{2,1,0:T(8,128)(2,1)S(1)}, bf16[1,512,1024]{2,1,0:T(8,128)(2,1)}, u32[]{:S(2)}, u32[]{:S(2)}) collective-permute-start(bf16[1,512,1024]{2,1,0:T(8,128)(2,1)S(1)} %slice.56.refs_8_), channel_id=1, source_target_pairs={{0,1},{1,0},{2,3},{3,2},{4,5},{5,4},{6,7},{7,6},{8,9},{9,8},{10,11... | collective-permute-start | bytes 3145736 | tf_op jit(solution)/shard_map/ppermute | solution.py:889
  150.3 15.2 %collective-permute-start.19 = (bf16[2,512,1024]{2,1,0:T(8,128)(2,1)}, bf16[2,512,1024]{2,1,0:T(8,128)(2,1)}, u32[]{:S(2)}, u32[]{:S(2)}) collective-permute-start(bf16[2,512,1024]{2,1,0:T(8,128)(2,1)} %get-tuple-element.167), channel_id=1, source_target_pairs={{0,4},{4,0},{8,12},{12,8},{16,20},{20,16},{24,28},{28,24},{1,5},{5... | collective-permute-start | bytes 6291464 | tf_op jit(solution)/shard_map/ppermute | solution.py:892
  164.9 11.4 %collective-permute-start.16 = (bf16[1,512,1024]{2,1,0:T(8,128)(2,1)}, bf16[1,512,1024]{2,1,0:T(8,128)(2,1)S(1)}, u32[]{:S(2)}, u32[]{:S(2)}) collective-permute-start(bf16[1,512,1024]{2,1,0:T(8,128)(2,1)} %get-tuple-element.162.refs_2_.refs_10_), channel_id=1, source_target_pairs={{0,4},{4,0},{8,12},{12,8},{16,20},{20,16},{24,28},{28,24},{1,5},{5... | collective-permute-start | bytes 3145736 | tf_op jit(solution)/shard_map/ppermute | solution.py:892
  165.0 11.3 %collective-permute-start.17 = (bf16[1,512,1024]{2,1,0:T(8,128)(2,1)}, bf16[1,512,1024]{2,1,0:T(8,128)(2,1)S(1)}, u32[]{:S(2)}, u32[]{:S(2)}) collective-permute-start(bf16[1,512,1024]{2,1,0:T(8,128)(2,1)} %get-tuple-element.163.refs_3_.refs_10_), channel_id=1, source_target_pairs={{0,4},{4,0},{8,12},{12,8},{16,20},{20,16},{24,28},{28,24},{1,5},{5... | collective-permute-start | bytes 3145736 | tf_op jit(solution)/shard_map/ppermute | solution.py:892
  173.6 25.8 %collective-permute-start.22 = (bf16[512,1024]{1,0:T(8,128)(2,1)}, bf16[512,1024]{1,0:T(8,128)(2,1)}, u32[]{:S(2)}, u32[]{:S(2)}) collective-permute-start(bf16[512,1024]{1,0:T(8,128)(2,1)} %merge.11.refs_7_), channel_id=1, source_target_pairs={{0,2},{1,3},{2,0},{3,1},{4,6},{5,7},{6,4},{7,5},{8,10},{9,11},{10,... | collective-permute-start | bytes 3145736 | tf_op jit(solution)/shard_map/ppermute | solution.py:889
  175.2 25.2 %collective-permute-start.21 = (bf16[512,1024]{1,0:T(8,128)(2,1)S(1)}, bf16[512,1024]{1,0:T(8,128)(2,1)}, u32[]{:S(2)}, u32[]{:S(2)}) collective-permute-start(bf16[512,1024]{1,0:T(8,128)(2,1)S(1)} %copy-done.42), channel_id=1, source_target_pairs={{0,1},{1,0},{2,3},{3,2},{4,5},{5,4},{6,7},{7,6},{8,9},{9,8},{10,11... | collective-permute-start | bytes 3145736 | tf_op jit(solution)/shard_map/ppermute | solution.py:889
  203.9 25.8 %collective-permute-start.23 = (bf16[512,1024]{1,0:T(8,128)(2,1)}, bf16[512,1024]{1,0:T(8,128)(2,1)}, u32[]{:S(2)}, u32[]{:S(2)}) collective-permute-start(bf16[512,1024]{1,0:T(8,128)(2,1)} %get-tuple-element.173.refs_16_), channel_id=1, source_target_pairs={{0,1},{1,0},{2,3},{3,2},{4,5},{5,4},{6,7},{7,6},{8,9},{9,8},{10,11... | collective-permute-start | bytes 3145736 | tf_op jit(solution)/shard_map/ppermute | solution.py:889
  205.1 24.7 %collective-permute-start.24 = (bf16[512,1024]{1,0:T(8,128)(2,1)}, bf16[512,1024]{1,0:T(8,128)(2,1)}, u32[]{:S(2)}, u32[]{:S(2)}) collective-permute-start(bf16[512,1024]{1,0:T(8,128)(2,1)} %get-tuple-element.174.refs_17_), channel_id=1, source_target_pairs={{0,2},{1,3},{2,0},{3,1},{4,6},{5,7},{6,4},{7,5},{8,10},{9,11},{10,... | collective-permute-start | bytes 3145736 | tf_op jit(solution)/shard_map/ppermute | solution.py:889
  233.8 24.4 %collective-permute-start.26 = (bf16[512,1024]{1,0:T(8,128)(2,1)}, bf16[512,1024]{1,0:T(8,128)(2,1)}, u32[]{:S(2)}, u32[]{:S(2)}) collective-permute-start(bf16[512,1024]{1,0:T(8,128)(2,1)} %get-tuple-element.183.refs_15_), channel_id=1, source_target_pairs={{0,1},{1,0},{2,3},{3,2},{4,5},{5,4},{6,7},{7,6},{8,9},{9,8},{10,11... | collective-permute-start | bytes 3145736 | tf_op jit(solution)/shard_map/ppermute | solution.py:889
  234.7 24.1 %collective-permute-start.27 = (bf16[512,1024]{1,0:T(8,128)(2,1)}, bf16[512,1024]{1,0:T(8,128)(2,1)}, u32[]{:S(2)}, u32[]{:S(2)}) collective-permute-start(bf16[512,1024]{1,0:T(8,128)(2,1)} %get-tuple-element.184.refs_16_), channel_id=1, source_target_pairs={{0,2},{1,3},{2,0},{3,1},{4,6},{5,7},{6,4},{7,5},{8,10},{9,11},{10,... | collective-permute-start | bytes 3145736 | tf_op jit(solution)/shard_map/ppermute | solution.py:889
  236.2 22.6 %collective-permute-start.25 = (bf16[2,512,1024]{2,1,0:T(8,128)(2,1)}, bf16[2,512,1024]{2,1,0:T(8,128)(2,1)S(1)}, u32[]{:S(2)}, u32[]{:S(2)}) collective-permute-start(bf16[2,512,1024]{2,1,0:T(8,128)(2,1)} %get-tuple-element.194), channel_id=1, source_target_pairs={{0,4},{4,0},{8,12},{12,8},{16,20},{20,16},{24,28},{28,24},{1,5},{5... | collective-permute-start | bytes 6291464 | tf_op jit(solution)/shard_map/ppermute | solution.py:892
  268.0 23.2 %collective-permute-start.29 = (bf16[512,1024]{1,0:T(8,128)(2,1)}, bf16[512,1024]{1,0:T(8,128)(2,1)}, u32[]{:S(2)}, u32[]{:S(2)}) collective-permute-start(bf16[512,1024]{1,0:T(8,128)(2,1)} %get-tuple-element.202), channel_id=1, source_target_pairs={{0,8},{4,12},{8,0},{12,4},{16,24},{20,28},{24,16},{28,20},{1,9},{5... | collective-permute-start | bytes 3145736 | tf_op jit(solution)/shard_map/ppermute | solution.py:892
  293.3 23.1 %collective-permute-start.30 = (bf16[256,1024]{1,0:T(8,128)(2,1)}, bf16[256,1024]{1,0:T(8,128)(2,1)}, u32[]{:S(2)}, u32[]{:S(2)}) collective-permute-start(bf16[256,1024]{1,0:T(8,128)(2,1)} %merge.14.refs_10_), channel_id=1, source_target_pairs={{0,16},{4,20},{8,24},{12,28},{16,0},{20,4},{24,8},{28,12},{1,17},{... | collective-permute-start | bytes 1572872 | tf_op jit(solution)/shard_map/ppermute | solution.py:892
  296.6 22.9 %collective-permute-start.28 = (bf16[512,1024]{1,0:T(8,128)(2,1)}, bf16[512,1024]{1,0:T(8,128)(2,1)}, u32[]{:S(2)}, u32[]{:S(2)}) collective-permute-start(bf16[512,1024]{1,0:T(8,128)(2,1)} %get-tuple-element.201), channel_id=1, source_target_pairs={{0,4},{4,0},{8,12},{12,8},{16,20},{20,16},{24,28},{28,24},{1,5},{5... | collective-permute-start | bytes 3145736 | tf_op jit(solution)/shard_map/ppermute | solution.py:892
  319.5 25.8 %collective-permute-start.32 = (bf16[256,1024]{1,0:T(8,128)(2,1)}, bf16[256,1024]{1,0:T(8,128)(2,1)}, u32[]{:S(2)}, u32[]{:S(2)}) collective-permute-start(bf16[256,1024]{1,0:T(8,128)(2,1)} %merge.15.refs_4_), channel_id=1, source_target_pairs={{0,16},{4,20},{8,24},{12,28},{16,0},{20,4},{24,8},{28,12},{1,17},{... | collective-permute-start | bytes 1572872 | tf_op jit(solution)/shard_map/ppermute | solution.py:892
  322.3 23.1 %collective-permute-start.33 = (bf16[256,1024]{1,0:T(8,128)(2,1)}, bf16[256,1024]{1,0:T(8,128)(2,1)}, u32[]{:S(2)}, u32[]{:S(2)}) collective-permute-start(bf16[256,1024]{1,0:T(8,128)(2,1)} %get-tuple-element.207.refs_9_), channel_id=1, source_target_pairs={{0,1},{1,0},{2,3},{3,2},{4,5},{5,4},{6,7},{7,6},{8,9},{9,8},{10,11... | collective-permute-start | bytes 1572872 | tf_op jit(solution)/shard_map/ppermute | solution.py:889
  323.4 21.9 %collective-permute-start.34 = (bf16[256,1024]{1,0:T(8,128)(2,1)}, bf16[256,1024]{1,0:T(8,128)(2,1)}, u32[]{:S(2)}, u32[]{:S(2)}) collective-permute-start(bf16[256,1024]{1,0:T(8,128)(2,1)} %get-tuple-element.208.refs_10_), channel_id=1, source_target_pairs={{0,2},{1,3},{2,0},{3,1},{4,6},{5,7},{6,4},{7,5},{8,10},{9,11},{10,... | collective-permute-start | bytes 1572872 | tf_op jit(solution)/shard_map/ppermute | solution.py:889
  326.5 25.1 %collective-permute-start.35 = (bf16[512,1024]{1,0:T(8,128)(2,1)}, bf16[512,1024]{1,0:T(8,128)(2,1)}, u32[]{:S(2)}, u32[]{:S(2)}) collective-permute-start(bf16[512,1024]{1,0:T(8,128)(2,1)} %get-tuple-element.216), channel_id=1, source_target_pairs={{0,4},{4,0},{8,12},{12,8},{16,20},{20,16},{24,28},{28,24},{1,5},{5... | collective-permute-start | bytes 3145736 | tf_op jit(solution)/shard_map/ppermute | solution.py:892
  347.6 30.4 %collective-permute-start.37 = (bf16[512,1024]{1,0:T(8,128)(2,1)}, bf16[512,1024]{1,0:T(8,128)(2,1)}, u32[]{:S(2)}, u32[]{:S(2)}) collective-permute-start(bf16[512,1024]{1,0:T(8,128)(2,1)} %pad_maximum_fusion.refs_11_.refs_1_), channel_id=1, source_target_pairs={{0,8},{4,12},{8,0},{12,4},{16,24},{20,28},{24,16},{28,20},{1,9},{5... | collective-permute-start | bytes 3145736 | tf_op jit(solution)/shard_map/ppermute | solution.py:892
  354.3 25.1 %collective-permute-start.38 = (bf16[512,1024]{1,0:T(8,128)(2,1)}, bf16[512,1024]{1,0:T(8,128)(2,1)}, u32[]{:S(2)}, u32[]{:S(2)}) collective-permute-start(bf16[512,1024]{1,0:T(8,128)(2,1)} %merge.17.refs_3_), channel_id=1, source_target_pairs={{0,1},{1,0},{2,3},{3,2},{4,5},{5,4},{6,7},{7,6},{8,9},{9,8},{10,11... | collective-permute-start | bytes 3145736 | tf_op jit(solution)/shard_map/ppermute | solution.py:889
  357.9 24.9 %collective-permute-start.39 = (bf16[512,1024]{1,0:T(8,128)(2,1)}, bf16[512,1024]{1,0:T(8,128)(2,1)}, u32[]{:S(2)}, u32[]{:S(2)}) collective-permute-start(bf16[512,1024]{1,0:T(8,128)(2,1)} %merge.18.refs_10_), channel_id=1, source_target_pairs={{0,2},{1,3},{2,0},{3,1},{4,6},{5,7},{6,4},{7,5},{8,10},{9,11},{10,... | collective-permute-start | bytes 3145736 | tf_op jit(solution)/shard_map/ppermute | solution.py:889
  359.3 50.7 %collective-permute-start.43 = (bf16[512,1024]{1,0:T(8,128)(2,1)}, bf16[512,1024]{1,0:T(8,128)(2,1)}, u32[]{:S(2)}, u32[]{:S(2)}) collective-permute-start(bf16[512,1024]{1,0:T(8,128)(2,1)} %pad_maximum_fusion.refs_11_.refs_1_), channel_id=1, source_target_pairs={{0,4},{4,0},{8,12},{12,8},{16,20},{20,16},{24,28},{28,24},{1,5},{5... | collective-permute-start | bytes 3145736 | tf_op jit(solution)/shard_map/ppermute | solution.py:892
  382.7 30.8 %collective-permute-start.44 = (bf16[512,1024]{1,0:T(8,128)(2,1)}, bf16[512,1024]{1,0:T(8,128)(2,1)S(1)}, u32[]{:S(2)}, u32[]{:S(2)}) collective-permute-start(bf16[512,1024]{1,0:T(8,128)(2,1)} %get-tuple-element.229.refs_2_), channel_id=1, source_target_pairs={{0,4},{4,0},{8,12},{12,8},{16,20},{20,16},{24,28},{28,24},{1,5},{5... | collective-permute-start | bytes 3145736 | tf_op jit(solution)/shard_map/ppermute | solution.py:892
  385.9 25.3 %collective-permute-start.40 = (bf16[128,1024]{1,0:T(8,128)(2,1)}, bf16[128,1024]{1,0:T(8,128)(2,1)S(1)}, u32[]{:S(2)}, u32[]{:S(2)}) collective-permute-start(bf16[128,1024]{1,0:T(8,128)(2,1)} %get-tuple-element.225.refs_16_), channel_id=1, source_target_pairs={{0,8},{4,12},{8,0},{12,4},{16,24},{20,28},{24,16},{28,20},{1,9},{5... | collective-permute-start | bytes 786440 | tf_op jit(solution)/shard_map/ppermute | solution.py:892
  386.2 26.4 %collective-permute-start.41 = (bf16[128,1024]{1,0:T(8,128)(2,1)}, bf16[128,1024]{1,0:T(8,128)(2,1)S(1)}, u32[]{:S(2)}, u32[]{:S(2)}) collective-permute-start(bf16[128,1024]{1,0:T(8,128)(2,1)} %get-tuple-element.226.refs_17_), channel_id=1, source_target_pairs={{0,16},{4,20},{8,24},{12,28},{16,0},{20,4},{24,8},{28,12},{1,17},{... | collective-permute-start | bytes 786440 | tf_op jit(solution)/shard_map/ppermute | solution.py:892
  386.8 26.7 %collective-permute-start.42 = (bf16[128,1024]{1,0:T(8,128)(2,1)}, bf16[128,1024]{1,0:T(8,128)(2,1)S(1)}, u32[]{:S(2)}, u32[]{:S(2)}) collective-permute-start(bf16[128,1024]{1,0:T(8,128)(2,1)} %get-tuple-element.227.refs_18_), channel_id=1, source_target_pairs={{0,24},{4,28},{8,16},{12,20},{16,8},{20,12},{24,0},{28,4},{1,25},{... | collective-permute-start | bytes 786440 | tf_op jit(solution)/shard_map/ppermute | solution.py:892
  410.0 19.3 %collective-permute-start.45 = (f32[4,1536]{1,0:T(4,128)S(1)}, f32[4,1536]{1,0:T(4,128)S(1)}, u32[]{:S(2)}, u32[]{:S(2)}) collective-permute-start(f32[4,1536]{1,0:T(4,128)S(1)} %bitcast.98), channel_id=1, source_target_pairs={{0,1},{1,0},{2,3},{3,2},{4,5},{5,4},{6,7},{7,6},{8,9},{9,8},{10,11... | collective-permute-start | bytes 73736 | tf_op jit(solution)/shard_map/ppermute | solution.py:889
  411.2 21.4 %collective-permute-start.46 = (f32[4,1536]{1,0:T(4,128)S(1)}, f32[4,1536]{1,0:T(4,128)S(1)}, u32[]{:S(2)}, u32[]{:S(2)}) collective-permute-start(f32[4,1536]{1,0:T(4,128)S(1)} %bitcast.97), channel_id=1, source_target_pairs={{0,2},{1,3},{2,0},{3,1},{4,6},{5,7},{6,4},{7,5},{8,10},{9,11},{10,... | collective-permute-start | bytes 73736 | tf_op jit(solution)/shard_map/ppermute | solution.py:889
  412.6 20.0 %collective-permute-start.47 = (f32[4,1536]{1,0:T(4,128)S(1)}, f32[4,1536]{1,0:T(4,128)S(1)}, u32[]{:S(2)}, u32[]{:S(2)}) collective-permute-start(f32[4,1536]{1,0:T(4,128)S(1)} %bitcast.96), channel_id=1, source_target_pairs={{0,3},{1,2},{2,1},{3,0},{4,7},{5,6},{6,5},{7,4},{8,11},{9,10},{10,... | collective-permute-start | bytes 73736 | tf_op jit(solution)/shard_map/ppermute | solution.py:889
  417.3 15.4 %collective-permute-start.48 = (bf16[128,1024]{1,0:T(8,128)(2,1)}, bf16[128,1024]{1,0:T(8,128)(2,1)S(1)}, u32[]{:S(2)}, u32[]{:S(2)}) collective-permute-start(bf16[128,1024]{1,0:T(8,128)(2,1)} %merge.19.refs_4_), channel_id=1, source_target_pairs={{0,24},{4,28},{8,16},{12,20},{16,8},{20,12},{24,0},{28,4},{1,25},{... | collective-permute-start | bytes 786440 | tf_op jit(solution)/shard_map/ppermute | solution.py:892
  417.6 23.6 %collective-permute-start.52 = (bf16[128,1024]{1,0:T(8,128)(2,1)}, bf16[128,1024]{1,0:T(8,128)(2,1)S(1)}, u32[]{:S(2)}, u32[]{:S(2)}) collective-permute-start(bf16[128,1024]{1,0:T(8,128)(2,1)} %merge.19.refs_4_), channel_id=1, source_target_pairs={{0,16},{4,20},{8,24},{12,28},{16,0},{20,4},{24,8},{28,12},{1,17},{... | collective-permute-start | bytes 786440 | tf_op jit(solution)/shard_map/ppermute | solution.py:892
  429.3 13.6 %collective-permute-start.53 = (bf16[128,1024]{1,0:T(8,128)(2,1)S(1)}, bf16[128,1024]{1,0:T(8,128)(2,1)S(1)}, u32[]{:S(2)}, u32[]{:S(2)}) collective-permute-start(bf16[128,1024]{1,0:T(8,128)(2,1)S(1)} %copy-done.43), channel_id=1, source_target_pairs={{0,8},{4,12},{8,0},{12,4},{16,24},{20,28},{24,16},{28,20},{1,9},{5... | collective-permute-start | bytes 786440 | tf_op jit(solution)/shard_map/ppermute | solution.py:892
  447.8 14.9 %collective-permute-start.54 = (bf16[512,1024]{1,0:T(8,128)(2,1)S(1)}, bf16[512,1024]{1,0:T(8,128)(2,1)S(1)}, u32[]{:S(2)}, u32[]{:S(2)}) collective-permute-start(bf16[512,1024]{1,0:T(8,128)(2,1)S(1)} %pad_maximum_fusion.1.refs_1_), channel_id=1, source_target_pairs={{0,4},{4,0},{8,12},{12,8},{16,20},{20,16},{24,28},{28,24},{1,5},{5... | collective-permute-start | bytes 3145736 | tf_op jit(solution)/shard_map/ppermute | solution.py:892
  450.2 12.5 %collective-permute-start.56 = (bf16[16,3840]{1,0:T(8,128)(2,1)}, bf16[16,3840]{1,0:T(8,128)(2,1)S(1)}, u32[]{:S(2)}, u32[]{:S(2)}) collective-permute-start(bf16[16,3840]{1,0:T(8,128)(2,1)} %mode_rows.1.refs_1_), channel_id=1, source_target_pairs={{0,8},{4,12},{8,0},{12,4},{16,24},{20,28},{24,16},{28,20},{1,9},{5... | collective-permute-start | bytes 368648 | tf_op jit(solution)/shard_map/ppermute | solution.py:892
  455.3 15.6 %collective-permute-start.57 = (bf16[16,3840]{1,0:T(8,128)(2,1)}, bf16[16,3840]{1,0:T(8,128)(2,1)S(1)}, u32[]{:S(2)}, u32[]{:S(2)}) collective-permute-start(bf16[16,3840]{1,0:T(8,128)(2,1)} %mode_rows.1.refs_1_), channel_id=1, source_target_pairs={{0,12},{4,8},{8,4},{12,0},{16,28},{20,24},{24,20},{28,16},{1,13},{... | collective-permute-start | bytes 368648 | tf_op jit(solution)/shard_map/ppermute | solution.py:892
  455.3 15.6 %collective-permute-start.58 = (bf16[16,3840]{1,0:T(8,128)(2,1)}, bf16[16,3840]{1,0:T(8,128)(2,1)S(1)}, u32[]{:S(2)}, u32[]{:S(2)}) collective-permute-start(bf16[16,3840]{1,0:T(8,128)(2,1)} %mode_rows.1.refs_1_), channel_id=1, source_target_pairs={{0,16},{4,20},{8,24},{12,28},{16,0},{20,4},{24,8},{28,12},{1,17},{... | collective-permute-start | bytes 368648 | tf_op jit(solution)/shard_map/ppermute | solution.py:892
  456.4 17.8 %collective-permute-start.59 = (bf16[16,3840]{1,0:T(8,128)(2,1)}, bf16[16,3840]{1,0:T(8,128)(2,1)S(1)}, u32[]{:S(2)}, u32[]{:S(2)}) collective-permute-start(bf16[16,3840]{1,0:T(8,128)(2,1)} %mode_rows.1.refs_1_), channel_id=1, source_target_pairs={{0,20},{4,16},{8,28},{12,24},{16,4},{20,0},{24,12},{28,8},{1,21},{... | collective-permute-start | bytes 368648 | tf_op jit(solution)/shard_map/ppermute | solution.py:892
  462.8 11.4 %collective-permute-start.60 = (bf16[16,3840]{1,0:T(8,128)(2,1)}, bf16[16,3840]{1,0:T(8,128)(2,1)S(1)}, u32[]{:S(2)}, u32[]{:S(2)}) collective-permute-start(bf16[16,3840]{1,0:T(8,128)(2,1)} %mode_rows.1.refs_1_), channel_id=1, source_target_pairs={{0,24},{4,28},{8,16},{12,20},{16,8},{20,12},{24,0},{28,4},{1,25},{... | collective-permute-start | bytes 368648 | tf_op jit(solution)/shard_map/ppermute | solution.py:892
  462.8 11.4 %collective-permute-start.61 = (bf16[16,3840]{1,0:T(8,128)(2,1)}, bf16[16,3840]{1,0:T(8,128)(2,1)S(1)}, u32[]{:S(2)}, u32[]{:S(2)}) collective-permute-start(bf16[16,3840]{1,0:T(8,128)(2,1)} %mode_rows.1.refs_1_), channel_id=1, source_target_pairs={{0,28},{4,24},{8,20},{12,16},{16,12},{20,8},{24,4},{28,0},{1,29},{... | collective-permute-start | bytes 368648 | tf_op jit(solution)/shard_map/ppermute | solution.py:892
  (93 other events, 547.8 us)

commit v4 on v3

--- a/solution.py
+++ b/solution.py
@@ -174,13 +174,13 @@
         own[QKV:] = out_ref[pl.ds(pl.multiple_of((core ^ h) * 128, 128), 128)]
 
 
-def feed_rows_kernel(core_ref, up_ref, down_ref, own0, own1):
+def feed_rows_kernel(core_ref, up_ref, down_ref, up0, down0, up1, down1):
     core = core_ref[0]
     hot, _ = hot_rows(2 * HALF, lambda row: row ^ (core * HALF))
     rows = mm(jnp.where(hot, 1.0, 0.0).astype(bf16), up_ref[...], NT).astype(bf16)
-    for h, own in enumerate((own0, own1)):
-        own[0] = rows[h * HALF : (h + 1) * HALF]
-        own[1] = down_ref[pl.ds(pl.multiple_of((core ^ h) * HALF, HALF), HALF)]
+    for h, (up, down) in enumerate(((up0, down0), (up1, down1))):
+        up[0] = rows[h * HALF : (h + 1) * HALF]
+        down[0] = down_ref[pl.ds(pl.multiple_of((core ^ h) * HALF, HALF), HALF)]
 
 
 def attn_rows(core, qkv, out, after):
@@ -190,9 +190,9 @@
 
 
 def feed_rows(core, up, down, after):
-    half = (shape((2, HALF, D), bf16), whole(2, HALF, D))
+    half = (shape((1, HALF, D), bf16), whole(1, HALF, D))
     ins = [(up, whole(D, 2 * HALF)), (down, whole(2 * HALF, D))]
-    return run(feed_rows_kernel, "feed_rows", 1, ins, [half, half], (), after, [core], 2e9, 8e6)
+    return run(feed_rows_kernel, "feed_rows", 1, ins, [half] * 4, (), after, [core], 2e9, 8e6)
 
 
 def attend_kernel(len_ref, x_ref, mode_ref, wa_ref, wb_ref, tbl_ref, e_ref, *rest):
@@ -235,7 +235,7 @@
             ex = jnp.exp(s - jnp.max(s, axis=0, keepdims=True))
             pr = (ex * (1.0 / jnp.sum(ex, axis=0, keepdims=True))).astype(bf16)
             probs_ref[2 * p + i] = pr
-            outs.append(mm(v_rows, pr)[i * HD : (i + 1) * HD])
+            outs.append(mm(v_rows[i * HD : (i + 1) * HD], pr))
         heads_ref[:, p * 128 : (p + 1) * 128] = jnp.concatenate(outs, axis=0).T.astype(bf16)
 
 
@@ -488,7 +488,7 @@
             t = pr * dp
             ds = (t - pr * jnp.sum(t, axis=0, keepdims=True)).astype(bf16)
             dv.append(mm(prl, do))
-            dq.append(mm(k_rows, ds)[i * HD : (i + 1) * HD])
+            dq.append(mm(k_rows[i * HD : (i + 1) * HD], ds))
             dk.append(mm(ds, qa))
         dq = jnp.concatenate(dq, axis=0).T
         block = jnp.concatenate(
@@ -635,7 +635,7 @@
 
 def merge_parts(terms, z, count, outputs):
     size = HALF // count
-    sums = 2 if any(type(term) is tuple for term in terms) else 1
+    sums = 2 if terms[0].ndim == 3 else 1
     ins, only = [], []
     for j in range(outputs):
         for term in terms:
@@ -782,20 +782,20 @@
         rows[pl.ds(pl.multiple_of((dp_ref[0] ^ k) * size, size), size)] = ref[...]
     modes, classes, rel, cond, index = [rows[:, i:j] for i, j in zip(marks, marks[1:])]
     ada_ref[...] = mm(cond, modes, TN)
-    bias_ref[...] = jnp.sum(modes.astype(f32), axis=0, keepdims=True)
+    bias_ref[...] = jnp.sum(modes.astype(f32), axis=0)
     lane = lax.broadcasted_iota(jnp.int32, index.shape, 1).astype(f32)
     hot = jnp.where(lane == index[:, :1].astype(f32), 1.0, 0.0).astype(bf16)
     class_ref[...] = mm(hot, classes, TN)[: class_ref.shape[0]]
     total = rel[:size].astype(f32)
     for i in range(1, len(parts)):
         total = total + rel[i * size : (i + 1) * size].astype(f32)
-    rel_ref[...] = total
-
-
-def mode_final(dp, parts, columns, class_count):
+    rel_ref[...] = total[: rel_ref.shape[0], : rel_ref.shape[1]]
+
+
+def mode_final(dp, parts, columns, class_count, rel_shape):
     size, width = parts[0].shape
     ins = [(v, whole(size, width)) for v in parts]
-    outs = [(shape(dims, f32), whole(*dims)) for dims in ((D, columns), (1, columns), (class_count, D), (size, 128))]
+    outs = [(shape(dims, f32), whole(*dims)) for dims in ((D, columns), (columns,), (class_count, D), rel_shape)]
     scratch = [pltpu.VMEM((len(parts) * size, width), bf16)]
     return run(mode_final_kernel, "mode_final", 1, ins, outs, scratch, (), [dp], vmem=32)
 
@@ -922,22 +922,27 @@
     (attn_own[0],) = hold(attn_own[:1], [messages])
     ax, ay = px(attn_own[0]), py(attn_own[0])
     normed_one, packed[0], heads[0], probs[0] = attend(own_lengths, tokens, modes, attn_own, tables[0], query_hot)
-    feed_own = list(feed_rows(core_row, up_weight, down_weight, [heads[0]]))
-    ax, ay = hold([ax, ay], [feed_own[1]])
+    up0, down0, up1, down1 = feed_rows(core_row, up_weight, down_weight, [heads[0]])
+    ax, ay = hold([ax, ay], [down1])
     adx, ady = py(ax[: HALF // 2]), px(ay[HALF // 2 :])
     attn_w = [attn_own] + [[Moved(v), Moved(pc(v))] for v in (ax, ay)]
     packed[1], heads[1], probs[1] = attend(
-        own_lengths, normed_one, modes, attn_w[1], tables[1], query_hot, [feed_own[1]]
+        own_lengths, normed_one, modes, attn_w[1], tables[1], query_hot, [down1]
     )
     adx, ady = hold([adx, ady], [heads[1]])
-    (feed_own[0],) = hold(feed_own[:1], [adx, ady])
-    fx, fy = px(feed_own[0]), py(feed_own[0])
     ad = cat(adx, ady)
+    up0, down0 = hold([up0, down0], [ad])
+    x_up, y_down = px(up0), py(down0)
     attn_w.append([ad, Moved(pc(ad))])
-    for r in (2, 3):
-        packed[r], heads[r], probs[r] = attend(
-            own_lengths, normed_one, modes, attn_w[r], tables[r], query_hot, [heads[r - 1]]
-        )
+    packed[2], heads[2], probs[2] = attend(
+        own_lengths, normed_one, modes, attn_w[2], tables[2], query_hot, [heads[1]]
+    )
+    packed[3], heads[3], probs[3] = attend(
+        own_lengths, normed_one, modes, attn_w[3], tables[3], query_hot, [heads[2]]
+    )
+    x_up, y_down = hold([x_up, y_down], [heads[3]])
+    d_up, d_down = py(x_up), px(y_down)
+    attn_w = [[v.array if isinstance(v, Moved) else v for v in halves] for halves in attn_w]
     attn_out, middle, normed_two, down_in = middle_step(heads, attn_w, tokens, cotangent, modes)
 
     hid, pre, mine, other = [None] * 4, [None] * 4, [None] * 4, [None] * 4
@@ -949,32 +954,37 @@
     def pair(r, which):
         return [(mine[r], which, 0), (Moved(other[r]), which, 0)]
 
-    feed_w = [[((v, 0), (v, 1)) for v in feed_own]]
+    def weight_of(up, down):
+        return [((Moved(u), 0), (Moved(v), 0)) for u, v in ((up, down), (pc(up), pc(down)))]
+
+    feed_w = [[((up0, 0), (down0, 0)), ((up1, 0), (down1, 0))], None, None, None]
     feed_step(0, feed_w[0], [])
-    fx, fy = hold([fx, fy], [hid[0]])
-    fu, fd = fx[:1], fy[1:]
-    feed_w += [[((Moved(v), 0), (Moved(v), 1)) for v in (u, pc(u))] for u in (fx, fy)]
-    feed_step(1, feed_w[1], [hid[0], fu, fd])
-    fu, fd = py(fu), px(fd)
+    d_up, d_down = hold([d_up, d_down], [hid[0]])
+    feed_w[3] = weight_of(d_up, d_down)
+    feed_step(3, feed_w[3], [hid[0]])
+    x_down, y_up = arrive([px(down0), py(up0)], [hid[3]])
+    feed_w[1], feed_w[2] = weight_of(x_up, x_down), weight_of(y_up, y_down)
+    diag_x, diag_y = merge(pair(3, 0), pair(3, 1), after=[hid[3]])
+    feed_step(1, feed_w[1], [hid[3], diag_x])
     feed_step(2, feed_w[2], [hid[1]])
-    fu, fd = arrive([fu, fd], [hid[2]])
-    feed_w += [[((Moved(u), 0), (Moved(v), 0)) for u, v in ((fu, fd), (pc(fu), pc(fd)))]]
-    (send_x,) = merge(pair(1, 0), after=[fu])
-    (send_y,) = merge(pair(2, 1), after=[send_x])
-    feed_step(3, feed_w[3], [hid[2], send_y])
-    send_x, send_y = arrive([px(send_x), py(send_y)], [hid[3]])
-    diag_x, diag_y = merge(pair(3, 0), pair(3, 1), after=[send_x])
+    diag_x, diag_y = arrive([px(diag_x), py(diag_y)], [hid[2]])
+    both = 2 * HALF
+    flat = [v.reshape(both, D) for v in mine]
+    flat_other = [v.reshape(both, D) for v in other]
+    (last_x,) = merge(
+        [(flat[1], None, 0), (Moved(flat_other[1]), None, 0), (Moved(diag_y), None, -HALF, HALF, both)], rows=both
+    )
+    (last_y,) = merge(
+        [(flat[2], None, 0), (Moved(flat_other[2]), None, 0), (Moved(diag_x), None, 0, 0, HALF)], rows=both, after=[last_x]
+    )
     middle_grad, out_in, turn_sums = turn_step(
-        pre, feed_w, middle, attn_out, cotangent, modes, [diag_x, diag_y]
-    )
-    diag_x, diag_y = arrive([px(diag_x), py(diag_y)], [middle_grad])
-    last_x, last_y = merge(pair(1, 1) + [(Moved(diag_y), None, 0)], pair(2, 0) + [(Moved(diag_x), None, 0)])
+        pre, feed_w, middle, attn_out, cotangent, modes, [last_x, last_y]
+    )
     still = [[[(v.array if isinstance(v, Moved) else v, at) for v, at in half] for half in halves] for halves in feed_w]
-    output, out_sums = out_step(hid, still, middle, cotangent, modes, [last_x, last_y])
+    output, out_sums = out_step(hid, still, middle, cotangent, modes, [turn_sums])
     last_x, last_y = arrive([px(last_x), py(last_y)], [out_sums])
     z_row = z.reshape(1)
-    terms = [mine[0], Moved(other[0])]
-    terms += [(Moved(send_x), 0), (Moved(last_y), 0), (Moved(last_x), 1), (Moved(send_y), 1)]
+    terms = [mine[0], Moved(other[0]), *[Moved(v.reshape(2, HALF, D)) for v in (last_x, last_y)]]
     feed_keep, feed_sent = merge_parts(terms, z_row, n_z, 2)
     z_one, z_two = swap_dp(2), swap_dp(4)
 
@@ -984,7 +994,6 @@
     cond_rel = jnp.take(cond_low, order, axis=1).transpose(1, 0, 2).reshape(4 * micro, D)
     slope, cond_rel = hold([share * (1.0 + own_pre * (1.0 - share)), cat(cond_rel, class_col, 1)])
 
-    attn_w = [[v.array if isinstance(v, Moved) else v for v in halves] for halves in attn_w]
     packed_grad, rel_grid, a_mine, a_other = [None] * 4, [None] * 4, [None] * 4, [None] * 4
 
     def back_step(r, after):
@@ -1043,10 +1052,8 @@
     grad_qkv, grad_out = attn_final(place, attn_own, Moved(attn_other))
     got = arrive(got, [grad_qkv])
     grad_ada, grad_ada_bias, class_grad, grad_rel = mode_final(
-        (2 * z + core).reshape(1), [grads, *got], columns, class_table.shape[0]
-    )
-    grad_ada_bias = grad_ada_bias.reshape(-1)
-    grad_rel = grad_rel[:4, : rel_bias.shape[1]]
+        (2 * z + core).reshape(1), [grads, *got], columns, class_table.shape[0], rel_bias.shape
+    )
 
     return (
         output,

time: 492 us -> 480 us (0.976)
  waiting for transfers between devices: 42.3 us -> 32.4 us
  starting transfers between devices: 59 us -> 68.7 us
    ppermute x35 -> x37, starting transfers between devices: 28.3 us -> 38.3 us  [swap_dp(): lax.ppermute(v, ('z', 'core'), [(i, i ^ bit) for i in range(n_dp)])]
    ppermute x35 -> x37, waiting for transfers between devices: 20.1 us -> 14.3 us  [swap_dp(): lax.ppermute(v, ('z', 'core'), [(i, i ^ bit) for i in range(n_dp)])]
    pallas_call x35 -> x34, Pallas kernels: 329 us -> 325 us  [run(): pl.pallas_call(body, grid_spec=pltpu.PrefetchScalarGridSpec(num_scalar_pr...]
    unnamed x165 -> x149, local copies, waits for them, and re-layouts: 20.3 us -> 20.2 us
  transfers between devices with their start and end apart: 62 -> 64, of which waited for: 17 -> 15; matrix products, arithmetic and copies ran while one was open for 4% -> 4% of each run, Pallas kernels for 64% -> 66%
where the time goes in v4:
time: 480 us; the launch traced here: 475 us
  Pallas kernels  325 us (68%)
  starting transfers between devices  68.7 us (14%)
  waiting for transfers between devices  32.4 us (7%)
  local copies, waits for them, and re-layouts  30.1 us (6%)
  other arithmetic  8.58 us (2%)
  matrix products  7.06 us (1%)
    pallas_call x34, Pallas kernels, run(): pl.pallas_call(body, grid_spec=pltpu.PrefetchScalarGridSpec(num_scalar_pr...  325 us
    ppermute x37, starting transfers between devices, swap_dp(): lax.ppermute(v, ('z', 'core'), [(i, i ^ bit) for i in range(n_dp)])  38.3 us
    ppermute x27, starting transfers between devices, swap_mp(): return lambda v: lax.ppermute(v, 'mp', [(i, i ^ bit) for i in range(n_mp)])  30.5 us
    unnamed x149, local copies, waits for them, and re-layouts  20.2 us
    ppermute x27, waiting for transfers between devices, swap_mp(): return lambda v: lax.ppermute(v, 'mp', [(i, i ^ bit) for i in range(n_mp)])  18 us
    ppermute x37, waiting for transfers between devices, swap_dp(): lax.ppermute(v, ('z', 'core'), [(i, i ^ bit) for i in range(n_dp)])  14.3 us
  transfers between devices with their start and end apart: 64, of which 15 were waited for; matrix products, arithmetic and copies ran while one was open for 4% of the time, Pallas kernels for 66%

profile of v4, /device:TPU:0, one launch (start us, length us, event | category | flops | bytes accessed | tf_op | source)
XLA Modules:
  0.0 474.6 jit_solution(8706077808517665252)
XLA Ops:
  4.0 2.5 fusion.2.refs_3_
  6.7 3.0 collective-permute-start
  11.3 4.2 attn_rows.1
  24.5 14.6 %attend.4 = (bf16[1280,1024]{1,0:T(8,128)(2,1)S(1)}, bf16[1280,768]{1,0:T(8,128)(2,1)}, bf16[1280,256]{1,0:T(8,128)(2,1)}, bf16[16,320,320]{2,1,0:T(8,128)(2,1)}) custom-call(s32[4]{0:T(128)S(1)} %fusion.19.refs_0_, bf16[4,320,1024]{2,1,0:T(8,128)(2,1)} %refs_12_.3, f32[4,6,1024]{2,1,0:T(8,128)} %reshape.127.refs_2_.refs_14_.refs_15_.refs_13_, ...), custom_call_target="tpu_custom_call" | custom-call | flops 1000 | bytes 1000 | tf_op jit(solution)/shard_map/attend/pallas_call | solution.py:104
  39.1 7.3 %feed_rows.1 = (bf16[1,512,1024]{2,1,0:T(8,128)(2,1)}, bf16[1,512,1024]{2,1,0:T(8,128)(2,1)}, bf16[1,512,1024]{2,1,0:T(8,128)(2,1)}, bf16[1,512,1024]{2,1,0:T(8,128)(2,1)}) custom-call(s32[1]{0:T(128)} %bitcast.8.refs_0_, bf16[1024,1024]{1,0:T(8,128)(2,1)} %refs_1_.5, bf16[1024,1024]{1,0:T(8,128)(2,1)} %refs_2_.3, ...), custom_call_target="tpu_custom_call" | custom-call | flops 1000 | bytes 1000 | tf_op jit(solution)/shard_map/feed_rows/pallas_call | solution.py:104
  51.1 12.2 %attend.5 = (bf16[1280,768]{1,0:T(8,128)(2,1)}, bf16[1280,256]{1,0:T(8,128)(2,1)}, bf16[16,320,320]{2,1,0:T(8,128)(2,1)}) custom-call(s32[4]{0:T(128)S(1)} %fusion.19.refs_0_, bf16[1280,1024]{1,0:T(8,128)(2,1)} %copy-done.3, f32[4,6,1024]{2,1,0:T(8,128)} %reshape.127.refs_2_.refs_14_.refs_15_.refs_13_, bf16[512,1024]{1,0:T(8,128)(2,1)S(1)} %copy-done.11, ...), custom_call_target="tpu_custom_call" | custom-call | flops 1000 | bytes 1000 | tf_op jit(solution)/shard_map/attend/pallas_call | solution.py:104
  71.9 12.2 %attend.6 = (bf16[1280,768]{1,0:T(8,128)(2,1)}, bf16[1280,256]{1,0:T(8,128)(2,1)}, bf16[16,320,320]{2,1,0:T(8,128)(2,1)}) custom-call(s32[4]{0:T(128)S(1)} %fusion.19.refs_0_, bf16[1280,1024]{1,0:T(8,128)(2,1)} %copy-done.3, f32[4,6,1024]{2,1,0:T(8,128)} %reshape.127.refs_2_.refs_14_.refs_15_.refs_13_, bf16[512,1024]{1,0:T(8,128)(2,1)S(1)} %copy-done.9, ...), custom_call_target="tpu_custom_call" | custom-call | flops 1000 | bytes 1000 | tf_op jit(solution)/shard_map/attend/pallas_call | solution.py:104
  84.1 13.2 %attend.7 = (bf16[1280,768]{1,0:T(8,128)(2,1)}, bf16[1280,256]{1,0:T(8,128)(2,1)}, bf16[16,320,320]{2,1,0:T(8,128)(2,1)}) custom-call(s32[4]{0:T(128)S(1)} %fusion.19.refs_0_, bf16[1280,1024]{1,0:T(8,128)(2,1)} %copy-done.3, f32[4,6,1024]{2,1,0:T(8,128)} %reshape.127.refs_2_.refs_14_.refs_15_.refs_13_, ...), custom_call_target="tpu_custom_call" | custom-call | flops 1000 | bytes 1000 | tf_op jit(solution)/shard_map/attend/pallas_call | solution.py:104
  98.9 10.7 %middle.1 = (bf16[1280,1024]{1,0:T(8,128)(2,1)}, f32[1280,1024]{1,0:T(8,128)}, bf16[1280,1024]{1,0:T(8,128)(2,1)S(1)}, bf16[1280,1024]{1,0:T(8,128)(2,1)S(1)}) custom-call(bf16[1280,256]{1,0:T(8,128)(2,1)} %get-tuple-element.146.refs_3_.refs_0_.refs_8_, bf16[1280,256]{1,0:T(8,128)(2,1)} %get-tuple-element.150.refs_7_.refs_2_.refs_1_.refs_8_, ...), custom_call_target="tpu_custom_call" | custom-call | flops 1000 | bytes 1000 | tf_op jit(solution)/shard_map/middle/pallas_call | solution.py:104
  109.6 16.1 %feed.4 = (bf16[1280,1024]{1,0:T(8,128)(2,1)}, bf16[1280,1024]{1,0:T(8,128)(2,1)}, bf16[2,512,1024]{2,1,0:T(8,128)(2,1)}, bf16[2,512,1024]{2,1,0:T(8,128)(2,1)}) custom-call(bf16[1280,1024]{1,0:T(8,128)(2,1)S(1)} %get-tuple-element.156.refs_0_, bf16[1280,1024]{1,0:T(8,128)(2,1)S(1)} %get-tuple-element.157.refs_1_, ...), custom_call_target="tpu_custom_call" | custom-call | flops 1000 | bytes 1000 | tf_op jit(solution)/shard_map/feed/pallas_call | solution.py:104
  132.0 14.2 %feed.5 = (bf16[1280,1024]{1,0:T(8,128)(2,1)}, bf16[1280,1024]{1,0:T(8,128)(2,1)}, bf16[2,512,1024]{2,1,0:T(8,128)(2,1)}, bf16[2,512,1024]{2,1,0:T(8,128)(2,1)}) custom-call(bf16[1280,1024]{1,0:T(8,128)(2,1)S(1)} %get-tuple-element.156.refs_0_, bf16[1280,1024]{1,0:T(8,128)(2,1)S(1)} %copy-done.6, bf16[1,512,1024]{2,1,0:T(8,128)(2,1)} %get-tuple-element.166.refs_2_.refs_10_, ...), custom_call_target="tpu_custom_call" | custom-call | flops 1000 | bytes 1000 | tf_op jit(solution)/shard_map/feed/pallas_call | solution.py:104
  146.4 5.4 %collective-permute-done.13.refs_1_ = bf16[1,512,1024]{2,1,0:T(8,128)(2,1)} collective-permute-done((bf16[1,512,1024]{2,1,0:T(8,128)(2,1)}, bf16[1,512,1024]{2,1,0:T(8,128)(2,1)}, u32[]{:S(2)}, u32[]{:S(2)}) %collective-permute-start.13) | collective-permute-done | bytes 1048608 | tf_op jit(solution)/shard_map/ppermute | solution.py:889
  153.1 3.5 merge.9
  159.1 15.3 %feed.6 = (bf16[1280,1024]{1,0:T(8,128)(2,1)}, bf16[1280,1024]{1,0:T(8,128)(2,1)}, bf16[2,512,1024]{2,1,0:T(8,128)(2,1)}, bf16[2,512,1024]{2,1,0:T(8,128)(2,1)}) custom-call(bf16[1280,1024]{1,0:T(8,128)(2,1)S(1)} %get-tuple-element.156.refs_0_, bf16[1280,1024]{1,0:T(8,128)(2,1)S(1)} %copy-done.7, bf16[1,512,1024]{2,1,0:T(8,128)(2,1)} %get-tuple-element.164.refs_2_.refs_6_, ...), custom_call_target="tpu_custom_call" | custom-call | flops 1000 | bytes 1000 | tf_op jit(solution)/shard_map/feed/pallas_call | solution.py:104
  174.5 14.0 %feed.7 = (bf16[1280,1024]{1,0:T(8,128)(2,1)}, bf16[1280,1024]{1,0:T(8,128)(2,1)}, bf16[2,512,1024]{2,1,0:T(8,128)(2,1)}, bf16[2,512,1024]{2,1,0:T(8,128)(2,1)}) custom-call(bf16[1280,1024]{1,0:T(8,128)(2,1)S(1)} %get-tuple-element.156.refs_0_, bf16[1280,1024]{1,0:T(8,128)(2,1)S(1)} %copy-done.7, bf16[1,512,1024]{2,1,0:T(8,128)(2,1)} %get-tuple-element.174.refs_2_.refs_8_, ...), custom_call_target="tpu_custom_call" | custom-call | flops 1000 | bytes 1000 | tf_op jit(solution)/shard_map/feed/pallas_call | solution.py:104
  189.1 4.9 %merge.10.refs_3_.refs_16_ = bf16[1024,1024]{1,0:T(8,128)(2,1)} custom-call(bf16[1024,1024]{1,0:T(8,128)(2,1)} %bitcast.90, bf16[1024,1024]{1,0:T(8,128)(2,1)} %bitcast.19.refs_1_, bf16[512,1024]{1,0:T(8,128)(2,1)} %get-tuple-element.185.refs_2_), custom_call_target="tpu_custom_call" | custom-call | flops 1000 | bytes 1000 | tf_op jit(solution)/shard_map/merge/pallas_call | solution.py:104
  194.5 4.8 %merge.11.refs_17_ = bf16[1024,1024]{1,0:T(8,128)(2,1)} custom-call(bf16[1024,1024]{1,0:T(8,128)(2,1)} %bitcast.91, bf16[1024,1024]{1,0:T(8,128)(2,1)} %bitcast.21.refs_1_, bf16[512,1024]{1,0:T(8,128)(2,1)} %get-tuple-element.188.refs_2_, bf16[1024,1024]{1,0:T(8,128)(2,1)} %merge.10.refs_3_.refs_16_), custom_call_target="tpu_custom_call" | custom-call | flops 1000 | bytes 1000 | tf_op jit(solution)/shard_map/merge/pallas_call | solution.py:104
  201.6 22.6 %turn.1 = (f32[1280,1024]{1,0:T(8,128)}, bf16[1280,1024]{1,0:T(8,128)(2,1)S(1)}, f32[4,3,1024]{2,1,0:T(4,128)}) custom-call(bf16[1280,1024]{1,0:T(8,128)(2,1)} %get-tuple-element.177.refs_0_, bf16[1280,1024]{1,0:T(8,128)(2,1)} %get-tuple-element.178.refs_1_, bf16[1280,1024]{1,0:T(8,128)(2,1)} %get-tuple-element.179.refs_2_, ...), custom_call_target="tpu_custom_call" | custom-call | flops 1000 | bytes 1000 | tf_op jit(solution)/shard_map/turn/pallas_call | solution.py:104
  224.2 19.0 %output.1 = (bf16[4,320,1024]{2,1,0:T(8,128)(2,1)}, f32[4,1,1024]{2,1,0:T(1,128)}) custom-call(bf16[1280,1024]{1,0:T(8,128)(2,1)} %get-tuple-element.163.refs_2_.refs_6_.refs_0_, bf16[1280,1024]{1,0:T(8,128)(2,1)} %get-tuple-element.173.refs_6_.refs_1_, bf16[1280,1024]{1,0:T(8,128)(2,1)} %get-tuple-element.175.refs_2_, ...), custom_call_target="tpu_custom_call" | custom-call | flops 1000 | bytes 1000 | tf_op jit(solution)/shard_map/output/pallas_call | solution.py:104
  243.2 3.6 collective-permute-done.29.refs_1_
  248.5 5.0 %merge_parts.2 = (bf16[512,1024]{1,0:T(8,128)(2,1)}, bf16[512,1024]{1,0:T(8,128)(2,1)}) custom-call(s32[1]{0:T(128)} %bitcast.22.refs_0_, bf16[2,512,1024]{2,1,0:T(8,128)(2,1)} %get-tuple-element.198.refs_1_.refs_5_, bf16[2,512,1024]{2,1,0:T(8,128)(2,1)} %collective-permute-done.27.refs_2_.refs_6_, bf16[2,512,1024]{2,1,0:T(8,128)(2,1)S(1)} %bitcast.88, ...), custom_call_target="tpu_custom_call" | custom-call | flops 1000 | bytes 1000 | tf_op jit(solution)/shard_map/merge_parts/pallas_call | solution.py:104
  255.0 17.9 %attend_back.4 = (bf16[1280,768]{1,0:T(8,128)(2,1)}, bf16[512,1024]{1,0:T(8,128)(2,1)}, bf16[512,1024]{1,0:T(8,128)(2,1)}, f32[2,32,128]{2,1,0:T(8,128)}) custom-call(bf16[1280,1024]{1,0:T(8,128)(2,1)} %copy-done.2, bf16[512,1024]{1,0:T(8,128)(2,1)} %constant_dynamic-update-slice_fusion.refs_3_.refs_10_.refs_2_.refs_1_, bf16[512,1024]{1,0:T(8,128)(2,1)} %copy-done.13, ...), custom_call_target="tpu_custom_call" | custom-call | flops 1000 | bytes 1000 | tf_op jit(solution)/shard_map/attend_back/pallas_call | solution.py:104
  273.0 4.7 collective-permute-done.31.refs_0_
  279.8 2.6 collective-permute-start.32
  283.2 17.8 %attend_back.5 = (bf16[1280,768]{1,0:T(8,128)(2,1)}, bf16[512,1024]{1,0:T(8,128)(2,1)}, bf16[512,1024]{1,0:T(8,128)(2,1)}, f32[2,32,128]{2,1,0:T(8,128)}) custom-call(bf16[1280,1024]{1,0:T(8,128)(2,1)} %copy-done.2, bf16[512,1024]{1,0:T(8,128)(2,1)} %get-tuple-element.149.refs_3_.refs_6_.refs_1_, bf16[512,1024]{1,0:T(8,128)(2,1)} %copy-done.14, ...), custom_call_target="tpu_custom_call" | custom-call | flops 1000 | bytes 1000 | tf_op jit(solution)/shard_map/attend_back/pallas_call | solution.py:104
  301.0 2.9 collective-permute-done.32.refs_0_
  308.8 2.7 merge.14
  316.5 18.0 %attend_back.6 = (bf16[1280,768]{1,0:T(8,128)(2,1)}, bf16[512,1024]{1,0:T(8,128)(2,1)}, bf16[512,1024]{1,0:T(8,128)(2,1)}, f32[2,32,128]{2,1,0:T(8,128)}) custom-call(bf16[1280,1024]{1,0:T(8,128)(2,1)} %copy-done.2, bf16[512,1024]{1,0:T(8,128)(2,1)} %get-tuple-element.151.refs_3_.refs_8_.refs_1_, bf16[512,1024]{1,0:T(8,128)(2,1)} %copy-done.12, ...), custom_call_target="tpu_custom_call" | custom-call | flops 1000 | bytes 1000 | tf_op jit(solution)/shard_map/attend_back/pallas_call | solution.py:104
  335.9 2.2 pad_maximum_fusion.refs_11_.refs_1_
  338.1 4.0 collective-permute-start.39
  342.2 2.7 merge.15.refs_3_
  345.4 2.6 merge.16.refs_10_
  349.0 17.8 %attend_back.7 = (bf16[1280,768]{1,0:T(8,128)(2,1)}, bf16[512,1024]{1,0:T(8,128)(2,1)}, bf16[512,1024]{1,0:T(8,128)(2,1)}, f32[2,32,128]{2,1,0:T(8,128)}) custom-call(bf16[1280,1024]{1,0:T(8,128)(2,1)} %copy-done.2, bf16[512,1024]{1,0:T(8,128)(2,1)} %hold.20.refs_3_.refs_4_.refs_1_, bf16[512,1024]{1,0:T(8,128)(2,1)} %get-tuple-element.145.refs_4_.refs_5_.refs_2_, ...), custom_call_target="tpu_custom_call" | custom-call | flops 1000 | bytes 1000 | tf_op jit(solution)/shard_map/attend_back/pallas_call | solution.py:104
  367.4 2.7 collective-permute-done.40.refs_1_
  370.0 2.8 collective-permute-done.41.refs_2_
  372.9 3.0 merge_parts.3
  376.9 3.5 collective-permute-start.44
  380.3 18.1 %last.1 = (bf16[4,320,1024]{2,1,0:T(8,128)(2,1)}, f32[4,2,1024]{2,1,0:T(2,128)}) custom-call(bf16[1280,768]{1,0:T(8,128)(2,1)} %get-tuple-element.223.refs_3_.refs_0_, bf16[1280,768]{1,0:T(8,128)(2,1)} %get-tuple-element.210.refs_1_, bf16[1280,768]{1,0:T(8,128)(2,1)} %get-tuple-element.215.refs_3_.refs_9_.refs_2_, ...), custom_call_target="tpu_custom_call" | custom-call | flops 1000 | bytes 1000 | tf_op jit(solution)/shard_map/last/pallas_call | solution.py:104
  410.9 7.8 %feed_final.1 = (f32[1024,1024]{1,0:T(8,128)}, f32[1024,1024]{1,0:T(8,128)}) custom-call(s32[2]{0:T(128)S(1)} %pad_add_fusion.refs_0_, bf16[512,1024]{1,0:T(8,128)(2,1)} %pad_maximum_fusion.refs_11_.refs_1_, bf16[512,1024]{1,0:T(8,128)(2,1)} %get-tuple-element.234.refs_2_, bf16[512,1024]{1,0:T(8,128)(2,1)} %get-tuple-element.239.refs_3_, ...), custom_call_target="tpu_custom_call" | custom-call | flops 1000 | bytes 1000 | tf_op jit(solution)/shard_map/feed_final/pallas_call | solution.py:104
  419.3 2.5 collective-permute-start.54
  422.6 3.6 mode_shares.1
  429.7 3.4 collective-permute-done.54.refs_3_
  440.4 2.4 collective-permute-start.62
  442.8 2.6 collective-permute-start.60
  446.6 9.6 %collective-permute-start.59 = (bf16[16,3840]{1,0:T(8,128)(2,1)}, bf16[16,3840]{1,0:T(8,128)(2,1)S(1)}, u32[]{:S(2)}, u32[]{:S(2)}) collective-permute-start(bf16[16,3840]{1,0:T(8,128)(2,1)} %mode_rows.1.refs_1_), channel_id=1, source_target_pairs={{0,12},{4,8},{8,4},{12,0},{16,28},{20,24},{24,20},{28,16},{1,13},{... | collective-permute-start | bytes 368648 | tf_op jit(solution)/shard_map/ppermute | solution.py:892
  456.2 3.2 collective-permute-start.58
  461.6 5.9 %attn_final.1 = (f32[1024,768]{1,0:T(8,128)}, f32[256,1024]{1,0:T(8,128)}) custom-call(s32[2]{0:T(128)S(1)} %pad_add_fusion.refs_0_, bf16[512,1024]{1,0:T(8,128)(2,1)} %copy-done.32, bf16[512,1024]{1,0:T(8,128)(2,1)S(1)} %copy-done.25), custom_call_target="tpu_custom_call" | custom-call | flops 1000 | bytes 1000 | tf_op jit(solution)/shard_map/attn_final/pallas_call | solution.py:104
  468.9 5.2 %mode_final.1 = (f32[1024,1536]{1,0:T(8,128)}, f32[1536]{0:T(1024)}, f32[101,1024]{1,0:T(8,128)}, f32[4,39]{1,0:T(4,128)}) custom-call(s32[1]{0:T(128)} %bitcast.38.refs_0_, bf16[16,3840]{1,0:T(8,128)(2,1)} %mode_rows.1.refs_1_, bf16[16,3840]{1,0:T(8,128)(2,1)} %get-tuple-element.267.refs_2_, bf16[16,3840]{1,0:T(8,128)(2,1)} %get-tuple-element.268.refs_3_, ...), custom_call_target="tpu_custom_call" | custom-call | flops 1000 | bytes 1000 | tf_op jit(solution)/shard_map/mode_final/pallas_call | solution.py:104
  (341 shorter events, 91.8 us)
Async XLA Ops:
  16.7 29.8 %collective-permute-start.4 = (bf16[512,1024]{1,0:T(8,128)(2,1)}, bf16[512,1024]{1,0:T(8,128)(2,1)S(1)}, u32[]{:S(2)}, u32[]{:S(2)}) collective-permute-start(bf16[512,1024]{1,0:T(8,128)(2,1)} %hold.20.refs_3_.refs_4_.refs_1_), channel_id=1, source_target_pairs={{0,2},{1,3},{2,0},{3,1},{4,6},{5,7},{6,4},{7,5},{8,10},{9,11},{10,... | collective-permute-start | bytes 3145736 | tf_op jit(solution)/shard_map/ppermute | solution.py:889
  18.4 28.0 %collective-permute-start.3 = (bf16[512,1024]{1,0:T(8,128)(2,1)}, bf16[512,1024]{1,0:T(8,128)(2,1)S(1)}, u32[]{:S(2)}, u32[]{:S(2)}) collective-permute-start(bf16[512,1024]{1,0:T(8,128)(2,1)} %hold.20.refs_3_.refs_4_.refs_1_), channel_id=1, source_target_pairs={{0,1},{1,0},{2,3},{3,2},{4,5},{5,4},{6,7},{7,6},{8,9},{9,8},{10,11... | collective-permute-start | bytes 3145736 | tf_op jit(solution)/shard_map/ppermute | solution.py:889
  50.2 14.2 %collective-permute-start.8 = (bf16[256,1024]{1,0:T(8,128)(2,1)S(1)}, bf16[256,1024]{1,0:T(8,128)(2,1)S(1)}, u32[]{:S(2)}, u32[]{:S(2)}) collective-permute-start(bf16[256,1024]{1,0:T(8,128)(2,1)S(1)} %slice.44), channel_id=1, source_target_pairs={{0,1},{1,0},{2,3},{3,2},{4,5},{5,4},{6,7},{7,6},{8,9},{9,8},{10,11... | collective-permute-start | bytes 1572872 | tf_op jit(solution)/shard_map/ppermute | solution.py:889
  50.8 13.9 %collective-permute-start.7 = (bf16[256,1024]{1,0:T(8,128)(2,1)S(1)}, bf16[256,1024]{1,0:T(8,128)(2,1)S(1)}, u32[]{:S(2)}, u32[]{:S(2)}) collective-permute-start(bf16[256,1024]{1,0:T(8,128)(2,1)S(1)} %slice.43), channel_id=1, source_target_pairs={{0,2},{1,3},{2,0},{3,1},{4,6},{5,7},{6,4},{7,5},{8,10},{9,11},{10,... | collective-permute-start | bytes 1572872 | tf_op jit(solution)/shard_map/ppermute | solution.py:889
  51.1 20.8 %collective-permute-start.6 = (bf16[512,1024]{1,0:T(8,128)(2,1)S(1)}, bf16[512,1024]{1,0:T(8,128)(2,1)S(1)}, u32[]{:S(2)}, u32[]{:S(2)}) collective-permute-start(bf16[512,1024]{1,0:T(8,128)(2,1)S(1)} %copy-done.9), channel_id=1, source_target_pairs={{0,4},{4,0},{8,12},{12,8},{16,20},{20,16},{24,28},{28,24},{1,5},{5... | collective-permute-start | bytes 3145736 | tf_op jit(solution)/shard_map/ppermute | solution.py:892
  69.3 14.8 %collective-permute-start.9 = (bf16[512,1024]{1,0:T(8,128)(2,1)}, bf16[512,1024]{1,0:T(8,128)(2,1)S(1)}, u32[]{:S(2)}, u32[]{:S(2)}) collective-permute-start(bf16[512,1024]{1,0:T(8,128)(2,1)} %constant_dynamic-update-slice_fusion.refs_3_.refs_10_.refs_2_.refs_1_), channel_id=1, source_target_pairs={{0,4},{4,0},{8,12},{12,8},{16,20},{20,16},{24,28},{28,24},{1,5},{5... | collective-permute-start | bytes 3145736 | tf_op jit(solution)/shard_map/ppermute | solution.py:892
  69.3 28.0 %collective-permute-start.10 = (bf16[1,512,1024]{2,1,0:T(8,128)(2,1)}, bf16[1,512,1024]{2,1,0:T(8,128)(2,1)}, u32[]{:S(2)}, u32[]{:S(2)}) collective-permute-start(bf16[1,512,1024]{2,1,0:T(8,128)(2,1)} %get-tuple-element.160.refs_2_.refs_4_), channel_id=1, source_target_pairs={{0,1},{1,0},{2,3},{3,2},{4,5},{5,4},{6,7},{7,6},{8,9},{9,8},{10,11... | collective-permute-start | bytes 3145736 | tf_op jit(solution)/shard_map/ppermute | solution.py:889
  70.8 26.5 %collective-permute-start.11 = (bf16[1,512,1024]{2,1,0:T(8,128)(2,1)}, bf16[1,512,1024]{2,1,0:T(8,128)(2,1)}, u32[]{:S(2)}, u32[]{:S(2)}) collective-permute-start(bf16[1,512,1024]{2,1,0:T(8,128)(2,1)} %get-tuple-element.161.refs_3_.refs_4_), channel_id=1, source_target_pairs={{0,2},{1,3},{2,0},{3,1},{4,6},{5,7},{6,4},{7,5},{8,10},{9,11},{10,... | collective-permute-start | bytes 3145736 | tf_op jit(solution)/shard_map/ppermute | solution.py:889
  97.3 28.4 %collective-permute-start.14 = (bf16[1,512,1024]{2,1,0:T(8,128)(2,1)}, bf16[1,512,1024]{2,1,0:T(8,128)(2,1)}, u32[]{:S(2)}, u32[]{:S(2)}) collective-permute-start(bf16[1,512,1024]{2,1,0:T(8,128)(2,1)} %get-tuple-element.164.refs_2_.refs_6_), channel_id=1, source_target_pairs={{0,2},{1,3},{2,0},{3,1},{4,6},{5,7},{6,4},{7,5},{8,10},{9,11},{10,... | collective-permute-start | bytes 3145736 | tf_op jit(solution)/shard_map/ppermute | solution.py:889
  98.4 27.4 %collective-permute-start.15 = (bf16[1,512,1024]{2,1,0:T(8,128)(2,1)}, bf16[1,512,1024]{2,1,0:T(8,128)(2,1)}, u32[]{:S(2)}, u32[]{:S(2)}) collective-permute-start(bf16[1,512,1024]{2,1,0:T(8,128)(2,1)} %get-tuple-element.165.refs_3_.refs_8_), channel_id=1, source_target_pairs={{0,1},{1,0},{2,3},{3,2},{4,5},{5,4},{6,7},{7,6},{8,9},{9,8},{10,11... | collective-permute-start | bytes 3145736 | tf_op jit(solution)/shard_map/ppermute | solution.py:889
  126.4 25.5 %collective-permute-start.13 = (bf16[1,512,1024]{2,1,0:T(8,128)(2,1)}, bf16[1,512,1024]{2,1,0:T(8,128)(2,1)}, u32[]{:S(2)}, u32[]{:S(2)}) collective-permute-start(bf16[1,512,1024]{2,1,0:T(8,128)(2,1)} %get-tuple-element.160.refs_2_.refs_4_), channel_id=1, source_target_pairs={{0,2},{1,3},{2,0},{3,1},{4,6},{5,7},{6,4},{7,5},{8,10},{9,11},{10,... | collective-permute-start | bytes 3145736 | tf_op jit(solution)/shard_map/ppermute | solution.py:889
  127.4 25.2 %collective-permute-start.12 = (bf16[1,512,1024]{2,1,0:T(8,128)(2,1)}, bf16[1,512,1024]{2,1,0:T(8,128)(2,1)}, u32[]{:S(2)}, u32[]{:S(2)}) collective-permute-start(bf16[1,512,1024]{2,1,0:T(8,128)(2,1)} %get-tuple-element.161.refs_3_.refs_4_), channel_id=1, source_target_pairs={{0,1},{1,0},{2,3},{3,2},{4,5},{5,4},{6,7},{7,6},{8,9},{9,8},{10,11... | collective-permute-start | bytes 3145736 | tf_op jit(solution)/shard_map/ppermute | solution.py:889
  128.9 28.6 %collective-permute-start.18 = (bf16[1,512,1024]{2,1,0:T(8,128)(2,1)}, bf16[1,512,1024]{2,1,0:T(8,128)(2,1)}, u32[]{:S(2)}, u32[]{:S(2)}) collective-permute-start(bf16[1,512,1024]{2,1,0:T(8,128)(2,1)} %get-tuple-element.164.refs_2_.refs_6_), channel_id=1, source_target_pairs={{0,4},{4,0},{8,12},{12,8},{16,20},{20,16},{24,28},{28,24},{1,5},{5... | collective-permute-start | bytes 3145736 | tf_op jit(solution)/shard_map/ppermute | solution.py:892
  152.6 21.8 %collective-permute-start.22 = (bf16[1,512,1024]{2,1,0:T(8,128)(2,1)}, bf16[1,512,1024]{2,1,0:T(8,128)(2,1)S(1)}, u32[]{:S(2)}, u32[]{:S(2)}) collective-permute-start(bf16[1,512,1024]{2,1,0:T(8,128)(2,1)} %get-tuple-element.165.refs_3_.refs_8_), channel_id=1, source_target_pairs={{0,4},{4,0},{8,12},{12,8},{16,20},{20,16},{24,28},{28,24},{1,5},{5... | collective-permute-start | bytes 3145736 | tf_op jit(solution)/shard_map/ppermute | solution.py:892
  153.1 21.3 %collective-permute-start.21 = (bf16[1,512,1024]{2,1,0:T(8,128)(2,1)}, bf16[1,512,1024]{2,1,0:T(8,128)(2,1)S(1)}, u32[]{:S(2)}, u32[]{:S(2)}) collective-permute-start(bf16[1,512,1024]{2,1,0:T(8,128)(2,1)} %get-tuple-element.174.refs_2_.refs_8_), channel_id=1, source_target_pairs={{0,4},{4,0},{8,12},{12,8},{16,20},{20,16},{24,28},{28,24},{1,5},{5... | collective-permute-start | bytes 3145736 | tf_op jit(solution)/shard_map/ppermute | solution.py:892
  156.6 32.5 %collective-permute-start.25 = (bf16[512,1024]{1,0:T(8,128)(2,1)}, bf16[512,1024]{1,0:T(8,128)(2,1)}, u32[]{:S(2)}, u32[]{:S(2)}) collective-permute-start(bf16[512,1024]{1,0:T(8,128)(2,1)} %get-tuple-element.184), channel_id=1, source_target_pairs={{0,2},{1,3},{2,0},{3,1},{4,6},{5,7},{6,4},{7,5},{8,10},{9,11},{10,... | collective-permute-start | bytes 3145736 | tf_op jit(solution)/shard_map/ppermute | solution.py:889
  157.5 31.5 %collective-permute-start.24 = (bf16[512,1024]{1,0:T(8,128)(2,1)}, bf16[512,1024]{1,0:T(8,128)(2,1)}, u32[]{:S(2)}, u32[]{:S(2)}) collective-permute-start(bf16[512,1024]{1,0:T(8,128)(2,1)} %get-tuple-element.172.refs_7_), channel_id=1, source_target_pairs={{0,1},{1,0},{2,3},{3,2},{4,5},{5,4},{6,7},{7,6},{8,9},{9,8},{10,11... | collective-permute-start | bytes 3145736 | tf_op jit(solution)/shard_map/ppermute | solution.py:889
  174.4 14.7 %collective-permute-start.23 = (bf16[2,512,1024]{2,1,0:T(8,128)(2,1)}, bf16[2,512,1024]{2,1,0:T(8,128)(2,1)}, u32[]{:S(2)}, u32[]{:S(2)}) collective-permute-start(bf16[2,512,1024]{2,1,0:T(8,128)(2,1)} %get-tuple-element.183), channel_id=1, source_target_pairs={{0,4},{4,0},{8,12},{12,8},{16,20},{20,16},{24,28},{28,24},{1,5},{5... | collective-permute-start | bytes 6291464 | tf_op jit(solution)/shard_map/ppermute | solution.py:892
  194.0 49.2 %collective-permute-start.28 = (bf16[1024,1024]{1,0:T(8,128)(2,1)}, bf16[1024,1024]{1,0:T(8,128)(2,1)S(1)}, u32[]{:S(2)}, u32[]{:S(2)}) collective-permute-start(bf16[1024,1024]{1,0:T(8,128)(2,1)} %merge.10.refs_3_.refs_16_), channel_id=1, source_target_pairs={{0,1},{1,0},{2,3},{3,2},{4,5},{5,4},{6,7},{7,6},{8,9},{9,8},{10,11... | collective-permute-start | bytes 6291464 | tf_op jit(solution)/shard_map/ppermute | solution.py:889
  199.3 47.6 %collective-permute-start.29 = (bf16[1024,1024]{1,0:T(8,128)(2,1)}, bf16[1024,1024]{1,0:T(8,128)(2,1)}, u32[]{:S(2)}, u32[]{:S(2)}) collective-permute-start(bf16[1024,1024]{1,0:T(8,128)(2,1)} %merge.11.refs_17_), channel_id=1, source_target_pairs={{0,2},{1,3},{2,0},{3,1},{4,6},{5,7},{6,4},{7,5},{8,10},{9,11},{10,... | collective-permute-start | bytes 6291464 | tf_op jit(solution)/shard_map/ppermute | solution.py:889
  200.3 46.6 %collective-permute-start.27 = (bf16[2,512,1024]{2,1,0:T(8,128)(2,1)}, bf16[2,512,1024]{2,1,0:T(8,128)(2,1)}, u32[]{:S(2)}, u32[]{:S(2)}) collective-permute-start(bf16[2,512,1024]{2,1,0:T(8,128)(2,1)} %get-tuple-element.199), channel_id=1, source_target_pairs={{0,4},{4,0},{8,12},{12,8},{16,20},{20,16},{24,28},{28,24},{1,5},{5... | collective-permute-start | bytes 6291464 | tf_op jit(solution)/shard_map/ppermute | solution.py:892
  253.5 24.3 %collective-permute-start.31 = (bf16[512,1024]{1,0:T(8,128)(2,1)}, bf16[512,1024]{1,0:T(8,128)(2,1)}, u32[]{:S(2)}, u32[]{:S(2)}) collective-permute-start(bf16[512,1024]{1,0:T(8,128)(2,1)} %get-tuple-element.206), channel_id=1, source_target_pairs={{0,8},{4,12},{8,0},{12,4},{16,24},{20,28},{24,16},{28,20},{1,9},{5... | collective-permute-start | bytes 3145736 | tf_op jit(solution)/shard_map/ppermute | solution.py:892
  279.8 24.1 %collective-permute-start.32 = (bf16[256,1024]{1,0:T(8,128)(2,1)}, bf16[256,1024]{1,0:T(8,128)(2,1)S(1)}, u32[]{:S(2)}, u32[]{:S(2)}) collective-permute-start(bf16[256,1024]{1,0:T(8,128)(2,1)} %merge.12.refs_10_), channel_id=1, source_target_pairs={{0,16},{4,20},{8,24},{12,28},{16,0},{20,4},{24,8},{28,12},{1,17},{... | collective-permute-start | bytes 1572872 | tf_op jit(solution)/shard_map/ppermute | solution.py:892
  283.2 25.6 %collective-permute-start.30 = (bf16[512,1024]{1,0:T(8,128)(2,1)}, bf16[512,1024]{1,0:T(8,128)(2,1)}, u32[]{:S(2)}, u32[]{:S(2)}) collective-permute-start(bf16[512,1024]{1,0:T(8,128)(2,1)} %get-tuple-element.205), channel_id=1, source_target_pairs={{0,4},{4,0},{8,12},{12,8},{16,20},{20,16},{24,28},{28,24},{1,5},{5... | collective-permute-start | bytes 3145736 | tf_op jit(solution)/shard_map/ppermute | solution.py:892
  308.7 26.4 %collective-permute-start.34 = (bf16[256,1024]{1,0:T(8,128)(2,1)}, bf16[256,1024]{1,0:T(8,128)(2,1)}, u32[]{:S(2)}, u32[]{:S(2)}) collective-permute-start(bf16[256,1024]{1,0:T(8,128)(2,1)} %merge.13.refs_4_), channel_id=1, source_target_pairs={{0,16},{4,20},{8,24},{12,28},{16,0},{20,4},{24,8},{28,12},{1,17},{... | collective-permute-start | bytes 1572872 | tf_op jit(solution)/shard_map/ppermute | solution.py:892
  311.4 23.7 %collective-permute-start.35 = (bf16[256,1024]{1,0:T(8,128)(2,1)}, bf16[256,1024]{1,0:T(8,128)(2,1)S(1)}, u32[]{:S(2)}, u32[]{:S(2)}) collective-permute-start(bf16[256,1024]{1,0:T(8,128)(2,1)} %get-tuple-element.211.refs_9_), channel_id=1, source_target_pairs={{0,1},{1,0},{2,3},{3,2},{4,5},{5,4},{6,7},{7,6},{8,9},{9,8},{10,11... | collective-permute-start | bytes 1572872 | tf_op jit(solution)/shard_map/ppermute | solution.py:889
  312.9 22.2 %collective-permute-start.36 = (bf16[256,1024]{1,0:T(8,128)(2,1)}, bf16[256,1024]{1,0:T(8,128)(2,1)}, u32[]{:S(2)}, u32[]{:S(2)}) collective-permute-start(bf16[256,1024]{1,0:T(8,128)(2,1)} %get-tuple-element.212.refs_10_), channel_id=1, source_target_pairs={{0,2},{1,3},{2,0},{3,1},{4,6},{5,7},{6,4},{7,5},{8,10},{9,11},{10,... | collective-permute-start | bytes 1572872 | tf_op jit(solution)/shard_map/ppermute | solution.py:889
  316.5 25.7 %collective-permute-start.37 = (bf16[512,1024]{1,0:T(8,128)(2,1)}, bf16[512,1024]{1,0:T(8,128)(2,1)}, u32[]{:S(2)}, u32[]{:S(2)}) collective-permute-start(bf16[512,1024]{1,0:T(8,128)(2,1)} %get-tuple-element.220), channel_id=1, source_target_pairs={{0,4},{4,0},{8,12},{12,8},{16,20},{20,16},{24,28},{28,24},{1,5},{5... | collective-permute-start | bytes 3145736 | tf_op jit(solution)/shard_map/ppermute | solution.py:892
  338.1 29.2 %collective-permute-start.39 = (bf16[512,1024]{1,0:T(8,128)(2,1)}, bf16[512,1024]{1,0:T(8,128)(2,1)}, u32[]{:S(2)}, u32[]{:S(2)}) collective-permute-start(bf16[512,1024]{1,0:T(8,128)(2,1)} %pad_maximum_fusion.refs_11_.refs_1_), channel_id=1, source_target_pairs={{0,8},{4,12},{8,0},{12,4},{16,24},{20,28},{24,16},{28,20},{1,9},{5... | collective-permute-start | bytes 3145736 | tf_op jit(solution)/shard_map/ppermute | solution.py:892
  344.9 25.1 %collective-permute-start.40 = (bf16[512,1024]{1,0:T(8,128)(2,1)}, bf16[512,1024]{1,0:T(8,128)(2,1)}, u32[]{:S(2)}, u32[]{:S(2)}) collective-permute-start(bf16[512,1024]{1,0:T(8,128)(2,1)} %merge.15.refs_3_), channel_id=1, source_target_pairs={{0,1},{1,0},{2,3},{3,2},{4,5},{5,4},{6,7},{7,6},{8,9},{9,8},{10,11... | collective-permute-start | bytes 3145736 | tf_op jit(solution)/shard_map/ppermute | solution.py:889
  348.0 24.8 %collective-permute-start.41 = (bf16[512,1024]{1,0:T(8,128)(2,1)}, bf16[512,1024]{1,0:T(8,128)(2,1)}, u32[]{:S(2)}, u32[]{:S(2)}) collective-permute-start(bf16[512,1024]{1,0:T(8,128)(2,1)} %merge.16.refs_10_), channel_id=1, source_target_pairs={{0,2},{1,3},{2,0},{3,1},{4,6},{5,7},{6,4},{7,5},{8,10},{9,11},{10,... | collective-permute-start | bytes 3145736 | tf_op jit(solution)/shard_map/ppermute | solution.py:889
  349.0 51.1 %collective-permute-start.45 = (bf16[512,1024]{1,0:T(8,128)(2,1)}, bf16[512,1024]{1,0:T(8,128)(2,1)}, u32[]{:S(2)}, u32[]{:S(2)}) collective-permute-start(bf16[512,1024]{1,0:T(8,128)(2,1)} %pad_maximum_fusion.refs_11_.refs_1_), channel_id=1, source_target_pairs={{0,4},{4,0},{8,12},{12,8},{16,20},{20,16},{24,28},{28,24},{1,5},{5... | collective-permute-start | bytes 3145736 | tf_op jit(solution)/shard_map/ppermute | solution.py:892
  372.8 30.8 %collective-permute-start.46 = (bf16[512,1024]{1,0:T(8,128)(2,1)}, bf16[512,1024]{1,0:T(8,128)(2,1)S(1)}, u32[]{:S(2)}, u32[]{:S(2)}) collective-permute-start(bf16[512,1024]{1,0:T(8,128)(2,1)} %get-tuple-element.234.refs_2_), channel_id=1, source_target_pairs={{0,4},{4,0},{8,12},{12,8},{16,20},{20,16},{24,28},{28,24},{1,5},{5... | collective-permute-start | bytes 3145736 | tf_op jit(solution)/shard_map/ppermute | solution.py:892
  375.9 25.7 %collective-permute-start.42 = (bf16[128,1024]{1,0:T(8,128)(2,1)}, bf16[128,1024]{1,0:T(8,128)(2,1)S(1)}, u32[]{:S(2)}, u32[]{:S(2)}) collective-permute-start(bf16[128,1024]{1,0:T(8,128)(2,1)} %get-tuple-element.230.refs_16_), channel_id=1, source_target_pairs={{0,8},{4,12},{8,0},{12,4},{16,24},{20,28},{24,16},{28,20},{1,9},{5... | collective-permute-start | bytes 786440 | tf_op jit(solution)/shard_map/ppermute | solution.py:892
  376.3 26.3 %collective-permute-start.43 = (bf16[128,1024]{1,0:T(8,128)(2,1)}, bf16[128,1024]{1,0:T(8,128)(2,1)S(1)}, u32[]{:S(2)}, u32[]{:S(2)}) collective-permute-start(bf16[128,1024]{1,0:T(8,128)(2,1)} %get-tuple-element.231.refs_17_), channel_id=1, source_target_pairs={{0,16},{4,20},{8,24},{12,28},{16,0},{20,4},{24,8},{28,12},{1,17},{... | collective-permute-start | bytes 786440 | tf_op jit(solution)/shard_map/ppermute | solution.py:892
  376.9 26.8 %collective-permute-start.44 = (bf16[128,1024]{1,0:T(8,128)(2,1)}, bf16[128,1024]{1,0:T(8,128)(2,1)S(1)}, u32[]{:S(2)}, u32[]{:S(2)}) collective-permute-start(bf16[128,1024]{1,0:T(8,128)(2,1)} %get-tuple-element.232.refs_18_), channel_id=1, source_target_pairs={{0,24},{4,28},{8,16},{12,20},{16,8},{20,12},{24,0},{28,4},{1,25},{... | collective-permute-start | bytes 786440 | tf_op jit(solution)/shard_map/ppermute | solution.py:892
  400.1 19.3 %collective-permute-start.47 = (f32[4,1536]{1,0:T(4,128)S(1)}, f32[4,1536]{1,0:T(4,128)S(1)}, u32[]{:S(2)}, u32[]{:S(2)}) collective-permute-start(f32[4,1536]{1,0:T(4,128)S(1)} %bitcast.108), channel_id=1, source_target_pairs={{0,1},{1,0},{2,3},{3,2},{4,5},{5,4},{6,7},{7,6},{8,9},{9,8},{10,11... | collective-permute-start | bytes 73736 | tf_op jit(solution)/shard_map/ppermute | solution.py:889
  401.6 20.2 %collective-permute-start.48 = (f32[4,1536]{1,0:T(4,128)S(1)}, f32[4,1536]{1,0:T(4,128)S(1)}, u32[]{:S(2)}, u32[]{:S(2)}) collective-permute-start(f32[4,1536]{1,0:T(4,128)S(1)} %bitcast.107), channel_id=1, source_target_pairs={{0,2},{1,3},{2,0},{3,1},{4,6},{5,7},{6,4},{7,5},{8,10},{9,11},{10,... | collective-permute-start | bytes 73736 | tf_op jit(solution)/shard_map/ppermute | solution.py:889
  402.6 19.2 %collective-permute-start.49 = (f32[4,1536]{1,0:T(4,128)S(1)}, f32[4,1536]{1,0:T(4,128)S(1)}, u32[]{:S(2)}, u32[]{:S(2)}) collective-permute-start(f32[4,1536]{1,0:T(4,128)S(1)} %bitcast.106), channel_id=1, source_target_pairs={{0,3},{1,2},{2,1},{3,0},{4,7},{5,6},{6,5},{7,4},{8,11},{9,10},{10,... | collective-permute-start | bytes 73736 | tf_op jit(solution)/shard_map/ppermute | solution.py:889
  407.4 22.3 %collective-permute-start.55 = (bf16[128,1024]{1,0:T(8,128)(2,1)}, bf16[128,1024]{1,0:T(8,128)(2,1)S(1)}, u32[]{:S(2)}, u32[]{:S(2)}) collective-permute-start(bf16[128,1024]{1,0:T(8,128)(2,1)} %merge.17.refs_4_), channel_id=1, source_target_pairs={{0,8},{4,12},{8,0},{12,4},{16,24},{20,28},{24,16},{28,20},{1,9},{5... | collective-permute-start | bytes 786440 | tf_op jit(solution)/shard_map/ppermute | solution.py:892
  407.4 14.5 %collective-permute-start.50 = (bf16[128,1024]{1,0:T(8,128)(2,1)}, bf16[128,1024]{1,0:T(8,128)(2,1)S(1)}, u32[]{:S(2)}, u32[]{:S(2)}) collective-permute-start(bf16[128,1024]{1,0:T(8,128)(2,1)} %merge.17.refs_4_), channel_id=1, source_target_pairs={{0,24},{4,28},{8,16},{12,20},{16,8},{20,12},{24,0},{28,4},{1,25},{... | collective-permute-start | bytes 786440 | tf_op jit(solution)/shard_map/ppermute | solution.py:892
  419.3 13.7 %collective-permute-start.54 = (bf16[128,1024]{1,0:T(8,128)(2,1)S(1)}, bf16[128,1024]{1,0:T(8,128)(2,1)S(1)}, u32[]{:S(2)}, u32[]{:S(2)}) collective-permute-start(bf16[128,1024]{1,0:T(8,128)(2,1)S(1)} %copy-done.33), channel_id=1, source_target_pairs={{0,16},{4,20},{8,24},{12,28},{16,0},{20,4},{24,8},{28,12},{1,17},{... | collective-permute-start | bytes 786440 | tf_op jit(solution)/shard_map/ppermute | solution.py:892
  436.9 22.4 %collective-permute-start.56 = (bf16[512,1024]{1,0:T(8,128)(2,1)S(1)}, bf16[512,1024]{1,0:T(8,128)(2,1)S(1)}, u32[]{:S(2)}, u32[]{:S(2)}) collective-permute-start(bf16[512,1024]{1,0:T(8,128)(2,1)S(1)} %pad_maximum_fusion.1.refs_1_), channel_id=1, source_target_pairs={{0,4},{4,0},{8,12},{12,8},{16,20},{20,16},{24,28},{28,24},{1,5},{5... | collective-permute-start | bytes 3145736 | tf_op jit(solution)/shard_map/ppermute | solution.py:892
  440.4 15.8 %collective-permute-start.62 = (bf16[16,3840]{1,0:T(8,128)(2,1)}, bf16[16,3840]{1,0:T(8,128)(2,1)S(1)}, u32[]{:S(2)}, u32[]{:S(2)}) collective-permute-start(bf16[16,3840]{1,0:T(8,128)(2,1)} %mode_rows.1.refs_1_), channel_id=1, source_target_pairs={{0,24},{4,28},{8,16},{12,20},{16,8},{20,12},{24,0},{28,4},{1,25},{... | collective-permute-start | bytes 368648 | tf_op jit(solution)/shard_map/ppermute | solution.py:892
  442.8 24.7 %collective-permute-start.61 = (bf16[16,3840]{1,0:T(8,128)(2,1)}, bf16[16,3840]{1,0:T(8,128)(2,1)S(1)}, u32[]{:S(2)}, u32[]{:S(2)}) collective-permute-start(bf16[16,3840]{1,0:T(8,128)(2,1)} %mode_rows.1.refs_1_), channel_id=1, source_target_pairs={{0,20},{4,16},{8,28},{12,24},{16,4},{20,0},{24,12},{28,8},{1,21},{... | collective-permute-start | bytes 368648 | tf_op jit(solution)/shard_map/ppermute | solution.py:892
  442.8 24.7 %collective-permute-start.60 = (bf16[16,3840]{1,0:T(8,128)(2,1)}, bf16[16,3840]{1,0:T(8,128)(2,1)S(1)}, u32[]{:S(2)}, u32[]{:S(2)}) collective-permute-start(bf16[16,3840]{1,0:T(8,128)(2,1)} %mode_rows.1.refs_1_), channel_id=1, source_target_pairs={{0,16},{4,20},{8,24},{12,28},{16,0},{20,4},{24,8},{28,12},{1,17},{... | collective-permute-start | bytes 368648 | tf_op jit(solution)/shard_map/ppermute | solution.py:892
  446.6 20.9 %collective-permute-start.59 = (bf16[16,3840]{1,0:T(8,128)(2,1)}, bf16[16,3840]{1,0:T(8,128)(2,1)S(1)}, u32[]{:S(2)}, u32[]{:S(2)}) collective-permute-start(bf16[16,3840]{1,0:T(8,128)(2,1)} %mode_rows.1.refs_1_), channel_id=1, source_target_pairs={{0,12},{4,8},{8,4},{12,0},{16,28},{20,24},{24,20},{28,16},{1,13},{... | collective-permute-start | bytes 368648 | tf_op jit(solution)/shard_map/ppermute | solution.py:892
  456.2 12.0 %collective-permute-start.58 = (bf16[16,3840]{1,0:T(8,128)(2,1)}, bf16[16,3840]{1,0:T(8,128)(2,1)S(1)}, u32[]{:S(2)}, u32[]{:S(2)}) collective-permute-start(bf16[16,3840]{1,0:T(8,128)(2,1)} %mode_rows.1.refs_1_), channel_id=1, source_target_pairs={{0,8},{4,12},{8,0},{12,4},{16,24},{20,28},{24,16},{28,20},{1,9},{5... | collective-permute-start | bytes 368648 | tf_op jit(solution)/shard_map/ppermute | solution.py:892
  (87 other events, 498.6 us)

commit v5 on v4

--- a/solution.py
+++ b/solution.py
@@ -773,13 +773,14 @@
     return run(mode_rows_kernel, "mode_rows", 1, ins, outs, (), (), [mp])[0]
 
 
-def mode_final_kernel(dp_ref, *refs):
-    *parts, ada_ref, bias_ref, class_ref, rel_ref, rows = refs
-    size = parts[0].shape[0]
+def mode_final_kernel(dp_ref, own_ref, other_ref, ada_ref, bias_ref, class_ref, rel_ref, rows, *, count):
+    size = own_ref.shape[0] // count
     columns = ada_ref.shape[1]
     marks = [0, columns, columns + D, columns + D + 128, columns + 2 * D + 128, columns + 2 * D + 256]
-    for k, ref in enumerate(parts):
-        rows[pl.ds(pl.multiple_of((dp_ref[0] ^ k) * size, size), size)] = ref[...]
+    for core, ref in enumerate((own_ref, other_ref)):
+        for k in range(count):
+            at = (dp_ref[0] ^ (2 * k + core)) * size
+            rows[pl.ds(pl.multiple_of(at, size), size)] = ref[k * size : (k + 1) * size]
     modes, classes, rel, cond, index = [rows[:, i:j] for i, j in zip(marks, marks[1:])]
     ada_ref[...] = mm(cond, modes, TN)
     bias_ref[...] = jnp.sum(modes.astype(f32), axis=0)
@@ -787,17 +788,17 @@
     hot = jnp.where(lane == index[:, :1].astype(f32), 1.0, 0.0).astype(bf16)
     class_ref[...] = mm(hot, classes, TN)[: class_ref.shape[0]]
     total = rel[:size].astype(f32)
-    for i in range(1, len(parts)):
+    for i in range(1, 2 * count):
         total = total + rel[i * size : (i + 1) * size].astype(f32)
     rel_ref[...] = total[: rel_ref.shape[0], : rel_ref.shape[1]]
 
 
-def mode_final(dp, parts, columns, class_count, rel_shape):
-    size, width = parts[0].shape
-    ins = [(v, whole(size, width)) for v in parts]
+def mode_final(dp, own, other, count, columns, class_count, rel_shape):
+    size, width = own.shape
     outs = [(shape(dims, f32), whole(*dims)) for dims in ((D, columns), (columns,), (class_count, D), rel_shape)]
-    scratch = [pltpu.VMEM((len(parts) * size, width), bf16)]
-    return run(mode_final_kernel, "mode_final", 1, ins, outs, scratch, (), [dp], vmem=32)
+    kernel = partial(mode_final_kernel, count=count)
+    ins = [(own, whole(size, width)), (other, whole(size, width))]
+    return run(kernel, "mode_final", 1, ins, outs, [pltpu.VMEM((2 * size, width), bf16)], (), [dp], vmem=32)
 
 
 def silu_plain(values):
@@ -1047,12 +1048,13 @@
     )
     grads = mode_rows(mp.reshape(1), mode_low, shares, slope, cond_rel)
     attn_own = jnp.concatenate([attn_own, attn_one, attn_two, attn_far])
-    got = [swap_dp(k)(grads) for k in range(1, n_dp)]
+    got = exchange([grads] * n_z)
     (attn_other,) = hold([pc(attn_own)], [grads])
     grad_qkv, grad_out = attn_final(place, attn_own, Moved(attn_other))
     got = arrive(got, [grad_qkv])
+    grads = jnp.concatenate([grads, *got])
     grad_ada, grad_ada_bias, class_grad, grad_rel = mode_final(
-        (2 * z + core).reshape(1), [grads, *got], columns, class_table.shape[0], rel_bias.shape
+        (2 * z + core).reshape(1), grads, pc(grads), n_z, columns, class_table.shape[0], rel_bias.shape
     )
 
     return (

time: 480 us -> 469 us (0.977)
  starting transfers between devices: 68.7 us -> 54.3 us
    ppermute x37 -> x34, starting transfers between devices: 38.3 us -> 23.8 us  [swap_dp(): lax.ppermute(v, ('z', 'core'), [(i, i ^ bit) for i in range(n_dp)])]
    unnamed x149 -> x147, local copies, waits for them, and re-layouts: 20.2 us -> 21.9 us
    ppermute x37 -> x34, waiting for transfers between devices: 14.3 us -> 15.6 us  [swap_dp(): lax.ppermute(v, ('z', 'core'), [(i, i ^ bit) for i in range(n_dp)])]
  transfers between devices with their start and end apart: 64 -> 61, of which waited for: 15 -> 15; matrix products, arithmetic and copies ran while one was open for 4% -> 5% of each run, Pallas kernels for 66% -> 68%
where the time goes in v5:
time: 469 us; the launch traced here: 464 us
  Pallas kernels  326 us (70%)
  starting transfers between devices  54.3 us (12%)
  waiting for transfers between devices  33.6 us (7%)
  local copies, waits for them, and re-layouts  31.9 us (7%)
  other arithmetic  9.63 us (2%)
  matrix products  7.06 us (2%)
    pallas_call x34, Pallas kernels, run(): pl.pallas_call(body, grid_spec=pltpu.PrefetchScalarGridSpec(num_scalar_pr...  326 us
    ppermute x27, starting transfers between devices, swap_mp(): return lambda v: lax.ppermute(v, 'mp', [(i, i ^ bit) for i in range(n_mp)])  30.5 us
    ppermute x34, starting transfers between devices, swap_dp(): lax.ppermute(v, ('z', 'core'), [(i, i ^ bit) for i in range(n_dp)])  23.8 us
    unnamed x147, local copies, waits for them, and re-layouts  21.9 us
    ppermute x27, waiting for transfers between devices, swap_mp(): return lambda v: lax.ppermute(v, 'mp', [(i, i ^ bit) for i in range(n_mp)])  18 us
    ppermute x34, waiting for transfers between devices, swap_dp(): lax.ppermute(v, ('z', 'core'), [(i, i ^ bit) for i in range(n_dp)])  15.6 us
  transfers between devices with their start and end apart: 61, of which 15 were waited for; matrix products, arithmetic and copies ran while one was open for 5% of the time, Pallas kernels for 68%

profile of v5, /device:TPU:0, one launch (start us, length us, event | category | flops | bytes accessed | tf_op | source)
XLA Modules:
  0.0 464.1 jit_solution(2751244019517425875)
XLA Ops:
  4.0 2.5 fusion.2.refs_3_
  6.7 3.0 collective-permute-start
  11.3 4.2 attn_rows.1
  21.4 2.1 fusion.5
  24.5 14.6 %attend.4 = (bf16[1280,1024]{1,0:T(8,128)(2,1)S(1)}, bf16[1280,768]{1,0:T(8,128)(2,1)}, bf16[1280,256]{1,0:T(8,128)(2,1)}, bf16[16,320,320]{2,1,0:T(8,128)(2,1)}) custom-call(s32[4]{0:T(128)S(1)} %fusion.19.refs_0_, bf16[4,320,1024]{2,1,0:T(8,128)(2,1)} %refs_12_.3, f32[4,6,1024]{2,1,0:T(8,128)} %reshape.127.refs_2_.refs_14_.refs_15_.refs_13_, ...), custom_call_target="tpu_custom_call" | custom-call | flops 1000 | bytes 1000 | tf_op jit(solution)/shard_map/attend/pallas_call | solution.py:104
  39.2 7.4 %feed_rows.1 = (bf16[1,512,1024]{2,1,0:T(8,128)(2,1)}, bf16[1,512,1024]{2,1,0:T(8,128)(2,1)}, bf16[1,512,1024]{2,1,0:T(8,128)(2,1)}, bf16[1,512,1024]{2,1,0:T(8,128)(2,1)}) custom-call(s32[1]{0:T(128)} %bitcast.8.refs_0_, bf16[1024,1024]{1,0:T(8,128)(2,1)} %refs_1_.5, bf16[1024,1024]{1,0:T(8,128)(2,1)} %refs_2_.3, ...), custom_call_target="tpu_custom_call" | custom-call | flops 1000 | bytes 1000 | tf_op jit(solution)/shard_map/feed_rows/pallas_call | solution.py:104
  51.2 12.2 %attend.5 = (bf16[1280,768]{1,0:T(8,128)(2,1)}, bf16[1280,256]{1,0:T(8,128)(2,1)}, bf16[16,320,320]{2,1,0:T(8,128)(2,1)}) custom-call(s32[4]{0:T(128)S(1)} %fusion.19.refs_0_, bf16[1280,1024]{1,0:T(8,128)(2,1)} %copy-done.3, f32[4,6,1024]{2,1,0:T(8,128)} %reshape.127.refs_2_.refs_14_.refs_15_.refs_13_, bf16[512,1024]{1,0:T(8,128)(2,1)S(1)} %copy-done.11, ...), custom_call_target="tpu_custom_call" | custom-call | flops 1000 | bytes 1000 | tf_op jit(solution)/shard_map/attend/pallas_call | solution.py:104
  72.0 12.2 %attend.6 = (bf16[1280,768]{1,0:T(8,128)(2,1)}, bf16[1280,256]{1,0:T(8,128)(2,1)}, bf16[16,320,320]{2,1,0:T(8,128)(2,1)}) custom-call(s32[4]{0:T(128)S(1)} %fusion.19.refs_0_, bf16[1280,1024]{1,0:T(8,128)(2,1)} %copy-done.3, f32[4,6,1024]{2,1,0:T(8,128)} %reshape.127.refs_2_.refs_14_.refs_15_.refs_13_, bf16[512,1024]{1,0:T(8,128)(2,1)S(1)} %copy-done.9, ...), custom_call_target="tpu_custom_call" | custom-call | flops 1000 | bytes 1000 | tf_op jit(solution)/shard_map/attend/pallas_call | solution.py:104
  84.2 13.1 %attend.7 = (bf16[1280,768]{1,0:T(8,128)(2,1)}, bf16[1280,256]{1,0:T(8,128)(2,1)}, bf16[16,320,320]{2,1,0:T(8,128)(2,1)}) custom-call(s32[4]{0:T(128)S(1)} %fusion.19.refs_0_, bf16[1280,1024]{1,0:T(8,128)(2,1)} %copy-done.3, f32[4,6,1024]{2,1,0:T(8,128)} %reshape.127.refs_2_.refs_14_.refs_15_.refs_13_, ...), custom_call_target="tpu_custom_call" | custom-call | flops 1000 | bytes 1000 | tf_op jit(solution)/shard_map/attend/pallas_call | solution.py:104
  99.0 10.7 %middle.1 = (bf16[1280,1024]{1,0:T(8,128)(2,1)}, f32[1280,1024]{1,0:T(8,128)}, bf16[1280,1024]{1,0:T(8,128)(2,1)S(1)}, bf16[1280,1024]{1,0:T(8,128)(2,1)S(1)}) custom-call(bf16[1280,256]{1,0:T(8,128)(2,1)} %get-tuple-element.142.refs_3_.refs_0_.refs_8_, bf16[1280,256]{1,0:T(8,128)(2,1)} %get-tuple-element.146.refs_7_.refs_2_.refs_1_.refs_8_, ...), custom_call_target="tpu_custom_call" | custom-call | flops 1000 | bytes 1000 | tf_op jit(solution)/shard_map/middle/pallas_call | solution.py:104
  109.7 16.1 %feed.4 = (bf16[1280,1024]{1,0:T(8,128)(2,1)}, bf16[1280,1024]{1,0:T(8,128)(2,1)}, bf16[2,512,1024]{2,1,0:T(8,128)(2,1)}, bf16[2,512,1024]{2,1,0:T(8,128)(2,1)}) custom-call(bf16[1280,1024]{1,0:T(8,128)(2,1)S(1)} %get-tuple-element.152.refs_0_, bf16[1280,1024]{1,0:T(8,128)(2,1)S(1)} %get-tuple-element.153.refs_1_, ...), custom_call_target="tpu_custom_call" | custom-call | flops 1000 | bytes 1000 | tf_op jit(solution)/shard_map/feed/pallas_call | solution.py:104
  132.0 14.2 %feed.5 = (bf16[1280,1024]{1,0:T(8,128)(2,1)}, bf16[1280,1024]{1,0:T(8,128)(2,1)}, bf16[2,512,1024]{2,1,0:T(8,128)(2,1)}, bf16[2,512,1024]{2,1,0:T(8,128)(2,1)}) custom-call(bf16[1280,1024]{1,0:T(8,128)(2,1)S(1)} %get-tuple-element.152.refs_0_, bf16[1280,1024]{1,0:T(8,128)(2,1)S(1)} %copy-done.6, bf16[1,512,1024]{2,1,0:T(8,128)(2,1)} %get-tuple-element.162.refs_2_.refs_10_, ...), custom_call_target="tpu_custom_call" | custom-call | flops 1000 | bytes 1000 | tf_op jit(solution)/shard_map/feed/pallas_call | solution.py:104
  146.5 5.4 %collective-permute-done.13.refs_1_ = bf16[1,512,1024]{2,1,0:T(8,128)(2,1)} collective-permute-done((bf16[1,512,1024]{2,1,0:T(8,128)(2,1)}, bf16[1,512,1024]{2,1,0:T(8,128)(2,1)}, u32[]{:S(2)}, u32[]{:S(2)}) %collective-permute-start.13) | collective-permute-done | bytes 1048608 | tf_op jit(solution)/shard_map/ppermute | solution.py:890
  153.2 3.5 merge.9
  159.2 15.3 %feed.6 = (bf16[1280,1024]{1,0:T(8,128)(2,1)}, bf16[1280,1024]{1,0:T(8,128)(2,1)}, bf16[2,512,1024]{2,1,0:T(8,128)(2,1)}, bf16[2,512,1024]{2,1,0:T(8,128)(2,1)}) custom-call(bf16[1280,1024]{1,0:T(8,128)(2,1)S(1)} %get-tuple-element.152.refs_0_, bf16[1280,1024]{1,0:T(8,128)(2,1)S(1)} %copy-done.7, bf16[1,512,1024]{2,1,0:T(8,128)(2,1)} %get-tuple-element.160.refs_2_.refs_6_, ...), custom_call_target="tpu_custom_call" | custom-call | flops 1000 | bytes 1000 | tf_op jit(solution)/shard_map/feed/pallas_call | solution.py:104
  174.6 14.0 %feed.7 = (bf16[1280,1024]{1,0:T(8,128)(2,1)}, bf16[1280,1024]{1,0:T(8,128)(2,1)}, bf16[2,512,1024]{2,1,0:T(8,128)(2,1)}, bf16[2,512,1024]{2,1,0:T(8,128)(2,1)}) custom-call(bf16[1280,1024]{1,0:T(8,128)(2,1)S(1)} %get-tuple-element.152.refs_0_, bf16[1280,1024]{1,0:T(8,128)(2,1)S(1)} %copy-done.7, bf16[1,512,1024]{2,1,0:T(8,128)(2,1)} %get-tuple-element.170.refs_2_.refs_8_, ...), custom_call_target="tpu_custom_call" | custom-call | flops 1000 | bytes 1000 | tf_op jit(solution)/shard_map/feed/pallas_call | solution.py:104
  189.2 4.9 %merge.10.refs_3_.refs_16_ = bf16[1024,1024]{1,0:T(8,128)(2,1)} custom-call(bf16[1024,1024]{1,0:T(8,128)(2,1)} %bitcast.90, bf16[1024,1024]{1,0:T(8,128)(2,1)} %bitcast.19.refs_1_, bf16[512,1024]{1,0:T(8,128)(2,1)} %get-tuple-element.181.refs_2_), custom_call_target="tpu_custom_call" | custom-call | flops 1000 | bytes 1000 | tf_op jit(solution)/shard_map/merge/pallas_call | solution.py:104
  194.7 4.8 %merge.11.refs_17_ = bf16[1024,1024]{1,0:T(8,128)(2,1)} custom-call(bf16[1024,1024]{1,0:T(8,128)(2,1)} %bitcast.91, bf16[1024,1024]{1,0:T(8,128)(2,1)} %bitcast.21.refs_1_, bf16[512,1024]{1,0:T(8,128)(2,1)} %get-tuple-element.184.refs_2_, bf16[1024,1024]{1,0:T(8,128)(2,1)} %merge.10.refs_3_.refs_16_), custom_call_target="tpu_custom_call" | custom-call | flops 1000 | bytes 1000 | tf_op jit(solution)/shard_map/merge/pallas_call | solution.py:104
  201.7 22.6 %turn.1 = (f32[1280,1024]{1,0:T(8,128)}, bf16[1280,1024]{1,0:T(8,128)(2,1)S(1)}, f32[4,3,1024]{2,1,0:T(4,128)}) custom-call(bf16[1280,1024]{1,0:T(8,128)(2,1)} %get-tuple-element.173.refs_0_, bf16[1280,1024]{1,0:T(8,128)(2,1)} %get-tuple-element.174.refs_1_, bf16[1280,1024]{1,0:T(8,128)(2,1)} %get-tuple-element.175.refs_2_, ...), custom_call_target="tpu_custom_call" | custom-call | flops 1000 | bytes 1000 | tf_op jit(solution)/shard_map/turn/pallas_call | solution.py:104
  224.3 19.0 %output.1 = (bf16[4,320,1024]{2,1,0:T(8,128)(2,1)}, f32[4,1,1024]{2,1,0:T(1,128)}) custom-call(bf16[1280,1024]{1,0:T(8,128)(2,1)} %get-tuple-element.159.refs_2_.refs_6_.refs_0_, bf16[1280,1024]{1,0:T(8,128)(2,1)} %get-tuple-element.169.refs_6_.refs_1_, bf16[1280,1024]{1,0:T(8,128)(2,1)} %get-tuple-element.171.refs_2_, ...), custom_call_target="tpu_custom_call" | custom-call | flops 1000 | bytes 1000 | tf_op jit(solution)/shard_map/output/pallas_call | solution.py:104
  243.4 3.6 collective-permute-done.29.refs_1_
  248.6 5.0 %merge_parts.2 = (bf16[512,1024]{1,0:T(8,128)(2,1)}, bf16[512,1024]{1,0:T(8,128)(2,1)}) custom-call(s32[1]{0:T(128)} %bitcast.22.refs_0_, bf16[2,512,1024]{2,1,0:T(8,128)(2,1)} %get-tuple-element.194.refs_1_.refs_5_, bf16[2,512,1024]{2,1,0:T(8,128)(2,1)} %collective-permute-done.27.refs_2_.refs_6_, bf16[2,512,1024]{2,1,0:T(8,128)(2,1)S(1)} %bitcast.88, ...), custom_call_target="tpu_custom_call" | custom-call | flops 1000 | bytes 1000 | tf_op jit(solution)/shard_map/merge_parts/pallas_call | solution.py:104
  255.2 18.0 %attend_back.4 = (bf16[1280,768]{1,0:T(8,128)(2,1)}, bf16[512,1024]{1,0:T(8,128)(2,1)}, bf16[512,1024]{1,0:T(8,128)(2,1)}, f32[2,32,128]{2,1,0:T(8,128)}) custom-call(bf16[1280,1024]{1,0:T(8,128)(2,1)} %copy-done.2, bf16[512,1024]{1,0:T(8,128)(2,1)} %constant_dynamic-update-slice_fusion.refs_3_.refs_10_.refs_2_.refs_1_, bf16[512,1024]{1,0:T(8,128)(2,1)} %copy-done.13, ...), custom_call_target="tpu_custom_call" | custom-call | flops 1000 | bytes 1000 | tf_op jit(solution)/shard_map/attend_back/pallas_call | solution.py:104
  273.1 4.7 %collective-permute-done.31.refs_0_ = bf16[512,1024]{1,0:T(8,128)(2,1)} collective-permute-done((bf16[512,1024]{1,0:T(8,128)(2,1)}, bf16[512,1024]{1,0:T(8,128)(2,1)}, u32[]{:S(2)}, u32[]{:S(2)}) %collective-permute-start.31) | collective-permute-done | bytes 1048608 | tf_op jit(solution)/shard_map/ppermute | solution.py:893
  277.9 2.1 merge.12.refs_10_
  280.0 2.6 collective-permute-start.32
  283.4 17.8 %attend_back.5 = (bf16[1280,768]{1,0:T(8,128)(2,1)}, bf16[512,1024]{1,0:T(8,128)(2,1)}, bf16[512,1024]{1,0:T(8,128)(2,1)}, f32[2,32,128]{2,1,0:T(8,128)}) custom-call(bf16[1280,1024]{1,0:T(8,128)(2,1)} %copy-done.2, bf16[512,1024]{1,0:T(8,128)(2,1)} %get-tuple-element.145.refs_3_.refs_6_.refs_1_, bf16[512,1024]{1,0:T(8,128)(2,1)} %copy-done.14, ...), custom_call_target="tpu_custom_call" | custom-call | flops 1000 | bytes 1000 | tf_op jit(solution)/shard_map/attend_back/pallas_call | solution.py:104
  301.2 2.9 collective-permute-done.32.refs_0_
  306.7 2.2 merge.13.refs_4_
  308.9 2.7 merge.14
  316.6 18.0 %attend_back.6 = (bf16[1280,768]{1,0:T(8,128)(2,1)}, bf16[512,1024]{1,0:T(8,128)(2,1)}, bf16[512,1024]{1,0:T(8,128)(2,1)}, f32[2,32,128]{2,1,0:T(8,128)}) custom-call(bf16[1280,1024]{1,0:T(8,128)(2,1)} %copy-done.2, bf16[512,1024]{1,0:T(8,128)(2,1)} %get-tuple-element.147.refs_3_.refs_8_.refs_1_, bf16[512,1024]{1,0:T(8,128)(2,1)} %copy-done.12, ...), custom_call_target="tpu_custom_call" | custom-call | flops 1000 | bytes 1000 | tf_op jit(solution)/shard_map/attend_back/pallas_call | solution.py:104
  336.1 2.2 pad_maximum_fusion.refs_11_.refs_1_
  338.3 4.0 collective-permute-start.39
  342.3 2.7 merge.15.refs_3_
  345.6 2.6 merge.16.refs_10_
  349.1 17.8 %attend_back.7 = (bf16[1280,768]{1,0:T(8,128)(2,1)}, bf16[512,1024]{1,0:T(8,128)(2,1)}, bf16[512,1024]{1,0:T(8,128)(2,1)}, f32[2,32,128]{2,1,0:T(8,128)}) custom-call(bf16[1280,1024]{1,0:T(8,128)(2,1)} %copy-done.2, bf16[512,1024]{1,0:T(8,128)(2,1)} %hold.20.refs_3_.refs_4_.refs_1_, bf16[512,1024]{1,0:T(8,128)(2,1)} %get-tuple-element.141.refs_4_.refs_5_.refs_2_, ...), custom_call_target="tpu_custom_call" | custom-call | flops 1000 | bytes 1000 | tf_op jit(solution)/shard_map/attend_back/pallas_call | solution.py:104
  367.5 2.7 collective-permute-done.40.refs_1_
  370.2 2.8 collective-permute-done.41.refs_2_
  373.1 3.0 merge_parts.3
  377.0 3.5 collective-permute-start.44
  380.5 18.1 %last.1 = (bf16[4,320,1024]{2,1,0:T(8,128)(2,1)}, f32[4,2,1024]{2,1,0:T(2,128)}) custom-call(bf16[1280,768]{1,0:T(8,128)(2,1)} %get-tuple-element.219.refs_3_.refs_0_, bf16[1280,768]{1,0:T(8,128)(2,1)} %get-tuple-element.206.refs_1_, bf16[1280,768]{1,0:T(8,128)(2,1)} %get-tuple-element.211.refs_3_.refs_9_.refs_2_, ...), custom_call_target="tpu_custom_call" | custom-call | flops 1000 | bytes 1000 | tf_op jit(solution)/shard_map/last/pallas_call | solution.py:104
  411.1 7.8 %feed_final.1 = (f32[1024,1024]{1,0:T(8,128)}, f32[1024,1024]{1,0:T(8,128)}) custom-call(s32[2]{0:T(128)S(1)} %pad_add_fusion.refs_0_, bf16[512,1024]{1,0:T(8,128)(2,1)} %pad_maximum_fusion.refs_11_.refs_1_, bf16[512,1024]{1,0:T(8,128)(2,1)} %get-tuple-element.230.refs_2_, bf16[512,1024]{1,0:T(8,128)(2,1)} %get-tuple-element.235.refs_3_, ...), custom_call_target="tpu_custom_call" | custom-call | flops 1000 | bytes 1000 | tf_op jit(solution)/shard_map/feed_final/pallas_call | solution.py:104
  419.5 2.5 collective-permute-start.54
  422.8 3.6 mode_shares.1
  429.9 3.4 collective-permute-done.54.refs_3_
  437.2 2.1 mode_rows.1.refs_1_
  445.9 5.9 %attn_final.1 = (f32[1024,768]{1,0:T(8,128)}, f32[256,1024]{1,0:T(8,128)}) custom-call(s32[2]{0:T(128)S(1)} %pad_add_fusion.refs_0_, bf16[512,1024]{1,0:T(8,128)(2,1)} %copy-done.32, bf16[512,1024]{1,0:T(8,128)(2,1)S(1)} %copy-done.25), custom_call_target="tpu_custom_call" | custom-call | flops 1000 | bytes 1000 | tf_op jit(solution)/shard_map/attn_final/pallas_call | solution.py:104
  458.6 5.1 %mode_final.1 = (f32[1024,1536]{1,0:T(8,128)}, f32[1536]{0:T(1024)}, f32[101,1024]{1,0:T(8,128)}, f32[4,39]{1,0:T(4,128)}) custom-call(s32[1]{0:T(128)} %bitcast.38.refs_0_, bf16[64,3840]{1,0:T(8,128)(2,1)} %copy-done.37, bf16[64,3840]{1,0:T(8,128)(2,1)} %copy-done.42), custom_call_target="tpu_custom_call" | custom-call | flops 1000 | bytes 1000 | tf_op jit(solution)/shard_map/mode_final/pallas_call | solution.py:104
  (334 shorter events, 90.5 us)
Async XLA Ops:
  6.7 9.1 %collective-permute-start = (f32[4,1664]{1,0:T(4,128)S(1)}, f32[4,1664]{1,0:T(4,128)S(1)}, u32[]{:S(2)}, u32[]{:S(2)}) collective-permute-start(f32[4,1664]{1,0:T(4,128)S(1)} %get-tuple-element.289), channel_id=1, source_target_pairs={{0,1},{1,0},{2,3},{3,2},{4,5},{5,4},{6,7},{7,6},{8,9},{9,8},{10,11... | collective-permute-start | bytes 79880 | tf_op jit(solution)/shard_map/ppermute | solution.py:890
  16.7 29.8 %collective-permute-start.4 = (bf16[512,1024]{1,0:T(8,128)(2,1)}, bf16[512,1024]{1,0:T(8,128)(2,1)S(1)}, u32[]{:S(2)}, u32[]{:S(2)}) collective-permute-start(bf16[512,1024]{1,0:T(8,128)(2,1)} %hold.20.refs_3_.refs_4_.refs_1_), channel_id=1, source_target_pairs={{0,2},{1,3},{2,0},{3,1},{4,6},{5,7},{6,4},{7,5},{8,10},{9,11},{10,... | collective-permute-start | bytes 3145736 | tf_op jit(solution)/shard_map/ppermute | solution.py:890
  18.5 28.1 %collective-permute-start.3 = (bf16[512,1024]{1,0:T(8,128)(2,1)}, bf16[512,1024]{1,0:T(8,128)(2,1)S(1)}, u32[]{:S(2)}, u32[]{:S(2)}) collective-permute-start(bf16[512,1024]{1,0:T(8,128)(2,1)} %hold.20.refs_3_.refs_4_.refs_1_), channel_id=1, source_target_pairs={{0,1},{1,0},{2,3},{3,2},{4,5},{5,4},{6,7},{7,6},{8,9},{9,8},{10,11... | collective-permute-start | bytes 3145736 | tf_op jit(solution)/shard_map/ppermute | solution.py:890
  50.3 14.2 %collective-permute-start.8 = (bf16[256,1024]{1,0:T(8,128)(2,1)S(1)}, bf16[256,1024]{1,0:T(8,128)(2,1)S(1)}, u32[]{:S(2)}, u32[]{:S(2)}) collective-permute-start(bf16[256,1024]{1,0:T(8,128)(2,1)S(1)} %slice.44), channel_id=1, source_target_pairs={{0,1},{1,0},{2,3},{3,2},{4,5},{5,4},{6,7},{7,6},{8,9},{9,8},{10,11... | collective-permute-start | bytes 1572872 | tf_op jit(solution)/shard_map/ppermute | solution.py:890
  50.9 13.9 %collective-permute-start.7 = (bf16[256,1024]{1,0:T(8,128)(2,1)S(1)}, bf16[256,1024]{1,0:T(8,128)(2,1)S(1)}, u32[]{:S(2)}, u32[]{:S(2)}) collective-permute-start(bf16[256,1024]{1,0:T(8,128)(2,1)S(1)} %slice.43), channel_id=1, source_target_pairs={{0,2},{1,3},{2,0},{3,1},{4,6},{5,7},{6,4},{7,5},{8,10},{9,11},{10,... | collective-permute-start | bytes 1572872 | tf_op jit(solution)/shard_map/ppermute | solution.py:890
  51.2 20.8 %collective-permute-start.6 = (bf16[512,1024]{1,0:T(8,128)(2,1)S(1)}, bf16[512,1024]{1,0:T(8,128)(2,1)S(1)}, u32[]{:S(2)}, u32[]{:S(2)}) collective-permute-start(bf16[512,1024]{1,0:T(8,128)(2,1)S(1)} %copy-done.9), channel_id=1, source_target_pairs={{0,4},{4,0},{8,12},{12,8},{16,20},{20,16},{24,28},{28,24},{1,5},{5... | collective-permute-start | bytes 3145736 | tf_op jit(solution)/shard_map/ppermute | solution.py:893
  69.4 14.8 %collective-permute-start.9 = (bf16[512,1024]{1,0:T(8,128)(2,1)}, bf16[512,1024]{1,0:T(8,128)(2,1)S(1)}, u32[]{:S(2)}, u32[]{:S(2)}) collective-permute-start(bf16[512,1024]{1,0:T(8,128)(2,1)} %constant_dynamic-update-slice_fusion.refs_3_.refs_10_.refs_2_.refs_1_), channel_id=1, source_target_pairs={{0,4},{4,0},{8,12},{12,8},{16,20},{20,16},{24,28},{28,24},{1,5},{5... | collective-permute-start | bytes 3145736 | tf_op jit(solution)/shard_map/ppermute | solution.py:893
  69.4 28.0 %collective-permute-start.10 = (bf16[1,512,1024]{2,1,0:T(8,128)(2,1)}, bf16[1,512,1024]{2,1,0:T(8,128)(2,1)}, u32[]{:S(2)}, u32[]{:S(2)}) collective-permute-start(bf16[1,512,1024]{2,1,0:T(8,128)(2,1)} %get-tuple-element.156.refs_2_.refs_4_), channel_id=1, source_target_pairs={{0,1},{1,0},{2,3},{3,2},{4,5},{5,4},{6,7},{7,6},{8,9},{9,8},{10,11... | collective-permute-start | bytes 3145736 | tf_op jit(solution)/shard_map/ppermute | solution.py:890
  70.9 26.5 %collective-permute-start.11 = (bf16[1,512,1024]{2,1,0:T(8,128)(2,1)}, bf16[1,512,1024]{2,1,0:T(8,128)(2,1)}, u32[]{:S(2)}, u32[]{:S(2)}) collective-permute-start(bf16[1,512,1024]{2,1,0:T(8,128)(2,1)} %get-tuple-element.157.refs_3_.refs_4_), channel_id=1, source_target_pairs={{0,2},{1,3},{2,0},{3,1},{4,6},{5,7},{6,4},{7,5},{8,10},{9,11},{10,... | collective-permute-start | bytes 3145736 | tf_op jit(solution)/shard_map/ppermute | solution.py:890
  97.4 28.4 %collective-permute-start.14 = (bf16[1,512,1024]{2,1,0:T(8,128)(2,1)}, bf16[1,512,1024]{2,1,0:T(8,128)(2,1)}, u32[]{:S(2)}, u32[]{:S(2)}) collective-permute-start(bf16[1,512,1024]{2,1,0:T(8,128)(2,1)} %get-tuple-element.160.refs_2_.refs_6_), channel_id=1, source_target_pairs={{0,2},{1,3},{2,0},{3,1},{4,6},{5,7},{6,4},{7,5},{8,10},{9,11},{10,... | collective-permute-start | bytes 3145736 | tf_op jit(solution)/shard_map/ppermute | solution.py:890
  98.5 27.4 %collective-permute-start.15 = (bf16[1,512,1024]{2,1,0:T(8,128)(2,1)}, bf16[1,512,1024]{2,1,0:T(8,128)(2,1)}, u32[]{:S(2)}, u32[]{:S(2)}) collective-permute-start(bf16[1,512,1024]{2,1,0:T(8,128)(2,1)} %get-tuple-element.161.refs_3_.refs_8_), channel_id=1, source_target_pairs={{0,1},{1,0},{2,3},{3,2},{4,5},{5,4},{6,7},{7,6},{8,9},{9,8},{10,11... | collective-permute-start | bytes 3145736 | tf_op jit(solution)/shard_map/ppermute | solution.py:890
  126.4 25.5 %collective-permute-start.13 = (bf16[1,512,1024]{2,1,0:T(8,128)(2,1)}, bf16[1,512,1024]{2,1,0:T(8,128)(2,1)}, u32[]{:S(2)}, u32[]{:S(2)}) collective-permute-start(bf16[1,512,1024]{2,1,0:T(8,128)(2,1)} %get-tuple-element.156.refs_2_.refs_4_), channel_id=1, source_target_pairs={{0,2},{1,3},{2,0},{3,1},{4,6},{5,7},{6,4},{7,5},{8,10},{9,11},{10,... | collective-permute-start | bytes 3145736 | tf_op jit(solution)/shard_map/ppermute | solution.py:890
  127.5 25.2 %collective-permute-start.12 = (bf16[1,512,1024]{2,1,0:T(8,128)(2,1)}, bf16[1,512,1024]{2,1,0:T(8,128)(2,1)}, u32[]{:S(2)}, u32[]{:S(2)}) collective-permute-start(bf16[1,512,1024]{2,1,0:T(8,128)(2,1)} %get-tuple-element.157.refs_3_.refs_4_), channel_id=1, source_target_pairs={{0,1},{1,0},{2,3},{3,2},{4,5},{5,4},{6,7},{7,6},{8,9},{9,8},{10,11... | collective-permute-start | bytes 3145736 | tf_op jit(solution)/shard_map/ppermute | solution.py:890
  129.0 28.7 %collective-permute-start.18 = (bf16[1,512,1024]{2,1,0:T(8,128)(2,1)}, bf16[1,512,1024]{2,1,0:T(8,128)(2,1)}, u32[]{:S(2)}, u32[]{:S(2)}) collective-permute-start(bf16[1,512,1024]{2,1,0:T(8,128)(2,1)} %get-tuple-element.160.refs_2_.refs_6_), channel_id=1, source_target_pairs={{0,4},{4,0},{8,12},{12,8},{16,20},{20,16},{24,28},{28,24},{1,5},{5... | collective-permute-start | bytes 3145736 | tf_op jit(solution)/shard_map/ppermute | solution.py:893
  146.3 6.9 %collective-permute-start.20 = (bf16[2,512,1024]{2,1,0:T(8,128)(2,1)}, bf16[2,512,1024]{2,1,0:T(8,128)(2,1)}, u32[]{:S(2)}, u32[]{:S(2)}) collective-permute-start(bf16[2,512,1024]{2,1,0:T(8,128)(2,1)} %get-tuple-element.167), channel_id=1, source_target_pairs={{0,4},{4,0},{8,12},{12,8},{16,20},{20,16},{24,28},{28,24},{1,5},{5... | collective-permute-start | bytes 6291464 | tf_op jit(solution)/shard_map/ppermute | solution.py:893
  152.7 21.9 %collective-permute-start.22 = (bf16[1,512,1024]{2,1,0:T(8,128)(2,1)}, bf16[1,512,1024]{2,1,0:T(8,128)(2,1)S(1)}, u32[]{:S(2)}, u32[]{:S(2)}) collective-permute-start(bf16[1,512,1024]{2,1,0:T(8,128)(2,1)} %get-tuple-element.161.refs_3_.refs_8_), channel_id=1, source_target_pairs={{0,4},{4,0},{8,12},{12,8},{16,20},{20,16},{24,28},{28,24},{1,5},{5... | collective-permute-start | bytes 3145736 | tf_op jit(solution)/shard_map/ppermute | solution.py:893
  153.2 21.4 %collective-permute-start.21 = (bf16[1,512,1024]{2,1,0:T(8,128)(2,1)}, bf16[1,512,1024]{2,1,0:T(8,128)(2,1)S(1)}, u32[]{:S(2)}, u32[]{:S(2)}) collective-permute-start(bf16[1,512,1024]{2,1,0:T(8,128)(2,1)} %get-tuple-element.170.refs_2_.refs_8_), channel_id=1, source_target_pairs={{0,4},{4,0},{8,12},{12,8},{16,20},{20,16},{24,28},{28,24},{1,5},{5... | collective-permute-start | bytes 3145736 | tf_op jit(solution)/shard_map/ppermute | solution.py:893
  156.7 32.5 %collective-permute-start.25 = (bf16[512,1024]{1,0:T(8,128)(2,1)}, bf16[512,1024]{1,0:T(8,128)(2,1)}, u32[]{:S(2)}, u32[]{:S(2)}) collective-permute-start(bf16[512,1024]{1,0:T(8,128)(2,1)} %get-tuple-element.180), channel_id=1, source_target_pairs={{0,2},{1,3},{2,0},{3,1},{4,6},{5,7},{6,4},{7,5},{8,10},{9,11},{10,... | collective-permute-start | bytes 3145736 | tf_op jit(solution)/shard_map/ppermute | solution.py:890
  157.7 31.5 %collective-permute-start.24 = (bf16[512,1024]{1,0:T(8,128)(2,1)}, bf16[512,1024]{1,0:T(8,128)(2,1)}, u32[]{:S(2)}, u32[]{:S(2)}) collective-permute-start(bf16[512,1024]{1,0:T(8,128)(2,1)} %get-tuple-element.168.refs_7_), channel_id=1, source_target_pairs={{0,1},{1,0},{2,3},{3,2},{4,5},{5,4},{6,7},{7,6},{8,9},{9,8},{10,11... | collective-permute-start | bytes 3145736 | tf_op jit(solution)/shard_map/ppermute | solution.py:890
  174.4 14.7 %collective-permute-start.23 = (bf16[2,512,1024]{2,1,0:T(8,128)(2,1)}, bf16[2,512,1024]{2,1,0:T(8,128)(2,1)}, u32[]{:S(2)}, u32[]{:S(2)}) collective-permute-start(bf16[2,512,1024]{2,1,0:T(8,128)(2,1)} %get-tuple-element.179), channel_id=1, source_target_pairs={{0,4},{4,0},{8,12},{12,8},{16,20},{20,16},{24,28},{28,24},{1,5},{5... | collective-permute-start | bytes 6291464 | tf_op jit(solution)/shard_map/ppermute | solution.py:893
  194.1 49.3 %collective-permute-start.28 = (bf16[1024,1024]{1,0:T(8,128)(2,1)}, bf16[1024,1024]{1,0:T(8,128)(2,1)S(1)}, u32[]{:S(2)}, u32[]{:S(2)}) collective-permute-start(bf16[1024,1024]{1,0:T(8,128)(2,1)} %merge.10.refs_3_.refs_16_), channel_id=1, source_target_pairs={{0,1},{1,0},{2,3},{3,2},{4,5},{5,4},{6,7},{7,6},{8,9},{9,8},{10,11... | collective-permute-start | bytes 6291464 | tf_op jit(solution)/shard_map/ppermute | solution.py:890
  199.4 47.6 %collective-permute-start.29 = (bf16[1024,1024]{1,0:T(8,128)(2,1)}, bf16[1024,1024]{1,0:T(8,128)(2,1)}, u32[]{:S(2)}, u32[]{:S(2)}) collective-permute-start(bf16[1024,1024]{1,0:T(8,128)(2,1)} %merge.11.refs_17_), channel_id=1, source_target_pairs={{0,2},{1,3},{2,0},{3,1},{4,6},{5,7},{6,4},{7,5},{8,10},{9,11},{10,... | collective-permute-start | bytes 6291464 | tf_op jit(solution)/shard_map/ppermute | solution.py:890
  200.5 46.6 %collective-permute-start.27 = (bf16[2,512,1024]{2,1,0:T(8,128)(2,1)}, bf16[2,512,1024]{2,1,0:T(8,128)(2,1)}, u32[]{:S(2)}, u32[]{:S(2)}) collective-permute-start(bf16[2,512,1024]{2,1,0:T(8,128)(2,1)} %get-tuple-element.195), channel_id=1, source_target_pairs={{0,4},{4,0},{8,12},{12,8},{16,20},{20,16},{24,28},{28,24},{1,5},{5... | collective-permute-start | bytes 6291464 | tf_op jit(solution)/shard_map/ppermute | solution.py:893
  253.6 24.3 %collective-permute-start.31 = (bf16[512,1024]{1,0:T(8,128)(2,1)}, bf16[512,1024]{1,0:T(8,128)(2,1)}, u32[]{:S(2)}, u32[]{:S(2)}) collective-permute-start(bf16[512,1024]{1,0:T(8,128)(2,1)} %get-tuple-element.202), channel_id=1, source_target_pairs={{0,8},{4,12},{8,0},{12,4},{16,24},{20,28},{24,16},{28,20},{1,9},{5... | collective-permute-start | bytes 3145736 | tf_op jit(solution)/shard_map/ppermute | solution.py:893
  280.0 24.1 %collective-permute-start.32 = (bf16[256,1024]{1,0:T(8,128)(2,1)}, bf16[256,1024]{1,0:T(8,128)(2,1)S(1)}, u32[]{:S(2)}, u32[]{:S(2)}) collective-permute-start(bf16[256,1024]{1,0:T(8,128)(2,1)} %merge.12.refs_10_), channel_id=1, source_target_pairs={{0,16},{4,20},{8,24},{12,28},{16,0},{20,4},{24,8},{28,12},{1,17},{... | collective-permute-start | bytes 1572872 | tf_op jit(solution)/shard_map/ppermute | solution.py:893
  283.3 25.5 %collective-permute-start.30 = (bf16[512,1024]{1,0:T(8,128)(2,1)}, bf16[512,1024]{1,0:T(8,128)(2,1)}, u32[]{:S(2)}, u32[]{:S(2)}) collective-permute-start(bf16[512,1024]{1,0:T(8,128)(2,1)} %get-tuple-element.201), channel_id=1, source_target_pairs={{0,4},{4,0},{8,12},{12,8},{16,20},{20,16},{24,28},{28,24},{1,5},{5... | collective-permute-start | bytes 3145736 | tf_op jit(solution)/shard_map/ppermute | solution.py:893
  308.9 26.4 %collective-permute-start.34 = (bf16[256,1024]{1,0:T(8,128)(2,1)}, bf16[256,1024]{1,0:T(8,128)(2,1)}, u32[]{:S(2)}, u32[]{:S(2)}) collective-permute-start(bf16[256,1024]{1,0:T(8,128)(2,1)} %merge.13.refs_4_), channel_id=1, source_target_pairs={{0,16},{4,20},{8,24},{12,28},{16,0},{20,4},{24,8},{28,12},{1,17},{... | collective-permute-start | bytes 1572872 | tf_op jit(solution)/shard_map/ppermute | solution.py:893
  311.6 23.7 %collective-permute-start.35 = (bf16[256,1024]{1,0:T(8,128)(2,1)}, bf16[256,1024]{1,0:T(8,128)(2,1)S(1)}, u32[]{:S(2)}, u32[]{:S(2)}) collective-permute-start(bf16[256,1024]{1,0:T(8,128)(2,1)} %get-tuple-element.207.refs_9_), channel_id=1, source_target_pairs={{0,1},{1,0},{2,3},{3,2},{4,5},{5,4},{6,7},{7,6},{8,9},{9,8},{10,11... | collective-permute-start | bytes 1572872 | tf_op jit(solution)/shard_map/ppermute | solution.py:890
  313.0 22.2 %collective-permute-start.36 = (bf16[256,1024]{1,0:T(8,128)(2,1)}, bf16[256,1024]{1,0:T(8,128)(2,1)}, u32[]{:S(2)}, u32[]{:S(2)}) collective-permute-start(bf16[256,1024]{1,0:T(8,128)(2,1)} %get-tuple-element.208.refs_10_), channel_id=1, source_target_pairs={{0,2},{1,3},{2,0},{3,1},{4,6},{5,7},{6,4},{7,5},{8,10},{9,11},{10,... | collective-permute-start | bytes 1572872 | tf_op jit(solution)/shard_map/ppermute | solution.py:890
  316.6 25.7 %collective-permute-start.37 = (bf16[512,1024]{1,0:T(8,128)(2,1)}, bf16[512,1024]{1,0:T(8,128)(2,1)}, u32[]{:S(2)}, u32[]{:S(2)}) collective-permute-start(bf16[512,1024]{1,0:T(8,128)(2,1)} %get-tuple-element.216), channel_id=1, source_target_pairs={{0,4},{4,0},{8,12},{12,8},{16,20},{20,16},{24,28},{28,24},{1,5},{5... | collective-permute-start | bytes 3145736 | tf_op jit(solution)/shard_map/ppermute | solution.py:893
  334.7 10.9 %collective-permute-start.33 = (bf16[512,1024]{1,0:T(8,128)(2,1)}, bf16[512,1024]{1,0:T(8,128)(2,1)}, u32[]{:S(2)}, u32[]{:S(2)}) collective-permute-start(bf16[512,1024]{1,0:T(8,128)(2,1)} %get-tuple-element.213), channel_id=1, source_target_pairs={{0,4},{4,0},{8,12},{12,8},{16,20},{20,16},{24,28},{28,24},{1,5},{5... | collective-permute-start | bytes 3145736 | tf_op jit(solution)/shard_map/ppermute | solution.py:893
  338.3 29.2 %collective-permute-start.39 = (bf16[512,1024]{1,0:T(8,128)(2,1)}, bf16[512,1024]{1,0:T(8,128)(2,1)}, u32[]{:S(2)}, u32[]{:S(2)}) collective-permute-start(bf16[512,1024]{1,0:T(8,128)(2,1)} %pad_maximum_fusion.refs_11_.refs_1_), channel_id=1, source_target_pairs={{0,8},{4,12},{8,0},{12,4},{16,24},{20,28},{24,16},{28,20},{1,9},{5... | collective-permute-start | bytes 3145736 | tf_op jit(solution)/shard_map/ppermute | solution.py:893
  345.1 25.1 %collective-permute-start.40 = (bf16[512,1024]{1,0:T(8,128)(2,1)}, bf16[512,1024]{1,0:T(8,128)(2,1)}, u32[]{:S(2)}, u32[]{:S(2)}) collective-permute-start(bf16[512,1024]{1,0:T(8,128)(2,1)} %merge.15.refs_3_), channel_id=1, source_target_pairs={{0,1},{1,0},{2,3},{3,2},{4,5},{5,4},{6,7},{7,6},{8,9},{9,8},{10,11... | collective-permute-start | bytes 3145736 | tf_op jit(solution)/shard_map/ppermute | solution.py:890
  348.1 24.9 %collective-permute-start.41 = (bf16[512,1024]{1,0:T(8,128)(2,1)}, bf16[512,1024]{1,0:T(8,128)(2,1)}, u32[]{:S(2)}, u32[]{:S(2)}) collective-permute-start(bf16[512,1024]{1,0:T(8,128)(2,1)} %merge.16.refs_10_), channel_id=1, source_target_pairs={{0,2},{1,3},{2,0},{3,1},{4,6},{5,7},{6,4},{7,5},{8,10},{9,11},{10,... | collective-permute-start | bytes 3145736 | tf_op jit(solution)/shard_map/ppermute | solution.py:890
  349.1 51.1 %collective-permute-start.45 = (bf16[512,1024]{1,0:T(8,128)(2,1)}, bf16[512,1024]{1,0:T(8,128)(2,1)}, u32[]{:S(2)}, u32[]{:S(2)}) collective-permute-start(bf16[512,1024]{1,0:T(8,128)(2,1)} %pad_maximum_fusion.refs_11_.refs_1_), channel_id=1, source_target_pairs={{0,4},{4,0},{8,12},{12,8},{16,20},{20,16},{24,28},{28,24},{1,5},{5... | collective-permute-start | bytes 3145736 | tf_op jit(solution)/shard_map/ppermute | solution.py:893
  373.0 30.8 %collective-permute-start.46 = (bf16[512,1024]{1,0:T(8,128)(2,1)}, bf16[512,1024]{1,0:T(8,128)(2,1)S(1)}, u32[]{:S(2)}, u32[]{:S(2)}) collective-permute-start(bf16[512,1024]{1,0:T(8,128)(2,1)} %get-tuple-element.230.refs_2_), channel_id=1, source_target_pairs={{0,4},{4,0},{8,12},{12,8},{16,20},{20,16},{24,28},{28,24},{1,5},{5... | collective-permute-start | bytes 3145736 | tf_op jit(solution)/shard_map/ppermute | solution.py:893
  376.1 25.7 %collective-permute-start.42 = (bf16[128,1024]{1,0:T(8,128)(2,1)}, bf16[128,1024]{1,0:T(8,128)(2,1)S(1)}, u32[]{:S(2)}, u32[]{:S(2)}) collective-permute-start(bf16[128,1024]{1,0:T(8,128)(2,1)} %get-tuple-element.226.refs_16_), channel_id=1, source_target_pairs={{0,8},{4,12},{8,0},{12,4},{16,24},{20,28},{24,16},{28,20},{1,9},{5... | collective-permute-start | bytes 786440 | tf_op jit(solution)/shard_map/ppermute | solution.py:893
  376.5 26.3 %collective-permute-start.43 = (bf16[128,1024]{1,0:T(8,128)(2,1)}, bf16[128,1024]{1,0:T(8,128)(2,1)S(1)}, u32[]{:S(2)}, u32[]{:S(2)}) collective-permute-start(bf16[128,1024]{1,0:T(8,128)(2,1)} %get-tuple-element.227.refs_17_), channel_id=1, source_target_pairs={{0,16},{4,20},{8,24},{12,28},{16,0},{20,4},{24,8},{28,12},{1,17},{... | collective-permute-start | bytes 786440 | tf_op jit(solution)/shard_map/ppermute | solution.py:893
  377.0 26.8 %collective-permute-start.44 = (bf16[128,1024]{1,0:T(8,128)(2,1)}, bf16[128,1024]{1,0:T(8,128)(2,1)S(1)}, u32[]{:S(2)}, u32[]{:S(2)}) collective-permute-start(bf16[128,1024]{1,0:T(8,128)(2,1)} %get-tuple-element.228.refs_18_), channel_id=1, source_target_pairs={{0,24},{4,28},{8,16},{12,20},{16,8},{20,12},{24,0},{28,4},{1,25},{... | collective-permute-start | bytes 786440 | tf_op jit(solution)/shard_map/ppermute | solution.py:893
  400.2 19.3 %collective-permute-start.47 = (f32[4,1536]{1,0:T(4,128)S(1)}, f32[4,1536]{1,0:T(4,128)S(1)}, u32[]{:S(2)}, u32[]{:S(2)}) collective-permute-start(f32[4,1536]{1,0:T(4,128)S(1)} %bitcast.108), channel_id=1, source_target_pairs={{0,1},{1,0},{2,3},{3,2},{4,5},{5,4},{6,7},{7,6},{8,9},{9,8},{10,11... | collective-permute-start | bytes 73736 | tf_op jit(solution)/shard_map/ppermute | solution.py:890
  401.8 20.2 %collective-permute-start.48 = (f32[4,1536]{1,0:T(4,128)S(1)}, f32[4,1536]{1,0:T(4,128)S(1)}, u32[]{:S(2)}, u32[]{:S(2)}) collective-permute-start(f32[4,1536]{1,0:T(4,128)S(1)} %bitcast.107), channel_id=1, source_target_pairs={{0,2},{1,3},{2,0},{3,1},{4,6},{5,7},{6,4},{7,5},{8,10},{9,11},{10,... | collective-permute-start | bytes 73736 | tf_op jit(solution)/shard_map/ppermute | solution.py:890
  402.8 19.2 %collective-permute-start.49 = (f32[4,1536]{1,0:T(4,128)S(1)}, f32[4,1536]{1,0:T(4,128)S(1)}, u32[]{:S(2)}, u32[]{:S(2)}) collective-permute-start(f32[4,1536]{1,0:T(4,128)S(1)} %bitcast.106), channel_id=1, source_target_pairs={{0,3},{1,2},{2,1},{3,0},{4,7},{5,6},{6,5},{7,4},{8,11},{9,10},{10,... | collective-permute-start | bytes 73736 | tf_op jit(solution)/shard_map/ppermute | solution.py:890
  407.6 22.3 %collective-permute-start.55 = (bf16[128,1024]{1,0:T(8,128)(2,1)}, bf16[128,1024]{1,0:T(8,128)(2,1)S(1)}, u32[]{:S(2)}, u32[]{:S(2)}) collective-permute-start(bf16[128,1024]{1,0:T(8,128)(2,1)} %merge.17.refs_4_), channel_id=1, source_target_pairs={{0,8},{4,12},{8,0},{12,4},{16,24},{20,28},{24,16},{28,20},{1,9},{5... | collective-permute-start | bytes 786440 | tf_op jit(solution)/shard_map/ppermute | solution.py:893
  407.6 14.5 %collective-permute-start.50 = (bf16[128,1024]{1,0:T(8,128)(2,1)}, bf16[128,1024]{1,0:T(8,128)(2,1)S(1)}, u32[]{:S(2)}, u32[]{:S(2)}) collective-permute-start(bf16[128,1024]{1,0:T(8,128)(2,1)} %merge.17.refs_4_), channel_id=1, source_target_pairs={{0,24},{4,28},{8,16},{12,20},{16,8},{20,12},{24,0},{28,4},{1,25},{... | collective-permute-start | bytes 786440 | tf_op jit(solution)/shard_map/ppermute | solution.py:893
  419.5 13.7 %collective-permute-start.54 = (bf16[128,1024]{1,0:T(8,128)(2,1)S(1)}, bf16[128,1024]{1,0:T(8,128)(2,1)S(1)}, u32[]{:S(2)}, u32[]{:S(2)}) collective-permute-start(bf16[128,1024]{1,0:T(8,128)(2,1)S(1)} %copy-done.33), channel_id=1, source_target_pairs={{0,16},{4,20},{8,24},{12,28},{16,0},{20,4},{24,8},{28,12},{1,17},{... | collective-permute-start | bytes 786440 | tf_op jit(solution)/shard_map/ppermute | solution.py:893
  439.4 12.5 %collective-permute-start.59 = (bf16[16,3840]{1,0:T(8,128)(2,1)}, bf16[16,3840]{1,0:T(8,128)(2,1)S(1)}, u32[]{:S(2)}, u32[]{:S(2)}) collective-permute-start(bf16[16,3840]{1,0:T(8,128)(2,1)} %mode_rows.1.refs_1_), channel_id=1, source_target_pairs={{0,24},{4,28},{8,16},{12,20},{16,8},{20,12},{24,0},{28,4},{1,25},{... | collective-permute-start | bytes 368648 | tf_op jit(solution)/shard_map/ppermute | solution.py:893
  440.8 12.4 %collective-permute-start.58 = (bf16[16,3840]{1,0:T(8,128)(2,1)}, bf16[16,3840]{1,0:T(8,128)(2,1)S(1)}, u32[]{:S(2)}, u32[]{:S(2)}) collective-permute-start(bf16[16,3840]{1,0:T(8,128)(2,1)} %mode_rows.1.refs_1_), channel_id=1, source_target_pairs={{0,16},{4,20},{8,24},{12,28},{16,0},{20,4},{24,8},{28,12},{1,17},{... | collective-permute-start | bytes 368648 | tf_op jit(solution)/shard_map/ppermute | solution.py:893
  441.7 11.5 %collective-permute-start.57 = (bf16[16,3840]{1,0:T(8,128)(2,1)}, bf16[16,3840]{1,0:T(8,128)(2,1)S(1)}, u32[]{:S(2)}, u32[]{:S(2)}) collective-permute-start(bf16[16,3840]{1,0:T(8,128)(2,1)} %mode_rows.1.refs_1_), channel_id=1, source_target_pairs={{0,8},{4,12},{8,0},{12,4},{16,24},{20,28},{24,16},{28,20},{1,9},{5... | collective-permute-start | bytes 368648 | tf_op jit(solution)/shard_map/ppermute | solution.py:893
  (83 other events, 422.4 us)

commit v6 on v5

--- a/solution.py
+++ b/solution.py
@@ -454,7 +454,7 @@
 
 
 def attend_back_kernel(
-    oi_ref, o0, o1, pk_ref, pr_ref, e_ref, n1_ref, oi_all, ho_hbm, pg_ref, g0_ref, g1_ref, rel_ref, *scratch
+    o0, o1, pk_ref, pr_ref, e_ref, n1_ref, oi_all, ho_hbm, pg_ref, g0_ref, g1_ref, rel_ref, *scratch
 ):
     pg_all, t_all, ow, ho_ref, sems = scratch
     w = pl.program_id(0)
@@ -469,7 +469,7 @@
         for copy in weights:
             copy.wait()
 
-    hg = mm(oi_ref[...], ow[...], NT).astype(bf16)
+    hg = mm(oi_all[pl.ds(pl.multiple_of(w * WIN, WIN), WIN)], ow[...], NT).astype(bf16)
     pk = pk_ref[...]
     low = lax.broadcasted_iota(jnp.int32, (WIN, 128), 1) < 64
     for p in range(2):
@@ -519,7 +519,6 @@
         "attend_back",
         rows // WIN,
         [
-            (out_in, rows_of(D)),
             (weight[0], HBM),
             (weight[1], HBM),
             (packed, rows_of(2 * QKV)),
@@ -540,6 +539,7 @@
         after,
         flops=13e9,
         moved=20e6,
+        vmem=18,
     )
 
 
@@ -773,32 +773,38 @@
     return run(mode_rows_kernel, "mode_rows", 1, ins, outs, (), (), [mp])[0]
 
 
-def mode_final_kernel(dp_ref, own_ref, other_ref, ada_ref, bias_ref, class_ref, rel_ref, rows, *, count):
+def mode_final_kernel(dp_ref, own_ref, other_ref, ada_ref, bias_ref, class_ref, rel_ref, rows, *, count, columns):
     size = own_ref.shape[0] // count
-    columns = ada_ref.shape[1]
-    marks = [0, columns, columns + D, columns + D + 128, columns + 2 * D + 128, columns + 2 * D + 256]
-    for core, ref in enumerate((own_ref, other_ref)):
-        for k in range(count):
-            at = (dp_ref[0] ^ (2 * k + core)) * size
-            rows[pl.ds(pl.multiple_of(at, size), size)] = ref[k * size : (k + 1) * size]
-    modes, classes, rel, cond, index = [rows[:, i:j] for i, j in zip(marks, marks[1:])]
-    ada_ref[...] = mm(cond, modes, TN)
-    bias_ref[...] = jnp.sum(modes.astype(f32), axis=0)
-    lane = lax.broadcasted_iota(jnp.int32, index.shape, 1).astype(f32)
-    hot = jnp.where(lane == index[:, :1].astype(f32), 1.0, 0.0).astype(bf16)
-    class_ref[...] = mm(hot, classes, TN)[: class_ref.shape[0]]
-    total = rel[:size].astype(f32)
-    for i in range(1, 2 * count):
-        total = total + rel[i * size : (i + 1) * size].astype(f32)
-    rel_ref[...] = total[: rel_ref.shape[0], : rel_ref.shape[1]]
+    i, width = pl.program_id(0), ada_ref.shape[1]
+    marks = [columns, columns + D, columns + D + 128, columns + 2 * D + 128, columns + 2 * D + 256]
+
+    @pl.when(i == 0)
+    def _():
+        for core, ref in enumerate((own_ref, other_ref)):
+            for k in range(count):
+                at = (dp_ref[0] ^ (2 * k + core)) * size
+                rows[pl.ds(pl.multiple_of(at, size), size)] = ref[k * size : (k + 1) * size]
+        classes, rel, _, index = [rows[:, i:j] for i, j in zip(marks, marks[1:])]
+        lane = lax.broadcasted_iota(jnp.int32, index.shape, 1).astype(f32)
+        hot = jnp.where(lane == index[:, :1].astype(f32), 1.0, 0.0).astype(bf16)
+        class_ref[...] = mm(hot, classes, TN)[: class_ref.shape[0]]
+        total = rel[:size].astype(f32)
+        for k in range(1, 2 * count):
+            total = total + rel[k * size : (k + 1) * size].astype(f32)
+        rel_ref[...] = total[: rel_ref.shape[0], : rel_ref.shape[1]]
+        bias_ref[...] = jnp.sum(rows[:, :columns].astype(f32), axis=0)
+
+    modes = rows[:, pl.ds(pl.multiple_of(i * width, width), width)]
+    ada_ref[...] = mm(rows[:, marks[2] : marks[3]], modes, TN)
 
 
 def mode_final(dp, own, other, count, columns, class_count, rel_shape):
     size, width = own.shape
-    outs = [(shape(dims, f32), whole(*dims)) for dims in ((D, columns), (columns,), (class_count, D), rel_shape)]
-    kernel = partial(mode_final_kernel, count=count)
+    outs = [(shape((D, columns), f32), pl.BlockSpec((D, columns // 3), lambda i, *_: (0, i)))]
+    outs += [(shape(dims, f32), whole(*dims)) for dims in ((columns,), (class_count, D), rel_shape)]
+    kernel = partial(mode_final_kernel, count=count, columns=columns)
     ins = [(own, whole(size, width)), (other, whole(size, width))]
-    return run(kernel, "mode_final", 1, ins, outs, [pltpu.VMEM((2 * size, width), bf16)], (), [dp], vmem=32)
+    return run(kernel, "mode_final", 3, ins, outs, [pltpu.VMEM((2 * size, width), bf16)], (), [dp], vmem=32)
 
 
 def silu_plain(values):
@@ -899,6 +905,8 @@
     def cat(a, b, axis=0):
         return jnp.concatenate([a, b], axis=axis)
 
+    cut = HALF // 2
+
     pre_cond = condition(timesteps, classes, class_table)
     cond_low = silu_plain(pre_cond).astype(bf16)
     mode_cols = jnp.einsum("mwd,de->mwe", cond_low, ada_weight, preferred_element_type=f32) + ada_bias.astype(f32)
@@ -931,7 +939,7 @@
         own_lengths, normed_one, modes, attn_w[1], tables[1], query_hot, [down1]
     )
     adx, ady = hold([adx, ady], [heads[1]])
-    ad = cat(adx, ady)
+    (ad,) = merge([(Moved(adx), None, 0, 0, cut), (Moved(ady), None, -cut, cut, HALF)])
     up0, down0 = hold([up0, down0], [ad])
     x_up, y_down = px(up0), py(down0)
     attn_w.append([ad, Moved(pc(ad))])
@@ -981,14 +989,6 @@
     middle_grad, out_in, turn_sums = turn_step(
         pre, feed_w, middle, attn_out, cotangent, modes, [last_x, last_y]
     )
-    still = [[[(v.array if isinstance(v, Moved) else v, at) for v, at in half] for half in halves] for halves in feed_w]
-    output, out_sums = out_step(hid, still, middle, cotangent, modes, [turn_sums])
-    last_x, last_y = arrive([px(last_x), py(last_y)], [out_sums])
-    z_row = z.reshape(1)
-    terms = [mine[0], Moved(other[0]), *[Moved(v.reshape(2, HALF, D)) for v in (last_x, last_y)]]
-    feed_keep, feed_sent = merge_parts(terms, z_row, n_z, 2)
-    z_one, z_two = swap_dp(2), swap_dp(4)
-
     own_pre = jnp.take(pre_cond.transpose(1, 0, 2), order, axis=0).reshape(4 * micro, D)
     share = 1.0 / (1.0 + jnp.exp(-own_pre))
     class_col = jnp.pad(classes.T.reshape(-1, 1).astype(bf16), ((0, 0), (0, 127)))
@@ -1003,34 +1003,37 @@
         )
         a_other[r] = pc(sent)
 
-    cut = HALF // 2
-
     def a_pair(r, start):
         return [(a_mine[r], None, start), (Moved(a_other[r]), None, start)]
 
-    back_step(3, [feed_keep])
-    (feed_got,) = arrive([z_one(feed_sent)], [packed_grad[3]])
+    back_step(3, [turn_sums])
+    last_x, last_y = arrive([px(last_x), py(last_y)], [packed_grad[3]])
+    z_row = z.reshape(1)
+    terms = [mine[0], Moved(other[0]), *[Moved(v.reshape(2, HALF, D)) for v in (last_x, last_y)]]
+    feed_keep, feed_sent = merge_parts(terms, z_row, n_z, 2)
+    z_one, z_two = swap_dp(2), swap_dp(4)
+
+    back_step(1, [feed_keep])
+    (feed_got,) = arrive([z_one(feed_sent)], [packed_grad[1]])
     (feed_sent,) = merge([(feed_keep, None, cut), (Moved(feed_got), None, cut)], rows=cut)
-    back_step(1, [packed_grad[3], feed_sent])
-    (feed_two,) = arrive([z_two(feed_sent)], [packed_grad[1]])
+    a_diag_x, a_diag_y = merge(a_pair(3, 0), a_pair(3, cut), rows=cut, after=[feed_sent])
+    back_step(2, [feed_sent, a_diag_x, a_diag_y, slope, cond_rel])
+    feed_two, a_diag_x, a_diag_y = arrive([z_two(feed_sent), px(a_diag_x), py(a_diag_y)], [packed_grad[2]])
     (feed_one,) = merge([(feed_keep, None, 0), (Moved(feed_got), None, 0), (Moved(feed_two), None, 0)], rows=cut)
-    a_diag_x, a_diag_y = merge(a_pair(3, 0), a_pair(3, cut), rows=cut, after=[feed_one])
-    back_step(2, [a_diag_x, a_diag_y, slope, cond_rel])
-    feed_two, a_diag_x, a_diag_y = arrive([z_two(feed_one), px(a_diag_x), py(a_diag_y)], [packed_grad[2]])
+    (a_last_x,) = merge(a_pair(1, 0) + [(Moved(a_diag_y), None, -cut, cut, HALF)], after=[feed_one])
+    (a_last_y,) = merge(a_pair(2, 0) + [(Moved(a_diag_x), None, 0, 0, cut)], after=[a_last_x])
+    back_step(0, [feed_one, a_last_y])
+    feed_two, a_last_x, a_last_y = arrive([z_two(feed_one), px(a_last_x), py(a_last_y)], [packed_grad[0]])
     feed_even = cat(feed_one, feed_two)
-    (a_last_x,) = merge(a_pair(1, 0) + [(Moved(a_diag_y), None, -cut, cut, HALF)])
-    (a_last_y,) = merge(a_pair(2, 0) + [(Moved(a_diag_x), None, 0, 0, cut)], after=[a_last_x])
-    back_step(0, [packed_grad[2], a_last_y, feed_even])
-    feed_odd, a_last_x, a_last_y = arrive([z_one(feed_even), px(a_last_x), py(a_last_y)], [packed_grad[0]])
 
     def exchange(parts):
         return [swap_dp(2 * k)(v) for k, v in enumerate(parts) if k]
 
     attn_parts = merge_parts([a_mine[0], *map(Moved, (a_other[0], a_last_x, a_last_y))], z_row, n_z, n_z)
-    token_grads, last_sums = last_step(packed_grad, attn_w, tokens, modes, middle_grad, attn_parts)
-    attn_got = exchange(attn_parts)
-    feed_other = [pc(feed_even), pc(feed_odd)]
-    *attn_got, feed_other[0], feed_other[1] = arrive(attn_got + feed_other, [last_sums])
+    still = [[[(v.array if isinstance(v, Moved) else v, at) for v, at in half] for half in halves] for halves in feed_w]
+    output, out_sums = out_step(hid, still, middle, cotangent, modes, [*attn_parts, feed_even])
+    token_grads, last_sums = last_step(packed_grad, attn_w, tokens, modes, middle_grad, [out_sums])
+    feed_odd, *attn_got = arrive([z_one(feed_even), *exchange(attn_parts)], [last_sums])
     (attn_own,) = merge([(v, None, 0) for v in (attn_parts[0], *attn_got)], rows=HALF // n_z)
 
     place = jnp.stack([core, z])
@@ -1038,13 +1041,13 @@
     messages = [lax.dynamic_index_in_dim(mode_grad, mp ^ r, axis=0, keepdims=False) for r in range(4)]
     rel_grid = hold(rel_grid, [attn_own])
     rel_part = jnp.pad(rel_sums(jnp.stack(rel_grid), core), ((0, 0), (0, 4 * (micro - 1)), (0, 128 - rel_bias.shape[1])))
-    grad_up, grad_down = feed_final(place, feed_even, Moved(feed_odd), *map(Moved, feed_other))
-    *messages[1:], attn_far = arrive(
-        [by_rel[r](messages[r]) for r in (1, 2, 3)] + [swap_dp(6)(attn_own)], [attn_own, grad_up]
+    *messages[1:], attn_far, feed_even_other, feed_odd_other = arrive(
+        [by_rel[r](messages[r]) for r in (1, 2, 3)] + [swap_dp(6)(attn_own), pc(feed_even), pc(feed_odd)], [attn_own]
     )
     mode_low, *shares = mode_shares(messages, rel_part, ada_weight)
+    grad_up, grad_down = feed_final(place, feed_even, Moved(feed_odd), Moved(feed_even_other), Moved(feed_odd_other))
     *shares[1:], attn_two, attn_one = arrive(
-        [by_rel[r](shares[r]) for r in (1, 2, 3)] + [swap_dp(4)(attn_own), swap_dp(2)(attn_own)], [attn_far]
+        [by_rel[r](shares[r]) for r in (1, 2, 3)] + [swap_dp(4)(attn_own), swap_dp(2)(attn_own)], [attn_far, grad_up]
     )
     grads = mode_rows(mp.reshape(1), mode_low, shares, slope, cond_rel)
     attn_own = jnp.concatenate([attn_own, attn_one, attn_two, attn_far])

time: 469 us -> 465 us (level)
  local copies, waits for them, and re-layouts: 31.9 us -> 37.3 us
    unnamed x147 -> x146, local copies, waits for them, and re-layouts: 21.9 us -> 27.4 us
    ppermute x27, waiting for transfers between devices: 18 us -> 13.2 us  [swap_mp(): return lambda v: lax.ppermute(v, 'mp', [(i, i ^ bit) for i in range(n_mp)])]
    pallas_call x34 -> x35, Pallas kernels: 326 us -> 322 us  [run(): pl.pallas_call(body, grid_spec=pltpu.PrefetchScalarGridSpec(num_scalar_pr...]
  transfers between devices with their start and end apart: 61 -> 61, of which waited for: 15 -> 12; matrix products, arithmetic and copies ran while one was open for 5% -> 5% of each run, Pallas kernels for 68% -> 68%
where the time goes in v6:
time: 465 us; the launch traced here: 459 us
  Pallas kernels  322 us (69%)
  starting transfers between devices  51.9 us (11%)
  local copies, waits for them, and re-layouts  37.3 us (8%)
  waiting for transfers between devices  29.6 us (6%)
  other arithmetic  8.59 us (2%)
  matrix products  8.14 us (2%)
    pallas_call x35, Pallas kernels, run(): pl.pallas_call(body, grid_spec=pltpu.PrefetchScalarGridSpec(num_scalar_pr...  322 us
    ppermute x27, starting transfers between devices, swap_mp(): return lambda v: lax.ppermute(v, 'mp', [(i, i ^ bit) for i in range(n_mp)])  30.4 us
    unnamed x146, local copies, waits for them, and re-layouts  27.4 us
    ppermute x34, starting transfers between devices, swap_dp(): lax.ppermute(v, ('z', 'core'), [(i, i ^ bit) for i in range(n_dp)])  21.4 us
    ppermute x34, waiting for transfers between devices, swap_dp(): lax.ppermute(v, ('z', 'core'), [(i, i ^ bit) for i in range(n_dp)])  16.4 us
    ppermute x27, waiting for transfers between devices, swap_mp(): return lambda v: lax.ppermute(v, 'mp', [(i, i ^ bit) for i in range(n_mp)])  13.2 us
  transfers between devices with their start and end apart: 61, of which 12 were waited for; matrix products, arithmetic and copies ran while one was open for 5% of the time, Pallas kernels for 68%

profile of v6, /device:TPU:0, one launch (start us, length us, event | category | flops | bytes accessed | tf_op | source)
XLA Modules:
  0.0 459.1 jit_solution(7768138639490266110)
XLA Ops:
  4.0 2.5 fusion.2.refs_3_
  6.7 3.0 collective-permute-start
  11.3 4.2 attn_rows.1
  16.7 1.8 collective-permute-start.4
  21.4 2.1 fusion.5
  24.5 14.6 %attend.4 = (bf16[1280,1024]{1,0:T(8,128)(2,1)S(1)}, bf16[1280,768]{1,0:T(8,128)(2,1)}, bf16[1280,256]{1,0:T(8,128)(2,1)}, bf16[16,320,320]{2,1,0:T(8,128)(2,1)}) custom-call(s32[4]{0:T(128)S(1)} %fusion.19.refs_0_, bf16[4,320,1024]{2,1,0:T(8,128)(2,1)} %refs_12_.3, f32[4,6,1024]{2,1,0:T(8,128)} %reshape.127.refs_2_.refs_14_.refs_15_.refs_13_, ...), custom_call_target="tpu_custom_call" | custom-call | flops 1000 | bytes 1000 | tf_op jit(solution)/shard_map/attend/pallas_call | solution.py:104
  39.2 7.5 %feed_rows.1 = (bf16[1,512,1024]{2,1,0:T(8,128)(2,1)}, bf16[1,512,1024]{2,1,0:T(8,128)(2,1)}, bf16[1,512,1024]{2,1,0:T(8,128)(2,1)}, bf16[1,512,1024]{2,1,0:T(8,128)(2,1)}) custom-call(s32[1]{0:T(128)} %bitcast.8.refs_0_, bf16[1024,1024]{1,0:T(8,128)(2,1)} %refs_1_.5, bf16[1024,1024]{1,0:T(8,128)(2,1)} %refs_2_.3, ...), custom_call_target="tpu_custom_call" | custom-call | flops 1000 | bytes 1000 | tf_op jit(solution)/shard_map/feed_rows/pallas_call | solution.py:104
  51.3 12.2 %attend.5 = (bf16[1280,768]{1,0:T(8,128)(2,1)}, bf16[1280,256]{1,0:T(8,128)(2,1)}, bf16[16,320,320]{2,1,0:T(8,128)(2,1)}) custom-call(s32[4]{0:T(128)S(1)} %fusion.19.refs_0_, bf16[1280,1024]{1,0:T(8,128)(2,1)} %copy-done.2, f32[4,6,1024]{2,1,0:T(8,128)} %reshape.127.refs_2_.refs_14_.refs_15_.refs_13_, bf16[512,1024]{1,0:T(8,128)(2,1)S(1)} %copy-done.14, ...), custom_call_target="tpu_custom_call" | custom-call | flops 1000 | bytes 1000 | tf_op jit(solution)/shard_map/attend/pallas_call | solution.py:104
  71.6 12.2 %attend.6 = (bf16[1280,768]{1,0:T(8,128)(2,1)}, bf16[1280,256]{1,0:T(8,128)(2,1)}, bf16[16,320,320]{2,1,0:T(8,128)(2,1)}) custom-call(s32[4]{0:T(128)S(1)} %fusion.19.refs_0_, bf16[1280,1024]{1,0:T(8,128)(2,1)} %copy-done.2, f32[4,6,1024]{2,1,0:T(8,128)} %reshape.127.refs_2_.refs_14_.refs_15_.refs_13_, bf16[512,1024]{1,0:T(8,128)(2,1)S(1)} %copy-done.12, ...), custom_call_target="tpu_custom_call" | custom-call | flops 1000 | bytes 1000 | tf_op jit(solution)/shard_map/attend/pallas_call | solution.py:104
  83.9 13.1 %attend.7 = (bf16[1280,768]{1,0:T(8,128)(2,1)}, bf16[1280,256]{1,0:T(8,128)(2,1)}, bf16[16,320,320]{2,1,0:T(8,128)(2,1)}) custom-call(s32[4]{0:T(128)S(1)} %fusion.19.refs_0_, bf16[1280,1024]{1,0:T(8,128)(2,1)} %copy-done.2, f32[4,6,1024]{2,1,0:T(8,128)} %reshape.127.refs_2_.refs_14_.refs_15_.refs_13_, ...), custom_call_target="tpu_custom_call" | custom-call | flops 1000 | bytes 1000 | tf_op jit(solution)/shard_map/attend/pallas_call | solution.py:104
  98.6 10.7 %middle.1 = (bf16[1280,1024]{1,0:T(8,128)(2,1)}, f32[1280,1024]{1,0:T(8,128)}, bf16[1280,1024]{1,0:T(8,128)(2,1)S(1)}, bf16[1280,1024]{1,0:T(8,128)(2,1)S(1)}) custom-call(bf16[1280,256]{1,0:T(8,128)(2,1)} %get-tuple-element.143.refs_3_.refs_0_.refs_7_, bf16[1280,256]{1,0:T(8,128)(2,1)} %get-tuple-element.147.refs_7_.refs_2_.refs_1_, ...), custom_call_target="tpu_custom_call" | custom-call | flops 1000 | bytes 1000 | tf_op jit(solution)/shard_map/middle/pallas_call | solution.py:104
  109.3 16.1 %feed.4 = (bf16[1280,1024]{1,0:T(8,128)(2,1)}, bf16[1280,1024]{1,0:T(8,128)(2,1)}, bf16[2,512,1024]{2,1,0:T(8,128)(2,1)}, bf16[2,512,1024]{2,1,0:T(8,128)(2,1)}) custom-call(bf16[1280,1024]{1,0:T(8,128)(2,1)S(1)} %get-tuple-element.153.refs_0_, bf16[1280,1024]{1,0:T(8,128)(2,1)S(1)} %get-tuple-element.154.refs_1_, ...), custom_call_target="tpu_custom_call" | custom-call | flops 1000 | bytes 1000 | tf_op jit(solution)/shard_map/feed/pallas_call | solution.py:104
  131.7 14.2 %feed.5 = (bf16[1280,1024]{1,0:T(8,128)(2,1)}, bf16[1280,1024]{1,0:T(8,128)(2,1)}, bf16[2,512,1024]{2,1,0:T(8,128)(2,1)}, bf16[2,512,1024]{2,1,0:T(8,128)(2,1)}) custom-call(bf16[1280,1024]{1,0:T(8,128)(2,1)S(1)} %get-tuple-element.153.refs_0_, bf16[1280,1024]{1,0:T(8,128)(2,1)S(1)} %copy-done.9, bf16[1,512,1024]{2,1,0:T(8,128)(2,1)} %get-tuple-element.163.refs_2_.refs_10_, ...), custom_call_target="tpu_custom_call" | custom-call | flops 1000 | bytes 1000 | tf_op jit(solution)/shard_map/feed/pallas_call | solution.py:104
  146.1 5.4 %collective-permute-done.13.refs_1_ = bf16[1,512,1024]{2,1,0:T(8,128)(2,1)} collective-permute-done((bf16[1,512,1024]{2,1,0:T(8,128)(2,1)}, bf16[1,512,1024]{2,1,0:T(8,128)(2,1)}, u32[]{:S(2)}, u32[]{:S(2)}) %collective-permute-start.13) | collective-permute-done | bytes 1048608 | tf_op jit(solution)/shard_map/ppermute | solution.py:896
  152.8 3.5 merge.11
  158.8 15.3 %feed.6 = (bf16[1280,1024]{1,0:T(8,128)(2,1)}, bf16[1280,1024]{1,0:T(8,128)(2,1)}, bf16[2,512,1024]{2,1,0:T(8,128)(2,1)}, bf16[2,512,1024]{2,1,0:T(8,128)(2,1)}) custom-call(bf16[1280,1024]{1,0:T(8,128)(2,1)S(1)} %get-tuple-element.153.refs_0_, bf16[1280,1024]{1,0:T(8,128)(2,1)S(1)} %copy-done.10, bf16[1,512,1024]{2,1,0:T(8,128)(2,1)} %get-tuple-element.161.refs_2_.refs_6_, ...), custom_call_target="tpu_custom_call" | custom-call | flops 1000 | bytes 1000 | tf_op jit(solution)/shard_map/feed/pallas_call | solution.py:104
  174.2 14.0 %feed.7 = (bf16[1280,1024]{1,0:T(8,128)(2,1)}, bf16[1280,1024]{1,0:T(8,128)(2,1)}, bf16[2,512,1024]{2,1,0:T(8,128)(2,1)}, bf16[2,512,1024]{2,1,0:T(8,128)(2,1)}) custom-call(bf16[1280,1024]{1,0:T(8,128)(2,1)S(1)} %get-tuple-element.153.refs_0_, bf16[1280,1024]{1,0:T(8,128)(2,1)S(1)} %copy-done.10, bf16[1,512,1024]{2,1,0:T(8,128)(2,1)} %get-tuple-element.171.refs_2_.refs_8_, ...), custom_call_target="tpu_custom_call" | custom-call | flops 1000 | bytes 1000 | tf_op jit(solution)/shard_map/feed/pallas_call | solution.py:104
  188.8 4.9 %merge.12.refs_3_.refs_16_ = bf16[1024,1024]{1,0:T(8,128)(2,1)} custom-call(bf16[1024,1024]{1,0:T(8,128)(2,1)} %bitcast.89, bf16[1024,1024]{1,0:T(8,128)(2,1)} %bitcast.20.refs_1_, bf16[512,1024]{1,0:T(8,128)(2,1)} %get-tuple-element.184.refs_2_), custom_call_target="tpu_custom_call" | custom-call | flops 1000 | bytes 1000 | tf_op jit(solution)/shard_map/merge/pallas_call | solution.py:104
  194.3 4.3 merge.13.refs_17_
  202.1 22.9 %turn.1 = (f32[1280,1024]{1,0:T(8,128)}, bf16[1280,1024]{1,0:T(8,128)(2,1)S(1)}, f32[4,3,1024]{2,1,0:T(4,128)}) custom-call(bf16[1280,1024]{1,0:T(8,128)(2,1)} %get-tuple-element.176.refs_0_, bf16[1280,1024]{1,0:T(8,128)(2,1)} %get-tuple-element.177.refs_1_, bf16[1280,1024]{1,0:T(8,128)(2,1)} %get-tuple-element.178.refs_2_, ...), custom_call_target="tpu_custom_call" | custom-call | flops 1000 | bytes 1000 | tf_op jit(solution)/shard_map/turn/pallas_call | solution.py:104
  225.0 17.2 %attend_back.4 = (bf16[1280,768]{1,0:T(8,128)(2,1)}, bf16[512,1024]{1,0:T(8,128)(2,1)}, bf16[512,1024]{1,0:T(8,128)(2,1)}, f32[2,32,128]{2,1,0:T(8,128)}) custom-call(bf16[512,1024]{1,0:T(8,128)(2,1)} %merge.10.refs_3_.refs_10_.refs_2_.refs_0_, bf16[512,1024]{1,0:T(8,128)(2,1)} %copy-done.17, bf16[1280,768]{1,0:T(8,128)(2,1)} %get-tuple-element.191.refs_2_, ...), custom_call_target="tpu_custom_call" | custom-call | flops 1000 | bytes 1000 | tf_op jit(solution)/shard_map/attend_back/pallas_call | solution.py:104
  242.3 4.0 collective-permute-done.29.refs_1_
  246.2 5.4 %merge_parts.2 = (bf16[512,1024]{1,0:T(8,128)(2,1)}, bf16[512,1024]{1,0:T(8,128)(2,1)}) custom-call(s32[1]{0:T(128)} %bitcast.18.refs_0_, bf16[2,512,1024]{2,1,0:T(8,128)(2,1)} %get-tuple-element.189.refs_1_.refs_5_, bf16[2,512,1024]{2,1,0:T(8,128)(2,1)} %collective-permute-done.27.refs_2_.refs_6_, bf16[2,512,1024]{2,1,0:T(8,128)(2,1)} %bitcast.23.refs_3_.refs_7_, ...), custom_call_target="tpu_custom_call" | custom-call | flops 1000 | bytes 1000 | tf_op jit(solution)/shard_map/merge_parts/pallas_call | solution.py:104
  255.8 16.4 %attend_back.5 = (bf16[1280,768]{1,0:T(8,128)(2,1)}, bf16[512,1024]{1,0:T(8,128)(2,1)}, bf16[512,1024]{1,0:T(8,128)(2,1)}, f32[2,32,128]{2,1,0:T(8,128)}) custom-call(bf16[512,1024]{1,0:T(8,128)(2,1)} %get-tuple-element.146.refs_3_.refs_6_.refs_0_, bf16[512,1024]{1,0:T(8,128)(2,1)} %copy-done.15, bf16[1280,768]{1,0:T(8,128)(2,1)} %get-tuple-element.199.refs_2_, ...), custom_call_target="tpu_custom_call" | custom-call | flops 1000 | bytes 1000 | tf_op jit(solution)/shard_map/attend_back/pallas_call | solution.py:104
  272.2 3.7 collective-permute-done.30.refs_0_
  276.6 2.1 merge.14.refs_4_.refs_8_
  278.8 2.6 collective-permute-start.31
  281.4 2.7 merge.15
  290.9 16.3 %attend_back.6 = (bf16[1280,768]{1,0:T(8,128)(2,1)}, bf16[512,1024]{1,0:T(8,128)(2,1)}, bf16[512,1024]{1,0:T(8,128)(2,1)}, f32[2,32,128]{2,1,0:T(8,128)}) custom-call(bf16[512,1024]{1,0:T(8,128)(2,1)} %get-tuple-element.148.refs_3_.refs_8_.refs_0_, bf16[512,1024]{1,0:T(8,128)(2,1)} %copy-done.16, bf16[1280,768]{1,0:T(8,128)(2,1)} %get-tuple-element.206.refs_2_, ...), custom_call_target="tpu_custom_call" | custom-call | flops 1000 | bytes 1000 | tf_op jit(solution)/shard_map/attend_back/pallas_call | solution.py:104
  308.6 2.3 merge.16.refs_3_.refs_8_
  310.9 2.8 merge.17.refs_3_
  314.3 2.8 merge.18.refs_9_
  318.3 16.5 %attend_back.7 = (bf16[1280,768]{1,0:T(8,128)(2,1)}, bf16[512,1024]{1,0:T(8,128)(2,1)}, bf16[512,1024]{1,0:T(8,128)(2,1)}, f32[2,32,128]{2,1,0:T(8,128)}) custom-call(bf16[512,1024]{1,0:T(8,128)(2,1)} %hold.19.refs_3_.refs_4_.refs_0_, bf16[512,1024]{1,0:T(8,128)(2,1)} %get-tuple-element.142.refs_4_.refs_5_.refs_1_, ...), custom_call_target="tpu_custom_call" | custom-call | flops 1000 | bytes 1000 | tf_op jit(solution)/shard_map/attend_back/pallas_call | solution.py:104
  335.0 8.5 %collective-permute-done.38.refs_0_ = bf16[256,1024]{1,0:T(8,128)(2,1)S(1)} collective-permute-done((bf16[256,1024]{1,0:T(8,128)(2,1)S(1)}, bf16[256,1024]{1,0:T(8,128)(2,1)S(1)}, u32[]{:S(2)}, u32[]{:S(2)}) %collective-permute-start.38) | collective-permute-done | bytes 524320 | tf_op jit(solution)/shard_map/ppermute | solution.py:899
  346.5 3.3 merge_parts.3
  351.6 2.6 collective-permute-start.44
  354.2 18.1 %output.1 = (bf16[4,320,1024]{2,1,0:T(8,128)(2,1)}, f32[4,1,1024]{2,1,0:T(1,128)}) custom-call(bf16[1280,1024]{1,0:T(8,128)(2,1)} %get-tuple-element.160.refs_2_.refs_6_.refs_0_, bf16[1280,1024]{1,0:T(8,128)(2,1)} %get-tuple-element.170.refs_6_.refs_1_, bf16[1280,1024]{1,0:T(8,128)(2,1)} %get-tuple-element.172.refs_2_, ...), custom_call_target="tpu_custom_call" | custom-call | flops 1000 | bytes 1000 | tf_op jit(solution)/shard_map/output/pallas_call | solution.py:104
  372.3 18.1 %last.1 = (bf16[4,320,1024]{2,1,0:T(8,128)(2,1)}, f32[4,2,1024]{2,1,0:T(2,128)}) custom-call(bf16[1280,768]{1,0:T(8,128)(2,1)} %get-tuple-element.220.refs_3_.refs_0_, bf16[1280,768]{1,0:T(8,128)(2,1)} %get-tuple-element.201.refs_1_, bf16[1280,768]{1,0:T(8,128)(2,1)} %get-tuple-element.210.refs_3_.refs_2_, ...), custom_call_target="tpu_custom_call" | custom-call | flops 1000 | bytes 1000 | tf_op jit(solution)/shard_map/last/pallas_call | solution.py:104
  397.8 2.0 merge.19.refs_6_.refs_4_
  405.4 2.0 convolution_bitcast_fusion
  409.4 1.7 collective-permute-start.54
  413.1 3.8 mode_shares.1
  420.5 7.5 %feed_final.1 = (f32[1024,1024]{1,0:T(8,128)}, f32[1024,1024]{1,0:T(8,128)}) custom-call(s32[2]{0:T(128)S(1)} %pad_add_fusion.refs_0_, bf16[512,1024]{1,0:T(8,128)(2,1)} %copy-done.37, bf16[512,1024]{1,0:T(8,128)(2,1)} %get-tuple-element.236.refs_2_, bf16[512,1024]{1,0:T(8,128)(2,1)S(1)} %copy-done.32, bf16[512,1024]{1,0:T(8,128)(2,1)S(1)} %copy-done.34), custom_call_target="tpu_custom_call" | custom-call | flops 1000 | bytes 1000 | tf_op jit(solution)/shard_map/feed_final/pallas_call | solution.py:104
  430.9 2.1 mode_rows.1.refs_1_
  434.2 5.0 %collective-permute-start.58 = (bf16[16,3840]{1,0:T(8,128)(2,1)}, bf16[16,3840]{1,0:T(8,128)(2,1)S(1)}, u32[]{:S(2)}, u32[]{:S(2)}) collective-permute-start(bf16[16,3840]{1,0:T(8,128)(2,1)} %mode_rows.1.refs_1_), channel_id=1, source_target_pairs={{0,16},{4,20},{8,24},{12,28},{16,0},{20,4},{24,8},{28,12},{1,17},{... | collective-permute-start | bytes 368648 | tf_op jit(solution)/shard_map/ppermute | solution.py:899
  441.4 5.9 %attn_final.1 = (f32[1024,768]{1,0:T(8,128)}, f32[256,1024]{1,0:T(8,128)}) custom-call(s32[2]{0:T(128)S(1)} %pad_add_fusion.refs_0_, bf16[512,1024]{1,0:T(8,128)(2,1)} %copy-done.40, bf16[512,1024]{1,0:T(8,128)(2,1)S(1)} %copy-done.26), custom_call_target="tpu_custom_call" | custom-call | flops 1000 | bytes 1000 | tf_op jit(solution)/shard_map/attn_final/pallas_call | solution.py:104
  451.1 1.8 collective-permute-done.60.refs_2_
  453.7 5.1 %mode_final.1 = (f32[1024,1536]{1,0:T(8,128)}, f32[1536]{0:T(1024)}, f32[101,1024]{1,0:T(8,128)}, f32[4,39]{1,0:T(4,128)}) custom-call(s32[1]{0:T(128)} %bitcast.38.refs_0_, bf16[64,3840]{1,0:T(8,128)(2,1)} %copy-done.43, bf16[64,3840]{1,0:T(8,128)(2,1)} %copy-done.48), custom_call_target="tpu_custom_call" | custom-call | flops 1000 | bytes 1000 | tf_op jit(solution)/shard_map/mode_final/pallas_call | solution.py:104
  (332 shorter events, 90.1 us)
Async XLA Ops:
  6.7 9.0 %collective-permute-start = (f32[4,1664]{1,0:T(4,128)S(1)}, f32[4,1664]{1,0:T(4,128)S(1)}, u32[]{:S(2)}, u32[]{:S(2)}) collective-permute-start(f32[4,1664]{1,0:T(4,128)S(1)} %get-tuple-element.291), channel_id=1, source_target_pairs={{0,1},{1,0},{2,3},{3,2},{4,5},{5,4},{6,7},{7,6},{8,9},{9,8},{10,11... | collective-permute-start | bytes 79880 | tf_op jit(solution)/shard_map/ppermute | solution.py:896
  16.7 30.0 %collective-permute-start.4 = (bf16[512,1024]{1,0:T(8,128)(2,1)}, bf16[512,1024]{1,0:T(8,128)(2,1)S(1)}, u32[]{:S(2)}, u32[]{:S(2)}) collective-permute-start(bf16[512,1024]{1,0:T(8,128)(2,1)} %hold.19.refs_3_.refs_4_.refs_0_), channel_id=1, source_target_pairs={{0,2},{1,3},{2,0},{3,1},{4,6},{5,7},{6,4},{7,5},{8,10},{9,11},{10,... | collective-permute-start | bytes 3145736 | tf_op jit(solution)/shard_map/ppermute | solution.py:896
  18.5 28.2 %collective-permute-start.3 = (bf16[512,1024]{1,0:T(8,128)(2,1)}, bf16[512,1024]{1,0:T(8,128)(2,1)S(1)}, u32[]{:S(2)}, u32[]{:S(2)}) collective-permute-start(bf16[512,1024]{1,0:T(8,128)(2,1)} %hold.19.refs_3_.refs_4_.refs_0_), channel_id=1, source_target_pairs={{0,1},{1,0},{2,3},{3,2},{4,5},{5,4},{6,7},{7,6},{8,9},{9,8},{10,11... | collective-permute-start | bytes 3145736 | tf_op jit(solution)/shard_map/ppermute | solution.py:896
  50.5 14.2 %collective-permute-start.8 = (bf16[256,1024]{1,0:T(8,128)(2,1)S(1)}, bf16[256,1024]{1,0:T(8,128)(2,1)S(1)}, u32[]{:S(2)}, u32[]{:S(2)}) collective-permute-start(bf16[256,1024]{1,0:T(8,128)(2,1)S(1)} %slice.44), channel_id=1, source_target_pairs={{0,1},{1,0},{2,3},{3,2},{4,5},{5,4},{6,7},{7,6},{8,9},{9,8},{10,11... | collective-permute-start | bytes 1572872 | tf_op jit(solution)/shard_map/ppermute | solution.py:896
  51.1 13.9 %collective-permute-start.7 = (bf16[256,1024]{1,0:T(8,128)(2,1)S(1)}, bf16[256,1024]{1,0:T(8,128)(2,1)S(1)}, u32[]{:S(2)}, u32[]{:S(2)}) collective-permute-start(bf16[256,1024]{1,0:T(8,128)(2,1)S(1)} %slice.43), channel_id=1, source_target_pairs={{0,2},{1,3},{2,0},{3,1},{4,6},{5,7},{6,4},{7,5},{8,10},{9,11},{10,... | collective-permute-start | bytes 1572872 | tf_op jit(solution)/shard_map/ppermute | solution.py:896
  51.3 20.3 %collective-permute-start.6 = (bf16[512,1024]{1,0:T(8,128)(2,1)S(1)}, bf16[512,1024]{1,0:T(8,128)(2,1)S(1)}, u32[]{:S(2)}, u32[]{:S(2)}) collective-permute-start(bf16[512,1024]{1,0:T(8,128)(2,1)S(1)} %copy-done.12), channel_id=1, source_target_pairs={{0,4},{4,0},{8,12},{12,8},{16,20},{20,16},{24,28},{28,24},{1,5},{5... | collective-permute-start | bytes 3145736 | tf_op jit(solution)/shard_map/ppermute | solution.py:899
  69.0 14.8 %collective-permute-start.9 = (bf16[512,1024]{1,0:T(8,128)(2,1)}, bf16[512,1024]{1,0:T(8,128)(2,1)S(1)}, u32[]{:S(2)}, u32[]{:S(2)}) collective-permute-start(bf16[512,1024]{1,0:T(8,128)(2,1)} %merge.10.refs_3_.refs_10_.refs_2_.refs_0_), channel_id=1, source_target_pairs={{0,4},{4,0},{8,12},{12,8},{16,20},{20,16},{24,28},{28,24},{1,5},{5... | collective-permute-start | bytes 3145736 | tf_op jit(solution)/shard_map/ppermute | solution.py:899
  69.0 28.0 %collective-permute-start.10 = (bf16[1,512,1024]{2,1,0:T(8,128)(2,1)}, bf16[1,512,1024]{2,1,0:T(8,128)(2,1)}, u32[]{:S(2)}, u32[]{:S(2)}) collective-permute-start(bf16[1,512,1024]{2,1,0:T(8,128)(2,1)} %get-tuple-element.157.refs_2_.refs_4_), channel_id=1, source_target_pairs={{0,1},{1,0},{2,3},{3,2},{4,5},{5,4},{6,7},{7,6},{8,9},{9,8},{10,11... | collective-permute-start | bytes 3145736 | tf_op jit(solution)/shard_map/ppermute | solution.py:896
  70.5 26.5 %collective-permute-start.11 = (bf16[1,512,1024]{2,1,0:T(8,128)(2,1)}, bf16[1,512,1024]{2,1,0:T(8,128)(2,1)}, u32[]{:S(2)}, u32[]{:S(2)}) collective-permute-start(bf16[1,512,1024]{2,1,0:T(8,128)(2,1)} %get-tuple-element.158.refs_3_.refs_4_), channel_id=1, source_target_pairs={{0,2},{1,3},{2,0},{3,1},{4,6},{5,7},{6,4},{7,5},{8,10},{9,11},{10,... | collective-permute-start | bytes 3145736 | tf_op jit(solution)/shard_map/ppermute | solution.py:896
  97.1 28.4 %collective-permute-start.14 = (bf16[1,512,1024]{2,1,0:T(8,128)(2,1)}, bf16[1,512,1024]{2,1,0:T(8,128)(2,1)}, u32[]{:S(2)}, u32[]{:S(2)}) collective-permute-start(bf16[1,512,1024]{2,1,0:T(8,128)(2,1)} %get-tuple-element.161.refs_2_.refs_6_), channel_id=1, source_target_pairs={{0,2},{1,3},{2,0},{3,1},{4,6},{5,7},{6,4},{7,5},{8,10},{9,11},{10,... | collective-permute-start | bytes 3145736 | tf_op jit(solution)/shard_map/ppermute | solution.py:896
  98.1 27.4 %collective-permute-start.15 = (bf16[1,512,1024]{2,1,0:T(8,128)(2,1)}, bf16[1,512,1024]{2,1,0:T(8,128)(2,1)}, u32[]{:S(2)}, u32[]{:S(2)}) collective-permute-start(bf16[1,512,1024]{2,1,0:T(8,128)(2,1)} %get-tuple-element.162.refs_3_.refs_8_), channel_id=1, source_target_pairs={{0,1},{1,0},{2,3},{3,2},{4,5},{5,4},{6,7},{7,6},{8,9},{9,8},{10,11... | collective-permute-start | bytes 3145736 | tf_op jit(solution)/shard_map/ppermute | solution.py:896
  126.1 25.5 %collective-permute-start.13 = (bf16[1,512,1024]{2,1,0:T(8,128)(2,1)}, bf16[1,512,1024]{2,1,0:T(8,128)(2,1)}, u32[]{:S(2)}, u32[]{:S(2)}) collective-permute-start(bf16[1,512,1024]{2,1,0:T(8,128)(2,1)} %get-tuple-element.157.refs_2_.refs_4_), channel_id=1, source_target_pairs={{0,2},{1,3},{2,0},{3,1},{4,6},{5,7},{6,4},{7,5},{8,10},{9,11},{10,... | collective-permute-start | bytes 3145736 | tf_op jit(solution)/shard_map/ppermute | solution.py:896
  127.1 25.2 %collective-permute-start.12 = (bf16[1,512,1024]{2,1,0:T(8,128)(2,1)}, bf16[1,512,1024]{2,1,0:T(8,128)(2,1)}, u32[]{:S(2)}, u32[]{:S(2)}) collective-permute-start(bf16[1,512,1024]{2,1,0:T(8,128)(2,1)} %get-tuple-element.158.refs_3_.refs_4_), channel_id=1, source_target_pairs={{0,1},{1,0},{2,3},{3,2},{4,5},{5,4},{6,7},{7,6},{8,9},{9,8},{10,11... | collective-permute-start | bytes 3145736 | tf_op jit(solution)/shard_map/ppermute | solution.py:896
  128.6 28.6 %collective-permute-start.18 = (bf16[1,512,1024]{2,1,0:T(8,128)(2,1)}, bf16[1,512,1024]{2,1,0:T(8,128)(2,1)}, u32[]{:S(2)}, u32[]{:S(2)}) collective-permute-start(bf16[1,512,1024]{2,1,0:T(8,128)(2,1)} %get-tuple-element.161.refs_2_.refs_6_), channel_id=1, source_target_pairs={{0,4},{4,0},{8,12},{12,8},{16,20},{20,16},{24,28},{28,24},{1,5},{5... | collective-permute-start | bytes 3145736 | tf_op jit(solution)/shard_map/ppermute | solution.py:899
  152.3 21.9 %collective-permute-start.22 = (bf16[1,512,1024]{2,1,0:T(8,128)(2,1)}, bf16[1,512,1024]{2,1,0:T(8,128)(2,1)S(1)}, u32[]{:S(2)}, u32[]{:S(2)}) collective-permute-start(bf16[1,512,1024]{2,1,0:T(8,128)(2,1)} %get-tuple-element.162.refs_3_.refs_8_), channel_id=1, source_target_pairs={{0,4},{4,0},{8,12},{12,8},{16,20},{20,16},{24,28},{28,24},{1,5},{5... | collective-permute-start | bytes 3145736 | tf_op jit(solution)/shard_map/ppermute | solution.py:899
  152.8 21.4 %collective-permute-start.21 = (bf16[1,512,1024]{2,1,0:T(8,128)(2,1)}, bf16[1,512,1024]{2,1,0:T(8,128)(2,1)S(1)}, u32[]{:S(2)}, u32[]{:S(2)}) collective-permute-start(bf16[1,512,1024]{2,1,0:T(8,128)(2,1)} %get-tuple-element.171.refs_2_.refs_8_), channel_id=1, source_target_pairs={{0,4},{4,0},{8,12},{12,8},{16,20},{20,16},{24,28},{28,24},{1,5},{5... | collective-permute-start | bytes 3145736 | tf_op jit(solution)/shard_map/ppermute | solution.py:899
  156.3 32.5 %collective-permute-start.25 = (bf16[512,1024]{1,0:T(8,128)(2,1)}, bf16[512,1024]{1,0:T(8,128)(2,1)}, u32[]{:S(2)}, u32[]{:S(2)}) collective-permute-start(bf16[512,1024]{1,0:T(8,128)(2,1)} %get-tuple-element.183), channel_id=1, source_target_pairs={{0,2},{1,3},{2,0},{3,1},{4,6},{5,7},{6,4},{7,5},{8,10},{9,11},{10,... | collective-permute-start | bytes 3145736 | tf_op jit(solution)/shard_map/ppermute | solution.py:896
  157.3 31.5 %collective-permute-start.24 = (bf16[512,1024]{1,0:T(8,128)(2,1)}, bf16[512,1024]{1,0:T(8,128)(2,1)}, u32[]{:S(2)}, u32[]{:S(2)}) collective-permute-start(bf16[512,1024]{1,0:T(8,128)(2,1)} %get-tuple-element.169.refs_7_), channel_id=1, source_target_pairs={{0,1},{1,0},{2,3},{3,2},{4,5},{5,4},{6,7},{7,6},{8,9},{9,8},{10,11... | collective-permute-start | bytes 3145736 | tf_op jit(solution)/shard_map/ppermute | solution.py:896
  174.1 14.7 %collective-permute-start.23 = (bf16[2,512,1024]{2,1,0:T(8,128)(2,1)}, bf16[2,512,1024]{2,1,0:T(8,128)(2,1)}, u32[]{:S(2)}, u32[]{:S(2)}) collective-permute-start(bf16[2,512,1024]{2,1,0:T(8,128)(2,1)} %get-tuple-element.182), channel_id=1, source_target_pairs={{0,4},{4,0},{8,12},{12,8},{16,20},{20,16},{24,28},{28,24},{1,5},{5... | collective-permute-start | bytes 6291464 | tf_op jit(solution)/shard_map/ppermute | solution.py:899
  193.8 48.5 %collective-permute-start.28 = (bf16[1024,1024]{1,0:T(8,128)(2,1)}, bf16[1024,1024]{1,0:T(8,128)(2,1)}, u32[]{:S(2)}, u32[]{:S(2)}) collective-permute-start(bf16[1024,1024]{1,0:T(8,128)(2,1)} %merge.12.refs_3_.refs_16_), channel_id=1, source_target_pairs={{0,1},{1,0},{2,3},{3,2},{4,5},{5,4},{6,7},{7,6},{8,9},{9,8},{10,11... | collective-permute-start | bytes 6291464 | tf_op jit(solution)/shard_map/ppermute | solution.py:896
  198.6 47.6 %collective-permute-start.29 = (bf16[1024,1024]{1,0:T(8,128)(2,1)}, bf16[1024,1024]{1,0:T(8,128)(2,1)}, u32[]{:S(2)}, u32[]{:S(2)}) collective-permute-start(bf16[1024,1024]{1,0:T(8,128)(2,1)} %merge.13.refs_17_), channel_id=1, source_target_pairs={{0,2},{1,3},{2,0},{3,1},{4,6},{5,7},{6,4},{7,5},{8,10},{9,11},{10,... | collective-permute-start | bytes 6291464 | tf_op jit(solution)/shard_map/ppermute | solution.py:896
  199.7 46.6 %collective-permute-start.27 = (bf16[2,512,1024]{2,1,0:T(8,128)(2,1)}, bf16[2,512,1024]{2,1,0:T(8,128)(2,1)}, u32[]{:S(2)}, u32[]{:S(2)}) collective-permute-start(bf16[2,512,1024]{2,1,0:T(8,128)(2,1)} %get-tuple-element.190), channel_id=1, source_target_pairs={{0,4},{4,0},{8,12},{12,8},{16,20},{20,16},{24,28},{28,24},{1,5},{5... | collective-permute-start | bytes 6291464 | tf_op jit(solution)/shard_map/ppermute | solution.py:899
  251.6 24.3 %collective-permute-start.30 = (bf16[512,1024]{1,0:T(8,128)(2,1)}, bf16[512,1024]{1,0:T(8,128)(2,1)}, u32[]{:S(2)}, u32[]{:S(2)}) collective-permute-start(bf16[512,1024]{1,0:T(8,128)(2,1)} %get-tuple-element.198), channel_id=1, source_target_pairs={{0,8},{4,12},{8,0},{12,4},{16,24},{20,28},{24,16},{28,20},{1,9},{5... | collective-permute-start | bytes 3145736 | tf_op jit(solution)/shard_map/ppermute | solution.py:899
  253.9 27.4 %collective-permute-start.32 = (bf16[512,1024]{1,0:T(8,128)(2,1)}, bf16[512,1024]{1,0:T(8,128)(2,1)}, u32[]{:S(2)}, u32[]{:S(2)}) collective-permute-start(bf16[512,1024]{1,0:T(8,128)(2,1)} %get-tuple-element.203), channel_id=1, source_target_pairs={{0,4},{4,0},{8,12},{12,8},{16,20},{20,16},{24,28},{28,24},{1,5},{5... | collective-permute-start | bytes 3145736 | tf_op jit(solution)/shard_map/ppermute | solution.py:899
  278.8 29.0 %collective-permute-start.31 = (bf16[256,1024]{1,0:T(8,128)(2,1)}, bf16[256,1024]{1,0:T(8,128)(2,1)}, u32[]{:S(2)}, u32[]{:S(2)}) collective-permute-start(bf16[256,1024]{1,0:T(8,128)(2,1)} %merge.14.refs_4_.refs_8_), channel_id=1, source_target_pairs={{0,16},{4,20},{8,24},{12,28},{16,0},{20,4},{24,8},{28,12},{1,17},{... | collective-permute-start | bytes 1572872 | tf_op jit(solution)/shard_map/ppermute | solution.py:899
  284.1 23.7 %collective-permute-start.33 = (bf16[256,1024]{1,0:T(8,128)(2,1)}, bf16[256,1024]{1,0:T(8,128)(2,1)S(1)}, u32[]{:S(2)}, u32[]{:S(2)}) collective-permute-start(bf16[256,1024]{1,0:T(8,128)(2,1)} %get-tuple-element.204.refs_9_), channel_id=1, source_target_pairs={{0,1},{1,0},{2,3},{3,2},{4,5},{5,4},{6,7},{7,6},{8,9},{9,8},{10,11... | collective-permute-start | bytes 1572872 | tf_op jit(solution)/shard_map/ppermute | solution.py:896
  285.6 22.2 %collective-permute-start.34 = (bf16[256,1024]{1,0:T(8,128)(2,1)}, bf16[256,1024]{1,0:T(8,128)(2,1)}, u32[]{:S(2)}, u32[]{:S(2)}) collective-permute-start(bf16[256,1024]{1,0:T(8,128)(2,1)} %get-tuple-element.205.refs_10_), channel_id=1, source_target_pairs={{0,2},{1,3},{2,0},{3,1},{4,6},{5,7},{6,4},{7,5},{8,10},{9,11},{10,... | collective-permute-start | bytes 1572872 | tf_op jit(solution)/shard_map/ppermute | solution.py:896
  289.2 21.8 %collective-permute-start.36 = (bf16[512,1024]{1,0:T(8,128)(2,1)}, bf16[512,1024]{1,0:T(8,128)(2,1)}, u32[]{:S(2)}, u32[]{:S(2)}) collective-permute-start(bf16[512,1024]{1,0:T(8,128)(2,1)} %get-tuple-element.216), channel_id=1, source_target_pairs={{0,4},{4,0},{8,12},{12,8},{16,20},{20,16},{24,28},{28,24},{1,5},{5... | collective-permute-start | bytes 3145736 | tf_op jit(solution)/shard_map/ppermute | solution.py:899
  313.7 29.7 %collective-permute-start.39 = (bf16[512,1024]{1,0:T(8,128)(2,1)}, bf16[512,1024]{1,0:T(8,128)(2,1)}, u32[]{:S(2)}, u32[]{:S(2)}) collective-permute-start(bf16[512,1024]{1,0:T(8,128)(2,1)} %merge.17.refs_3_), channel_id=1, source_target_pairs={{0,1},{1,0},{2,3},{3,2},{4,5},{5,4},{6,7},{7,6},{8,9},{9,8},{10,11... | collective-permute-start | bytes 3145736 | tf_op jit(solution)/shard_map/ppermute | solution.py:896
  317.1 26.4 %collective-permute-start.40 = (bf16[512,1024]{1,0:T(8,128)(2,1)}, bf16[512,1024]{1,0:T(8,128)(2,1)}, u32[]{:S(2)}, u32[]{:S(2)}) collective-permute-start(bf16[512,1024]{1,0:T(8,128)(2,1)} %merge.18.refs_9_), channel_id=1, source_target_pairs={{0,2},{1,3},{2,0},{3,1},{4,6},{5,7},{6,4},{7,5},{8,10},{9,11},{10,... | collective-permute-start | bytes 3145736 | tf_op jit(solution)/shard_map/ppermute | solution.py:896
  318.0 25.4 %collective-permute-start.38 = (bf16[256,1024]{1,0:T(8,128)(2,1)S(1)}, bf16[256,1024]{1,0:T(8,128)(2,1)S(1)}, u32[]{:S(2)}, u32[]{:S(2)}) collective-permute-start(bf16[256,1024]{1,0:T(8,128)(2,1)S(1)} %copy-done.38), channel_id=1, source_target_pairs={{0,16},{4,20},{8,24},{12,28},{16,0},{20,4},{24,8},{28,12},{1,17},{... | collective-permute-start | bytes 1572872 | tf_op jit(solution)/shard_map/ppermute | solution.py:899
  334.9 11.6 %collective-permute-start.37 = (bf16[512,1024]{1,0:T(8,128)(2,1)}, bf16[512,1024]{1,0:T(8,128)(2,1)S(1)}, u32[]{:S(2)}, u32[]{:S(2)}) collective-permute-start(bf16[512,1024]{1,0:T(8,128)(2,1)} %get-tuple-element.219), channel_id=1, source_target_pairs={{0,4},{4,0},{8,12},{12,8},{16,20},{20,16},{24,28},{28,24},{1,5},{5... | collective-permute-start | bytes 3145736 | tf_op jit(solution)/shard_map/ppermute | solution.py:899
  346.4 45.0 %collective-permute-start.41 = (bf16[512,1024]{1,0:T(8,128)(2,1)S(1)}, bf16[512,1024]{1,0:T(8,128)(2,1)}, u32[]{:S(2)}, u32[]{:S(2)}) collective-permute-start(bf16[512,1024]{1,0:T(8,128)(2,1)S(1)} %pad_maximum_fusion.refs_19_.refs_1_), channel_id=1, source_target_pairs={{0,8},{4,12},{8,0},{12,4},{16,24},{20,28},{24,16},{28,20},{1,9},{5... | collective-permute-start | bytes 3145736 | tf_op jit(solution)/shard_map/ppermute | solution.py:899
  349.8 41.5 %collective-permute-start.42 = (bf16[128,1024]{1,0:T(8,128)(2,1)}, bf16[128,1024]{1,0:T(8,128)(2,1)S(1)}, u32[]{:S(2)}, u32[]{:S(2)}) collective-permute-start(bf16[128,1024]{1,0:T(8,128)(2,1)} %get-tuple-element.224.refs_16_), channel_id=1, source_target_pairs={{0,8},{4,12},{8,0},{12,4},{16,24},{20,28},{24,16},{28,20},{1,9},{5... | collective-permute-start | bytes 786440 | tf_op jit(solution)/shard_map/ppermute | solution.py:899
  351.5 39.8 %collective-permute-start.43 = (bf16[128,1024]{1,0:T(8,128)(2,1)}, bf16[128,1024]{1,0:T(8,128)(2,1)S(1)}, u32[]{:S(2)}, u32[]{:S(2)}) collective-permute-start(bf16[128,1024]{1,0:T(8,128)(2,1)} %get-tuple-element.225.refs_17_), channel_id=1, source_target_pairs={{0,16},{4,20},{8,24},{12,28},{16,0},{20,4},{24,8},{28,12},{1,17},{... | collective-permute-start | bytes 786440 | tf_op jit(solution)/shard_map/ppermute | solution.py:899
  351.6 39.8 %collective-permute-start.44 = (bf16[128,1024]{1,0:T(8,128)(2,1)}, bf16[128,1024]{1,0:T(8,128)(2,1)S(1)}, u32[]{:S(2)}, u32[]{:S(2)}) collective-permute-start(bf16[128,1024]{1,0:T(8,128)(2,1)} %get-tuple-element.226.refs_18_), channel_id=1, source_target_pairs={{0,24},{4,28},{8,16},{12,20},{16,8},{20,12},{24,0},{28,4},{1,25},{... | collective-permute-start | bytes 786440 | tf_op jit(solution)/shard_map/ppermute | solution.py:899
  354.2 57.0 %collective-permute-start.49 = (bf16[512,1024]{1,0:T(8,128)(2,1)S(1)}, bf16[512,1024]{1,0:T(8,128)(2,1)S(1)}, u32[]{:S(2)}, u32[]{:S(2)}) collective-permute-start(bf16[512,1024]{1,0:T(8,128)(2,1)S(1)} %pad_maximum_fusion.refs_19_.refs_1_), channel_id=1, source_target_pairs={{0,4},{4,0},{8,12},{12,8},{16,20},{20,16},{24,28},{28,24},{1,5},{5... | collective-permute-start | bytes 3145736 | tf_op jit(solution)/shard_map/ppermute | solution.py:899
  392.2 19.0 %collective-permute-start.50 = (bf16[512,1024]{1,0:T(8,128)(2,1)}, bf16[512,1024]{1,0:T(8,128)(2,1)S(1)}, u32[]{:S(2)}, u32[]{:S(2)}) collective-permute-start(bf16[512,1024]{1,0:T(8,128)(2,1)} %get-tuple-element.236.refs_2_), channel_id=1, source_target_pairs={{0,4},{4,0},{8,12},{12,8},{16,20},{20,16},{24,28},{28,24},{1,5},{5... | collective-permute-start | bytes 3145736 | tf_op jit(solution)/shard_map/ppermute | solution.py:899
  395.3 9.2 %collective-permute-start.45 = (f32[4,1536]{1,0:T(4,128)}, f32[4,1536]{1,0:T(4,128)}, u32[]{:S(2)}, u32[]{:S(2)}) collective-permute-start(f32[4,1536]{1,0:T(4,128)} %bitcast.86), channel_id=1, source_target_pairs={{0,1},{1,0},{2,3},{3,2},{4,5},{5,4},{6,7},{7,6},{8,9},{9,8},{10,11... | collective-permute-start | bytes 73736 | tf_op jit(solution)/shard_map/ppermute | solution.py:896
  396.8 11.2 %collective-permute-start.46 = (f32[4,1536]{1,0:T(4,128)}, f32[4,1536]{1,0:T(4,128)}, u32[]{:S(2)}, u32[]{:S(2)}) collective-permute-start(f32[4,1536]{1,0:T(4,128)} %bitcast.85), channel_id=1, source_target_pairs={{0,2},{1,3},{2,0},{3,1},{4,6},{5,7},{6,4},{7,5},{8,10},{9,11},{10,... | collective-permute-start | bytes 73736 | tf_op jit(solution)/shard_map/ppermute | solution.py:896
  399.8 11.4 %collective-permute-start.48 = (bf16[128,1024]{1,0:T(8,128)(2,1)}, bf16[128,1024]{1,0:T(8,128)(2,1)}, u32[]{:S(2)}, u32[]{:S(2)}) collective-permute-start(bf16[128,1024]{1,0:T(8,128)(2,1)} %merge.19.refs_6_.refs_4_), channel_id=1, source_target_pairs={{0,24},{4,28},{8,16},{12,20},{16,8},{20,12},{24,0},{28,4},{1,25},{... | collective-permute-start | bytes 786440 | tf_op jit(solution)/shard_map/ppermute | solution.py:899
  408.0 19.9 %collective-permute-start.55 = (bf16[128,1024]{1,0:T(8,128)(2,1)S(1)}, bf16[128,1024]{1,0:T(8,128)(2,1)}, u32[]{:S(2)}, u32[]{:S(2)}) collective-permute-start(bf16[128,1024]{1,0:T(8,128)(2,1)S(1)} %copy-done.41), channel_id=1, source_target_pairs={{0,8},{4,12},{8,0},{12,4},{16,24},{20,28},{24,16},{28,20},{1,9},{5... | collective-permute-start | bytes 786440 | tf_op jit(solution)/shard_map/ppermute | solution.py:899
  409.4 18.5 %collective-permute-start.54 = (bf16[128,1024]{1,0:T(8,128)(2,1)S(1)}, bf16[128,1024]{1,0:T(8,128)(2,1)}, u32[]{:S(2)}, u32[]{:S(2)}) collective-permute-start(bf16[128,1024]{1,0:T(8,128)(2,1)S(1)} %copy-done.41), channel_id=1, source_target_pairs={{0,16},{4,20},{8,24},{12,28},{16,0},{20,4},{24,8},{28,12},{1,17},{... | collective-permute-start | bytes 786440 | tf_op jit(solution)/shard_map/ppermute | solution.py:899
  416.9 11.1 %collective-permute-start.51 = (f32[16,1152]{1,0:T(8,128)}, f32[16,1152]{1,0:T(8,128)S(1)}, u32[]{:S(2)}, u32[]{:S(2)}) collective-permute-start(f32[16,1152]{1,0:T(8,128)} %get-tuple-element.248), channel_id=1, source_target_pairs={{0,1},{1,0},{2,3},{3,2},{4,5},{5,4},{6,7},{7,6},{8,9},{9,8},{10,11... | collective-permute-start | bytes 221192 | tf_op jit(solution)/shard_map/ppermute | solution.py:896
  418.4 9.6 %collective-permute-start.52 = (f32[16,1152]{1,0:T(8,128)}, f32[16,1152]{1,0:T(8,128)S(1)}, u32[]{:S(2)}, u32[]{:S(2)}) collective-permute-start(f32[16,1152]{1,0:T(8,128)} %get-tuple-element.249), channel_id=1, source_target_pairs={{0,2},{1,3},{2,0},{3,1},{4,6},{5,7},{6,4},{7,5},{8,10},{9,11},{10,... | collective-permute-start | bytes 221192 | tf_op jit(solution)/shard_map/ppermute | solution.py:896
  433.0 14.2 %collective-permute-start.59 = (bf16[16,3840]{1,0:T(8,128)(2,1)}, bf16[16,3840]{1,0:T(8,128)(2,1)S(1)}, u32[]{:S(2)}, u32[]{:S(2)}) collective-permute-start(bf16[16,3840]{1,0:T(8,128)(2,1)} %mode_rows.1.refs_1_), channel_id=1, source_target_pairs={{0,24},{4,28},{8,16},{12,20},{16,8},{20,12},{24,0},{28,4},{1,25},{... | collective-permute-start | bytes 368648 | tf_op jit(solution)/shard_map/ppermute | solution.py:899
  434.2 14.1 %collective-permute-start.58 = (bf16[16,3840]{1,0:T(8,128)(2,1)}, bf16[16,3840]{1,0:T(8,128)(2,1)S(1)}, u32[]{:S(2)}, u32[]{:S(2)}) collective-permute-start(bf16[16,3840]{1,0:T(8,128)(2,1)} %mode_rows.1.refs_1_), channel_id=1, source_target_pairs={{0,16},{4,20},{8,24},{12,28},{16,0},{20,4},{24,8},{28,12},{1,17},{... | collective-permute-start | bytes 368648 | tf_op jit(solution)/shard_map/ppermute | solution.py:899
  439.2 9.2 %collective-permute-start.57 = (bf16[16,3840]{1,0:T(8,128)(2,1)}, bf16[16,3840]{1,0:T(8,128)(2,1)S(1)}, u32[]{:S(2)}, u32[]{:S(2)}) collective-permute-start(bf16[16,3840]{1,0:T(8,128)(2,1)} %mode_rows.1.refs_1_), channel_id=1, source_target_pairs={{0,8},{4,12},{8,0},{12,4},{16,24},{20,28},{24,16},{28,20},{1,9},{5... | collective-permute-start | bytes 368648 | tf_op jit(solution)/shard_map/ppermute | solution.py:899
  (83 other events, 449.4 us)
